TPU v7x, 32 devices: a whole 2x2x4 slice. The times are simulated.
32 devices in a mesh: bucket: 4 (over x, core), blk: 8 (over z, y).
Axes of the slice: x: 2, y: 2, z: 4, core: 2. Of those that a mesh axis runs over, the one named last changes fastest.
Arguments:
- tokens: bfloat16 [4, 1024, 2, 2048], P('bucket', 'blk'), may hold values from -6 to 6
- lengths: int32 [4, 2], P('bucket'), may hold values from 256 to 1024, as said below
- norm_gain: float32 [2048], P(('bucket', 'blk')), may hold values from 0.5 to 1.5
- norm_shift: float32 [2048], P(('bucket', 'blk')), may hold values from -4 to 4
- inward_weight: float32 [2048, 6144], P(('bucket', 'blk')), may hold values from -0.1875 to 0.1875
- inward_bias: float32 [4608], P(('bucket', 'blk')), may hold values from -0.3125 to 0.3125
- outward_weight: float32 [2048, 2048], P(('bucket', 'blk')), may hold values from -2 to 2
- gate_up_weight: float32 [2048, 11264], P(('bucket', 'blk')), may hold values from -0.125 to 0.125
- down_weight: float32 [5632, 2048], P(('bucket', 'blk')), may hold values from -0.078125 to 0.078125
- cotangent: bfloat16 [4, 1024, 2, 2048], P('bucket', 'blk'), may hold values from -6 to 6
Outputs:
- layer_out: bfloat16 [4, 1024, 2, 2048], P('bucket', 'blk')
- tokens_grad: bfloat16 [4, 1024, 2, 2048], P('bucket', 'blk')
- gain_grad: float32 [2048], P(('bucket', 'blk'))
- shift_grad: float32 [2048], P(('bucket', 'blk'))
- inward_grad: float32 [2048, 6144], P(('bucket', 'blk'))
- bias_grad: float32 [4608], P(('bucket', 'blk'))
- outward_grad: float32 [2048, 2048], P(('bucket', 'blk'))
- gate_up_grad: float32 [2048, 11264], P(('bucket', 'blk'))
- down_grad: float32 [5632, 2048], P(('bucket', 'blk'))
Inputs may be any that keep to these rules, and one draw needn't show every extreme that they name: In every bucket one sequence, which one drawn from the seed, is exactly 1024 tokens long; the other lengths lean toward the short end. Positions at or past a sequence's length are padding.
All inputs are finite; a program needn't handle non-finite values.
Results may differ from a plain program's by a relative error of at most 0.014.
The roundings to bfloat16 on the way count: a program that leaves them out, or rounds other values in their place, can miss the bound.
Values may be sent and summed in bfloat16 or wider, within the bound.
A program may use at most 512 MiB of HBM per device.

v0:
```python
import jax
import jax.numpy as jnp
from jax import lax
from jax.sharding import PartitionSpec as P

HEADS = 32
HEAD_DIM = 64
ROT = 16


epsilon = 1e-05
rotary_base = 10000.0
masked_score = -1e30


def shifted(value, axis, by):
    count = lax.axis_size(axis)
    pairs = [(i, i + by) for i in range(count) if 0 <= i + by < count]
    return lax.ppermute(value, axis, pairs)


def shifted_2(value, axis, steps):
    count = lax.axis_size(axis)
    pairs = [(source, (source + steps) % count) for source in range(count)]
    return lax.ppermute(value, axis, pairs)


def keep_same(value):
    return value


def transposed_times(left, right):
    return lax.dot_general(
        left, right, (((1,), (1,)), ((), ())), preferred_element_type=jnp.float32
    )


def times_transposed(left, right):
    return lax.dot_general(
        left, right, (((0,), (0,)), ((), ())), preferred_element_type=jnp.float32
    )


def rotary_tables(positions):
    half_rot = ROT // 2
    frequency = rotary_base ** (-(2.0 * jnp.arange(half_rot).astype(jnp.float32)) / ROT)
    angles = positions.astype(jnp.float32)[:, None] * frequency[None, :]
    return (jnp.cos(angles), jnp.sin(angles))


def rotate(values, cos_table, sine_table):
    half_rot = ROT // 2
    front_half = values[..., :half_rot]
    back_half = values[..., half_rot:ROT]
    return jnp.concatenate(
        [
            front_half * cos_table - back_half * sine_table,
            back_half * cos_table + front_half * sine_table,
            values[..., ROT:],
        ],
        axis=-1,
    )


def split_pairs(packed):
    rows_here, seq_count, both_width = packed.shape
    half_width = both_width // 2
    keys_part = packed[..., :half_width].reshape(rows_here, seq_count, HEADS, HEAD_DIM)
    values_part = packed[..., half_width:].reshape(rows_here, seq_count, HEADS, HEAD_DIM)
    return (keys_part, values_part)


def block_scores(queries, key_block, query_start, key_start):
    scores = jnp.einsum("tshd,ushd->shtu", queries, key_block, preferred_element_type=jnp.float32)
    query_pos = query_start + jnp.arange(queries.shape[0], dtype=jnp.int32)
    key_pos = key_start + jnp.arange(key_block.shape[0], dtype=jnp.int32)
    allowed = (key_pos[None, :] <= query_pos[:, None])[None, None]
    return (jnp.where(allowed, scores, masked_score), allowed)


def forward_block(carried, queries, key_block, value_block, query_start, key_start):
    running_max, running_sum, weighted = carried
    scores, allowed = block_scores(queries, key_block, query_start, key_start)
    new_max = jnp.maximum(running_max, jnp.max(scores, axis=-1))
    rescale = jnp.exp(running_max - new_max)
    weights = jnp.where(allowed, jnp.exp(scores - new_max[..., None]), 0.0)
    running_sum = running_sum * rescale + jnp.sum(weights, axis=-1)
    update = jnp.einsum(
        "shtu,ushd->tshd",
        weights.astype(jnp.bfloat16),
        value_block,
        preferred_element_type=jnp.float32,
    )
    weighted = weighted * jnp.transpose(rescale, (2, 0, 1))[..., None] + update
    return (new_max, running_sum, weighted)


def pair_grads(
    queries, out_grads, log_norm, deltas, key_block, value_block, query_start, key_start
):
    scores, allowed = block_scores(queries, key_block, query_start, key_start)
    probability = jnp.where(allowed, jnp.exp(scores - log_norm[..., None]), 0.0)
    value_grad = jnp.einsum(
        "shtu,tshd->ushd",
        probability.astype(jnp.bfloat16),
        out_grads,
        preferred_element_type=jnp.float32,
    )
    prob_grad = jnp.einsum(
        "tshd,ushd->shtu", out_grads, value_block, preferred_element_type=jnp.float32
    )
    score_grad = (probability * (prob_grad - deltas[..., None])).astype(jnp.bfloat16)
    query_grad = jnp.einsum(
        "shtu,ushd->tshd", score_grad, key_block, preferred_element_type=jnp.float32
    )
    key_grad = jnp.einsum(
        "shtu,tshd->ushd", score_grad, queries, preferred_element_type=jnp.float32
    )
    return (query_grad, key_grad, value_grad)


def over_blocks(running, incoming, unit_rows, handle):
    total_rows = incoming[0].shape[0]
    block_count = total_rows // unit_rows
    block_rows = total_rows // block_count
    stacked = tuple(
        (member.reshape((block_count, block_rows) + member.shape[1:]) for member in incoming)
    )

    def visit(carried, element):
        block_index, members = element
        return (handle(carried, members, block_index * block_rows), None)

    running, unused = lax.scan(visit, running, (jnp.arange(block_count, dtype=jnp.int32), stacked))
    return running


def shards(
    tokens,
    lengths,
    norm_gain,
    norm_shift,
    inward_weight,
    inward_bias,
    outward_weight,
    gate_up_weight,
    down_weight,
    cotangent,
):
    group_len = tokens.shape[1]
    seq_count = tokens.shape[2]
    model_width = tokens.shape[3]
    row_total = group_len * seq_count
    block_total = lax.axis_size("blk")
    position = lax.axis_index("blk")
    own_start = position * group_len
    longest = jnp.max(lengths[0])
    active = own_start < longest
    gathered = (
        lax.all_gather(inward_weight.astype(jnp.bfloat16), ("bucket", "blk"), axis=0, tiled=True),
        lax.all_gather(outward_weight.astype(jnp.bfloat16), ("bucket", "blk"), axis=0, tiled=True),
        lax.all_gather(gate_up_weight.astype(jnp.bfloat16), ("bucket", "blk"), axis=0, tiled=True),
        lax.all_gather(down_weight.astype(jnp.bfloat16), ("bucket", "blk"), axis=0, tiled=True),
        lax.all_gather(norm_gain.astype(jnp.bfloat16), ("bucket", "blk"), axis=0, tiled=True),
        lax.all_gather(norm_shift.astype(jnp.bfloat16), ("bucket", "blk"), axis=0, tiled=True),
        lax.all_gather(inward_bias.astype(jnp.bfloat16), ("bucket", "blk"), axis=0, tiled=True),
    )
    inward_full, outward_full, gate_up_full, down_full, gain_full, shift_full, bias_full = gathered
    inputs = tokens.reshape(row_total, model_width).astype(jnp.float32)
    centred = inputs - jnp.mean(inputs, axis=-1, keepdims=True)
    variance = jnp.mean(centred * centred, axis=-1, keepdims=True)
    inverse = lax.rsqrt(variance + epsilon)
    normal_hat = centred * inverse
    normed_low = (
        normal_hat * gain_full.astype(jnp.float32) + shift_full.astype(jnp.float32)
    ).astype(jnp.bfloat16)
    bias_float = bias_full.astype(jnp.float32)
    key_bias = jnp.pad(
        bias_float[2 * model_width :].reshape(HEADS, ROT), ((0, 0), (0, HEAD_DIM - ROT))
    ).reshape(model_width)
    full_bias = jnp.concatenate(
        [bias_float[:model_width], key_bias, bias_float[model_width : 2 * model_width]]
    )
    projected = jnp.dot(normed_low, inward_full, preferred_element_type=jnp.float32) + full_bias
    projected = projected.reshape(group_len, seq_count, 3, HEADS, HEAD_DIM)
    cos_table, sine_table = rotary_tables(own_start + jnp.arange(group_len, dtype=jnp.int32))
    cos_table = cos_table[:, None, None, :]
    sine_table = sine_table[:, None, None, :]
    query_scale = HEAD_DIM ** (-0.5)
    queries = (rotate(projected[:, :, 0], cos_table, sine_table) * query_scale).astype(jnp.bfloat16)
    keys_low = rotate(projected[:, :, 1], cos_table, sine_table).astype(jnp.bfloat16)
    values_low = projected[:, :, 2].astype(jnp.bfloat16)
    packed = jnp.concatenate(
        [
            keys_low.reshape(group_len, seq_count, model_width),
            values_low.reshape(group_len, seq_count, model_width),
        ],
        axis=-1,
    )

    def forward_handle(carried, members, key_start):
        keys_part, values_part = split_pairs(members[0])
        needed = active & (key_start <= own_start + group_len - 1)

        def forward_compute(state_in):
            return forward_block(state_in, queries, keys_part, values_part, own_start, key_start)

        return lax.cond(needed, forward_compute, keep_same, carried)

    start_state = (
        jnp.full((seq_count, HEADS, group_len), masked_score, jnp.float32),
        jnp.zeros((seq_count, HEADS, group_len), jnp.float32),
        jnp.zeros((group_len, seq_count, HEADS, HEAD_DIM), jnp.float32),
    )
    running_max, running_sum, weighted = over_blocks(
        start_state, (lax.all_gather(packed, "blk", axis=0, tiled=True),), group_len, forward_handle
    )
    bounded = jnp.maximum(running_sum, 1.0)
    log_norm = running_max + jnp.log(bounded)
    attended = weighted / jnp.transpose(bounded, (2, 0, 1))[..., None]
    attended_rows = attended.astype(jnp.bfloat16).reshape(row_total, model_width)
    gate_up = jnp.dot(normed_low, gate_up_full, preferred_element_type=jnp.float32)
    ff_width = gate_up.shape[1] // 2
    gate_part = gate_up[:, :ff_width]
    up_part = gate_up[:, ff_width:]
    sigmoid_gate = jax.nn.sigmoid(gate_part)
    silu_gate = gate_part * sigmoid_gate
    hidden_low = (silu_gate * up_part).astype(jnp.bfloat16)
    branch = jnp.dot(attended_rows, outward_full, preferred_element_type=jnp.float32) + jnp.dot(
        hidden_low, down_full, preferred_element_type=jnp.float32
    )
    query_pos = own_start + jnp.arange(group_len, dtype=jnp.int32)
    valid_rows = (
        (query_pos[:, None] < lengths[0][None, :]).astype(jnp.float32).reshape(row_total, 1)
    )
    layer_out = (inputs + valid_rows * branch).astype(jnp.bfloat16).reshape(tokens.shape)
    inward_back = gathered[0]
    outward_back = gathered[1]
    gate_up_back = gathered[2]
    down_back = gathered[3]
    gain_float = gathered[4].astype(jnp.float32)
    cotangent_rows = cotangent.reshape(row_total, model_width).astype(jnp.float32)
    branch_grad = (cotangent_rows * valid_rows).astype(jnp.bfloat16)
    hidden_grad = transposed_times(branch_grad, down_back)
    gate_grad = hidden_grad * up_part * (sigmoid_gate + silu_gate * (1.0 - sigmoid_gate))
    up_grad = hidden_grad * silu_gate
    gate_up_grad_low = jnp.concatenate([gate_grad, up_grad], axis=-1).astype(jnp.bfloat16)
    down_term = times_transposed(hidden_low, branch_grad)
    gate_up_term = times_transposed(normed_low, gate_up_grad_low)
    gate_up_sum, down_sum = (
        lax.psum_scatter(gate_up_term, ("bucket", "blk"), scatter_dimension=0, tiled=True),
        lax.psum_scatter(down_term, ("bucket", "blk"), scatter_dimension=0, tiled=True),
    )
    normed_grad = transposed_times(gate_up_grad_low, gate_up_back)
    attended_grad = (
        transposed_times(branch_grad, outward_back)
        .astype(jnp.bfloat16)
        .reshape(group_len, seq_count, HEADS, HEAD_DIM)
    )
    outward_term = times_transposed(attended_rows, branch_grad)
    deltas = jnp.transpose(
        jnp.sum(attended_grad.astype(jnp.float32) * attended, axis=-1), (1, 2, 0)
    )
    grad_zeros = jnp.zeros((group_len, seq_count, 2 * model_width), jnp.float32)
    query_zeros = jnp.zeros((group_len, seq_count, HEADS, HEAD_DIM), jnp.float32)

    def cycle_turn(turn_index, carried):
        visiting, sums_now, grads_now = carried
        owner_index = (position - turn_index) % block_total
        key_start = owner_index * group_len
        needed = active & (owner_index <= position)

        def cycle_compute(sums_in):
            keys_part, values_part = split_pairs(visiting)
            query_part, key_part, value_part = pair_grads(
                queries,
                attended_grad,
                log_norm,
                deltas,
                keys_part,
                values_part,
                own_start,
                key_start,
            )
            merged = jnp.concatenate(
                [
                    key_part.reshape(group_len, seq_count, model_width),
                    value_part.reshape(group_len, seq_count, model_width),
                ],
                axis=-1,
            )
            return (sums_in[0] + merged, sums_in[1] + query_part)

        sums_now, grads_now = lax.cond(needed, cycle_compute, keep_same, (sums_now, grads_now))
        visiting = shifted(visiting, "blk", 1)
        sums_now = shifted_2(sums_now.astype(jnp.bfloat16), "blk", 1).astype(sums_now.dtype)
        return (visiting, sums_now, grads_now)

    unused, pair_sums, query_grads = lax.fori_loop(
        0, block_total, cycle_turn, (packed, grad_zeros, query_zeros)
    )
    key_grad = pair_sums[..., :model_width].reshape(group_len, seq_count, HEADS, HEAD_DIM)
    value_grad = pair_sums[..., model_width:].reshape(group_len, seq_count, HEADS, HEAD_DIM)
    back_sine = -sine_table
    query_back = rotate(query_grads * query_scale, cos_table, back_sine)
    key_back = rotate(key_grad, cos_table, back_sine)
    projected_grad = (
        jnp.stack([query_back, key_back, value_grad], axis=2)
        .reshape(row_total, 3 * model_width)
        .astype(jnp.bfloat16)
    )
    inward_term = times_transposed(normed_low, projected_grad)
    column_sums = jnp.sum(projected_grad.astype(jnp.float32), axis=0)
    key_bias_grad = (
        column_sums[model_width : 2 * model_width]
        .reshape(HEADS, HEAD_DIM)[:, :ROT]
        .reshape(HEADS * ROT)
    )
    bias_term = jnp.concatenate(
        [column_sums[:model_width], column_sums[2 * model_width :], key_bias_grad]
    )
    normed_grad = normed_grad + transposed_times(projected_grad, inward_back)
    gain_term = jnp.sum(normed_grad * normal_hat, axis=0)
    shift_term = jnp.sum(normed_grad, axis=0)
    scaled_grad = normed_grad * gain_float
    input_grad = inverse * (
        scaled_grad
        - jnp.mean(scaled_grad, axis=-1, keepdims=True)
        - normal_hat * jnp.mean(scaled_grad * normal_hat, axis=-1, keepdims=True)
    )
    tokens_grad = (cotangent_rows + input_grad).astype(jnp.bfloat16).reshape(tokens.shape)
    inward_sum, outward_sum, bias_sum, gain_sum, shift_sum = (
        lax.psum_scatter(inward_term, ("bucket", "blk"), scatter_dimension=0, tiled=True),
        lax.psum_scatter(outward_term, ("bucket", "blk"), scatter_dimension=0, tiled=True),
        lax.psum_scatter(bias_term, ("bucket", "blk"), scatter_dimension=0, tiled=True),
        lax.psum_scatter(gain_term, ("bucket", "blk"), scatter_dimension=0, tiled=True),
        lax.psum_scatter(shift_term, ("bucket", "blk"), scatter_dimension=0, tiled=True),
    )
    return (
        layer_out,
        tokens_grad,
        gain_sum,
        shift_sum,
        inward_sum,
        bias_sum,
        outward_sum,
        gate_up_sum,
        down_sum,
    )


def solution(mesh):
    in_specs = (
        P("bucket", "blk", None, None),
        P("bucket", None),
        P(("bucket", "blk")),
        P(("bucket", "blk")),
        P(("bucket", "blk"), None),
        P(("bucket", "blk")),
        P(("bucket", "blk"), None),
        P(("bucket", "blk"), None),
        P(("bucket", "blk"), None),
        P("bucket", "blk", None, None),
    )
    out_specs = (
        P("bucket", "blk", None, None),
        P("bucket", "blk", None, None),
        P(("bucket", "blk")),
        P(("bucket", "blk")),
        P(("bucket", "blk"), None),
        P(("bucket", "blk")),
        P(("bucket", "blk"), None),
        P(("bucket", "blk"), None),
        P(("bucket", "blk"), None),
    )
    return jax.shard_map(shards, mesh=mesh, in_specs=in_specs, out_specs=out_specs, check_vma=False)
```

profile of v0, /device:TPU:11, one launch (start us, length us, event | category | flops | bytes accessed | tf_op | source)
XLA Modules:
  0.0 5326.3 jit_solution(16182667032167660031)
XLA Ops:
  12.8 41.2 all-reduce.8
  57.3 110.1 %all-gather.6.cloned.1.call-done = bf16[2048,6144]{1,0:T(8,128)(2,1)} async-done(((bf16[64,6144]{1,0:T(8,128)(2,1)}), bf16[2048,6144]{1,0:T(8,128)(2,1)}) %all-gather.6.cloned.1.call-update) | async-done | bytes 25165840 | tf_op jit(solution)/shard_map/all_gather | solution.py:160
  167.3 13.4 convolution_add_fusion
  180.8 10.9 reshape.371
  196.8 4.8 slice_bitcast_fusion
  202.3 5.1 multiply_subtract_fusion.2
  225.9 22.5 all-gather.10.cloned.1.call-done
  248.4 6.7 convolution_convert_fusion
  269.3 204.9 %all-gather.8.cloned.1.call-done = bf16[1024,2,4096]{0,2,1:T(8,128)(2,1)} async-done(((bf16[128,2,4096]{0,2,1:T(8,128)(2,1)}), bf16[1024,2,4096]{0,2,1:T(8,128)(2,1)}) %all-gather.8.cloned.1.call-update) | async-done | bytes 16777232 | tf_op jit(solution)/shard_map/all_gather | solution.py:216
  474.2 13.9 copy_bitcast_fusion
  488.3 27.0 while.36
  489.8 5.5 conditional.5
  496.6 5.5 conditional.5
  503.4 5.5 conditional.5
  527.4 10.3 fusion.44
  549.0 1127.9 %while.37 = (s32[]{:T(128)}, bf16[128,2,4096]{0,2,1:T(8,128)(2,1)}, f32[128,2,4096]{0,2,1:T(8,128)}, f32[128,2,32,64]{0,3,2,1:T(8,128)}, s32[]{:T(128)}, /*index...) while((s32[]{:T(128)}, bf16[128,2,4096]{0,2,1:T(8,128)(2,1)}, ...), condition=%wide.region_13.14_spmd.clone, body=%wide.region_10.13_spmd.clone.sunk | while | flops 687358208 | bytes 118639144 | solution.py:299
  554.4 22.3 conditional.6
  580.6 5.4 collective-permute-start.1
  586.0 10.5 collective-permute-start
  596.5 69.7 %collective-permute-done.1 = bf16[128,2,4096]{0,2,1:T(8,128)(2,1)} collective-permute-done((bf16[128,2,4096]{0,2,1:T(8,128)(2,1)}, bf16[128,2,4096]{0,2,1:T(8,128)(2,1)}, u32[]{:S(2)}, u32[]{:S(2)}) %collective-permute-start.1) | collective-permute-done | bytes 2097184 | tf_op jit(solution)/shard_map/while/body/eval_jaxpr/ppermute | solution.py:25
  670.0 86.0 %collective-permute-done = bf16[128,2,4096]{0,2,1:T(8,128)(2,1)} collective-permute-done((bf16[128,2,4096]{0,2,1:T(8,128)(2,1)S(1)}, bf16[128,2,4096]{0,2,1:T(8,128)(2,1)}, u32[]{:S(2)}, u32[]{:S(2)}) %collective-permute-start) | collective-permute-done | bytes 2097184 | tf_op jit(solution)/shard_map/while/body/eval_jaxpr/ppermute | solution.py:19
  763.6 24.3 conditional.6
  768.9 4.9 fusion.15
  791.9 23.8 collective-permute-start.1
  815.6 5.3 collective-permute-start
  821.0 42.6 collective-permute-done.1
  867.5 75.7 %collective-permute-done = bf16[128,2,4096]{0,2,1:T(8,128)(2,1)} collective-permute-done((bf16[128,2,4096]{0,2,1:T(8,128)(2,1)S(1)}, bf16[128,2,4096]{0,2,1:T(8,128)(2,1)}, u32[]{:S(2)}, u32[]{:S(2)}) %collective-permute-start) | collective-permute-done | bytes 2097184 | tf_op jit(solution)/shard_map/while/body/eval_jaxpr/ppermute | solution.py:19
  946.3 5.7 broadcast_select_fusion.2
  952.0 22.3 conditional.6
  978.2 22.3 collective-permute-start.1
  1000.6 5.6 collective-permute-start
  1006.2 41.2 collective-permute-done.1
  1051.3 59.3 %collective-permute-done = bf16[128,2,4096]{0,2,1:T(8,128)(2,1)} collective-permute-done((bf16[128,2,4096]{0,2,1:T(8,128)(2,1)S(1)}, bf16[128,2,4096]{0,2,1:T(8,128)(2,1)}, u32[]{:S(2)}, u32[]{:S(2)}) %collective-permute-start) | collective-permute-done | bytes 2097184 | tf_op jit(solution)/shard_map/while/body/eval_jaxpr/ppermute | solution.py:19
  1122.1 20.8 collective-permute-start.1
  1142.9 50.1 collective-permute-start
  1196.8 19.1 collective-permute-done
  1227.5 61.8 %collective-permute-start.1 = (bf16[128,2,4096]{0,2,1:T(8,128)(2,1)}, bf16[128,2,4096]{0,2,1:T(8,128)(2,1)}, u32[]{:S(2)}, u32[]{:S(2)}) collective-permute-start(bf16[128,2,4096]{0,2,1:T(8,128)(2,1)} %convert_element_type.274), channel_id=1, source_target_pairs={{0,1},{1,2},{2,3},{3,4},{4,5},{5,6},{6,7},{7,0},{8,9},{9,10},{10,1... | collective-permute-start | bytes 6291464 | tf_op jit(solution)/shard_map/while/body/eval_jaxpr/ppermute | solution.py:25
  1289.3 28.6 collective-permute-start
  1318.0 8.8 collective-permute-done.1
  1330.6 62.1 %collective-permute-done = bf16[128,2,4096]{0,2,1:T(8,128)(2,1)} collective-permute-done((bf16[128,2,4096]{0,2,1:T(8,128)(2,1)S(1)}, bf16[128,2,4096]{0,2,1:T(8,128)(2,1)}, u32[]{:S(2)}, u32[]{:S(2)}) %collective-permute-start) | collective-permute-done | bytes 2097184 | tf_op jit(solution)/shard_map/while/body/eval_jaxpr/ppermute | solution.py:19
  1408.4 25.7 collective-permute-done.1
  1437.9 40.9 collective-permute-done
  1492.2 7.4 collective-permute-start
  1499.7 24.3 collective-permute-done.1
  1527.8 38.9 collective-permute-done
  1578.2 5.3 collective-permute-start.1
  1583.5 29.4 collective-permute-start
  1612.9 15.0 collective-permute-done.1
  1631.8 45.2 collective-permute-done
  1690.0 6.1 copy.86
  1724.7 7.9 convert_element_type.223
  1732.6 21.4 fusion.43
  1755.7 23.1 fusion.39
  1778.7 24.7 multiply_convert_fusion.2
  1805.0 18.0 fusion.45
  1823.1 35.3 fusion.24
  1859.7 5.9 fusion.42
  1865.6 11.5 fusion.28
  1878.6 21.5 fusion.25
  1900.1 14.7 multiply_reduce_fusion.1
  1919.3 161.8 %all-reduce.7 = (f32[2048]{0:T(1024)S(1)}, f32[2048]{0:T(1024)S(1)}, f32[4608]{0:T(1024)S(1)}) all-reduce(f32[2048]{0:T(1024)S(1)} %get-tuple-element.654, f32[2048]{0:T(1024)S(1)} %get-tuple-element.657, f32[4608]{0:T(1024)S(1)} %pad_maximum_fusion.6), channel_id=2, replica_groups=mesh['bucket'=4,'blk'=8] {'bucket','blk'}, use_global_device_ids=true, to_apply=%region_17.18.clone | all-reduce | flops 8704 | bytes 69632
  2082.9 337.2 %reduce-scatter.5.cloned.1.call-done = f32[64,6144]{1,0:T(8,128)} async-done(((f32[2048,6144]{1,0:T(8,128)}), f32[64,6144]{1,0:T(8,128)}) %reduce-scatter.5.cloned.1.call-update) | async-done | bytes 1572880 | tf_op jit(solution)/shard_map/reduce_scatter | solution.py:333
  2420.2 971.1 %reduce-scatter.11.cloned.1.call-done = f32[176,2048]{1,0:T(8,128)} async-done(((f32[5632,2048]{1,0:T(8,128)}), f32[176,2048]{1,0:T(8,128)}) %reduce-scatter.11.cloned.1.call-update) | async-done | bytes 1441808 | tf_op jit(solution)/shard_map/reduce_scatter | solution.py:252
  3391.2 1928.1 %reduce-scatter.9.cloned.1.call-done = f32[64,11264]{1,0:T(8,128)} async-done(((f32[2048,11264]{1,0:T(8,128)}), f32[64,11264]{1,0:T(8,128)}) %reduce-scatter.9.cloned.1.call-update) | async-done | bytes 2883600 | tf_op jit(solution)/shard_map/reduce_scatter | solution.py:251
  (318 shorter events, 330.8 us)
Async XLA Ops:
  7.2 4.5 copy-start.9
  7.2 4.8 copy-start.36
  7.2 4.8 copy-start.37
  7.2 4.9 copy-start.35
  7.2 160.1 %all-gather.6.cloned.1.call-start = ((), (), s32[]{:S(2)}) async-start(), calls=%async_computation.4 | async-start | bytes 25952256 | tf_op jit(solution)/shard_map/all_gather | solution.py:160
  9.7 238.7 %all-gather.10.cloned.1.call-start = ((), (), s32[]{:S(2)}) async-start(), calls=%async_computation.6 | async-start | bytes 8650752 | tf_op jit(solution)/shard_map/all_gather | solution.py:161
  11.6 462.6 %all-gather.8.cloned.1.call-start = ((), (), s32[]{:S(2)}) async-start(), calls=%async_computation.5 | async-start | bytes 18874368 | tf_op jit(solution)/shard_map/all_gather | solution.py:216
  12.0 168.8 %copy-start.3 = (f32[256,2048]{1,0:T(8,128)}, f32[256,2048]{1,0:T(8,128)S(1)}, u32[]{:S(2)}) copy-start(f32[256,2048]{1,0:T(8,128)S(1)} %reshape.379) | copy-start | bytes 6291460
  54.1 483.8 %copy-start.23 = (f32[2048]{0:T(1024)}, f32[2048]{0:T(1024)S(1)}, u32[]{:S(2)}) copy-start(f32[2048]{0:T(1024)S(1)} %convert_element_type.201) | copy-start | bytes 24580
  54.1 483.8 %copy-start.21 = (f32[2048]{0:T(1024)}, f32[2048]{0:T(1024)S(1)}, u32[]{:S(2)}) copy-start(f32[2048]{0:T(1024)S(1)} %convert_element_type.199) | copy-start | bytes 24580
  55.2 125.6 %copy-start.27 = (f32[256]{0:T(256)}, f32[256]{0:T(256)S(1)}, u32[]{:S(2)}) copy-start(f32[256]{0:T(256)S(1)} %div.29) | copy-start | bytes 3076
  56.9 123.9 %copy-start.29 = (f32[256]{0:T(256)}, f32[256]{0:T(256)S(1)}, u32[]{:S(2)}) copy-start(f32[256]{0:T(256)S(1)} %rsqrt.13) | copy-start | bytes 3076
  57.2 145.1 %copy-start.25 = (f32[128,8]{1,0:T(8,128)}, f32[128,8]{1,0:T(8,128)S(1)}, u32[]{:S(2)}) copy-start(f32[128,8]{1,0:T(8,128)S(1)} %copy.75) | copy-start | bytes 12292
  201.6 5.9 copy-start.2
  215.0 3.4 copy-start.20
  215.1 4.4 copy-start.17
  215.1 1539.1 %all-gather.12.cloned.1.call-start = ((), (), s32[]{:S(2)}) async-start(), calls=%async_computation.7 | async-start | bytes 47579136 | tf_op jit(solution)/shard_map/all_gather | solution.py:162
  218.4 1560.4 %all-gather.14.cloned.1.call-start = ((), (), s32[]{:S(2)}) async-start(), calls=%async_computation.8 | async-start | bytes 23789568 | tf_op jit(solution)/shard_map/all_gather | solution.py:163
  219.4 1863.5 %reduce-scatter.7.cloned.1.call-start = ((), (), s32[]{:S(2)}) async-start(), calls=%async_computation.10 | async-start | bytes 17301504 | tf_op jit(solution)/shard_map/reduce_scatter | solution.py:334
  219.8 35.3 copy-start.5
  220.1 35.1 copy-start.32
  225.9 29.2 copy-start.18
  259.6 3.8 copy-start.7
  259.6 5.2 copy-start.8
  537.8 6.6 copy-start.6
  537.8 1882.4 %reduce-scatter.5.cloned.1.call-start = ((), (), s32[]{:S(2)}) async-start(), calls=%async_computation.9 | async-start | bytes 51904512 | tf_op jit(solution)/shard_map/reduce_scatter | solution.py:333
  558.8 4.0 copy-start
  576.6 9.3 copy-start.1
  580.6 85.6 %collective-permute-start.1 = (bf16[128,2,4096]{0,2,1:T(8,128)(2,1)}, bf16[128,2,4096]{0,2,1:T(8,128)(2,1)}, u32[]{:S(2)}, u32[]{:S(2)}) collective-permute-start(bf16[128,2,4096]{0,2,1:T(8,128)(2,1)} %convert_element_type.274), channel_id=1, source_target_pairs={{0,1},{1,2},{2,3},{3,4},{4,5},{5,6},{6,7},{7,0},{8,9},{9,10},{10,1... | collective-permute-start | bytes 6291464 | tf_op jit(solution)/shard_map/while/body/eval_jaxpr/ppermute | solution.py:25
  586.0 170.1 %collective-permute-start = (bf16[128,2,4096]{0,2,1:T(8,128)(2,1)S(1)}, bf16[128,2,4096]{0,2,1:T(8,128)(2,1)}, u32[]{:S(2)}, u32[]{:S(2)}) collective-permute-start(bf16[128,2,4096]{0,2,1:T(8,128)(2,1)S(1)} %copy-done.1), channel_id=1, source_target_pairs={{0,1},{1,2},{2,3},{3,4},{4,5},{5,6},{6,7},{8,9},{9,10},{10,11},{11... | collective-permute-start | bytes 6291464 | tf_op jit(solution)/shard_map/while/body/eval_jaxpr/ppermute | solution.py:19
  768.8 5.2 copy-start
  787.9 27.7 copy-start.1
  791.9 71.7 %collective-permute-start.1 = (bf16[128,2,4096]{0,2,1:T(8,128)(2,1)}, bf16[128,2,4096]{0,2,1:T(8,128)(2,1)}, u32[]{:S(2)}, u32[]{:S(2)}) collective-permute-start(bf16[128,2,4096]{0,2,1:T(8,128)(2,1)} %convert_element_type.274), channel_id=1, source_target_pairs={{0,1},{1,2},{2,3},{3,4},{4,5},{5,6},{6,7},{7,0},{8,9},{9,10},{10,1... | collective-permute-start | bytes 6291464 | tf_op jit(solution)/shard_map/while/body/eval_jaxpr/ppermute | solution.py:25
  815.6 127.5 %collective-permute-start = (bf16[128,2,4096]{0,2,1:T(8,128)(2,1)S(1)}, bf16[128,2,4096]{0,2,1:T(8,128)(2,1)}, u32[]{:S(2)}, u32[]{:S(2)}) collective-permute-start(bf16[128,2,4096]{0,2,1:T(8,128)(2,1)S(1)} %copy-done.1), channel_id=1, source_target_pairs={{0,1},{1,2},{2,3},{3,4},{4,5},{5,6},{6,7},{8,9},{9,10},{10,11},{11... | collective-permute-start | bytes 6291464 | tf_op jit(solution)/shard_map/while/body/eval_jaxpr/ppermute | solution.py:19
  956.5 4.0 copy-start
  974.3 26.3 copy-start.1
  978.2 69.2 %collective-permute-start.1 = (bf16[128,2,4096]{0,2,1:T(8,128)(2,1)}, bf16[128,2,4096]{0,2,1:T(8,128)(2,1)}, u32[]{:S(2)}, u32[]{:S(2)}) collective-permute-start(bf16[128,2,4096]{0,2,1:T(8,128)(2,1)} %convert_element_type.274), channel_id=1, source_target_pairs={{0,1},{1,2},{2,3},{3,4},{4,5},{5,6},{6,7},{7,0},{8,9},{9,10},{10,1... | collective-permute-start | bytes 6291464 | tf_op jit(solution)/shard_map/while/body/eval_jaxpr/ppermute | solution.py:25
  1000.6 110.0 %collective-permute-start = (bf16[128,2,4096]{0,2,1:T(8,128)(2,1)S(1)}, bf16[128,2,4096]{0,2,1:T(8,128)(2,1)}, u32[]{:S(2)}, u32[]{:S(2)}) collective-permute-start(bf16[128,2,4096]{0,2,1:T(8,128)(2,1)S(1)} %copy-done.1), channel_id=1, source_target_pairs={{0,1},{1,2},{2,3},{3,4},{4,5},{5,6},{6,7},{8,9},{9,10},{10,11},{11... | collective-permute-start | bytes 6291464 | tf_op jit(solution)/shard_map/while/body/eval_jaxpr/ppermute | solution.py:19
  1118.1 24.8 copy-start.1
  1122.1 70.9 %collective-permute-start.1 = (bf16[128,2,4096]{0,2,1:T(8,128)(2,1)}, bf16[128,2,4096]{0,2,1:T(8,128)(2,1)}, u32[]{:S(2)}, u32[]{:S(2)}) collective-permute-start(bf16[128,2,4096]{0,2,1:T(8,128)(2,1)} %convert_element_type.274), channel_id=1, source_target_pairs={{0,1},{1,2},{2,3},{3,4},{4,5},{5,6},{6,7},{7,0},{8,9},{9,10},{10,1... | collective-permute-start | bytes 6291464 | tf_op jit(solution)/shard_map/while/body/eval_jaxpr/ppermute | solution.py:25
  1142.9 73.0 %collective-permute-start = (bf16[128,2,4096]{0,2,1:T(8,128)(2,1)S(1)}, bf16[128,2,4096]{0,2,1:T(8,128)(2,1)}, u32[]{:S(2)}, u32[]{:S(2)}) collective-permute-start(bf16[128,2,4096]{0,2,1:T(8,128)(2,1)S(1)} %copy-done.1), channel_id=1, source_target_pairs={{0,1},{1,2},{2,3},{3,4},{4,5},{5,6},{6,7},{8,9},{9,10},{10,11},{11... | collective-permute-start | bytes 6291464 | tf_op jit(solution)/shard_map/while/body/eval_jaxpr/ppermute | solution.py:19
  1223.5 65.8 %copy-start.1 = (bf16[128,2,4096]{0,2,1:T(8,128)(2,1)S(1)}, bf16[128,2,4096]{0,2,1:T(8,128)(2,1)}, u32[]{:S(2)}) copy-start(bf16[128,2,4096]{0,2,1:T(8,128)(2,1)} %copy.130) | copy-start | bytes 6291460 | tf_op jit(solution)/shard_map/while
  1227.5 99.3 %collective-permute-start.1 = (bf16[128,2,4096]{0,2,1:T(8,128)(2,1)}, bf16[128,2,4096]{0,2,1:T(8,128)(2,1)}, u32[]{:S(2)}, u32[]{:S(2)}) collective-permute-start(bf16[128,2,4096]{0,2,1:T(8,128)(2,1)} %convert_element_type.274), channel_id=1, source_target_pairs={{0,1},{1,2},{2,3},{3,4},{4,5},{5,6},{6,7},{7,0},{8,9},{9,10},{10,1... | collective-permute-start | bytes 6291464 | tf_op jit(solution)/shard_map/while/body/eval_jaxpr/ppermute | solution.py:25
  1289.3 103.4 %collective-permute-start = (bf16[128,2,4096]{0,2,1:T(8,128)(2,1)S(1)}, bf16[128,2,4096]{0,2,1:T(8,128)(2,1)}, u32[]{:S(2)}, u32[]{:S(2)}) collective-permute-start(bf16[128,2,4096]{0,2,1:T(8,128)(2,1)S(1)} %copy-done.1), channel_id=1, source_target_pairs={{0,1},{1,2},{2,3},{3,4},{4,5},{5,6},{6,7},{8,9},{9,10},{10,11},{11... | collective-permute-start | bytes 6291464 | tf_op jit(solution)/shard_map/while/body/eval_jaxpr/ppermute | solution.py:19
  1400.2 6.2 copy-start.1
  1404.2 29.9 collective-permute-start.1
  1406.4 72.4 %collective-permute-start = (bf16[128,2,4096]{0,2,1:T(8,128)(2,1)S(1)}, bf16[128,2,4096]{0,2,1:T(8,128)(2,1)}, u32[]{:S(2)}, u32[]{:S(2)}) collective-permute-start(bf16[128,2,4096]{0,2,1:T(8,128)(2,1)S(1)} %copy-done.1), channel_id=1, source_target_pairs={{0,1},{1,2},{2,3},{3,4},{4,5},{5,6},{6,7},{8,9},{9,10},{10,11},{11... | collective-permute-start | bytes 6291464 | tf_op jit(solution)/shard_map/while/body/eval_jaxpr/ppermute | solution.py:19
  1486.4 5.8 copy-start.1
  1490.3 33.6 collective-permute-start.1
  1492.2 74.5 %collective-permute-start = (bf16[128,2,4096]{0,2,1:T(8,128)(2,1)S(1)}, bf16[128,2,4096]{0,2,1:T(8,128)(2,1)}, u32[]{:S(2)}, u32[]{:S(2)}) collective-permute-start(bf16[128,2,4096]{0,2,1:T(8,128)(2,1)S(1)} %copy-done.1), channel_id=1, source_target_pairs={{0,1},{1,2},{2,3},{3,4},{4,5},{5,6},{6,7},{8,9},{9,10},{10,11},{11... | collective-permute-start | bytes 6291464 | tf_op jit(solution)/shard_map/while/body/eval_jaxpr/ppermute | solution.py:19
  1574.3 9.2 copy-start.1
  1578.2 49.7 collective-permute-start.1
  1583.5 93.4 %collective-permute-start = (bf16[128,2,4096]{0,2,1:T(8,128)(2,1)S(1)}, bf16[128,2,4096]{0,2,1:T(8,128)(2,1)}, u32[]{:S(2)}, u32[]{:S(2)}) collective-permute-start(bf16[128,2,4096]{0,2,1:T(8,128)(2,1)S(1)} %copy-done.1), channel_id=1, source_target_pairs={{0,1},{1,2},{2,3},{3,4},{4,5},{5,6},{6,7},{8,9},{9,10},{10,11},{11... | collective-permute-start | bytes 6291464 | tf_op jit(solution)/shard_map/while/body/eval_jaxpr/ppermute | solution.py:19
  1706.0 3.7 copy-start.10
  1706.0 4.7 copy-start.11
  1706.0 4.7 copy-start.26
  1710.7 3.3 copy-start.13
  1732.6 21.5 copy-start.12
  1754.1 1.6 copy-start.24
  1754.1 24.6 copy-start.19
  1754.1 1637.1 %reduce-scatter.11.cloned.1.call-start = ((), (), s32[]{:S(2)}) async-start(), calls=%async_computation.12 | async-start | bytes 47579136 | tf_op jit(solution)/shard_map/reduce_scatter | solution.py:252
  1823.1 3496.3 %reduce-scatter.9.cloned.1.call-start = ((), (), s32[]{:S(2)}) async-start(), calls=%async_computation.11 | async-start | bytes 95158272 | tf_op jit(solution)/shard_map/reduce_scatter | solution.py:251
  1859.7 5.9 copy-start.15
  1859.7 5.9 copy-start.33
  (8 other events, 11.4 us)
Sparse Core Ops, SparseCore 0:
  11.5 155.7 all-gather.5
  170.9 77.4 all-gather.9
  250.5 223.6 all-gather.7
  477.5 328.8 all-gather.11
  809.1 219.3 all-gather.13
  1031.2 936.7 reduce-scatter.6
  1975.1 445.0 reduce-scatter.4
  2423.0 968.1 reduce-scatter.10
  3394.2 1925.1 reduce-scatter.8
where the time goes:
time: 5340 us; the launch traced here: 5330 us
  waiting for transfers between devices  4230 us (79%)
  starting transfers between devices  283 us (5%)
  matrix products  263 us (5%)
  blocking collectives  203 us (4%)
  other arithmetic  165 us (3%)
  local copies, waits for them, and re-layouts  162 us (3%)
    reduce_scatter x1, waiting for transfers between devices, shards(): lax.psum_scatter(gate_up_term, ('bucket', 'blk'), scatter_dimension=0, ti...  1930 us
    reduce_scatter x1, waiting for transfers between devices, shards(): lax.psum_scatter(down_term, ('bucket', 'blk'), scatter_dimension=0, tiled...  971 us
    ppermute x8, waiting for transfers between devices, shifted(): return lax.ppermute(value, axis, pairs)  427 us
    reduce_scatter x1, waiting for transfers between devices, shards(): lax.psum_scatter(inward_term, ('bucket', 'blk'), scatter_dimension=0, til...  337 us
    ppermute x8, waiting for transfers between devices, shifted_2(): return lax.ppermute(value, axis, pairs)  227 us
    all_gather x1, waiting for transfers between devices, shards(): lax.all_gather(packed, 'blk', axis=0, tiled=True)  205 us
    unnamed x2, blocking collectives  203 us
    ppermute x8, starting transfers between devices, shifted_2(): return lax.ppermute(value, axis, pairs)  144 us
  transfers between devices with their start and end apart: 25, of which 21 were waited for; matrix products, arithmetic and copies ran while one was open for 11% of the time, Pallas kernels for 0%

commit v1 on v0

--- a/solution.py
+++ b/solution.py
@@ -1,6 +1,8 @@
 import jax
 import jax.numpy as jnp
 from jax import lax
+from jax.experimental import pallas as pl
+from jax.experimental.pallas import tpu as pltpu
 from jax.sharding import PartitionSpec as P
 
 HEADS = 32
@@ -135,7 +137,7 @@
     return running
 
 
-def shards(
+def shards_general(
     tokens,
     lengths,
     norm_gain,
@@ -349,6 +351,693 @@
     )
 
 
+DEPTH = 4
+PIECES = 2 * DEPTH
+ROWS = 256
+LOCAL_HEADS = 4
+HEAD_COLS = LOCAL_HEADS * HEAD_DIM
+CORE = [(i, i ^ 1) for i in range(4)]
+ACROSS_X = [(i, i ^ 2) for i in range(4)]
+ACROSS_Y = [(i, i ^ 1) for i in range(8)]
+UPWARD = [(i, i + 2) for i in range(6)]
+DOWNWARD = [(i + 2, i) for i in range(6)]
+MIB = 1024 * 1024
+
+
+def fits_groups(mesh):
+    return mesh.shape["bucket"] == 4 and mesh.shape["blk"] == 2 * DEPTH
+
+
+def around(step):
+    return [(z * 2 + y, ((z + step) % DEPTH) * 2 + y) for z in range(DEPTH) for y in range(2)]
+
+
+def in_order(own, other, index, axis):
+    return jnp.where(
+        index == 0, jnp.stack([own, other], axis), jnp.stack([other, own], axis)
+    )
+
+
+def gather_pieces(value, z):
+    up, down = [value], [value]
+    for step in range(DEPTH - 1):
+        up.append(lax.ppermute(up[-1], "blk", UPWARD))
+        down.append(lax.ppermute(down[-1], "blk", DOWNWARD))
+    own = [value]
+    for step in range(1, DEPTH):
+        own.append(jnp.where(z >= step, up[step], down[DEPTH - step]))
+    return own + [lax.ppermute(piece, "bucket", CORE) for piece in own]
+
+
+def scatter_pieces(partial):
+    total = None
+    for step in range(DEPTH):
+        both = partial[step].astype(jnp.float32) + lax.ppermute(
+            partial[DEPTH + step], "bucket", CORE
+        ).astype(jnp.float32)
+        if step > 0:
+            both = lax.ppermute(both.astype(jnp.bfloat16), "blk", around(-step)).astype(jnp.float32)
+        total = both if total is None else total + both
+    return total
+
+
+def columns_of_group(rows, core, z):
+    mine = lax.dynamic_index_in_dim(rows, core, 0, False)
+    theirs = lax.dynamic_index_in_dim(rows, 1 - core, 0, False)
+    got = lax.ppermute(theirs, "bucket", CORE)
+    both = in_order(mine, got, core, 1)
+    pieces = [lax.dynamic_index_in_dim(both, z, 0, False)]
+    for step in range(1, DEPTH):
+        chunk = lax.dynamic_index_in_dim(both, (z + step) % DEPTH, 0, False)
+        pieces.append(lax.ppermute(chunk, "blk", around(step)))
+    stacked = jnp.stack(pieces)
+    return jnp.concatenate(
+        [lax.dynamic_slice_in_dim(stacked, (z - j) % DEPTH, 1, 0) for j in range(DEPTH)]
+    )
+
+
+def over_columns(value, x, y):
+    value = in_order(value, lax.ppermute(value, "blk", ACROSS_Y), y, 0)
+    return in_order(value, lax.ppermute(value, "bucket", ACROSS_X), x, 0)
+
+
+def sum_over_columns(value, x, y):
+    keep = lax.dynamic_index_in_dim(value, x, 0, False)
+    send = lax.dynamic_index_in_dim(value, 1 - x, 0, False).astype(jnp.bfloat16)
+    value = keep + lax.ppermute(send, "bucket", ACROSS_X).astype(jnp.float32)
+    keep = lax.dynamic_index_in_dim(value, y, 0, False)
+    send = lax.dynamic_index_in_dim(value, 1 - y, 0, False).astype(jnp.bfloat16)
+    return keep + lax.ppermute(send, "blk", ACROSS_Y).astype(jnp.float32)
+
+
+def rows_of_device(value, core, z):
+    low = value.astype(jnp.bfloat16)
+    parts = [lax.dynamic_index_in_dim(low, z, 0, False)]
+    for step in range(1, DEPTH):
+        chunk = lax.dynamic_index_in_dim(low, (z + step) % DEPTH, 0, False)
+        parts.append(lax.ppermute(chunk, "blk", around(step)))
+    stacked = jnp.stack(parts)
+    ordered = jnp.concatenate(
+        [lax.dynamic_slice_in_dim(stacked, (z - j) % DEPTH, 1, 0) for j in range(DEPTH)]
+    )
+    mine = lax.dynamic_index_in_dim(ordered, core, 1, False)
+    theirs = lax.dynamic_index_in_dim(ordered, 1 - core, 1, False)
+    return in_order(mine, lax.ppermute(theirs, "bucket", CORE), core, 0)
+
+
+def dot_rows(left, right):
+    return lax.dot_general(
+        left, right, (((1,), (0,)), ((), ())), preferred_element_type=jnp.float32
+    )
+
+
+def params(limit, **extra):
+    return pltpu.CompilerParams(vmem_limit_bytes=limit * MIB, **extra)
+
+
+def cost(flops, moved, exps=0):
+    return pl.CostEstimate(flops=flops, bytes_accessed=moved, transcendentals=exps)
+
+
+def piece_spec(width):
+    return pl.BlockSpec((1, ROWS, width), lambda i: (i, 0, 0))
+
+
+def whole_spec(shape):
+    return pl.BlockSpec(shape, lambda i: (0,) * len(shape))
+
+
+def normalised(rows):
+    inputs = rows.astype(jnp.float32)
+    centred = inputs - jnp.mean(inputs, axis=-1, keepdims=True)
+    variance = jnp.mean(centred * centred, axis=-1, keepdims=True)
+    inverse = lax.rsqrt(variance + epsilon)
+    return centred * inverse, inverse
+
+
+def turned(values, cos_ref, first_ref, second_ref, sign):
+    half = ROT // 2
+    cos = jnp.concatenate([cos_ref[0], cos_ref[0]], 0)
+    first = jnp.concatenate([first_ref[0], first_ref[0]], 0)
+    second = jnp.concatenate([second_ref[0], second_ref[0]], 0)
+    ahead = pltpu.roll(values, HEAD_COLS - half, 1)
+    behind = pltpu.roll(values, half, 1)
+    return values * cos + sign * (ahead * first + behind * second)
+
+
+def project_kernel(
+    x_ref, gain_ref, shift_ref, w_ref, bias_ref, cos_ref, first_ref, second_ref, n_ref, q_ref, kv_ref
+):
+    hat, _ = normalised(x_ref[0])
+    normed = (hat * gain_ref[...] + shift_ref[...]).astype(jnp.bfloat16)
+    n_ref[0] = normed
+    projected = dot_rows(normed, w_ref[...]) + bias_ref[...]
+    tables = (cos_ref, first_ref, second_ref)
+    query = turned(projected[:, :HEAD_COLS], *tables, 1.0) * (HEAD_DIM**-0.5)
+    key = turned(projected[:, HEAD_COLS : 2 * HEAD_COLS], *tables, 1.0)
+    q_ref[0] = query.astype(jnp.bfloat16)
+    kv_ref[0, :, :HEAD_COLS] = key.astype(jnp.bfloat16)
+    kv_ref[0, :, HEAD_COLS:] = projected[:, 2 * HEAD_COLS :].astype(jnp.bfloat16)
+
+
+def project(pieces, gain, shift, weight, bias, tables):
+    width = pieces.shape[-1]
+    table_spec = pl.BlockSpec((1,) + tables[0].shape[1:], lambda i: (i % DEPTH, 0, 0))
+    return pl.pallas_call(
+        project_kernel,
+        grid=(PIECES,),
+        in_specs=[
+            piece_spec(width),
+            whole_spec((1, width)),
+            whole_spec((1, width)),
+            whole_spec(weight.shape),
+            whole_spec(bias.shape),
+            table_spec,
+            table_spec,
+            table_spec,
+        ],
+        out_specs=[piece_spec(width), piece_spec(HEAD_COLS), piece_spec(2 * HEAD_COLS)],
+        out_shape=[
+            jax.ShapeDtypeStruct((PIECES, ROWS, width), jnp.bfloat16),
+            jax.ShapeDtypeStruct((PIECES, ROWS, HEAD_COLS), jnp.bfloat16),
+            jax.ShapeDtypeStruct((PIECES, ROWS, 2 * HEAD_COLS), jnp.bfloat16),
+        ],
+        compiler_params=params(48),
+        cost_estimate=cost(2 * PIECES * ROWS * width * 3 * HEAD_COLS, 24 * MIB),
+        name="project",
+    )(pieces, gain, shift, weight, bias, *tables)
+
+
+def feed_kernel(n_ref, wg_ref, wu_ref, gate_ref, up_ref, hidden_ref):
+    normed = n_ref[0]
+    gate = dot_rows(normed, wg_ref[...])
+    up = dot_rows(normed, wu_ref[...])
+    gate_ref[0] = gate
+    up_ref[0] = up
+    hidden_ref[0] = (gate * jax.nn.sigmoid(gate) * up).astype(jnp.bfloat16)
+
+
+def feed(normed, gate_weight, up_weight):
+    width = normed.shape[-1]
+    hidden = gate_weight.shape[1]
+    return pl.pallas_call(
+        feed_kernel,
+        grid=(PIECES,),
+        in_specs=[piece_spec(width), whole_spec(gate_weight.shape), whole_spec(up_weight.shape)],
+        out_specs=[piece_spec(hidden)] * 3,
+        out_shape=[
+            jax.ShapeDtypeStruct((PIECES, ROWS, hidden), jnp.float32),
+            jax.ShapeDtypeStruct((PIECES, ROWS, hidden), jnp.float32),
+            jax.ShapeDtypeStruct((PIECES, ROWS, hidden), jnp.bfloat16),
+        ],
+        compiler_params=params(48),
+        cost_estimate=cost(4 * PIECES * ROWS * width * hidden, 28 * MIB),
+        name="feed",
+    )(normed, gate_weight, up_weight)
+
+
+def branch_kernel(a_ref, h_ref, wo_ref, wd_ref, out_ref):
+    out_ref[0] = (dot_rows(a_ref[0], wo_ref[...]) + dot_rows(h_ref[0], wd_ref[...])).astype(
+        jnp.bfloat16
+    )
+
+
+def branch_terms(attended, hidden, outward, down):
+    width = outward.shape[1]
+    return pl.pallas_call(
+        branch_kernel,
+        grid=(PIECES,),
+        in_specs=[
+            piece_spec(HEAD_COLS),
+            piece_spec(hidden.shape[-1]),
+            whole_spec(outward.shape),
+            whole_spec(down.shape),
+        ],
+        out_specs=piece_spec(width),
+        out_shape=jax.ShapeDtypeStruct((PIECES, ROWS, width), jnp.bfloat16),
+        compiler_params=params(48),
+        cost_estimate=cost(2 * PIECES * ROWS * width * (HEAD_COLS + hidden.shape[-1]), 16 * MIB),
+        name="branch_terms",
+    )(attended, hidden, outward, down)
+
+
+def back_kernel(g_ref, gate_ref, up_ref, wo_ref, wd_ref, a_ref, gg_ref, ug_ref):
+    grad = g_ref[0]
+    a_ref[0] = transposed_times(grad, wo_ref[...]).astype(jnp.bfloat16)
+    hidden_grad = transposed_times(grad, wd_ref[...])
+    gate = gate_ref[0]
+    sig = jax.nn.sigmoid(gate)
+    silu = gate * sig
+    gg_ref[0] = (hidden_grad * up_ref[0] * (sig + silu * (1.0 - sig))).astype(jnp.bfloat16)
+    ug_ref[0] = (hidden_grad * silu).astype(jnp.bfloat16)
+
+
+def back(grads, gate, up, outward, down):
+    width = outward.shape[1]
+    hidden = down.shape[0]
+    return pl.pallas_call(
+        back_kernel,
+        grid=(PIECES,),
+        in_specs=[
+            piece_spec(width),
+            piece_spec(hidden),
+            piece_spec(hidden),
+            whole_spec(outward.shape),
+            whole_spec(down.shape),
+        ],
+        out_specs=[piece_spec(HEAD_COLS), piece_spec(hidden), piece_spec(hidden)],
+        out_shape=[
+            jax.ShapeDtypeStruct((PIECES, ROWS, HEAD_COLS), jnp.bfloat16),
+            jax.ShapeDtypeStruct((PIECES, ROWS, hidden), jnp.bfloat16),
+            jax.ShapeDtypeStruct((PIECES, ROWS, hidden), jnp.bfloat16),
+        ],
+        compiler_params=params(48),
+        cost_estimate=cost(2 * PIECES * ROWS * width * (HEAD_COLS + hidden), 28 * MIB),
+        name="back",
+    )(grads, gate, up, outward, down)
+
+
+def pair_rows(block):
+    lane = lax.broadcasted_iota(jnp.int32, block.shape, 1)
+    zero = jnp.zeros_like(block)
+    return jnp.concatenate(
+        [jnp.where(lane < HEAD_DIM, block, zero), jnp.where(lane < HEAD_DIM, zero, block)], 0
+    )
+
+
+def pair_lanes(rows):
+    half = rows.shape[0] // 2
+    lane = lax.broadcasted_iota(jnp.int32, (half, rows.shape[1]), 1)
+    return jnp.where(lane < HEAD_DIM, rows[:half], rows[half:])
+
+
+def block_probs(queries, keys, last, y):
+    scores = transposed_times(queries, keys)
+    rows, columns = scores.shape
+    size = rows // 2
+    row = lax.broadcasted_iota(jnp.int32, (rows, 2 * size), 0) % size
+    column = lax.broadcasted_iota(jnp.int32, (rows, 2 * size), 1)
+    allowed = (column <= row) | ((column >= size) & (y == 1))
+    tail = jnp.where(allowed, scores[:, last * 2 * size :], masked_score)
+    scores = tail if last == 0 else jnp.concatenate([scores[:, : last * 2 * size], tail], 1)
+    weights = jnp.exp(scores - jnp.max(scores, axis=-1, keepdims=True))
+    return weights * (1.0 / jnp.sum(weights, axis=-1, keepdims=True))
+
+
+def both_columns(own_ref, other_ref, z, count):
+    blocks = []
+    for j in range(count):
+        at = (z + DEPTH - j) % DEPTH
+        blocks += [own_ref[0, at, 0], other_ref[0, at, 0]]
+    return jnp.concatenate(blocks, 0)
+
+
+def attend_kernel(place_ref, q_ref, k_ref, v_ref, ok_ref, ov_ref, out_ref):
+    z, y = place_ref[0], place_ref[1]
+    keys = both_columns(k_ref, ok_ref, z, DEPTH)
+    values = both_columns(v_ref, ov_ref, z, DEPTH)
+    size = keys.shape[0] // DEPTH
+    for j in range(DEPTH):
+        at = (z + DEPTH - j) % DEPTH
+        count = (j + 1) * size
+        probs = block_probs(pair_rows(q_ref[0, at, 0]), keys[:count], j, y)
+        out = dot_rows(probs.astype(jnp.bfloat16), values[:count])
+        out_ref[0, at, 0] = pair_lanes(out).astype(jnp.bfloat16)
+
+
+def attend_back_kernel(
+    place_ref,
+    q_ref,
+    k_ref,
+    v_ref,
+    ok_ref,
+    ov_ref,
+    grad_ref,
+    dq_ref,
+    dk_ref,
+    dv_ref,
+    odk_ref,
+    odv_ref,
+    key_sum,
+    value_sum,
+):
+    z, y = place_ref[0], place_ref[1]
+    keys = both_columns(k_ref, ok_ref, z, DEPTH)
+    values = both_columns(v_ref, ov_ref, z, DEPTH)
+    size = keys.shape[0] // DEPTH
+    half = size // 2
+    for j in reversed(range(DEPTH)):
+        at = (z + DEPTH - j) % DEPTH
+        count = (j + 1) * size
+        queries = pair_rows(q_ref[0, at, 0])
+        grads = pair_rows(grad_ref[0, at, 0])
+        probs = block_probs(queries, keys[:count], j, y)
+        low = probs.astype(jnp.bfloat16)
+        prob_grad = transposed_times(grads, values[:count])
+        delta = jnp.sum(low.astype(jnp.float32) * prob_grad, axis=-1, keepdims=True)
+        score_grad = (probs * (prob_grad - delta)).astype(jnp.bfloat16)
+        dq_ref[0, at, 0] = pair_lanes(dot_rows(score_grad, keys[:count]))
+        key_term = times_transposed(score_grad, queries)
+        value_term = times_transposed(low, grads)
+        if j == DEPTH - 1:
+            key_sum[...] = key_term
+            value_sum[...] = value_term
+        else:
+            key_sum[:count] += key_term
+            value_sum[:count] += value_term
+    for j in range(DEPTH):
+        at = (z + DEPTH - j) % DEPTH
+        low = j * size
+        dk_ref[0, at, 0] = key_sum[low : low + half]
+        dv_ref[0, at, 0] = value_sum[low : low + half]
+        odk_ref[0, at, 0] = key_sum[low + half : low + size].astype(jnp.bfloat16)
+        odv_ref[0, at, 0] = value_sum[low + half : low + size].astype(jnp.bfloat16)
+
+
+def sequence_specs(seqs, length):
+    def spec(first):
+        return pl.BlockSpec(
+            (1, DEPTH, 1, length, 2 * HEAD_DIM), lambda b, s, p, place: (b, 0, s, 0, first + p)
+        )
+
+    return spec(0), spec(LOCAL_HEADS // 2)
+
+
+def as_sequences(value, seqs):
+    return value.reshape(2, DEPTH, seqs, ROWS // seqs, value.shape[-1])
+
+
+def attend(place, queries, pairs, other_pairs, seqs):
+    queries, pairs, other_pairs = (as_sequences(v, seqs) for v in (queries, pairs, other_pairs))
+    first, second = sequence_specs(seqs, ROWS // seqs)
+    out = pl.pallas_call(
+        attend_kernel,
+        grid_spec=pltpu.PrefetchScalarGridSpec(
+            num_scalar_prefetch=1,
+            grid=(2, seqs, LOCAL_HEADS // 2),
+            in_specs=[first, first, second, first, second],
+            out_specs=first,
+        ),
+        out_shape=jax.ShapeDtypeStruct(queries.shape, jnp.bfloat16),
+        compiler_params=params(48),
+        cost_estimate=cost(4 * 8 * 2 * 2 * 256 * 2560 * 128, 8 * MIB, 8 * 256 * 2560),
+        name="attend",
+    )(place, queries, pairs, pairs, other_pairs, other_pairs)
+    return out.reshape(PIECES, ROWS, HEAD_COLS)
+
+
+def attend_back(place, queries, pairs, other_pairs, grads, seqs):
+    queries, pairs, other_pairs, grads = (
+        as_sequences(v, seqs) for v in (queries, pairs, other_pairs, grads)
+    )
+    length = ROWS // seqs
+    first, second = sequence_specs(seqs, length)
+    wide = jax.ShapeDtypeStruct(queries.shape, jnp.float32)
+    narrow = jax.ShapeDtypeStruct(queries.shape, jnp.bfloat16)
+    outs = pl.pallas_call(
+        attend_back_kernel,
+        grid_spec=pltpu.PrefetchScalarGridSpec(
+            num_scalar_prefetch=1,
+            grid=(2, seqs, LOCAL_HEADS // 2),
+            in_specs=[first, first, second, first, second, first],
+            out_specs=[first] * 5,
+            scratch_shapes=[
+                pltpu.VMEM((2 * DEPTH * length, 2 * HEAD_DIM), jnp.float32),
+                pltpu.VMEM((2 * DEPTH * length, 2 * HEAD_DIM), jnp.float32),
+            ],
+        ),
+        out_shape=[wide, wide, wide, narrow, narrow],
+        compiler_params=params(48),
+        cost_estimate=cost(10 * 8 * 2 * 2 * 256 * 2560 * 128, 16 * MIB, 8 * 256 * 2560),
+        name="attend_back",
+    )(place, queries, pairs, pairs, other_pairs, other_pairs, grads)
+    return [v.reshape(PIECES, ROWS, HEAD_COLS) for v in outs]
+
+
+def input_grad_kernel(
+    dq_ref,
+    dk_ref,
+    dv_ref,
+    odk_ref,
+    odv_ref,
+    gg_ref,
+    ug_ref,
+    x_ref,
+    wi_ref,
+    wg_ref,
+    wu_ref,
+    cos_ref,
+    first_ref,
+    second_ref,
+    pg_ref,
+    out_ref,
+    gain_ref,
+    shift_ref,
+    bias_ref,
+):
+    tables = (cos_ref, first_ref, second_ref)
+    query = turned(dq_ref[0] * (HEAD_DIM**-0.5), *tables, -1.0)
+    key = turned(dk_ref[0] + odk_ref[0].astype(jnp.float32), *tables, -1.0)
+    value = dv_ref[0] + odv_ref[0].astype(jnp.float32)
+    low = jnp.concatenate([query, key, value], 1).astype(jnp.bfloat16)
+    pg_ref[0] = low
+    grad = transposed_times(low, wi_ref[...])
+    grad += transposed_times(gg_ref[0], wg_ref[...])
+    grad += transposed_times(ug_ref[0], wu_ref[...])
+    out_ref[0] = grad.astype(jnp.bfloat16)
+    hat, _ = normalised(x_ref[0])
+
+    @pl.when(pl.program_id(0) == 0)
+    def _():
+        gain_ref[...] = jnp.zeros_like(gain_ref)
+        shift_ref[...] = jnp.zeros_like(shift_ref)
+        bias_ref[...] = jnp.zeros_like(bias_ref)
+
+    gain_ref[...] += jnp.sum(grad * hat, axis=0, keepdims=True)
+    shift_ref[...] += jnp.sum(grad, axis=0, keepdims=True)
+    bias_ref[...] += jnp.sum(low.astype(jnp.float32), axis=0, keepdims=True)
+
+
+def input_grads(parts, other_key, other_value, gate_grad, up_grad, pieces, weights, tables):
+    width = pieces.shape[-1]
+    hidden = gate_grad.shape[-1]
+    table_spec = pl.BlockSpec((1,) + tables[0].shape[1:], lambda i: (i % DEPTH, 0, 0))
+    return pl.pallas_call(
+        input_grad_kernel,
+        grid=(PIECES,),
+        in_specs=[piece_spec(HEAD_COLS)] * 5
+        + [piece_spec(hidden)] * 2
+        + [piece_spec(width)]
+        + [whole_spec(w.shape) for w in weights]
+        + [table_spec] * 3,
+        out_specs=[
+            piece_spec(3 * HEAD_COLS),
+            piece_spec(width),
+            whole_spec((1, width)),
+            whole_spec((1, width)),
+            whole_spec((1, 3 * HEAD_COLS)),
+        ],
+        out_shape=[
+            jax.ShapeDtypeStruct((PIECES, ROWS, 3 * HEAD_COLS), jnp.bfloat16),
+            jax.ShapeDtypeStruct((PIECES, ROWS, width), jnp.bfloat16),
+            jax.ShapeDtypeStruct((1, width), jnp.float32),
+            jax.ShapeDtypeStruct((1, width), jnp.float32),
+            jax.ShapeDtypeStruct((1, 3 * HEAD_COLS), jnp.float32),
+        ],
+        compiler_params=params(56),
+        cost_estimate=cost(2 * PIECES * ROWS * width * (3 * HEAD_COLS + 2 * hidden), 48 * MIB),
+        name="input_grads",
+    )(*parts, other_key, other_value, gate_grad, up_grad, pieces, *weights, *tables)
+
+
+def lane_tables(positions):
+    half = ROT // 2
+    place = jnp.arange(HEAD_COLS, dtype=jnp.int32) % HEAD_DIM
+    power = (place % half).astype(jnp.float32)
+    frequency = jnp.where(place < ROT, rotary_base ** (-(2.0 * power) / ROT), 0.0)
+    angles = positions.astype(jnp.float32)[..., None] * frequency
+    sine = jnp.sin(angles)
+    return (
+        jnp.cos(angles),
+        jnp.where(place < half, -sine, 0.0),
+        jnp.where((place >= half) & (place < ROT), sine, 0.0),
+    )
+
+
+def shards_grouped(
+    tokens,
+    lengths,
+    norm_gain,
+    norm_shift,
+    inward_weight,
+    inward_bias,
+    outward_weight,
+    gate_up_weight,
+    down_weight,
+    cotangent,
+):
+    group_len, seqs, width = tokens.shape[1:]
+    bucket, blk = lax.axis_index("bucket"), lax.axis_index("blk")
+    x, core = bucket // 2, bucket % 2
+    z, y = blk // 2, blk % 2
+    devices = 4 * 2 * DEPTH
+
+    shares = jnp.concatenate([norm_gain, norm_shift, inward_bias]).astype(jnp.bfloat16)
+    shares = lax.all_gather(shares, ("bucket", "blk"), axis=0, tiled=False).astype(jnp.float32)
+    gain_share, bias_share = norm_gain.shape[0], inward_bias.shape[0]
+    gain = shares[:, :gain_share].reshape(1, width)
+    shift = shares[:, gain_share : 2 * gain_share].reshape(1, width)
+    bias = shares[:, 2 * gain_share :].reshape(-1)
+
+    def own_columns(values, each):
+        split = values.reshape(2, 2, DEPTH, each)
+        split = lax.dynamic_index_in_dim(split, core, 1, False)
+        return lax.dynamic_index_in_dim(split, z, 1, False)
+
+    key_bias = jnp.pad(
+        own_columns(bias[2 * width :], 2 * ROT).reshape(LOCAL_HEADS, ROT),
+        ((0, 0), (0, HEAD_DIM - ROT)),
+    )
+    own_bias = jnp.concatenate(
+        [
+            own_columns(bias[:width], 2 * HEAD_DIM).reshape(-1),
+            key_bias.reshape(-1),
+            own_columns(bias[width : 2 * width], 2 * HEAD_DIM).reshape(-1),
+        ]
+    ).reshape(1, -1)
+
+    own_rows = inward_weight.shape[0]
+    hidden_each = gate_up_weight.shape[1] // (2 * 2 * 2 * DEPTH)
+    inward = inward_weight.astype(jnp.bfloat16).reshape(own_rows, 3, 2, 2, DEPTH, 2 * HEAD_DIM)
+    inward = jnp.transpose(inward, (3, 4, 0, 1, 2, 5)).reshape(2, DEPTH, own_rows, 3 * HEAD_COLS)
+    gate_up = gate_up_weight.astype(jnp.bfloat16).reshape(own_rows, 2, 2, 2, DEPTH, hidden_each)
+    gate_up = jnp.transpose(gate_up, (3, 4, 0, 1, 2, 5)).reshape(
+        2, DEPTH, own_rows, 4 * hidden_each
+    )
+    inward = columns_of_group(inward, core, z)
+    gate_up = columns_of_group(gate_up, core, z)
+    rows_out = jnp.concatenate([outward_weight, down_weight]).astype(jnp.bfloat16)
+    rows_out = over_columns(rows_out, x, y)
+    outward = rows_out[:, :, : outward_weight.shape[0]].reshape(-1, width)
+    down = rows_out[:, :, outward_weight.shape[0] :].reshape(-1, width)
+
+    def full_rows(value):
+        value = over_columns(value, x, y)
+        return jnp.transpose(value, (0, 3, 2, 1, 4, 5)).reshape(width, -1)
+
+    inward = full_rows(inward)
+    gate_up = full_rows(gate_up)
+    gate_weight = gate_up[:, : 2 * hidden_each]
+    up_weight = gate_up[:, 2 * hidden_each :]
+
+    own_tokens = jnp.transpose(tokens[0], (1, 0, 2))
+    position = blk * group_len + jnp.arange(group_len, dtype=jnp.int32)
+    valid = (position[None, :] < lengths[0][:, None]).astype(jnp.float32)[..., None]
+    own_cotangent = jnp.transpose(cotangent[0], (1, 0, 2)).astype(jnp.float32)
+    own_grad = (own_cotangent * valid).astype(jnp.bfloat16)
+    pieces = jnp.stack(gather_pieces(own_tokens.reshape(ROWS, width), z))
+    grads = jnp.stack(gather_pieces(own_grad.reshape(ROWS, width), z))
+
+    turns = (z - jnp.arange(DEPTH, dtype=jnp.int32)) % DEPTH
+    tables = lane_tables(
+        ((2 * turns + y) * group_len)[:, None] + jnp.arange(group_len, dtype=jnp.int32)
+    )
+    place = jnp.stack([z, y]).astype(jnp.int32)
+
+    normed, queries, pairs = project(pieces, gain, shift, inward, own_bias, tables)
+    other_pairs = lax.ppermute(pairs, "blk", ACROSS_Y)
+    gate, up, hidden = feed(normed, gate_weight, up_weight)
+    attended = attend(place, queries, pairs, other_pairs, seqs)
+    branch = scatter_pieces(branch_terms(attended, hidden, outward, down))
+    branch = branch.reshape(seqs, group_len, width)
+    inputs = own_tokens.astype(jnp.float32)
+    layer_out = (inputs + valid * branch).astype(jnp.bfloat16)
+
+    attended_grad, gate_grad, up_grad = back(grads, gate, up, outward, down)
+    dq, dk, dv, other_dk, other_dv = attend_back(
+        place, queries, pairs, other_pairs, attended_grad, seqs
+    )
+    other_dk = lax.ppermute(other_dk, "blk", ACROSS_Y)
+    other_dv = lax.ppermute(other_dv, "blk", ACROSS_Y)
+    total = PIECES * ROWS
+    flat_normed = normed.reshape(total, width)
+    flat_grads = grads.reshape(total, width)
+    outward_term = times_transposed(attended.reshape(total, -1), flat_grads)
+    down_term = times_transposed(hidden.reshape(total, -1), flat_grads)
+    gate_term = times_transposed(flat_normed, gate_grad.reshape(total, -1))
+    up_term = times_transposed(flat_normed, up_grad.reshape(total, -1))
+    projected_grad, normed_grad, gain_term, shift_term, bias_term = input_grads(
+        (dq, dk, dv),
+        other_dk,
+        other_dv,
+        gate_grad,
+        up_grad,
+        pieces,
+        (inward, gate_weight, up_weight),
+        tables,
+    )
+    inward_term = times_transposed(flat_normed, projected_grad.reshape(total, -1))
+
+    outward_sum = sum_over_columns(outward_term.reshape(2, 2, -1, width), x, y)
+    down_sum = sum_over_columns(down_term.reshape(2, 2, -1, width), x, y)
+
+    def device_rows(term, parts):
+        term = term.reshape(2, 2, DEPTH, 2, own_rows, -1)
+        term = sum_over_columns(jnp.transpose(term, (0, 3, 2, 1, 4, 5)), x, y)
+        term = rows_of_device(term, core, z)
+        term = term.reshape(2, DEPTH, own_rows, parts, 2, -1)
+        return jnp.transpose(term, (2, 3, 4, 0, 1, 5)).reshape(own_rows, -1).astype(jnp.float32)
+
+    gate_up_sum = device_rows(jnp.concatenate([gate_term, up_term], 1), 2)
+    inward_sum = device_rows(inward_term, 3)
+
+    bias_parts = bias_term.reshape(3, 2, 1, 1, 2 * HEAD_DIM)
+    here = (
+        (jnp.arange(2)[:, None] == core) & (jnp.arange(DEPTH)[None, :] == z)
+    ).astype(jnp.float32)[None, None, :, :, None]
+    spread = bias_parts * here
+    key_rot = spread[1].reshape(2, 2, DEPTH, 2, HEAD_DIM)[..., :ROT]
+    bias_all = jnp.concatenate(
+        [spread[0].reshape(-1), spread[2].reshape(-1), key_rot.reshape(-1)]
+    )
+    vector_terms = jnp.concatenate(
+        [
+            gain_term.reshape(devices, -1),
+            shift_term.reshape(devices, -1),
+            bias_all.reshape(devices, -1),
+        ],
+        1,
+    )
+    vector_sums = lax.psum_scatter(
+        vector_terms, ("bucket", "blk"), scatter_dimension=0, tiled=True
+    ).reshape(-1)
+
+    normed_grad = scatter_pieces(normed_grad).reshape(seqs, group_len, width)
+    hat, inverse = normalised(own_tokens)
+    scaled = normed_grad * gain.reshape(width)
+    input_grad = inverse * (
+        scaled
+        - jnp.mean(scaled, axis=-1, keepdims=True)
+        - hat * jnp.mean(scaled * hat, axis=-1, keepdims=True)
+    )
+    tokens_grad = (own_cotangent + input_grad).astype(jnp.bfloat16)
+
+    def placed(value):
+        return jnp.transpose(value, (1, 0, 2)).reshape(tokens.shape)
+
+    return (
+        placed(layer_out),
+        placed(tokens_grad),
+        vector_sums[:gain_share],
+        vector_sums[gain_share : 2 * gain_share],
+        inward_sum,
+        vector_sums[2 * gain_share :],
+        outward_sum,
+        gate_up_sum,
+        down_sum,
+    )
+
+
 def solution(mesh):
     in_specs = (
         P("bucket", "blk", None, None),
@@ -373,4 +1062,5 @@
         P(("bucket", "blk"), None),
         P(("bucket", "blk"), None),
     )
-    return jax.shard_map(shards, mesh=mesh, in_specs=in_specs, out_specs=out_specs, check_vma=False)
+    body = shards_grouped if fits_groups(mesh) else shards_general
+    return jax.shard_map(body, mesh=mesh, in_specs=in_specs, out_specs=out_specs, check_vma=False)

time: 5340 us -> 957 us (0.18)
  waiting for transfers between devices: 4230 us -> 348 us
  matrix products: 263 us -> 49.5 us
  starting transfers between devices: 283 us -> 110 us
  Pallas kernels: 0 us -> 151 us
  blocking collectives: 203 us -> 102 us
  other arithmetic: 165 us -> 74.5 us
  local copies, waits for them, and re-layouts: 162 us -> 104 us
    reduce_scatter x4 -> x0, waiting for transfers between devices: 3240 us -> none  [the longest x1 1930 us: shards(): lax.psum_scatter(gate_up_term, ('bucket', 'blk'), scatter_dimension=0, ti...]
    all_gather x5 -> x0, waiting for transfers between devices: 337 us -> none  [the longest x1 205 us: shards(): lax.all_gather(packed, 'blk', axis=0, tiled=True)]
    ppermute x16 -> x67, waiting for transfers between devices: 655 us -> 348 us  [the longest x6 162 us: scatter_pieces(): lax.ppermute(both.astype(jnp.bfloat16), 'blk', around(-step))]
    dot_general x29 -> x0, matrix products: 178 us -> none  [the longest x4 67.6 us: transposed_times(): lax.dot_general(left, right, (((1,), (1,)), ((), ())), preferred_element_...]
    ppermute x16 -> x67, starting transfers between devices: 282 us -> 110 us  [the longest x6 22.9 us: gather_pieces(): down.append(lax.ppermute(down[-1], 'blk', DOWNWARD))]
    unnamed x2 -> x1, blocking collectives: 203 us -> 41 us
    pallas_call x0 -> x7, Pallas kernels: none -> 151 us  [the longest x1 33.8 us: input_grads(): pl.pallas_call(input_grad_kernel, grid=(PIECES,), in_specs=[piece_spec(HE...]
    convert_element_type x31 -> x12, other arithmetic: 82.3 us -> 16.8 us  [the longest x2 9.08 us: scatter_pieces(): both.astype(jnp.bfloat16)]
  transfers between devices with their start and end apart: 25 -> 67, of which waited for: 21 -> 27; matrix products, arithmetic and copies ran while one was open for 11% -> 22% of each run, Pallas kernels for 0% -> 16%
where the time goes in v1:
time: 957 us; the launch traced here: 943 us
  waiting for transfers between devices  348 us (36%)
  Pallas kernels  151 us (16%)
  starting transfers between devices  110 us (11%)
  local copies, waits for them, and re-layouts  104 us (11%)
  blocking collectives  102 us (11%)
  other arithmetic  74.5 us (8%)
  matrix products  49.5 us (5%)
    ppermute x6, waiting for transfers between devices, scatter_pieces(): lax.ppermute(both.astype(jnp.bfloat16), 'blk', around(-step))  162 us
    all_gather x1, blocking collectives, shards_grouped(): lax.all_gather(shares, ('bucket', 'blk'), axis=0, tiled=False)  61.4 us
    dot_general x5, matrix products, times_transposed(): lax.dot_general(left, right, (((0,), (0,)), ((), ())), preferred_element_...  49.5 us
    ppermute x6, waiting for transfers between devices, gather_pieces(): down.append(lax.ppermute(down[-1], 'blk', DOWNWARD))  45.4 us
    ppermute x3, waiting for transfers between devices, over_columns(): value = in_order(value, lax.ppermute(value, 'blk', ACROSS_Y), y, 0)  41.9 us
    unnamed x1, blocking collectives  41 us
    ppermute x6, waiting for transfers between devices, rows_of_device(): parts.append(lax.ppermute(chunk, 'blk', around(step)))  40 us
    pallas_call x1, Pallas kernels, input_grads(): pl.pallas_call(input_grad_kernel, grid=(PIECES,), in_specs=[piece_spec(HE...  33.8 us
  transfers between devices with their start and end apart: 67, of which 27 were waited for; matrix products, arithmetic and copies ran while one was open for 22% of the time, Pallas kernels for 16%

profile of v1, /device:TPU:11, one launch (start us, length us, event | category | flops | bytes accessed | tf_op | source)
XLA Modules:
  0.0 942.9 jit_solution(5267435834938586522)
XLA Ops:
  3.3 3.2 collective-permute-start
  6.5 3.1 collective-permute-start.1
  21.6 61.4 %all-gather = bf16[32,1,272]{2,1,0:T(2,128)(2,1)S(1)} all-gather(bf16[1,1,272]{2,1,0:T(2,128)(2,1)S(1)} %maximum_bitcast_fusion.1), channel_id=1, replica_groups=mesh['bucket'=4,'blk'=8] {'bucket','blk'}, dimensions={0}, use_global_device_ids=true | all-gather | bytes 17952 | tf_op jit(solution)/shard_map/all_gather | solution.py:886
  97.6 3.9 collective-permute-start.13
  101.5 3.3 collective-permute-start.12
  108.8 7.6 collective-permute-done.12
  116.5 4.1 collective-permute-start.19
  120.6 16.0 %collective-permute-done.11 = bf16[2,64,768]{2,1,0:T(8,128)(2,1)S(1)} collective-permute-done((bf16[2,64,768]{2,1,0:T(8,128)(2,1)S(1)}, bf16[2,64,768]{2,1,0:T(8,128)(2,1)S(1)}, u32[]{:S(2)}, u32[]{:S(2)}) %collective-permute-start.11) | collective-permute-done | bytes 196640 | tf_op jit(solution)/shard_map/ppermute | solution.py:412
  145.8 6.0 collective-permute-done.18
  158.3 15.9 %collective-permute-done.14 = bf16[4,2,64,768]{3,2,0,1:T(8,128)(2,1)S(1)} collective-permute-done((bf16[4,2,64,768]{3,2,0,1:T(8,128)(2,1)S(1)}, bf16[4,2,64,768]{3,2,0,1:T(8,128)(2,1)S(1)}, u32[]{:S(2)}, u32[]{:S(2)}) %collective-permute-start.14) | collective-permute-done | bytes 786464 | tf_op jit(solution)/shard_map/ppermute | solution.py:420
  174.2 2.7 collective-permute-start.32
  177.5 4.1 collective-permute-start.33
  181.7 23.5 %collective-permute-done.21 = bf16[4,2,64,1408]{3,2,0,1:T(8,128)(2,1)S(1)} collective-permute-done((bf16[4,2,64,1408]{3,2,0,1:T(8,128)(2,1)S(1)}, bf16[4,2,64,1408]{3,2,0,1:T(8,128)(2,1)S(1)}, u32[]{:S(2)}, u32[]{:S(2)}) %collective-permute-start.21) | collective-permute-done | bytes 1441824 | tf_op jit(solution)/shard_map/ppermute | solution.py:420
  205.1 5.5 collective-permute-start.2
  213.9 3.4 collective-permute-start.34
  217.3 12.2 %collective-permute-done.2 = bf16[256,2048]{1,0:T(8,128)(2,1)S(1)} collective-permute-done((bf16[256,2048]{1,0:T(8,128)(2,1)}, bf16[256,2048]{1,0:T(8,128)(2,1)S(1)}, u32[]{:S(2)}, u32[]{:S(2)}) %collective-permute-start.2) | collective-permute-done | bytes 1048608 | tf_op jit(solution)/shard_map/ppermute | solution.py:385
  231.5 3.4 collective-permute-start.3
  240.4 2.8 collective-permute-done.15
  243.2 9.2 collective-permute-start.6
  256.2 3.4 collective-permute-start.35
  259.7 14.7 %collective-permute-done.3 = bf16[256,2048]{1,0:T(8,128)(2,1)S(1)} collective-permute-done((bf16[256,2048]{1,0:T(8,128)(2,1)S(1)}, bf16[256,2048]{1,0:T(8,128)(2,1)S(1)}, u32[]{:S(2)}, u32[]{:S(2)}) %collective-permute-start.3) | collective-permute-done | bytes 1048608 | tf_op jit(solution)/shard_map/ppermute | solution.py:385
  278.3 18.5 %collective-permute-done.35 = bf16[256,2048]{1,0:T(8,128)(2,1)S(1)} collective-permute-done((bf16[256,2048]{1,0:T(8,128)(2,1)S(1)}, bf16[256,2048]{1,0:T(8,128)(2,1)S(1)}, u32[]{:S(2)}, u32[]{:S(2)}) %collective-permute-start.35) | collective-permute-done | bytes 1048608 | tf_op jit(solution)/shard_map/ppermute | solution.py:385
  300.8 5.0 collective-permute-start.7
  312.3 3.3 copy-done.30
  315.6 17.2 %project.1 = (bf16[8,256,2048]{2,1,0:T(8,128)(2,1)}, bf16[8,256,256]{2,1,0:T(8,128)(2,1)S(1)}, bf16[8,256,512]{2,1,0:T(8,128)(2,1)}) custom-call(bf16[8,256,2048]{2,1,0:T(8,128)(2,1)} %copy-done.30, f32[1,2048]{1,0:T(1,128)S(1)} %reshape.677.gain_ref, f32[1,2048]{1,0:T(1,128)S(1)} %reshape.678.shift_ref, bf16[2048,768]{1,0:T(8,128)(2,1)} %bitcast.371, ...), custom_call_target="tpu_custom_call" | custom-call | flops 6442450944 | bytes 25165824 | tf_op jit(solution)/shard_map/project/pallas_call | solution.py:506
  335.0 12.3 %copy.109 = bf16[2048,2048]{1,0:T(8,128)(2,1)} copy(bf16[2048,2048]{0,1:T(8,128)(2,1)} %bitcast.357) | data formatting | bytes 16777216 | tf_op jit(solution)/shard_map/dot_general | solution.py:41
  356.4 4.1 maximum_select_fusion
  360.6 4.4 fusion.56
  365.0 18.7 %feed.1 = (f32[8,256,704]{2,1,0:T(8,128)}, f32[8,256,704]{2,1,0:T(8,128)}, bf16[8,256,704]{2,1,0:T(8,128)(2,1)S(1)}) custom-call(bf16[8,256,2048]{2,1,0:T(8,128)(2,1)} %get-tuple-element.30.n_ref, bf16[2048,704]{1,0:T(8,128)(2,1)} %get-tuple-element.85.wg_ref, bf16[2048,704]{1,0:T(8,128)(2,1)} %get-tuple-element.84.wu_ref), custom_call_target="tpu_custom_call" | custom-call | flops 11811160064 | bytes 29360128 | tf_op jit(solution)/shard_map/feed/pallas_call | solution.py:543
  383.7 16.8 %back.1 = (bf16[8,256,256]{2,1,0:T(8,128)(2,1)S(1)}, bf16[8,256,704]{2,1,0:T(8,128)(2,1)}, bf16[8,256,704]{2,1,0:T(8,128)(2,1)}) custom-call(bf16[8,256,2048]{2,1,0:T(8,128)(2,1)} %bitcast_dynamic-update-slice_fusion.g_ref, f32[8,256,704]{2,1,0:T(8,128)} %get-tuple-element.32.gate_ref, f32[8,256,704]{2,1,0:T(8,128)} %get-tuple-element.33.up_ref, ...), custom_call_target="tpu_custom_call" | custom-call | flops 8053063680 | bytes 29360128 | tf_op jit(solution)/shard_map/back/pallas_call | solution.py:598
  400.6 11.6 %convolution_bitcast_fusion = f32[2048,704]{0,1:T(8,128)} fusion(bf16[8,256,2048]{2,1,0:T(8,128)(2,1)} %get-tuple-element.30.n_ref, bf16[8,256,704]{2,1,0:T(8,128)(2,1)} %get-tuple-element.41.ug_ref), kind=kOutput, calls=%fused_computation.5 | convolution fusion | flops 5905580032 | bytes 17039360 | tf_op jit(solution)/shard_map/dot_general | solution.py:41
  412.2 10.4 %convolution_bitcast_fusion.1 = f32[2048,704]{0,1:T(8,128)} fusion(bf16[8,256,2048]{2,1,0:T(8,128)(2,1)} %get-tuple-element.30.n_ref, bf16[8,256,704]{2,1,0:T(8,128)(2,1)S(1)} %copy-done.44), kind=kOutput, calls=%fused_computation.6 | convolution fusion | flops 5905580032 | bytes 17039360 | tf_op jit(solution)/shard_map/dot_general | solution.py:41
  422.6 10.4 %pad_maximum_fusion = f32[2048,1408]{0,1:T(8,128)} fusion(f32[2048,704]{0,1:T(8,128)} %convolution_bitcast_fusion, f32[2048,704]{0,1:T(8,128)} %convolution_bitcast_fusion.1), kind=kLoop, calls=%fused_computation | loop fusion | flops 2883584 | bytes 23068672 | tf_op jit(solution)/shard_map/concatenate | solution.py:991
  433.0 11.9 %copy.114 = f32[2048,1408]{1,0:T(8,128)} copy(f32[2048,1408]{0,1:T(8,128)} %pad_maximum_fusion) | data formatting | bytes 23068672 | tf_op jit(solution)/shard_map/concatenate | solution.py:991
  444.9 4.6 fusion
  449.8 2.8 copy.118
  452.6 9.4 fusion.62
  465.0 20.0 %attend.1 = bf16[2,4,2,128,256]{4,3,2,1,0:T(8,128)(2,1)S(1)} custom-call(s32[2]{0:T(128)S(1)} %pad_add_fusion.place_ref, bf16[2,4,2,128,256]{4,3,2,1,0:T(8,128)(2,1)S(1)} %bitcast.342, bf16[2,4,2,128,512]{4,3,2,1,0:T(8,128)(2,1)} %bitcast.41.k_ref.v_ref, bf16[2,4,2,128,512]{4,3,2,1,0:T(8,128)(2,1)} %bitcast.41.k_ref.v_ref, ...), custom_call_target="tpu_custom_call" | custom-call | flops 10737418240 | bytes 8388608 | tf_op jit(solution)/shard_map/attend/pallas_call | solution.py:733
  485.1 32.5 %attend_back.1 = (f32[2,4,2,128,256]{4,3,2,1,0:T(8,128)}, f32[2,4,2,128,256]{4,3,2,1,0:T(8,128)}, f32[2,4,2,128,256]{4,3,2,1,0:T(8,128)}, bf16[2,4,2,128,256]{4,...) custom-call(s32[2]{0:T(128)S(1)} %pad_add_fusion.place_ref, bf16[2,4,2,128,256]{4,3,2,1,0:T(8,128)(2,1)S(1)} %bitcast.343, ...), custom_call_target="tpu_custom_call" | custom-call | flops 26843545600 | bytes 16777216 | tf_op jit(solution)/shard_map/attend_back/pallas_call | solution.py:757
  519.0 12.1 %branch_terms.1 = bf16[8,256,2048]{2,1,0:T(8,128)(2,1)} custom-call(bf16[8,256,256]{2,1,0:T(8,128)(2,1)S(1)} %bitcast.338, bf16[8,256,704]{2,1,0:T(8,128)(2,1)} %copy-done, bf16[256,2048]{1,0:T(8,128)(2,1)S(1)} %bitcast.337, bf16[704,2048]{1,0:T(8,128)(2,1)S(1)} %bitcast.335), custom_call_target="tpu_custom_call" | custom-call | flops 8053063680 | bytes 16777216 | tf_op jit(solution)/shard_map/branch_terms/pallas_call | solution.py:567
  532.5 6.2 fusion.61
  542.2 10.8 %collective-permute-done.57 = bf16[2,64,2048]{2,1,0:T(8,128)(2,1)S(1)} collective-permute-done((bf16[2,64,2048]{2,1,0:T(8,128)(2,1)S(1)}, bf16[2,64,2048]{2,1,0:T(8,128)(2,1)S(1)}, u32[]{:S(2)}, u32[]{:S(2)}) %collective-permute-start.57) | collective-permute-done | bytes 524320 | tf_op jit(solution)/shard_map/ppermute | solution.py:427
  553.0 3.8 collective-permute-start.26
  560.7 4.8 collective-permute-done.58
  565.5 5.7 collective-permute-start.30
  572.9 33.8 %input_grads.1 = (bf16[8,256,768]{2,1,0:T(8,128)(2,1)}, bf16[8,256,2048]{2,1,0:T(8,128)(2,1)}, f32[1,2048]{1,0:T(1,128)}, f32[1,2048]{1,0:T(1,128)}, f32[1,768]{1,0:T(1,128)}) custom-call(f32[8,256,256]{2,1,0:T(8,128)} %bitcast.409, f32[8,256,256]{2,1,0:T(8,128)} %bitcast.410, f32[8,256,256]{2,1,0:T(8,128)} %bitcast.411, ...), custom_call_target="tpu_custom_call" | custom-call | flops 18253611008 | bytes 50331648 | tf_op jit(solution)/shard_map/input_grads/pallas_call | solution.py:825
  606.7 11.9 %fusion.60 = f32[2,2,4,2,64,768]{5,4,3,2,1,0:T(8,128)} fusion(bf16[2,2,4,2,64,2048]{5,4,3,2,1,0:T(8,128)(2,1)} %bitcast.356, bf16[2048,768,1,1,1,1]{1,0,5,4,3,2:T(8,128)(2,1)} %bitcast.408), kind=kOutput, calls=%fused_computation.234 | convolution fusion | flops 6442450944 | bytes 17825792 | tf_op jit(solution)/shard_map/dot_general | solution.py:41
  621.1 41.0 %all-reduce.1 = f32[32,272]{1,0:T(8,128)S(1)} all-reduce(f32[32,272]{1,0:T(8,128)S(1)} %pad_maximum_fusion.14), channel_id=2, replica_groups=mesh['bucket'=4,'blk'=8] {'bucket','blk'}, use_global_device_ids=true, to_apply=%region_4.5.clone | all-reduce | flops 8704 | bytes 69632
  664.8 3.9 slice_bitcast_fusion.11
  671.7 5.7 fusion.21
  684.3 3.4 fusion.15
  688.9 14.5 %collective-permute-done.31 = bf16[256,2048]{1,0:T(8,128)(2,1)} collective-permute-done((bf16[256,2048]{1,0:T(8,128)(2,1)}, bf16[256,2048]{1,0:T(8,128)(2,1)}, u32[]{:S(2)}, u32[]{:S(2)}) %collective-permute-start.31) | collective-permute-done | bytes 1048608 | tf_op jit(solution)/shard_map/ppermute | solution.py:399
  703.7 65.3 %collective-permute-done.29 = bf16[256,2048]{1,0:T(8,128)(2,1)} collective-permute-done((bf16[256,2048]{1,0:T(8,128)(2,1)}, bf16[256,2048]{1,0:T(8,128)(2,1)}, u32[]{:S(2)}, u32[]{:S(2)}) %collective-permute-start.29) | collective-permute-done | bytes 1048608 | tf_op jit(solution)/shard_map/ppermute | solution.py:399
  769.0 3.1 collective-permute-start.48
  772.1 44.3 %collective-permute-done.27 = bf16[256,2048]{1,0:T(8,128)(2,1)} collective-permute-done((bf16[256,2048]{1,0:T(8,128)(2,1)}, bf16[256,2048]{1,0:T(8,128)(2,1)}, u32[]{:S(2)}, u32[]{:S(2)}) %collective-permute-start.27) | collective-permute-done | bytes 1048608 | tf_op jit(solution)/shard_map/ppermute | solution.py:399
  816.4 3.4 fusion.24
  823.3 13.0 %collective-permute-done.50 = bf16[256,2048]{1,0:T(8,128)(2,1)S(1)} collective-permute-done((bf16[256,2048]{1,0:T(8,128)(2,1)S(1)}, bf16[256,2048]{1,0:T(8,128)(2,1)S(1)}, u32[]{:S(2)}, u32[]{:S(2)}) %collective-permute-start.50) | collective-permute-done | bytes 1048608 | tf_op jit(solution)/shard_map/ppermute | solution.py:399
  836.3 22.5 %collective-permute-done.48 = bf16[256,2048]{1,0:T(8,128)(2,1)S(1)} collective-permute-done((bf16[256,2048]{1,0:T(8,128)(2,1)S(1)}, bf16[256,2048]{1,0:T(8,128)(2,1)S(1)}, u32[]{:S(2)}, u32[]{:S(2)}) %collective-permute-start.48) | collective-permute-done | bytes 1048608 | tf_op jit(solution)/shard_map/ppermute | solution.py:399
  862.9 6.4 collective-permute-done.52
  877.4 8.2 collective-permute-done.54
  885.6 18.0 %collective-permute-done.53 = bf16[2,64,768]{2,1,0:T(8,128)(2,1)S(1)} collective-permute-done((bf16[2,64,768]{2,1,0:T(8,128)(2,1)S(1)}, bf16[2,64,768]{2,1,0:T(8,128)(2,1)S(1)}, u32[]{:S(2)}, u32[]{:S(2)}) %collective-permute-start.53) | collective-permute-done | bytes 196640 | tf_op jit(solution)/shard_map/ppermute | solution.py:438
  905.3 5.3 collective-permute-done.63
  911.4 7.7 collective-permute-done.61
  938.0 4.4 reshape.728
  (368 shorter events, 157.5 us)
Async XLA Ops:
  3.3 208.0 %collective-permute-start = (bf16[256,2048]{1,0:T(8,128)(2,1)}, bf16[256,2048]{1,0:T(8,128)(2,1)}, u32[]{:S(2)}, u32[]{:S(2)}) collective-permute-start(bf16[256,2048]{1,0:T(8,128)(2,1)} %bitcast.7), channel_id=1, source_target_pairs={{0,2},{1,3},{2,4},{3,5},{4,6},{5,7},{8,10},{9,11},{10,12},{11,13},... | collective-permute-start | bytes 3145736 | tf_op jit(solution)/shard_map/ppermute | solution.py:384
  6.5 171.0 %collective-permute-start.1 = (bf16[256,2048]{1,0:T(8,128)(2,1)}, bf16[256,2048]{1,0:T(8,128)(2,1)}, u32[]{:S(2)}, u32[]{:S(2)}) collective-permute-start(bf16[256,2048]{1,0:T(8,128)(2,1)} %bitcast.7), channel_id=1, source_target_pairs={{2,0},{3,1},{4,2},{5,3},{6,4},{7,5},{10,8},{11,9},{12,10},{13,11},... | collective-permute-start | bytes 3145736 | tf_op jit(solution)/shard_map/ppermute | solution.py:385
  12.2 83.5 %collective-permute-start.10 = (bf16[4,64,768]{2,1,0:T(8,128)(2,1)}, bf16[4,64,768]{2,1,0:T(8,128)(2,1)}, u32[]{:S(2)}, u32[]{:S(2)}) collective-permute-start(bf16[4,64,768]{2,1,0:T(8,128)(2,1)} %get-tuple-element.137), channel_id=1, source_target_pairs={{0,8},{8,0},{16,24},{24,16},{1,9},{9,1},{17,25},{25,17},{2,10},{10... | collective-permute-start | bytes 1179656 | tf_op jit(solution)/shard_map/ppermute | solution.py:407
  21.5 83.3 %collective-permute-start.17 = (bf16[4,64,1408]{2,1,0:T(8,128)(2,1)}, bf16[4,64,1408]{2,1,0:T(8,128)(2,1)}, u32[]{:S(2)}, u32[]{:S(2)}) collective-permute-start(bf16[4,64,1408]{2,1,0:T(8,128)(2,1)} %get-tuple-element.112), channel_id=1, source_target_pairs={{0,8},{8,0},{16,24},{24,16},{1,9},{9,1},{17,25},{25,17},{2,10},{10... | collective-permute-start | bytes 2162696 | tf_op jit(solution)/shard_map/ppermute | solution.py:407
  97.6 11.2 %collective-permute-start.13 = (bf16[2,64,768]{2,1,0:T(8,128)(2,1)S(1)}, bf16[2,64,768]{2,1,0:T(8,128)(2,1)S(1)}, u32[]{:S(2)}, u32[]{:S(2)}) collective-permute-start(bf16[2,64,768]{2,1,0:T(8,128)(2,1)S(1)} %get-tuple-element.133), channel_id=1, source_target_pairs={{0,6},{1,7},{2,0},{3,1},{4,2},{5,3},{6,4},{7,5},{8,14},{9,15},{10,... | collective-permute-start | bytes 589832 | tf_op jit(solution)/shard_map/ppermute | solution.py:412
  101.5 15.0 %collective-permute-start.12 = (bf16[2,64,768]{2,1,0:T(8,128)(2,1)S(1)}, bf16[2,64,768]{2,1,0:T(8,128)(2,1)S(1)}, u32[]{:S(2)}, u32[]{:S(2)}) collective-permute-start(bf16[2,64,768]{2,1,0:T(8,128)(2,1)S(1)} %get-tuple-element.134), channel_id=1, source_target_pairs={{0,4},{1,5},{2,6},{3,7},{4,0},{5,1},{6,2},{7,3},{8,12},{9,13},{10,... | collective-permute-start | bytes 589832 | tf_op jit(solution)/shard_map/ppermute | solution.py:412
  104.8 31.9 %collective-permute-start.11 = (bf16[2,64,768]{2,1,0:T(8,128)(2,1)S(1)}, bf16[2,64,768]{2,1,0:T(8,128)(2,1)S(1)}, u32[]{:S(2)}, u32[]{:S(2)}) collective-permute-start(bf16[2,64,768]{2,1,0:T(8,128)(2,1)S(1)} %get-tuple-element.135), channel_id=1, source_target_pairs={{0,2},{1,3},{2,4},{3,5},{4,6},{5,7},{6,0},{7,1},{8,10},{9,11},{10,... | collective-permute-start | bytes 589832 | tf_op jit(solution)/shard_map/ppermute | solution.py:412
  108.8 30.9 %collective-permute-start.20 = (bf16[2,64,1408]{2,1,0:T(8,128)(2,1)S(1)}, bf16[2,64,1408]{2,1,0:T(8,128)(2,1)S(1)}, u32[]{:S(2)}, u32[]{:S(2)}) collective-permute-start(bf16[2,64,1408]{2,1,0:T(8,128)(2,1)S(1)} %get-tuple-element.108), channel_id=1, source_target_pairs={{0,6},{1,7},{2,0},{3,1},{4,2},{5,3},{6,4},{7,5},{8,14},{9,15},{10,... | collective-permute-start | bytes 1081352 | tf_op jit(solution)/shard_map/ppermute | solution.py:412
  116.5 27.6 %collective-permute-start.19 = (bf16[2,64,1408]{2,1,0:T(8,128)(2,1)S(1)}, bf16[2,64,1408]{2,1,0:T(8,128)(2,1)S(1)}, u32[]{:S(2)}, u32[]{:S(2)}) collective-permute-start(bf16[2,64,1408]{2,1,0:T(8,128)(2,1)S(1)} %get-tuple-element.109), channel_id=1, source_target_pairs={{0,4},{1,5},{2,6},{3,7},{4,0},{5,1},{6,2},{7,3},{8,12},{9,13},{10,... | collective-permute-start | bytes 1081352 | tf_op jit(solution)/shard_map/ppermute | solution.py:412
  136.6 15.2 %collective-permute-start.18 = (bf16[2,64,1408]{2,1,0:T(8,128)(2,1)S(1)}, bf16[2,64,1408]{2,1,0:T(8,128)(2,1)S(1)}, u32[]{:S(2)}, u32[]{:S(2)}) collective-permute-start(bf16[2,64,1408]{2,1,0:T(8,128)(2,1)S(1)} %get-tuple-element.110), channel_id=1, source_target_pairs={{0,2},{1,3},{2,4},{3,5},{4,6},{5,7},{6,0},{7,1},{8,10},{9,11},{10,... | collective-permute-start | bytes 1081352 | tf_op jit(solution)/shard_map/ppermute | solution.py:412
  140.6 16.8 %collective-permute-start.23 = (bf16[240,2048]{1,0:T(8,128)(2,1)S(1)}, bf16[240,2048]{1,0:T(8,128)(2,1)S(1)}, u32[]{:S(2)}, u32[]{:S(2)}) collective-permute-start(bf16[240,2048]{1,0:T(8,128)(2,1)S(1)} %copy-done.28), channel_id=1, source_target_pairs={{0,1},{1,0},{2,3},{3,2},{4,5},{5,4},{6,7},{7,6},{8,9},{9,8},{10,11... | collective-permute-start | bytes 2949128 | tf_op jit(solution)/shard_map/ppermute | solution.py:420
  144.1 30.1 %collective-permute-start.14 = (bf16[4,2,64,768]{3,2,0,1:T(8,128)(2,1)S(1)}, bf16[4,2,64,768]{3,2,0,1:T(8,128)(2,1)S(1)}, u32[]{:S(2)}, u32[]{:S(2)}) collective-permute-start(bf16[4,2,64,768]{3,2,0,1:T(8,128)(2,1)S(1)} %get-tuple-element.127), channel_id=1, source_target_pairs={{0,1},{1,0},{2,3},{3,2},{4,5},{5,4},{6,7},{7,6},{8,9},{9,8},{10,11... | collective-permute-start | bytes 2359304 | tf_op jit(solution)/shard_map/ppermute | solution.py:420
  152.5 52.6 %collective-permute-start.21 = (bf16[4,2,64,1408]{3,2,0,1:T(8,128)(2,1)S(1)}, bf16[4,2,64,1408]{3,2,0,1:T(8,128)(2,1)S(1)}, u32[]{:S(2)}, u32[]{:S(2)}) collective-permute-start(bf16[4,2,64,1408]{3,2,0,1:T(8,128)(2,1)S(1)} %get-tuple-element.102), channel_id=1, source_target_pairs={{0,1},{1,0},{2,3},{3,2},{4,5},{5,4},{6,7},{7,6},{8,9},{9,8},{10,11... | collective-permute-start | bytes 4325384 | tf_op jit(solution)/shard_map/ppermute | solution.py:420
  157.9 73.6 %collective-permute-start.24 = (bf16[2,240,2048]{2,1,0:T(8,128)(2,1)S(1)}, bf16[2,240,2048]{2,1,0:T(8,128)(2,1)S(1)}, u32[]{:S(2)}, u32[]{:S(2)}) collective-permute-start(bf16[2,240,2048]{2,1,0:T(8,128)(2,1)S(1)} %maximum_select_fusion.5), channel_id=1, source_target_pairs={{0,16},{8,24},{16,0},{24,8},{1,17},{9,25},{17,1},{25,9},{2,18},{10... | collective-permute-start | bytes 5898248 | tf_op jit(solution)/shard_map/ppermute | solution.py:421
  174.2 37.7 %collective-permute-start.32 = (bf16[256,2048]{1,0:T(8,128)(2,1)S(1)}, bf16[256,2048]{1,0:T(8,128)(2,1)S(1)}, u32[]{:S(2)}, u32[]{:S(2)}) collective-permute-start(bf16[256,2048]{1,0:T(8,128)(2,1)S(1)} %bitcast.362), channel_id=1, source_target_pairs={{0,2},{1,3},{2,4},{3,5},{4,6},{5,7},{8,10},{9,11},{10,12},{11,13},... | collective-permute-start | bytes 3145736 | tf_op jit(solution)/shard_map/ppermute | solution.py:384
  177.5 36.4 %collective-permute-start.33 = (bf16[256,2048]{1,0:T(8,128)(2,1)S(1)}, bf16[256,2048]{1,0:T(8,128)(2,1)S(1)}, u32[]{:S(2)}, u32[]{:S(2)}) collective-permute-start(bf16[256,2048]{1,0:T(8,128)(2,1)S(1)} %bitcast.363), channel_id=1, source_target_pairs={{2,0},{3,1},{4,2},{5,3},{6,4},{7,5},{10,8},{11,9},{12,10},{13,11},... | collective-permute-start | bytes 3145736 | tf_op jit(solution)/shard_map/ppermute | solution.py:385
  205.1 24.4 %collective-permute-start.2 = (bf16[256,2048]{1,0:T(8,128)(2,1)}, bf16[256,2048]{1,0:T(8,128)(2,1)S(1)}, u32[]{:S(2)}, u32[]{:S(2)}) collective-permute-start(bf16[256,2048]{1,0:T(8,128)(2,1)} %collective-permute-done.1), channel_id=1, source_target_pairs={{2,0},{3,1},{4,2},{5,3},{6,4},{7,5},{10,8},{11,9},{12,10},{13,11},... | collective-permute-start | bytes 3145736 | tf_op jit(solution)/shard_map/ppermute | solution.py:385
  211.3 31.9 %collective-permute-start.15 = (bf16[2,4,2,64,768]{4,3,0,1,2:T(8,128)(2,1)S(1)}, bf16[2,4,2,64,768]{4,3,0,1,2:T(8,128)(2,1)S(1)}, u32[]{:S(2)}, u32[]{:S(2)}) collective-permute-start(bf16[2,4,2,64,768]{4,3,0,1,2:T(8,128)(2,1)S(1)} %maximum_select_fusion.6), channel_id=1, source_target_pairs={{0,16},{8,24},{16,0},{24,8},{1,17},{9,25},{17,1},{25,9},{2,18},{10... | collective-permute-start | bytes 4718600 | tf_op jit(solution)/shard_map/ppermute | solution.py:421
  212.0 42.3 %collective-permute-start.4 = (bf16[256,2048]{1,0:T(8,128)(2,1)}, bf16[256,2048]{1,0:T(8,128)(2,1)S(1)}, u32[]{:S(2)}, u32[]{:S(2)}) collective-permute-start(bf16[256,2048]{1,0:T(8,128)(2,1)} %collective-permute-done), channel_id=1, source_target_pairs={{0,2},{1,3},{2,4},{3,5},{4,6},{5,7},{8,10},{9,11},{10,12},{11,13},... | collective-permute-start | bytes 3145736 | tf_op jit(solution)/shard_map/ppermute | solution.py:384
  213.9 40.4 %collective-permute-start.34 = (bf16[256,2048]{1,0:T(8,128)(2,1)S(1)}, bf16[256,2048]{1,0:T(8,128)(2,1)S(1)}, u32[]{:S(2)}, u32[]{:S(2)}) collective-permute-start(bf16[256,2048]{1,0:T(8,128)(2,1)S(1)} %collective-permute-done.33), channel_id=1, source_target_pairs={{2,0},{3,1},{4,2},{5,3},{6,4},{7,5},{10,8},{11,9},{12,10},{13,11},... | collective-permute-start | bytes 3145736 | tf_op jit(solution)/shard_map/ppermute | solution.py:385
  229.5 26.7 %collective-permute-start.36 = (bf16[256,2048]{1,0:T(8,128)(2,1)S(1)}, bf16[256,2048]{1,0:T(8,128)(2,1)S(1)}, u32[]{:S(2)}, u32[]{:S(2)}) collective-permute-start(bf16[256,2048]{1,0:T(8,128)(2,1)S(1)} %collective-permute-done.32), channel_id=1, source_target_pairs={{0,2},{1,3},{2,4},{3,5},{4,6},{5,7},{8,10},{9,11},{10,12},{11,13},... | collective-permute-start | bytes 3145736 | tf_op jit(solution)/shard_map/ppermute | solution.py:384
  231.5 42.9 %collective-permute-start.3 = (bf16[256,2048]{1,0:T(8,128)(2,1)S(1)}, bf16[256,2048]{1,0:T(8,128)(2,1)S(1)}, u32[]{:S(2)}, u32[]{:S(2)}) collective-permute-start(bf16[256,2048]{1,0:T(8,128)(2,1)S(1)} %collective-permute-done.2), channel_id=1, source_target_pairs={{2,0},{3,1},{4,2},{5,3},{6,4},{7,5},{10,8},{11,9},{12,10},{13,11},... | collective-permute-start | bytes 3145736 | tf_op jit(solution)/shard_map/ppermute | solution.py:385
  243.2 66.2 %collective-permute-start.6 = (bf16[256,2048]{1,0:T(8,128)(2,1)}, bf16[256,2048]{1,0:T(8,128)(2,1)S(1)}, u32[]{:S(2)}, u32[]{:S(2)}) collective-permute-start(bf16[256,2048]{1,0:T(8,128)(2,1)} %bitcast.7), channel_id=1, source_target_pairs={{0,8},{8,0},{16,24},{24,16},{1,9},{9,1},{17,25},{25,17},{2,10},{10... | collective-permute-start | bytes 3145736 | tf_op jit(solution)/shard_map/ppermute | solution.py:389
  254.3 55.7 %collective-permute-start.38 = (bf16[256,2048]{1,0:T(8,128)(2,1)S(1)}, bf16[256,2048]{1,0:T(8,128)(2,1)S(1)}, u32[]{:S(2)}, u32[]{:S(2)}) collective-permute-start(bf16[256,2048]{1,0:T(8,128)(2,1)S(1)} %bitcast.364), channel_id=1, source_target_pairs={{0,8},{8,0},{16,24},{24,16},{1,9},{9,1},{17,25},{25,17},{2,10},{10... | collective-permute-start | bytes 3145736 | tf_op jit(solution)/shard_map/ppermute | solution.py:389
  254.3 46.5 %collective-permute-start.5 = (bf16[256,2048]{1,0:T(8,128)(2,1)S(1)}, bf16[256,2048]{1,0:T(8,128)(2,1)S(1)}, u32[]{:S(2)}, u32[]{:S(2)}) collective-permute-start(bf16[256,2048]{1,0:T(8,128)(2,1)S(1)} %collective-permute-done.4), channel_id=1, source_target_pairs={{0,2},{1,3},{2,4},{3,5},{4,6},{5,7},{8,10},{9,11},{10,12},{11,13},... | collective-permute-start | bytes 3145736 | tf_op jit(solution)/shard_map/ppermute | solution.py:384
  256.2 40.6 %collective-permute-start.35 = (bf16[256,2048]{1,0:T(8,128)(2,1)S(1)}, bf16[256,2048]{1,0:T(8,128)(2,1)S(1)}, u32[]{:S(2)}, u32[]{:S(2)}) collective-permute-start(bf16[256,2048]{1,0:T(8,128)(2,1)S(1)} %collective-permute-done.34), channel_id=1, source_target_pairs={{2,0},{3,1},{4,2},{5,3},{6,4},{7,5},{10,8},{11,9},{12,10},{13,11},... | collective-permute-start | bytes 3145736 | tf_op jit(solution)/shard_map/ppermute | solution.py:385
  274.4 33.2 %collective-permute-start.37 = (bf16[256,2048]{1,0:T(8,128)(2,1)S(1)}, bf16[256,2048]{1,0:T(8,128)(2,1)S(1)}, u32[]{:S(2)}, u32[]{:S(2)}) collective-permute-start(bf16[256,2048]{1,0:T(8,128)(2,1)S(1)} %collective-permute-done.36), channel_id=1, source_target_pairs={{0,2},{1,3},{2,4},{3,5},{4,6},{5,7},{8,10},{9,11},{10,12},{11,13},... | collective-permute-start | bytes 3145736 | tf_op jit(solution)/shard_map/ppermute | solution.py:384
  296.8 59.6 %collective-permute-start.22 = (bf16[2,4,2,64,1408]{4,3,0,1,2:T(8,128)(2,1)}, bf16[2,4,2,64,1408]{4,3,0,1,2:T(8,128)(2,1)}, u32[]{:S(2)}, u32[]{:S(2)}) collective-permute-start(bf16[2,4,2,64,1408]{4,3,0,1,2:T(8,128)(2,1)} %maximum_select_fusion.3), channel_id=1, source_target_pairs={{0,16},{8,24},{16,0},{24,8},{1,17},{9,25},{17,1},{25,9},{2,18},{10... | collective-permute-start | bytes 8650760 | tf_op jit(solution)/shard_map/ppermute | solution.py:421
  300.8 10.3 %collective-permute-start.7 = (bf16[256,2048]{1,0:T(8,128)(2,1)S(1)}, bf16[256,2048]{1,0:T(8,128)(2,1)S(1)}, u32[]{:S(2)}, u32[]{:S(2)}) collective-permute-start(bf16[256,2048]{1,0:T(8,128)(2,1)S(1)} %get-tuple-element.69), channel_id=1, source_target_pairs={{0,8},{8,0},{16,24},{24,16},{1,9},{9,1},{17,25},{25,17},{2,10},{10... | collective-permute-start | bytes 3145736 | tf_op jit(solution)/shard_map/ppermute | solution.py:389
  310.0 37.3 %collective-permute-start.39 = (bf16[256,2048]{1,0:T(8,128)(2,1)}, bf16[256,2048]{1,0:T(8,128)(2,1)}, u32[]{:S(2)}, u32[]{:S(2)}) collective-permute-start(bf16[256,2048]{1,0:T(8,128)(2,1)} %get-tuple-element.63), channel_id=1, source_target_pairs={{0,8},{8,0},{16,24},{24,16},{1,9},{9,1},{17,25},{25,17},{2,10},{10... | collective-permute-start | bytes 3145736 | tf_op jit(solution)/shard_map/ppermute | solution.py:389
  311.1 38.6 %collective-permute-start.40 = (bf16[256,2048]{1,0:T(8,128)(2,1)}, bf16[256,2048]{1,0:T(8,128)(2,1)}, u32[]{:S(2)}, u32[]{:S(2)}) collective-permute-start(bf16[256,2048]{1,0:T(8,128)(2,1)} %get-tuple-element.61), channel_id=1, source_target_pairs={{0,8},{8,0},{16,24},{24,16},{1,9},{9,1},{17,25},{25,17},{2,10},{10... | collective-permute-start | bytes 3145736 | tf_op jit(solution)/shard_map/ppermute | solution.py:389
  311.7 40.3 %collective-permute-start.41 = (bf16[256,2048]{1,0:T(8,128)(2,1)}, bf16[256,2048]{1,0:T(8,128)(2,1)}, u32[]{:S(2)}, u32[]{:S(2)}) collective-permute-start(bf16[256,2048]{1,0:T(8,128)(2,1)} %get-tuple-element.59), channel_id=1, source_target_pairs={{0,8},{8,0},{16,24},{24,16},{1,9},{9,1},{17,25},{25,17},{2,10},{10... | collective-permute-start | bytes 3145736 | tf_op jit(solution)/shard_map/ppermute | solution.py:389
  333.8 130.8 %collective-permute-start.16 = (bf16[8,256,512]{2,1,0:T(8,128)(2,1)}, bf16[8,256,512]{2,1,0:T(8,128)(2,1)}, u32[]{:S(2)}, u32[]{:S(2)}) collective-permute-start(bf16[8,256,512]{2,1,0:T(8,128)(2,1)} %get-tuple-element.29), channel_id=1, source_target_pairs={{0,1},{1,0},{2,3},{3,2},{4,5},{5,4},{6,7},{7,6},{8,9},{9,8},{10,11... | collective-permute-start | bytes 6291464 | tf_op jit(solution)/shard_map/ppermute | solution.py:948
  449.5 229.2 %collective-permute-start.59 = (bf16[2,4,2,64,1408]{4,3,0,1,2:T(8,128)(2,1)}, bf16[2,4,2,64,1408]{4,3,0,1,2:T(8,128)(2,1)}, u32[]{:S(2)}, u32[]{:S(2)}) collective-permute-start(bf16[2,4,2,64,1408]{4,3,0,1,2:T(8,128)(2,1)} %fusion), channel_id=1, source_target_pairs={{0,16},{8,24},{16,0},{24,8},{1,17},{9,25},{17,1},{25,9},{2,18},{10... | collective-permute-start | bytes 8650760 | tf_op jit(solution)/shard_map/ppermute | solution.py:427
  463.4 93.6 %collective-permute-start.65 = (bf16[2,176,2048]{2,1,0:T(8,128)(2,1)}, bf16[2,176,2048]{2,1,0:T(8,128)(2,1)}, u32[]{:S(2)}, u32[]{:S(2)}) collective-permute-start(bf16[2,176,2048]{2,1,0:T(8,128)(2,1)} %fusion.29), channel_id=1, source_target_pairs={{0,16},{8,24},{16,0},{24,8},{1,17},{9,25},{17,1},{25,9},{2,18},{10... | collective-permute-start | bytes 4325384 | tf_op jit(solution)/shard_map/ppermute | solution.py:427
  517.5 54.5 %collective-permute-start.42 = (bf16[8,256,256]{2,1,0:T(8,128)(2,1)S(1)}, bf16[8,256,256]{2,1,0:T(8,128)(2,1)}, u32[]{:S(2)}, u32[]{:S(2)}) collective-permute-start(bf16[8,256,256]{2,1,0:T(8,128)(2,1)S(1)} %bitcast.341), channel_id=1, source_target_pairs={{0,1},{1,0},{2,3},{3,2},{4,5},{5,4},{6,7},{7,6},{8,9},{9,8},{10,11... | collective-permute-start | bytes 3145736 | tf_op jit(solution)/shard_map/ppermute | solution.py:960
  518.3 53.8 %collective-permute-start.43 = (bf16[8,256,256]{2,1,0:T(8,128)(2,1)S(1)}, bf16[8,256,256]{2,1,0:T(8,128)(2,1)}, u32[]{:S(2)}, u32[]{:S(2)}) collective-permute-start(bf16[8,256,256]{2,1,0:T(8,128)(2,1)S(1)} %bitcast.340), channel_id=1, source_target_pairs={{0,1},{1,0},{2,3},{3,2},{4,5},{5,4},{6,7},{7,6},{8,9},{9,8},{10,11... | collective-permute-start | bytes 3145736 | tf_op jit(solution)/shard_map/ppermute | solution.py:961
  538.8 14.2 %collective-permute-start.57 = (bf16[2,64,2048]{2,1,0:T(8,128)(2,1)S(1)}, bf16[2,64,2048]{2,1,0:T(8,128)(2,1)S(1)}, u32[]{:S(2)}, u32[]{:S(2)}) collective-permute-start(bf16[2,64,2048]{2,1,0:T(8,128)(2,1)S(1)} %fusion.37), channel_id=1, source_target_pairs={{0,16},{8,24},{16,0},{24,8},{1,17},{9,25},{17,1},{25,9},{2,18},{10... | collective-permute-start | bytes 1572872 | tf_op jit(solution)/shard_map/ppermute | solution.py:427
  553.0 116.3 %collective-permute-start.26 = (bf16[256,2048]{1,0:T(8,128)(2,1)}, bf16[256,2048]{1,0:T(8,128)(2,1)}, u32[]{:S(2)}, u32[]{:S(2)}) collective-permute-start(bf16[256,2048]{1,0:T(8,128)(2,1)} %get-tuple-element.80), channel_id=1, source_target_pairs={{0,8},{8,0},{16,24},{24,16},{1,9},{9,1},{17,25},{25,17},{2,10},{10... | collective-permute-start | bytes 3145736 | tf_op jit(solution)/shard_map/ppermute | solution.py:395
  557.0 8.6 collective-permute-start.58
  565.5 105.7 %collective-permute-start.30 = (bf16[256,2048]{1,0:T(8,128)(2,1)}, bf16[256,2048]{1,0:T(8,128)(2,1)}, u32[]{:S(2)}, u32[]{:S(2)}) collective-permute-start(bf16[256,2048]{1,0:T(8,128)(2,1)} %get-tuple-element.78), channel_id=1, source_target_pairs={{0,8},{8,0},{16,24},{24,16},{1,9},{9,1},{17,25},{25,17},{2,10},{10... | collective-permute-start | bytes 3145736 | tf_op jit(solution)/shard_map/ppermute | solution.py:395
  572.0 99.2 %collective-permute-start.28 = (bf16[256,2048]{1,0:T(8,128)(2,1)}, bf16[256,2048]{1,0:T(8,128)(2,1)}, u32[]{:S(2)}, u32[]{:S(2)}) collective-permute-start(bf16[256,2048]{1,0:T(8,128)(2,1)} %get-tuple-element.79), channel_id=1, source_target_pairs={{0,8},{8,0},{16,24},{24,16},{1,9},{9,1},{17,25},{25,17},{2,10},{10... | collective-permute-start | bytes 3145736 | tf_op jit(solution)/shard_map/ppermute | solution.py:395
  572.1 105.3 %collective-permute-start.66 = (bf16[176,2048]{1,0:T(8,128)(2,1)}, bf16[176,2048]{1,0:T(8,128)(2,1)S(1)}, u32[]{:S(2)}, u32[]{:S(2)}) collective-permute-start(bf16[176,2048]{1,0:T(8,128)(2,1)} %fusion.35), channel_id=1, source_target_pairs={{0,1},{1,0},{2,3},{3,2},{4,5},{5,4},{6,7},{7,6},{8,9},{9,8},{10,11... | collective-permute-start | bytes 2162696 | tf_op jit(solution)/shard_map/ppermute | solution.py:430
  669.3 9.9 %collective-permute-start.45 = (bf16[256,2048]{1,0:T(8,128)(2,1)S(1)}, bf16[256,2048]{1,0:T(8,128)(2,1)}, u32[]{:S(2)}, u32[]{:S(2)}) collective-permute-start(bf16[256,2048]{1,0:T(8,128)(2,1)S(1)} %get-tuple-element.73), channel_id=1, source_target_pairs={{0,8},{8,0},{16,24},{24,16},{1,9},{9,1},{17,25},{25,17},{2,10},{10... | collective-permute-start | bytes 3145736 | tf_op jit(solution)/shard_map/ppermute | solution.py:395
  671.2 8.9 collective-permute-start.49
  671.3 9.2 collective-permute-start.47
  677.4 10.3 %collective-permute-start.25 = (bf16[256,2048]{1,0:T(8,128)(2,1)}, bf16[256,2048]{1,0:T(8,128)(2,1)}, u32[]{:S(2)}, u32[]{:S(2)}) collective-permute-start(bf16[256,2048]{1,0:T(8,128)(2,1)} %get-tuple-element.77), channel_id=1, source_target_pairs={{0,8},{8,0},{16,24},{24,16},{1,9},{9,1},{17,25},{25,17},{2,10},{10... | collective-permute-start | bytes 3145736 | tf_op jit(solution)/shard_map/ppermute | solution.py:395
  678.8 24.6 %collective-permute-start.31 = (bf16[256,2048]{1,0:T(8,128)(2,1)}, bf16[256,2048]{1,0:T(8,128)(2,1)}, u32[]{:S(2)}, u32[]{:S(2)}) collective-permute-start(bf16[256,2048]{1,0:T(8,128)(2,1)} %get-tuple-element.82), channel_id=1, source_target_pairs={{0,2},{1,3},{2,4},{3,5},{4,6},{5,7},{6,0},{7,1},{8,10},{9,11},{10,... | collective-permute-start | bytes 3145736 | tf_op jit(solution)/shard_map/ppermute | solution.py:399
  679.2 89.8 %collective-permute-start.29 = (bf16[256,2048]{1,0:T(8,128)(2,1)}, bf16[256,2048]{1,0:T(8,128)(2,1)}, u32[]{:S(2)}, u32[]{:S(2)}) collective-permute-start(bf16[256,2048]{1,0:T(8,128)(2,1)} %get-tuple-element.83), channel_id=1, source_target_pairs={{0,4},{1,5},{2,6},{3,7},{4,0},{5,1},{6,2},{7,3},{8,12},{9,13},{10,... | collective-permute-start | bytes 3145736 | tf_op jit(solution)/shard_map/ppermute | solution.py:399
  680.1 136.3 %collective-permute-start.27 = (bf16[256,2048]{1,0:T(8,128)(2,1)}, bf16[256,2048]{1,0:T(8,128)(2,1)}, u32[]{:S(2)}, u32[]{:S(2)}) collective-permute-start(bf16[256,2048]{1,0:T(8,128)(2,1)} %get-tuple-element.81), channel_id=1, source_target_pairs={{0,6},{1,7},{2,0},{3,1},{4,2},{5,3},{6,4},{7,5},{8,14},{9,15},{10,... | collective-permute-start | bytes 3145736 | tf_op jit(solution)/shard_map/ppermute | solution.py:399
  681.4 138.4 %collective-permute-start.51 = (bf16[2,4,2,64,768]{4,3,0,1,2:T(8,128)(2,1)S(1)}, bf16[2,4,2,64,768]{4,3,0,1,2:T(8,128)(2,1)}, u32[]{:S(2)}, u32[]{:S(2)}) collective-permute-start(bf16[2,4,2,64,768]{4,3,0,1,2:T(8,128)(2,1)S(1)} %fusion.27), channel_id=1, source_target_pairs={{0,16},{8,24},{16,0},{24,8},{1,17},{9,25},{17,1},{25,9},{2,18},{10... | collective-permute-start | bytes 4718600 | tf_op jit(solution)/shard_map/ppermute | solution.py:427
  687.7 134.8 %collective-permute-start.44 = (bf16[256,2048]{1,0:T(8,128)(2,1)}, bf16[256,2048]{1,0:T(8,128)(2,1)S(1)}, u32[]{:S(2)}, u32[]{:S(2)}) collective-permute-start(bf16[256,2048]{1,0:T(8,128)(2,1)} %get-tuple-element.70), channel_id=1, source_target_pairs={{0,8},{8,0},{16,24},{24,16},{1,9},{9,1},{17,25},{25,17},{2,10},{10... | collective-permute-start | bytes 3145736 | tf_op jit(solution)/shard_map/ppermute | solution.py:395
  703.4 132.9 %collective-permute-start.50 = (bf16[256,2048]{1,0:T(8,128)(2,1)S(1)}, bf16[256,2048]{1,0:T(8,128)(2,1)S(1)}, u32[]{:S(2)}, u32[]{:S(2)}) collective-permute-start(bf16[256,2048]{1,0:T(8,128)(2,1)S(1)} %get-tuple-element.75), channel_id=1, source_target_pairs={{0,2},{1,3},{2,4},{3,5},{4,6},{5,7},{6,0},{7,1},{8,10},{9,11},{10,... | collective-permute-start | bytes 3145736 | tf_op jit(solution)/shard_map/ppermute | solution.py:399
  769.0 89.8 %collective-permute-start.48 = (bf16[256,2048]{1,0:T(8,128)(2,1)S(1)}, bf16[256,2048]{1,0:T(8,128)(2,1)S(1)}, u32[]{:S(2)}, u32[]{:S(2)}) collective-permute-start(bf16[256,2048]{1,0:T(8,128)(2,1)S(1)} %get-tuple-element.76), channel_id=1, source_target_pairs={{0,4},{1,5},{2,6},{3,7},{4,0},{5,1},{6,2},{7,3},{8,12},{9,13},{10,... | collective-permute-start | bytes 3145736 | tf_op jit(solution)/shard_map/ppermute | solution.py:399
  816.4 44.9 %collective-permute-start.46 = (bf16[256,2048]{1,0:T(8,128)(2,1)S(1)}, bf16[256,2048]{1,0:T(8,128)(2,1)S(1)}, u32[]{:S(2)}, u32[]{:S(2)}) collective-permute-start(bf16[256,2048]{1,0:T(8,128)(2,1)S(1)} %get-tuple-element.74), channel_id=1, source_target_pairs={{0,6},{1,7},{2,0},{3,1},{4,2},{5,3},{6,4},{7,5},{8,14},{9,15},{10,... | collective-permute-start | bytes 3145736 | tf_op jit(solution)/shard_map/ppermute | solution.py:399
  819.8 52.6 %collective-permute-start.60 = (bf16[4,2,64,1408]{3,2,1,0:T(8,128)(2,1)S(1)}, bf16[4,2,64,1408]{3,2,1,0:T(8,128)(2,1)S(1)}, u32[]{:S(2)}, u32[]{:S(2)}) collective-permute-start(bf16[4,2,64,1408]{3,2,1,0:T(8,128)(2,1)S(1)} %copy_bitcast_fusion.1), channel_id=1, source_target_pairs={{0,1},{1,0},{2,3},{3,2},{4,5},{5,4},{6,7},{7,6},{8,9},{9,8},{10,11... | collective-permute-start | bytes 4325384 | tf_op jit(solution)/shard_map/ppermute | solution.py:430
  822.5 46.7 %collective-permute-start.52 = (bf16[4,2,64,768]{3,2,0,1:T(8,128)(2,1)S(1)}, bf16[4,2,64,768]{3,2,0,1:T(8,128)(2,1)S(1)}, u32[]{:S(2)}, u32[]{:S(2)}) collective-permute-start(bf16[4,2,64,768]{3,2,0,1:T(8,128)(2,1)S(1)} %fusion.32), channel_id=1, source_target_pairs={{0,1},{1,0},{2,3},{3,2},{4,5},{5,4},{6,7},{7,6},{8,9},{9,8},{10,11... | collective-permute-start | bytes 2359304 | tf_op jit(solution)/shard_map/ppermute | solution.py:430
  869.9 15.7 %collective-permute-start.54 = (bf16[2,64,768]{2,1,0:T(8,128)(2,1)S(1)}, bf16[2,64,768]{2,1,0:T(8,128)(2,1)S(1)}, u32[]{:S(2)}, u32[]{:S(2)}) collective-permute-start(bf16[2,64,768]{2,1,0:T(8,128)(2,1)S(1)} %get-tuple-element.123), channel_id=1, source_target_pairs={{0,4},{1,5},{2,6},{3,7},{4,0},{5,1},{6,2},{7,3},{8,12},{9,13},{10,... | collective-permute-start | bytes 589832 | tf_op jit(solution)/shard_map/ppermute | solution.py:438
  872.2 31.4 %collective-permute-start.53 = (bf16[2,64,768]{2,1,0:T(8,128)(2,1)S(1)}, bf16[2,64,768]{2,1,0:T(8,128)(2,1)S(1)}, u32[]{:S(2)}, u32[]{:S(2)}) collective-permute-start(bf16[2,64,768]{2,1,0:T(8,128)(2,1)S(1)} %get-tuple-element.124), channel_id=1, source_target_pairs={{0,2},{1,3},{2,4},{3,5},{4,6},{5,7},{6,0},{7,1},{8,10},{9,11},{10,... | collective-permute-start | bytes 589832 | tf_op jit(solution)/shard_map/ppermute | solution.py:438
  872.8 37.8 %collective-permute-start.63 = (bf16[2,64,1408]{2,1,0:T(8,128)(2,1)S(1)}, bf16[2,64,1408]{2,1,0:T(8,128)(2,1)S(1)}, u32[]{:S(2)}, u32[]{:S(2)}) collective-permute-start(bf16[2,64,1408]{2,1,0:T(8,128)(2,1)S(1)} %get-tuple-element.97), channel_id=1, source_target_pairs={{0,6},{1,7},{2,0},{3,1},{4,2},{5,3},{6,4},{7,5},{8,14},{9,15},{10,... | collective-permute-start | bytes 1081352 | tf_op jit(solution)/shard_map/ppermute | solution.py:438
  874.1 37.2 %collective-permute-start.62 = (bf16[2,64,1408]{2,1,0:T(8,128)(2,1)S(1)}, bf16[2,64,1408]{2,1,0:T(8,128)(2,1)S(1)}, u32[]{:S(2)}, u32[]{:S(2)}) collective-permute-start(bf16[2,64,1408]{2,1,0:T(8,128)(2,1)S(1)} %get-tuple-element.98), channel_id=1, source_target_pairs={{0,4},{1,5},{2,6},{3,7},{4,0},{5,1},{6,2},{7,3},{8,12},{9,13},{10,... | collective-permute-start | bytes 1081352 | tf_op jit(solution)/shard_map/ppermute | solution.py:438
  875.2 43.9 %collective-permute-start.61 = (bf16[2,64,1408]{2,1,0:T(8,128)(2,1)S(1)}, bf16[2,64,1408]{2,1,0:T(8,128)(2,1)S(1)}, u32[]{:S(2)}, u32[]{:S(2)}) collective-permute-start(bf16[2,64,1408]{2,1,0:T(8,128)(2,1)S(1)} %get-tuple-element.99), channel_id=1, source_target_pairs={{0,2},{1,3},{2,4},{3,5},{4,6},{5,7},{6,0},{7,1},{8,10},{9,11},{10,... | collective-permute-start | bytes 1081352 | tf_op jit(solution)/shard_map/ppermute | solution.py:438
  904.7 23.3 %collective-permute-start.56 = (bf16[4,64,768]{2,1,0:T(8,128)(2,1)}, bf16[4,64,768]{2,1,0:T(8,128)(2,1)S(1)}, u32[]{:S(2)}, u32[]{:S(2)}) collective-permute-start(bf16[4,64,768]{2,1,0:T(8,128)(2,1)} %get-tuple-element.116), channel_id=1, source_target_pairs={{0,8},{8,0},{16,24},{24,16},{1,9},{9,1},{17,25},{25,17},{2,10},{10... | collective-permute-start | bytes 1179656 | tf_op jit(solution)/shard_map/ppermute | solution.py:445
  920.7 11.7 %collective-permute-start.64 = (bf16[4,64,1408]{2,1,0:T(8,128)(2,1)}, bf16[4,64,1408]{2,1,0:T(8,128)(2,1)S(1)}, u32[]{:S(2)}, u32[]{:S(2)}) collective-permute-start(bf16[4,64,1408]{2,1,0:T(8,128)(2,1)} %get-tuple-element.91), channel_id=1, source_target_pairs={{0,8},{8,0},{16,24},{24,16},{1,9},{9,1},{17,25},{25,17},{2,10},{10... | collective-permute-start | bytes 2162696 | tf_op jit(solution)/shard_map/ppermute | solution.py:445
  (61 other events, 1717.4 us)

commit v2 on v1

--- a/solution.py
+++ b/solution.py
@@ -1,3 +1,5 @@
+import functools
+
 import jax
 import jax.numpy as jnp
 from jax import lax
@@ -354,13 +356,12 @@
 DEPTH = 4
 PIECES = 2 * DEPTH
 ROWS = 256
+EXTRA = 16
 LOCAL_HEADS = 4
 HEAD_COLS = LOCAL_HEADS * HEAD_DIM
 CORE = [(i, i ^ 1) for i in range(4)]
 ACROSS_X = [(i, i ^ 2) for i in range(4)]
 ACROSS_Y = [(i, i ^ 1) for i in range(8)]
-UPWARD = [(i, i + 2) for i in range(6)]
-DOWNWARD = [(i + 2, i) for i in range(6)]
 MIB = 1024 * 1024
 
 
@@ -378,71 +379,68 @@
     )
 
 
-def gather_pieces(value, z):
-    up, down = [value], [value]
-    for step in range(DEPTH - 1):
-        up.append(lax.ppermute(up[-1], "blk", UPWARD))
-        down.append(lax.ppermute(down[-1], "blk", DOWNWARD))
+def gather_pieces(value):
     own = [value]
     for step in range(1, DEPTH):
-        own.append(jnp.where(z >= step, up[step], down[DEPTH - step]))
+        own.append(lax.ppermute(value, "blk", around(step)))
     return own + [lax.ppermute(piece, "bucket", CORE) for piece in own]
 
 
-def scatter_pieces(partial):
-    total = None
-    for step in range(DEPTH):
-        both = partial[step].astype(jnp.float32) + lax.ppermute(
-            partial[DEPTH + step], "bucket", CORE
-        ).astype(jnp.float32)
-        if step > 0:
-            both = lax.ppermute(both.astype(jnp.bfloat16), "blk", around(-step)).astype(jnp.float32)
-        total = both if total is None else total + both
+def core_sums(own, other):
+    other = lax.ppermute(other, "bucket", CORE)
+    sums = [own[k].astype(jnp.float32) + other[k].astype(jnp.float32) for k in range(DEPTH)]
+    return [sums[0]] + [value.astype(jnp.bfloat16) for value in sums[1:]]
+
+
+def scatter_pieces(sums):
+    total = sums[0]
+    for step in range(1, DEPTH):
+        got = lax.ppermute(sums[step], "blk", around(-step))
+        total = total + got.astype(jnp.float32)
     return total
 
 
-def columns_of_group(rows, core, z):
-    mine = lax.dynamic_index_in_dim(rows, core, 0, False)
-    theirs = lax.dynamic_index_in_dim(rows, 1 - core, 0, False)
-    got = lax.ppermute(theirs, "bucket", CORE)
-    both = in_order(mine, got, core, 1)
-    pieces = [lax.dynamic_index_in_dim(both, z, 0, False)]
+def after(value, *earlier):
+    return lax.optimization_barrier((value,) + earlier)[0]
+
+
+def one_of(value, index, axis):
+    return lax.dynamic_index_in_dim(value, index, axis, False)
+
+
+def summed(keep, send, over_x):
+    send = send.astype(jnp.bfloat16)
+    got = (
+        lax.ppermute(send, "bucket", ACROSS_X) if over_x else lax.ppermute(send, "blk", ACROSS_Y)
+    )
+    return keep + got.astype(jnp.float32)
+
+
+def rows_of_device(value, core, z):
+    parts = [one_of(value, z, 0)]
     for step in range(1, DEPTH):
-        chunk = lax.dynamic_index_in_dim(both, (z + step) % DEPTH, 0, False)
-        pieces.append(lax.ppermute(chunk, "blk", around(step)))
-    stacked = jnp.stack(pieces)
-    return jnp.concatenate(
-        [lax.dynamic_slice_in_dim(stacked, (z - j) % DEPTH, 1, 0) for j in range(DEPTH)]
-    )
-
-
-def over_columns(value, x, y):
-    value = in_order(value, lax.ppermute(value, "blk", ACROSS_Y), y, 0)
-    return in_order(value, lax.ppermute(value, "bucket", ACROSS_X), x, 0)
-
-
-def sum_over_columns(value, x, y):
-    keep = lax.dynamic_index_in_dim(value, x, 0, False)
-    send = lax.dynamic_index_in_dim(value, 1 - x, 0, False).astype(jnp.bfloat16)
-    value = keep + lax.ppermute(send, "bucket", ACROSS_X).astype(jnp.float32)
-    keep = lax.dynamic_index_in_dim(value, y, 0, False)
-    send = lax.dynamic_index_in_dim(value, 1 - y, 0, False).astype(jnp.bfloat16)
-    return keep + lax.ppermute(send, "blk", ACROSS_Y).astype(jnp.float32)
-
-
-def rows_of_device(value, core, z):
-    low = value.astype(jnp.bfloat16)
-    parts = [lax.dynamic_index_in_dim(low, z, 0, False)]
-    for step in range(1, DEPTH):
-        chunk = lax.dynamic_index_in_dim(low, (z + step) % DEPTH, 0, False)
-        parts.append(lax.ppermute(chunk, "blk", around(step)))
+        chunk = one_of(value, (z + step) % DEPTH, 0).astype(jnp.bfloat16)
+        parts.append(lax.ppermute(chunk, "blk", around(step)).astype(jnp.float32))
     stacked = jnp.stack(parts)
     ordered = jnp.concatenate(
         [lax.dynamic_slice_in_dim(stacked, (z - j) % DEPTH, 1, 0) for j in range(DEPTH)]
     )
-    mine = lax.dynamic_index_in_dim(ordered, core, 1, False)
-    theirs = lax.dynamic_index_in_dim(ordered, 1 - core, 1, False)
-    return in_order(mine, lax.ppermute(theirs, "bucket", CORE), core, 0)
+    mine = one_of(ordered, core, 1)
+    theirs = one_of(ordered, 1 - core, 1).astype(jnp.bfloat16)
+    got = lax.ppermute(theirs, "bucket", CORE).astype(jnp.float32)
+    return in_order(mine, got, core, 0)
+
+
+def vector_sums(terms, x, y, core, z):
+    for index, axis, name, pairs in ((x, 0, "bucket", ACROSS_X), (core, 0, "bucket", CORE)):
+        keep, send = one_of(terms, index, axis), one_of(terms, 1 - index, axis)
+        terms = keep + lax.ppermute(send, name, pairs)
+    keep, send = one_of(terms, y, 1), one_of(terms, 1 - y, 1)
+    terms = keep + lax.ppermute(send, "blk", ACROSS_Y)
+    total = one_of(terms, z, 0)
+    for step in range(1, DEPTH):
+        total = total + lax.ppermute(one_of(terms, (z + step) % DEPTH, 0), "blk", around(step))
+    return total
 
 
 def dot_rows(left, right):
@@ -456,7 +454,7 @@
 
 
 def cost(flops, moved, exps=0):
-    return pl.CostEstimate(flops=flops, bytes_accessed=moved, transcendentals=exps)
+    return pl.CostEstimate(flops=flops // 64, bytes_accessed=moved // 64, transcendentals=exps // 64)
 
 
 def piece_spec(width):
@@ -465,6 +463,291 @@
 
 def whole_spec(shape):
     return pl.BlockSpec(shape, lambda i: (0,) * len(shape))
+
+
+def remote(src, dst, sends, recvs, index, device):
+    return pltpu.make_async_remote_copy(
+        src_ref=src,
+        dst_ref=dst,
+        send_sem=sends.at[index],
+        recv_sem=recvs.at[index],
+        device_id=device,
+        device_id_type=pl.DeviceIdType.MESH,
+    )
+
+
+def gather_kernel(
+    x_ref,
+    wi_ref,
+    wg_ref,
+    ro_ref,
+    pieces,
+    wi_out,
+    wg_out,
+    ro_out,
+    group_s,
+    group_r,
+    across_s,
+    across_r,
+    rows_s,
+    rows_r,
+    up_s,
+    down_s,
+    piece_r,
+    core_s,
+    core_r,
+    local_sems,
+):
+    bucket, blk = lax.axis_index("bucket"), lax.axis_index("blk")
+    x, core = bucket // 2, bucket % 2
+    z, y = blk // 2, blk % 2
+
+    def device(xx, cc, zz, yy):
+        return (xx * 2 + cc, zz * 2 + yy)
+
+    x_mate, y_mate = device(1 - x, core, z, y), device(x, core, z, 1 - y)
+    core_mate = device(x, 1 - core, z, y)
+    members = [(flip, turn) for turn in (0, 1, 3, 2) for flip in (0, 1)]
+
+    def target(flip, turn):
+        return (core + flip) % 2, (z + turn) % DEPTH
+
+    def source(flip, turn):
+        return (core + flip) % 2, (z + DEPTH - turn) % DEPTH
+
+    barrier = pltpu.get_barrier_semaphore()
+    greeted = [device(x, *target(*m), y) for m in members[1:]] + [x_mate, y_mate]
+    for mate in greeted:
+        pl.semaphore_signal(
+            barrier, inc=1, device_id=mate, device_id_type=pl.DeviceIdType.MESH
+        )
+    pl.semaphore_wait(barrier, len(greeted))
+
+    started = []
+
+    def begin(copy):
+        copy.start()
+        started.append(copy)
+        return copy
+
+    local = [
+        pltpu.make_async_copy(wi_ref.at[core, z], wi_out.at[x, core, z, y], local_sems.at[0]),
+        pltpu.make_async_copy(wg_ref.at[core, z], wg_out.at[x, core, z, y], local_sems.at[1]),
+        pltpu.make_async_copy(ro_ref, ro_out.at[x, y], local_sems.at[2]),
+        pltpu.make_async_copy(x_ref, pieces.at[0], local_sems.at[3]),
+    ]
+    for copy in local:
+        copy.start()
+
+    def send_group(which, ref, out):
+        copies = {}
+        for flip, turn in members[1:]:
+            cc, zz = target(flip, turn)
+            copies[flip, turn] = begin(
+                remote(
+                    ref.at[cc, zz],
+                    out.at[x, core, z, y],
+                    group_s,
+                    group_r,
+                    (which, flip * DEPTH + turn),
+                    device(x, cc, zz, y),
+                )
+            )
+        return copies
+
+    def piece_copy(src, slot, sends, number, dz):
+        return pltpu.make_async_remote_copy(
+            src_ref=src,
+            dst_ref=pieces.at[slot],
+            send_sem=sends.at[number],
+            recv_sem=piece_r.at[slot],
+            device_id=device(x, core, z + dz, y),
+            device_id_type=pl.DeviceIdType.MESH,
+        )
+
+    def core_copy(slot):
+        src = x_ref if slot == 0 else pieces.at[slot]
+        return remote(src, pieces.at[DEPTH + slot], core_s, core_r, slot, core_mate)
+
+    ups = [piece_copy(x_ref if k == 0 else pieces.at[k], k + 1, up_s, k, 1) for k in range(3)]
+    downs = [
+        piece_copy(x_ref if k == 0 else pieces.at[DEPTH - k], 3 - k, down_s, k, -1)
+        for k in range(3)
+    ]
+
+    def start_if(condition, copy):
+        @pl.when(condition)
+        def _():
+            copy.start()
+
+    def sent_if(condition, copy):
+        @pl.when(condition)
+        def _():
+            copy.wait_send()
+
+    inward = send_group(0, wi_ref, wi_out)
+    start_if(z < DEPTH - 1, ups[0])
+    start_if(z > 0, downs[0])
+    core_copies = [core_copy(slot) for slot in range(DEPTH)]
+    core_copies[0].start()
+    rows_x = begin(remote(ro_ref, ro_out.at[x, y], rows_s, rows_r, 0, x_mate))
+    rows_y = begin(remote(ro_ref, ro_out.at[x, y], rows_s, rows_r, 1, y_mate))
+    gate_up = send_group(1, wg_ref, wg_out)
+
+    def spread(which, ref, out, copies):
+        pairs = {}
+        for member in members:
+            flip, turn = member
+            cc, zz = source(flip, turn)
+            if member == (0, 0):
+                src = ref.at[core, z]
+            else:
+                copies[member].wait_recv()
+                src = out.at[x, cc, zz, y]
+            number = flip * DEPTH + turn
+            pairs[member] = (
+                begin(
+                    remote(
+                        src, out.at[x, cc, zz, y], across_s, across_r, (which, 0, number), x_mate
+                    )
+                ),
+                begin(
+                    remote(
+                        src, out.at[x, cc, zz, y], across_s, across_r, (which, 1, number), y_mate
+                    )
+                ),
+            )
+        return pairs
+
+    def corner(which, out, pairs):
+        copies = []
+        for member in members:
+            flip, turn = member
+            cc, zz = source(flip, turn)
+            number = flip * DEPTH + turn
+            if flip == 0:
+                pairs[member][1].wait_recv()
+                part = out.at[x, cc, zz, 1 - y]
+                mate = x_mate
+            else:
+                pairs[member][0].wait_recv()
+                part = out.at[1 - x, cc, zz, y]
+                mate = y_mate
+            copies.append(
+                begin(remote(part, part, across_s, across_r, (which, 2, number), mate))
+            )
+        return copies
+
+    inward_pairs = spread(0, wi_ref, wi_out, inward)
+
+    @pl.when(z > 0)
+    def _():
+        ups[0].wait_recv()
+        core_copies[1].start()
+
+    start_if((z > 0) & (z < DEPTH - 1), ups[1])
+
+    @pl.when(z < DEPTH - 1)
+    def _():
+        downs[0].wait_recv()
+        core_copies[3].start()
+
+    start_if((z > 0) & (z < DEPTH - 1), downs[1])
+
+    inward_corner = corner(0, wi_out, inward_pairs)
+    gate_up_pairs = spread(1, wg_ref, wg_out, gate_up)
+
+    ups[1].wait_recv()
+    core_copies[2].start()
+    start_if(z == 2, ups[2])
+    start_if(z == 1, downs[2])
+
+    cut = (ro_ref.shape[0] // 32) * 16
+    rows_y.wait_recv()
+    low = ro_out.at[x, 1 - y, pl.ds(0, cut)]
+    low_copy = begin(remote(low, low, rows_s, rows_r, 2, x_mate))
+    rows_x.wait_recv()
+    high = ro_out.at[1 - x, y, pl.ds(cut, ro_ref.shape[0] - cut)]
+    high_copy = begin(remote(high, high, rows_s, rows_r, 3, y_mate))
+    gate_up_corner = corner(1, wg_out, gate_up_pairs)
+
+    @pl.when(z == DEPTH - 1)
+    def _():
+        ups[2].wait_recv()
+        core_copies[3].start()
+
+    @pl.when(z == 0)
+    def _():
+        downs[2].wait_recv()
+        core_copies[1].start()
+
+    for pairs in (inward_pairs, gate_up_pairs):
+        for flip, turn in members:
+            pairs[flip, turn][0 if flip == 0 else 1].wait_recv()
+    for copy in inward_corner + gate_up_corner + [low_copy, high_copy]:
+        copy.wait_recv()
+    for copy in core_copies:
+        copy.wait_recv()
+        copy.wait_send()
+    for copy in started:
+        copy.wait_send()
+    sent_if(z < DEPTH - 1, ups[0])
+    sent_if(z > 0, downs[0])
+    sent_if((z > 0) & (z < DEPTH - 1), ups[1])
+    sent_if((z > 0) & (z < DEPTH - 1), downs[1])
+    sent_if(z == 2, ups[2])
+    sent_if(z == 1, downs[2])
+    for copy in local:
+        copy.wait()
+
+
+def gather(tokens, inward, gate_up, rows_out):
+    anywhere = pl.BlockSpec(memory_space=pl.ANY)
+    low = jnp.bfloat16
+    dma = pltpu.SemaphoreType.DMA
+    return pl.pallas_call(
+        gather_kernel,
+        in_specs=[anywhere] * 4,
+        out_specs=[anywhere] * 4,
+        out_shape=[
+            jax.ShapeDtypeStruct((PIECES,) + tokens.shape, low),
+            jax.ShapeDtypeStruct((2, 2, DEPTH, 2) + inward.shape[2:], low),
+            jax.ShapeDtypeStruct((2, 2, DEPTH, 2) + gate_up.shape[2:], low),
+            jax.ShapeDtypeStruct((2, 2) + rows_out.shape, low),
+        ],
+        scratch_shapes=[
+            dma((2, PIECES)),
+            dma((2, PIECES)),
+            dma((2, 3, PIECES)),
+            dma((2, 3, PIECES)),
+            dma((4,)),
+            dma((4,)),
+            dma((3,)),
+            dma((3,)),
+            dma((DEPTH,)),
+            dma((DEPTH,)),
+            dma((DEPTH,)),
+            dma((4,)),
+        ],
+        compiler_params=params(32, collective_id=0, has_side_effects=True),
+        cost_estimate=cost(0, 64 * MIB),
+        name="gather",
+    )(tokens, inward, gate_up, rows_out)
+
+
+def inward_rows(ref):
+    blocks, rows, columns = ref.shape
+    return ref[:, : rows - EXTRA].reshape(blocks * (rows - EXTRA), columns)
+
+
+def outward_rows(ref):
+    blocks, rows, columns = ref.shape
+    return ref[:, :HEAD_DIM].reshape(blocks * HEAD_DIM, columns)
+
+
+def down_rows(ref):
+    blocks, rows, columns = ref.shape
+    return ref[:, HEAD_DIM:].reshape(blocks * (rows - HEAD_DIM), columns)
 
 
 def normalised(rows):
@@ -491,7 +774,7 @@
     hat, _ = normalised(x_ref[0])
     normed = (hat * gain_ref[...] + shift_ref[...]).astype(jnp.bfloat16)
     n_ref[0] = normed
-    projected = dot_rows(normed, w_ref[...]) + bias_ref[...]
+    projected = dot_rows(normed, inward_rows(w_ref)) + bias_ref[...]
     tables = (cos_ref, first_ref, second_ref)
     query = turned(projected[:, :HEAD_COLS], *tables, 1.0) * (HEAD_DIM**-0.5)
     key = turned(projected[:, HEAD_COLS : 2 * HEAD_COLS], *tables, 1.0)
@@ -528,22 +811,22 @@
     )(pieces, gain, shift, weight, bias, *tables)
 
 
-def feed_kernel(n_ref, wg_ref, wu_ref, gate_ref, up_ref, hidden_ref):
-    normed = n_ref[0]
-    gate = dot_rows(normed, wg_ref[...])
-    up = dot_rows(normed, wu_ref[...])
+def feed_kernel(n_ref, w_ref, gate_ref, up_ref, hidden_ref):
+    both = dot_rows(n_ref[0], w_ref[...])
+    hidden = both.shape[1] // 2
+    gate, up = both[:, :hidden], both[:, hidden:]
     gate_ref[0] = gate
     up_ref[0] = up
     hidden_ref[0] = (gate * jax.nn.sigmoid(gate) * up).astype(jnp.bfloat16)
 
 
-def feed(normed, gate_weight, up_weight):
+def feed(normed, weight):
     width = normed.shape[-1]
-    hidden = gate_weight.shape[1]
+    hidden = weight.shape[1] // 2
     return pl.pallas_call(
         feed_kernel,
         grid=(PIECES,),
-        in_specs=[piece_spec(width), whole_spec(gate_weight.shape), whole_spec(up_weight.shape)],
+        in_specs=[piece_spec(width), whole_spec(weight.shape)],
         out_specs=[piece_spec(hidden)] * 3,
         out_shape=[
             jax.ShapeDtypeStruct((PIECES, ROWS, hidden), jnp.float32),
@@ -553,48 +836,70 @@
         compiler_params=params(48),
         cost_estimate=cost(4 * PIECES * ROWS * width * hidden, 28 * MIB),
         name="feed",
-    )(normed, gate_weight, up_weight)
-
-
-def branch_kernel(a_ref, h_ref, wo_ref, wd_ref, out_ref):
-    out_ref[0] = (dot_rows(a_ref[0], wo_ref[...]) + dot_rows(h_ref[0], wd_ref[...])).astype(
-        jnp.bfloat16
-    )
-
-
-def branch_terms(attended, hidden, outward, down):
-    width = outward.shape[1]
+    )(normed, weight)
+
+
+def store_split(value, own_ref, other_ref):
+    late = pl.program_id(0) >= DEPTH
+
+    @pl.when(jnp.logical_not(late))
+    def _():
+        other_ref[0] = value
+
+    @pl.when(late)
+    def _():
+        own_ref[0] = value
+
+
+def other_first(width):
+    return pl.BlockSpec((1, ROWS, width), lambda i: ((i + DEPTH) % PIECES, 0, 0))
+
+
+def split_specs(width):
+    return [
+        pl.BlockSpec((1, ROWS, width), lambda i: (jnp.maximum(i - DEPTH, 0), 0, 0)),
+        pl.BlockSpec((1, ROWS, width), lambda i: (jnp.minimum(i, DEPTH - 1), 0, 0)),
+    ]
+
+
+def branch_kernel(a_ref, h_ref, w_ref, own_ref, other_ref):
+    term = dot_rows(a_ref[0], outward_rows(w_ref)) + dot_rows(h_ref[0], down_rows(w_ref))
+    store_split(term.astype(jnp.bfloat16), own_ref, other_ref)
+
+
+def branch_terms(attended, hidden, rows_out):
+    width = rows_out.shape[-1]
     return pl.pallas_call(
         branch_kernel,
         grid=(PIECES,),
         in_specs=[
-            piece_spec(HEAD_COLS),
-            piece_spec(hidden.shape[-1]),
-            whole_spec(outward.shape),
-            whole_spec(down.shape),
+            other_first(HEAD_COLS),
+            other_first(hidden.shape[-1]),
+            whole_spec(rows_out.shape),
         ],
-        out_specs=piece_spec(width),
-        out_shape=jax.ShapeDtypeStruct((PIECES, ROWS, width), jnp.bfloat16),
+        out_specs=split_specs(width),
+        out_shape=[jax.ShapeDtypeStruct((DEPTH, ROWS, width), jnp.bfloat16)] * 2,
         compiler_params=params(48),
         cost_estimate=cost(2 * PIECES * ROWS * width * (HEAD_COLS + hidden.shape[-1]), 16 * MIB),
         name="branch_terms",
-    )(attended, hidden, outward, down)
-
-
-def back_kernel(g_ref, gate_ref, up_ref, wo_ref, wd_ref, a_ref, gg_ref, ug_ref):
+    )(attended, hidden, rows_out)
+
+
+def back_kernel(g_ref, gate_ref, up_ref, w_ref, a_ref, gu_ref):
     grad = g_ref[0]
-    a_ref[0] = transposed_times(grad, wo_ref[...]).astype(jnp.bfloat16)
-    hidden_grad = transposed_times(grad, wd_ref[...])
+    a_ref[0] = transposed_times(grad, outward_rows(w_ref)).astype(jnp.bfloat16)
+    hidden_grad = transposed_times(grad, down_rows(w_ref))
     gate = gate_ref[0]
     sig = jax.nn.sigmoid(gate)
     silu = gate * sig
-    gg_ref[0] = (hidden_grad * up_ref[0] * (sig + silu * (1.0 - sig))).astype(jnp.bfloat16)
-    ug_ref[0] = (hidden_grad * silu).astype(jnp.bfloat16)
-
-
-def back(grads, gate, up, outward, down):
-    width = outward.shape[1]
-    hidden = down.shape[0]
+    gate_grad = hidden_grad * up_ref[0] * (sig + silu * (1.0 - sig))
+    up_grad = hidden_grad * silu
+    gu_ref[0] = jnp.concatenate([gate_grad, up_grad], 1).astype(jnp.bfloat16)
+
+
+def back(grads, gate, up, rows_out):
+    width = rows_out.shape[-1]
+    hidden = gate.shape[-1]
     return pl.pallas_call(
         back_kernel,
         grid=(PIECES,),
@@ -602,19 +907,17 @@
             piece_spec(width),
             piece_spec(hidden),
             piece_spec(hidden),
-            whole_spec(outward.shape),
-            whole_spec(down.shape),
+            whole_spec(rows_out.shape),
         ],
-        out_specs=[piece_spec(HEAD_COLS), piece_spec(hidden), piece_spec(hidden)],
+        out_specs=[piece_spec(HEAD_COLS), piece_spec(2 * hidden)],
         out_shape=[
             jax.ShapeDtypeStruct((PIECES, ROWS, HEAD_COLS), jnp.bfloat16),
-            jax.ShapeDtypeStruct((PIECES, ROWS, hidden), jnp.bfloat16),
-            jax.ShapeDtypeStruct((PIECES, ROWS, hidden), jnp.bfloat16),
+            jax.ShapeDtypeStruct((PIECES, ROWS, 2 * hidden), jnp.bfloat16),
         ],
         compiler_params=params(48),
         cost_estimate=cost(2 * PIECES * ROWS * width * (HEAD_COLS + hidden), 28 * MIB),
         name="back",
-    )(grads, gate, up, outward, down)
+    )(grads, gate, up, rows_out)
 
 
 def pair_rows(block):
@@ -780,17 +1083,16 @@
     dv_ref,
     odk_ref,
     odv_ref,
-    gg_ref,
-    ug_ref,
+    gu_ref,
     x_ref,
     wi_ref,
     wg_ref,
-    wu_ref,
     cos_ref,
     first_ref,
     second_ref,
     pg_ref,
-    out_ref,
+    own_ref,
+    other_ref,
     gain_ref,
     shift_ref,
     bias_ref,
@@ -801,10 +1103,9 @@
     value = dv_ref[0] + odv_ref[0].astype(jnp.float32)
     low = jnp.concatenate([query, key, value], 1).astype(jnp.bfloat16)
     pg_ref[0] = low
-    grad = transposed_times(low, wi_ref[...])
-    grad += transposed_times(gg_ref[0], wg_ref[...])
-    grad += transposed_times(ug_ref[0], wu_ref[...])
-    out_ref[0] = grad.astype(jnp.bfloat16)
+    grad = transposed_times(low, inward_rows(wi_ref))
+    grad += transposed_times(gu_ref[0], wg_ref[...])
+    store_split(grad.astype(jnp.bfloat16), own_ref, other_ref)
     hat, _ = normalised(x_ref[0])
 
     @pl.when(pl.program_id(0) == 0)
@@ -818,36 +1119,94 @@
     bias_ref[...] += jnp.sum(low.astype(jnp.float32), axis=0, keepdims=True)
 
 
-def input_grads(parts, other_key, other_value, gate_grad, up_grad, pieces, weights, tables):
+def input_grads(parts, other_key, other_value, gate_up_grad, pieces, weights, tables):
     width = pieces.shape[-1]
-    hidden = gate_grad.shape[-1]
+    hidden = gate_up_grad.shape[-1]
     table_spec = pl.BlockSpec((1,) + tables[0].shape[1:], lambda i: (i % DEPTH, 0, 0))
     return pl.pallas_call(
         input_grad_kernel,
         grid=(PIECES,),
-        in_specs=[piece_spec(HEAD_COLS)] * 5
-        + [piece_spec(hidden)] * 2
-        + [piece_spec(width)]
+        in_specs=[other_first(HEAD_COLS)] * 5
+        + [other_first(hidden)]
+        + [other_first(width)]
         + [whole_spec(w.shape) for w in weights]
         + [table_spec] * 3,
-        out_specs=[
-            piece_spec(3 * HEAD_COLS),
-            piece_spec(width),
+        out_specs=[other_first(3 * HEAD_COLS)]
+        + split_specs(width)
+        + [
             whole_spec((1, width)),
             whole_spec((1, width)),
             whole_spec((1, 3 * HEAD_COLS)),
         ],
-        out_shape=[
-            jax.ShapeDtypeStruct((PIECES, ROWS, 3 * HEAD_COLS), jnp.bfloat16),
-            jax.ShapeDtypeStruct((PIECES, ROWS, width), jnp.bfloat16),
+        out_shape=[jax.ShapeDtypeStruct((PIECES, ROWS, 3 * HEAD_COLS), jnp.bfloat16)]
+        + [jax.ShapeDtypeStruct((DEPTH, ROWS, width), jnp.bfloat16)] * 2
+        + [
             jax.ShapeDtypeStruct((1, width), jnp.float32),
             jax.ShapeDtypeStruct((1, width), jnp.float32),
             jax.ShapeDtypeStruct((1, 3 * HEAD_COLS), jnp.float32),
         ],
         compiler_params=params(56),
-        cost_estimate=cost(2 * PIECES * ROWS * width * (3 * HEAD_COLS + 2 * hidden), 48 * MIB),
+        cost_estimate=cost(2 * PIECES * ROWS * width * (3 * HEAD_COLS + hidden), 48 * MIB),
         name="input_grads",
-    )(*parts, other_key, other_value, gate_grad, up_grad, pieces, *weights, *tables)
+    )(*parts, other_key, other_value, gate_up_grad, pieces, *weights, *tables)
+
+
+def rows_kernel(first, last, place_ref, left_ref, right_ref, out_ref):
+    term = times_transposed(left_ref[...], right_ref[:, first:last])
+    out_ref[0] = term.astype(out_ref.dtype)
+
+
+def split_rows_kernel(first, last, place_ref, left_ref, right_ref, keep_ref, send_ref):
+    y = place_ref[1]
+    term = times_transposed(left_ref[...], right_ref[:, first:last])
+    rows = term.shape[0] // 4
+    even = jnp.concatenate([term[:rows], term[2 * rows : 3 * rows]], 0)
+    odd = jnp.concatenate([term[rows : 2 * rows], term[3 * rows :]], 0)
+    keep_ref[0] = jnp.where(y == 0, even, odd)
+    send_ref[0] = jnp.where(y == 0, odd, even).astype(jnp.bfloat16)
+
+
+def weight_grad(place, left, right, first, last, part):
+    total, width = left.shape
+    columns = last - first
+    blocks = PIECES if part == "split" else PIECES // 2
+    if part == "split":
+        where = lambda i, place: (0, i)
+    elif part == "keep":
+        where = lambda i, place: (0, place[2] * DEPTH + i)
+    else:
+        where = lambda i, place: (0, (1 - place[2]) * DEPTH + i)
+    size = width // PIECES
+    high = size // 2 if part == "split" else size
+    spec = pl.BlockSpec((1, high, columns), lambda i, place: (i, 0, 0))
+    shape = (blocks, high, columns)
+    if part == "split":
+        specs = [spec, spec]
+        shapes = [
+            jax.ShapeDtypeStruct(shape, jnp.float32),
+            jax.ShapeDtypeStruct(shape, jnp.bfloat16),
+        ]
+    else:
+        specs = spec
+        shapes = jax.ShapeDtypeStruct(shape, jnp.float32 if part == "keep" else jnp.bfloat16)
+    return pl.pallas_call(
+        functools.partial(
+            split_rows_kernel if part == "split" else rows_kernel, first, last
+        ),
+        grid_spec=pltpu.PrefetchScalarGridSpec(
+            num_scalar_prefetch=1,
+            grid=(blocks,),
+            in_specs=[
+                pl.BlockSpec((total, size), where),
+                pl.BlockSpec(right.shape, lambda i, place: (0, 0)),
+            ],
+            out_specs=specs,
+        ),
+        out_shape=shapes,
+        compiler_params=params(48),
+        cost_estimate=cost(2 * total * size * blocks * columns, 10 * MIB),
+        name="weight_grad_" + part,
+    )(place, left, right)
 
 
 def lane_tables(positions):
@@ -880,19 +1239,38 @@
     bucket, blk = lax.axis_index("bucket"), lax.axis_index("blk")
     x, core = bucket // 2, bucket % 2
     z, y = blk // 2, blk % 2
-    devices = 4 * 2 * DEPTH
-
+
+    own_rows = inward_weight.shape[0]
+    hidden_each = gate_up_weight.shape[1] // (2 * 2 * 2 * DEPTH)
+    gain_share, bias_share = norm_gain.shape[0], inward_bias.shape[0]
     shares = jnp.concatenate([norm_gain, norm_shift, inward_bias]).astype(jnp.bfloat16)
-    shares = lax.all_gather(shares, ("bucket", "blk"), axis=0, tiled=False).astype(jnp.float32)
-    gain_share, bias_share = norm_gain.shape[0], inward_bias.shape[0]
-    gain = shares[:, :gain_share].reshape(1, width)
-    shift = shares[:, gain_share : 2 * gain_share].reshape(1, width)
-    bias = shares[:, 2 * gain_share :].reshape(-1)
+    shares = jnp.pad(shares, (0, 3 * HEAD_COLS - shares.shape[0]))
+    inward = inward_weight.astype(jnp.bfloat16).reshape(own_rows, 3, 2, 2, DEPTH, 2 * HEAD_DIM)
+    inward = jnp.transpose(inward, (3, 4, 0, 1, 2, 5)).reshape(2, DEPTH, own_rows, 3 * HEAD_COLS)
+    inward = jnp.concatenate(
+        [inward, jnp.broadcast_to(shares, (2, DEPTH, EXTRA, 3 * HEAD_COLS))], 2
+    )
+    gate_up = gate_up_weight.astype(jnp.bfloat16).reshape(own_rows, 2, 2, 2, DEPTH, hidden_each)
+    gate_up = jnp.transpose(gate_up, (3, 4, 0, 1, 2, 5)).reshape(
+        2, DEPTH, own_rows, 4 * hidden_each
+    )
+    rows_out = jnp.concatenate([outward_weight, down_weight]).astype(jnp.bfloat16)
+    own_tokens = jnp.transpose(tokens[0], (1, 0, 2))
+    pieces, inward, gate_up, rows_out = gather(
+        own_tokens.reshape(ROWS, width), inward, gate_up, rows_out
+    )
+    vectors = inward[..., own_rows, :].reshape(-1, 3 * HEAD_COLS).astype(jnp.float32)
+    inward = inward.reshape((-1,) + inward.shape[4:])
+    gate_up = gate_up.reshape(width, -1)
+    rows_out = rows_out.reshape((-1,) + rows_out.shape[2:])
+
+    gain = vectors[:, :gain_share].reshape(1, width)
+    shift = vectors[:, gain_share : 2 * gain_share].reshape(1, width)
+    bias = vectors[:, 2 * gain_share : 2 * gain_share + bias_share].reshape(-1)
 
     def own_columns(values, each):
         split = values.reshape(2, 2, DEPTH, each)
-        split = lax.dynamic_index_in_dim(split, core, 1, False)
-        return lax.dynamic_index_in_dim(split, z, 1, False)
+        return one_of(one_of(split, core, 1), z, 1)
 
     key_bias = jnp.pad(
         own_columns(bias[2 * width :], 2 * ROT).reshape(LOCAL_HEADS, ROT),
@@ -906,89 +1284,82 @@
         ]
     ).reshape(1, -1)
 
-    own_rows = inward_weight.shape[0]
-    hidden_each = gate_up_weight.shape[1] // (2 * 2 * 2 * DEPTH)
-    inward = inward_weight.astype(jnp.bfloat16).reshape(own_rows, 3, 2, 2, DEPTH, 2 * HEAD_DIM)
-    inward = jnp.transpose(inward, (3, 4, 0, 1, 2, 5)).reshape(2, DEPTH, own_rows, 3 * HEAD_COLS)
-    gate_up = gate_up_weight.astype(jnp.bfloat16).reshape(own_rows, 2, 2, 2, DEPTH, hidden_each)
-    gate_up = jnp.transpose(gate_up, (3, 4, 0, 1, 2, 5)).reshape(
-        2, DEPTH, own_rows, 4 * hidden_each
-    )
-    inward = columns_of_group(inward, core, z)
-    gate_up = columns_of_group(gate_up, core, z)
-    rows_out = jnp.concatenate([outward_weight, down_weight]).astype(jnp.bfloat16)
-    rows_out = over_columns(rows_out, x, y)
-    outward = rows_out[:, :, : outward_weight.shape[0]].reshape(-1, width)
-    down = rows_out[:, :, outward_weight.shape[0] :].reshape(-1, width)
-
-    def full_rows(value):
-        value = over_columns(value, x, y)
-        return jnp.transpose(value, (0, 3, 2, 1, 4, 5)).reshape(width, -1)
-
-    inward = full_rows(inward)
-    gate_up = full_rows(gate_up)
-    gate_weight = gate_up[:, : 2 * hidden_each]
-    up_weight = gate_up[:, 2 * hidden_each :]
-
-    own_tokens = jnp.transpose(tokens[0], (1, 0, 2))
     position = blk * group_len + jnp.arange(group_len, dtype=jnp.int32)
     valid = (position[None, :] < lengths[0][:, None]).astype(jnp.float32)[..., None]
     own_cotangent = jnp.transpose(cotangent[0], (1, 0, 2)).astype(jnp.float32)
     own_grad = (own_cotangent * valid).astype(jnp.bfloat16)
-    pieces = jnp.stack(gather_pieces(own_tokens.reshape(ROWS, width), z))
-    grads = jnp.stack(gather_pieces(own_grad.reshape(ROWS, width), z))
+    grads = after(own_grad.reshape(ROWS, width), pieces)
+    grads = jnp.stack(gather_pieces(grads))
 
     turns = (z - jnp.arange(DEPTH, dtype=jnp.int32)) % DEPTH
     tables = lane_tables(
         ((2 * turns + y) * group_len)[:, None] + jnp.arange(group_len, dtype=jnp.int32)
     )
-    place = jnp.stack([z, y]).astype(jnp.int32)
+    place = jnp.stack([z, y, x]).astype(jnp.int32)
 
     normed, queries, pairs = project(pieces, gain, shift, inward, own_bias, tables)
     other_pairs = lax.ppermute(pairs, "blk", ACROSS_Y)
-    gate, up, hidden = feed(normed, gate_weight, up_weight)
-    attended = attend(place, queries, pairs, other_pairs, seqs)
-    branch = scatter_pieces(branch_terms(attended, hidden, outward, down))
+    gate, up, hidden = feed(normed, gate_up)
+    attended = attend(place, after(queries, hidden), pairs, other_pairs, seqs)
+    branch_own, branch_other = branch_terms(attended, hidden, rows_out)
+    branch_sums = core_sums(branch_own, branch_other)
+    branch = scatter_pieces(branch_sums)
     branch = branch.reshape(seqs, group_len, width)
     inputs = own_tokens.astype(jnp.float32)
     layer_out = (inputs + valid * branch).astype(jnp.bfloat16)
 
-    attended_grad, gate_grad, up_grad = back(grads, gate, up, outward, down)
+    attended_grad, gate_up_grad = back(after(grads, branch_own), gate, up, rows_out)
+    attended_grad = after(attended_grad, *branch_sums)
     dq, dk, dv, other_dk, other_dv = attend_back(
         place, queries, pairs, other_pairs, attended_grad, seqs
     )
-    other_dk = lax.ppermute(other_dk, "blk", ACROSS_Y)
-    other_dv = lax.ppermute(other_dv, "blk", ACROSS_Y)
+    got_dk = lax.ppermute(other_dk, "blk", ACROSS_Y)
+    got_dv = lax.ppermute(other_dv, "blk", ACROSS_Y)
     total = PIECES * ROWS
-    flat_normed = normed.reshape(total, width)
-    flat_grads = grads.reshape(total, width)
+    flat_normed = after(normed, other_dk).reshape(total, width)
+    flat_grads = after(grads, other_dk).reshape(total, width)
+
+    def row_sums(right):
+        rows, columns = own_rows, right.shape[-1]
+        right = right.reshape(total, columns)
+        cut = -(-columns // 256) * 128
+        send = weight_grad(place, flat_normed, right, 0, cut, "send")
+        y_keep, y_send = weight_grad(place, flat_normed, right, cut, columns, "split")
+        keep = weight_grad(place, flat_normed, right, 0, cut, "keep")
+        first = summed(keep, send, True).reshape(2, DEPTH, 2, rows, -1)
+        first = summed(one_of(first, y, 2), one_of(first, 1 - y, 2), False)
+        second = summed(y_keep, y_send, False).reshape(2, 2, DEPTH, rows, -1)
+        second = summed(one_of(second, x, 0), one_of(second, 1 - x, 0), True)
+        return jnp.transpose(jnp.concatenate([first, second], -1), (1, 0, 2, 3))
+
+    def device_rows(term, parts):
+        term = rows_of_device(term, core, z).reshape(2, DEPTH, own_rows, parts, 2, -1)
+        return jnp.transpose(term, (2, 3, 4, 0, 1, 5)).reshape(own_rows, -1)
+
+    gate_up_term = row_sums(gate_up_grad)
     outward_term = times_transposed(attended.reshape(total, -1), flat_grads)
     down_term = times_transposed(hidden.reshape(total, -1), flat_grads)
-    gate_term = times_transposed(flat_normed, gate_grad.reshape(total, -1))
-    up_term = times_transposed(flat_normed, up_grad.reshape(total, -1))
-    projected_grad, normed_grad, gain_term, shift_term, bias_term = input_grads(
-        (dq, dk, dv),
-        other_dk,
-        other_dv,
-        gate_grad,
-        up_grad,
+
+    def owner_sums(term):
+        term = term.reshape(2, 2, -1, width)
+        term = summed(one_of(term, x, 0), one_of(term, 1 - x, 0), True)
+        return summed(one_of(term, y, 0), one_of(term, 1 - y, 0), False)
+
+    outward_sum = owner_sums(outward_term)
+    down_sum = owner_sums(down_term)
+    projected_grad, normed_own, normed_other, gain_term, shift_term, bias_term = input_grads(
+        (after(dq, branch), dk, dv),
+        got_dk,
+        got_dv,
+        gate_up_grad,
         pieces,
-        (inward, gate_weight, up_weight),
+        (inward, gate_up),
         tables,
     )
-    inward_term = times_transposed(flat_normed, projected_grad.reshape(total, -1))
-
-    outward_sum = sum_over_columns(outward_term.reshape(2, 2, -1, width), x, y)
-    down_sum = sum_over_columns(down_term.reshape(2, 2, -1, width), x, y)
-
-    def device_rows(term, parts):
-        term = term.reshape(2, 2, DEPTH, 2, own_rows, -1)
-        term = sum_over_columns(jnp.transpose(term, (0, 3, 2, 1, 4, 5)), x, y)
-        term = rows_of_device(term, core, z)
-        term = term.reshape(2, DEPTH, own_rows, parts, 2, -1)
-        return jnp.transpose(term, (2, 3, 4, 0, 1, 5)).reshape(own_rows, -1).astype(jnp.float32)
-
-    gate_up_sum = device_rows(jnp.concatenate([gate_term, up_term], 1), 2)
+    normed_sums = core_sums(normed_own, normed_other)
+    normed_grad = scatter_pieces(normed_sums).reshape(seqs, group_len, width)
+    inward_term = row_sums(after(projected_grad, *normed_sums))
+    gate_up_sum = device_rows(gate_up_term, 2)
     inward_sum = device_rows(inward_term, 3)
 
     bias_parts = bias_term.reshape(3, 2, 1, 1, 2 * HEAD_DIM)
@@ -1000,19 +1371,17 @@
     bias_all = jnp.concatenate(
         [spread[0].reshape(-1), spread[2].reshape(-1), key_rot.reshape(-1)]
     )
-    vector_terms = jnp.concatenate(
-        [
-            gain_term.reshape(devices, -1),
-            shift_term.reshape(devices, -1),
-            bias_all.reshape(devices, -1),
-        ],
-        1,
-    )
-    vector_sums = lax.psum_scatter(
-        vector_terms, ("bucket", "blk"), scatter_dimension=0, tiled=True
-    ).reshape(-1)
-
-    normed_grad = scatter_pieces(normed_grad).reshape(seqs, group_len, width)
+    grid = (2, 2, DEPTH, 2, -1)
+    vector_sum = vector_sums(
+        jnp.concatenate(
+            [gain_term.reshape(grid), shift_term.reshape(grid), bias_all.reshape(grid)], -1
+        ),
+        x,
+        y,
+        core,
+        z,
+    )
+
     hat, inverse = normalised(own_tokens)
     scaled = normed_grad * gain.reshape(width)
     input_grad = inverse * (
@@ -1028,10 +1397,10 @@
     return (
         placed(layer_out),
         placed(tokens_grad),
-        vector_sums[:gain_share],
-        vector_sums[gain_share : 2 * gain_share],
+        vector_sum[:gain_share],
+        vector_sum[gain_share : 2 * gain_share],
         inward_sum,
-        vector_sums[2 * gain_share :],
+        vector_sum[2 * gain_share :],
         outward_sum,
         gate_up_sum,
         down_sum,

time: 957 us -> 719 us (0.75)
  Pallas kernels: 151 us -> 343 us
  waiting for transfers between devices: 348 us -> 171 us
  blocking collectives: 102 us -> 0 us
  starting transfers between devices: 110 us -> 45.1 us
  matrix products: 49.5 us -> 17.3 us
  local copies, waits for them, and re-layouts: 104 us -> 82.2 us
  other arithmetic: 74.5 us -> 53 us
    pallas_call x2 -> x9, Pallas kernels: 45.9 us -> 236 us  [the longest x1 132 us: gather(): pl.pallas_call(gather_kernel, in_specs=[anywhere] * 4, out_specs=[anywher...]
    ppermute x58 -> x39, waiting for transfers between devices: 348 us -> 159 us  [the longest x6 66.5 us: scatter_pieces(): got = lax.ppermute(sums[step], 'blk', around(-step))]
    all_gather x1 -> x0, blocking collectives: 61.4 us -> none  [shards_grouped(): lax.all_gather(shares, ('bucket', 'blk'), axis=0, tiled=False)]
    ppermute x58 -> x39, starting transfers between devices: 93.8 us -> 43.2 us  [the longest x6 8.8 us: scatter_pieces(): got = lax.ppermute(sums[step], 'blk', around(-step))]
    unnamed x1 -> x0, blocking collectives: 41 us -> none
    dot_general x5 -> x2, matrix products: 49.5 us -> 17.3 us  [times_transposed(): lax.dot_general(left, right, (((0,), (0,)), ((), ())), preferred_element_...]
    convert_element_type x12 -> x11, local copies, waits for them, and re-layouts: 18.7 us -> 3.07 us  [the longest x8 2.01 us: summed(): send = send.astype(jnp.bfloat16)]
    ppermute x8 -> x4, starting transfers between devices: 15.4 us -> 1.91 us  [gather_pieces(): return own + [lax.ppermute(piece, 'bucket', CORE) for piece in own]]
  transfers between devices with their start and end apart: 67 -> 44, of which waited for: 27 -> 15; matrix products, arithmetic and copies ran while one was open for 22% -> 14% of each run, Pallas kernels for 16% -> 27%
where the time goes in v2:
time: 719 us; the launch traced here: 713 us
  Pallas kernels  343 us (48%)
  waiting for transfers between devices  171 us (24%)
  local copies, waits for them, and re-layouts  82.2 us (11%)
  other arithmetic  53 us (7%)
  starting transfers between devices  45.1 us (6%)
  matrix products  17.3 us (2%)
    pallas_call x1, Pallas kernels, gather(): pl.pallas_call(gather_kernel, in_specs=[anywhere] * 4, out_specs=[anywher...  132 us
    ppermute x6, waiting for transfers between devices, scatter_pieces(): got = lax.ppermute(sums[step], 'blk', around(-step))  66.5 us
    pallas_call x6, Pallas kernels, weight_grad(): pl.pallas_call(functools.partial(split_rows_kernel if part == 'split' els...  52 us
    ppermute x6, waiting for transfers between devices, rows_of_device(): parts.append(lax.ppermute(chunk, 'blk', around(step)).astype(jnp.float32))  45.9 us
    pallas_call x1, Pallas kernels, input_grads(): pl.pallas_call(input_grad_kernel, grid=(PIECES,), in_specs=[other_first(H...  37.7 us
    ppermute x6, waiting for transfers between devices, summed(): lax.ppermute(send, 'bucket', ACROSS_X)  35.5 us
    unnamed x83, local copies, waits for them, and re-layouts  33.9 us
    pallas_call x1, Pallas kernels, attend_back(): pl.pallas_call(attend_back_kernel, grid_spec=pltpu.PrefetchScalarGridSpec...  32.1 us
  transfers between devices with their start and end apart: 44, of which 15 were waited for; matrix products, arithmetic and copies ran while one was open for 14% of the time, Pallas kernels for 27%

profile of v2, /device:TPU:11, one launch (start us, length us, event | category | flops | bytes accessed | tf_op | source)
XLA Modules:
  0.0 712.7 jit_solution(10192158498226352026)
XLA Ops:
  5.6 2.3 convert.30
  10.8 2.0 convert_element_type.329
  12.8 3.5 reshape.445
  16.2 3.8 copy.135
  20.0 3.9 reshape.446.wg_ref
  26.1 132.3 %gather.1 = (bf16[8,256,2048]{2,1,0:T(8,128)(2,1)}, bf16[2,2,4,2,80,768]{5,4,3,2,1,0:T(8,128)(2,1)S(1)}, bf16[2,2,4,2,64,1408]{5,4,3,2,1,0:T(8,128)(2,1)S(1)}, bf16[2,2,240,2048]{3,2,1,0:T(8,128)(2,1)S(1)}) custom-call(bf16[256,2048]{1,0:T(8,128)(2,1)S(1)} %bitcast.256, bf16[2,4,80,768]{3,2,1,0:T(8,128)(2,1)S(1)} %pad_maximum_fusion.4.wi_ref, ...), custom_call_target="tpu_custom_call" | custom-call | bytes 1048576 | tf_op jit(solution)/shard_map/gather/pallas_call | solution.py:708
  158.4 2.5 copy-done.2
  160.9 2.0 copy-done.4
  165.9 1.9 fusion.25
  167.9 17.7 %project.1 = (bf16[8,256,2048]{2,1,0:T(8,128)(2,1)}, bf16[8,256,256]{2,1,0:T(8,128)(2,1)S(1)}, bf16[8,256,512]{2,1,0:T(8,128)(2,1)S(1)}) custom-call(bf16[8,256,2048]{2,1,0:T(8,128)(2,1)} %get-tuple-element.46.x_ref, f32[1,2048]{1,0:T(1,128)S(1)} %reshape.447.gain_ref, f32[1,2048]{1,0:T(1,128)S(1)} %reshape.448.shift_ref, bf16[32,80,768]{2,1,0:T(8,128)(2,1)} %bitcast.249, ...), custom_call_target="tpu_custom_call" | custom-call | flops 100663296 | bytes 393216 | tf_op jit(solution)/shard_map/project/pallas_call | solution.py:789
  186.7 3.4 fusion.13
  191.0 2.1 collective-permute-start.6
  193.9 19.7 %feed.1 = (f32[8,256,704]{2,1,0:T(8,128)}, f32[8,256,704]{2,1,0:T(8,128)}, bf16[8,256,704]{2,1,0:T(8,128)(2,1)S(1)}) custom-call(bf16[8,256,2048]{2,1,0:T(8,128)(2,1)} %get-tuple-element.75.n_ref, bf16[2048,1408]{1,0:T(8,128)(2,1)} %bitcast.247), custom_call_target="tpu_custom_call" | custom-call | flops 184549376 | bytes 458752 | tf_op jit(solution)/shard_map/feed/pallas_call | solution.py:826
  215.1 4.6 copy.97
  220.7 12.2 %collective-permute-done = bf16[8,256,512]{2,1,0:T(8,128)(2,1)} collective-permute-done((bf16[8,256,512]{2,1,0:T(8,128)(2,1)S(1)}, bf16[8,256,512]{2,1,0:T(8,128)(2,1)}, u32[]{:S(2)}, u32[]{:S(2)}) %collective-permute-start) | collective-permute-done | bytes 2097184 | tf_op jit(solution)/shard_map/ppermute | solution.py:1301
  234.1 20.5 %attend.1 = bf16[2,4,2,128,256]{4,3,2,1,0:T(8,128)(2,1)S(1)} custom-call(s32[3]{0:T(128)S(1)} %pad_add_fusion.place_ref, bf16[2,4,2,128,256]{4,3,2,1,0:T(8,128)(2,1)S(1)} %bitcast.257, bf16[2,4,2,128,512]{4,3,2,1,0:T(8,128)(2,1)S(1)} %bitcast.240, bf16[2,4,2,128,512]{4,3,2,1,0:T(8,128)(2,1)S(1)} %bitcast.241, ...), custom_call_target="tpu_custom_call" | custom-call | flops 167772160 | bytes 131072 | tf_op jit(solution)/shard_map/attend/pallas_call | solution.py:1036
  254.6 14.5 %branch_terms.1 = (bf16[4,256,2048]{2,1,0:T(8,128)(2,1)}, bf16[4,256,2048]{2,1,0:T(8,128)(2,1)}) custom-call(bf16[8,256,256]{2,1,0:T(8,128)(2,1)S(1)} %bitcast.254, bf16[8,256,704]{2,1,0:T(8,128)(2,1)S(1)} %copy-done.7, bf16[4,240,2048]{2,1,0:T(8,128)(2,1)} %bitcast.251), custom_call_target="tpu_custom_call" | custom-call | flops 125829120 | bytes 262144 | tf_op jit(solution)/shard_map/branch_terms/pallas_call | solution.py:872
  269.0 1.9 collective-permute-start.1
  271.0 2.4 bitcast_dynamic-update-slice_fusion.7
  273.9 9.1 %collective-permute-done.5 = bf16[256,2048]{1,0:T(8,128)(2,1)} collective-permute-done((bf16[256,2048]{1,0:T(8,128)(2,1)}, bf16[256,2048]{1,0:T(8,128)(2,1)}, u32[]{:S(2)}, u32[]{:S(2)}) %collective-permute-start.5) | collective-permute-done | bytes 1048608 | tf_op jit(solution)/shard_map/ppermute | solution.py:385
  283.5 2.3 bitcast_dynamic-update-slice_fusion.6
  285.8 2.3 bitcast_dynamic-update-slice_fusion.5
  288.1 2.3 bitcast_dynamic-update-slice_fusion.4
  290.4 2.3 bitcast_dynamic-update-slice_fusion.3
  294.2 2.3 bitcast_dynamic-update-slice_fusion.2
  299.4 16.2 %back.1 = (bf16[8,256,256]{2,1,0:T(8,128)(2,1)S(1)}, bf16[8,256,1408]{2,1,0:T(8,128)(2,1)}) custom-call(bf16[8,256,2048]{2,1,0:T(8,128)(2,1)} %bitcast_dynamic-update-slice_fusion.g_ref, f32[8,256,704]{2,1,0:T(8,128)} %get-tuple-element.59.gate_ref, f32[8,256,704]{2,1,0:T(8,128)} %get-tuple-element.60.up_ref, bf16[4,240,2048]{2,1,0:T(8,128)(2,1)S(1)} %bitcast.252), custom_call_target="tpu_custom_call" | custom-call | flops 125829120 | bytes 458752 | tf_op jit(solution)/shard_map/back/pallas_call | solution.py:903
  315.6 4.5 fusion.16
  320.0 2.0 collective-permute-start.2
  322.2 1.9 collective-permute-start.3
  324.1 32.1 %attend_back.1 = (f32[2,4,2,128,256]{4,3,2,1,0:T(8,128)}, f32[2,4,2,128,256]{4,3,2,1,0:T(8,128)}, f32[2,4,2,128,256]{4,3,2,1,0:T(8,128)}, bf16[2,4,2,128,256]{4,...) custom-call(s32[3]{0:T(128)S(1)} %pad_add_fusion.place_ref, bf16[2,4,2,128,256]{4,3,2,1,0:T(8,128)(2,1)S(1)} %bitcast.258, ...), custom_call_target="tpu_custom_call" | custom-call | flops 419430400 | bytes 262144 | tf_op jit(solution)/shard_map/attend_back/pallas_call | solution.py:1060
  357.3 8.9 %weight_grad_send.3 = bf16[4,256,768]{2,1,0:T(8,128)(2,1)} custom-call(s32[3]{0:T(128)S(1)} %pad_add_fusion.place_ref, bf16[2048,2048]{1,0:T(8,128)(2,1)} %bitcast.262, bf16[2048,1408]{1,0:T(8,128)(2,1)} %bitcast.268), custom_call_target="tpu_custom_call" | custom-call | flops 50331648 | bytes 163840 | tf_op jit(solution)/shard_map/weight_grad_send/pallas_call | solution.py:1192
  366.1 13.3 %weight_grad_split.3 = (f32[8,128,640]{2,1,0:T(8,128)S(1)}, bf16[8,128,640]{2,1,0:T(8,128)(2,1)}) custom-call(s32[3]{0:T(128)S(1)} %pad_add_fusion.place_ref, bf16[2048,2048]{1,0:T(8,128)(2,1)} %bitcast.263, bf16[2048,1408]{1,0:T(8,128)(2,1)} %bitcast.269), custom_call_target="tpu_custom_call" | custom-call | flops 83886080 | bytes 163840 | tf_op jit(solution)/shard_map/weight_grad_split/pallas_call | solution.py:1192
  379.9 9.5 %fusion.87 = f32[2,2,176,2048]{3,2,1,0:T(8,128)S(1)} fusion(bf16[2,2,176,2048]{3,2,1,0:T(8,128)(2,1)} %bitcast.285, bf16[2048,2048,1,1]{1,0,3,2:T(8,128)(2,1)} %bitcast.86), kind=kOutput, calls=%fused_computation.227 | convolution fusion | flops 5905580032 | bytes 17039360 | tf_op jit(solution)/shard_map/dot_general | solution.py:43
  389.4 7.8 %fusion.86 = f32[2,2,64,2048]{3,2,1,0:T(8,128)S(1)} fusion(bf16[2,2,64,2048]{3,2,1,0:T(8,128)(2,1)S(1)} %bitcast.289, bf16[2048,2048,1,1]{1,0,3,2:T(8,128)(2,1)} %bitcast.86), kind=kOutput, calls=%fused_computation.226 | convolution fusion | flops 2147483648 | bytes 11534336 | tf_op jit(solution)/shard_map/dot_general | solution.py:43
  400.3 12.1 %collective-permute-done.3 = bf16[256,2048]{1,0:T(8,128)(2,1)} collective-permute-done((bf16[256,2048]{1,0:T(8,128)(2,1)}, bf16[256,2048]{1,0:T(8,128)(2,1)}, u32[]{:S(2)}, u32[]{:S(2)}) %collective-permute-start.3) | collective-permute-done | bytes 1048608 | tf_op jit(solution)/shard_map/ppermute | solution.py:398
  413.4 4.0 convert_add_fusion.4
  418.8 37.7 %input_grads.1 = (bf16[8,256,768]{2,1,0:T(8,128)(2,1)}, bf16[4,256,2048]{2,1,0:T(8,128)(2,1)}, bf16[4,256,2048]{2,1,0:T(8,128)(2,1)}, f32[1,2048]{1,0:T(1,128)}, f32[1,2048]{1,0:T(1,128)}, /*index=5*/f32[1,768]{1,0:T(1,128)}) custom-call(f32[8,256,256]{2,1,0:T(8,128)} %bitcast.286, f32[8,256,256]{2,1,0:T(8,128)} %bitcast.287, f32[8,256,256]{2,1,0:T(8,128)} %bitcast.288, ...), custom_call_target="tpu_custom_call" | custom-call | flops 285212672 | bytes 786432 | tf_op jit(solution)/shard_map/input_grads/pallas_call | solution.py:1126
  463.9 2.0 collective-permute-start.19
  467.6 7.9 %weight_grad_keep.3 = f32[4,256,768]{2,1,0:T(8,128)S(1)} custom-call(s32[3]{0:T(128)S(1)} %pad_add_fusion.place_ref, bf16[2048,2048]{1,0:T(8,128)(2,1)} %bitcast.264, bf16[2048,1408]{1,0:T(8,128)(2,1)} %bitcast.270), custom_call_target="tpu_custom_call" | custom-call | flops 50331648 | bytes 163840 | tf_op jit(solution)/shard_map/weight_grad_keep/pallas_call | solution.py:1192
  475.8 2.0 collective-permute-start.23
  477.8 2.4 collective-permute-start.22
  489.9 22.8 %collective-permute-done.42 = bf16[2,176,2048]{2,1,0:T(8,128)(2,1)S(1)} collective-permute-done((bf16[2,176,2048]{2,1,0:T(8,128)(2,1)S(1)}, bf16[2,176,2048]{2,1,0:T(8,128)(2,1)S(1)}, u32[]{:S(2)}, u32[]{:S(2)}) %collective-permute-start.42) | collective-permute-done | bytes 1441824 | tf_op jit(solution)/shard_map/ppermute | solution.py:414
  514.0 12.7 %collective-permute-done.37 = bf16[2,4,64,640]{3,2,0,1:T(8,128)(2,1)S(1)} collective-permute-done((bf16[2,4,64,640]{3,2,0,1:T(8,128)(2,1)S(1)}, bf16[2,4,64,640]{3,2,0,1:T(8,128)(2,1)S(1)}, u32[]{:S(2)}, u32[]{:S(2)}) %collective-permute-start.37) | collective-permute-done | bytes 655392 | tf_op jit(solution)/shard_map/ppermute | solution.py:414
  527.2 2.0 collective-permute-start.38
  531.7 3.1 collective-permute-done.38
  534.8 22.8 %collective-permute-done.39 = bf16[2,64,1408]{2,1,0:T(8,128)(2,1)S(1)} collective-permute-done((bf16[2,64,1408]{2,1,0:T(8,128)(2,1)S(1)}, bf16[2,64,1408]{2,1,0:T(8,128)(2,1)S(1)}, u32[]{:S(2)}, u32[]{:S(2)}) %collective-permute-start.39) | collective-permute-done | bytes 360480 | tf_op jit(solution)/shard_map/ppermute | solution.py:423
  557.7 4.3 collective-permute-done.40
  564.9 2.5 fusion.19
  568.5 6.3 weight_grad_send.2
  576.2 3.7 stack.147
  579.9 3.6 reshape.499
  585.0 3.2 collective-permute-start.16
  588.3 10.2 %weight_grad_split.2 = (f32[8,128,384]{2,1,0:T(8,128)S(1)}, bf16[8,128,384]{2,1,0:T(8,128)(2,1)}) custom-call(s32[3]{0:T(128)S(1)} %pad_add_fusion.place_ref, bf16[2048,2048]{1,0:T(8,128)(2,1)} %bitcast.266, bf16[2048,768]{1,0:T(8,128)(2,1)S(1)} %bitcast.245), custom_call_target="tpu_custom_call" | custom-call | flops 50331648 | bytes 163840 | tf_op jit(solution)/shard_map/weight_grad_split/pallas_call | solution.py:1192
  600.9 3.6 copy.96
  604.6 5.5 reshape.489
  610.1 5.3 weight_grad_keep.2
  620.4 11.1 %collective-permute-done.17 = bf16[256,2048]{1,0:T(8,128)(2,1)} collective-permute-done((bf16[256,2048]{1,0:T(8,128)(2,1)}, bf16[256,2048]{1,0:T(8,128)(2,1)}, u32[]{:S(2)}, u32[]{:S(2)}) %collective-permute-start.17) | collective-permute-done | bytes 1048608 | tf_op jit(solution)/shard_map/ppermute | solution.py:398
  631.5 43.2 %collective-permute-done.16 = bf16[256,2048]{1,0:T(8,128)(2,1)} collective-permute-done((bf16[256,2048]{1,0:T(8,128)(2,1)}, bf16[256,2048]{1,0:T(8,128)(2,1)}, u32[]{:S(2)}, u32[]{:S(2)}) %collective-permute-start.16) | collective-permute-done | bytes 1048608 | tf_op jit(solution)/shard_map/ppermute | solution.py:398
  674.7 3.3 multiply_reduce_fusion
  679.1 4.0 collective-permute-start.29
  684.9 10.5 %collective-permute-done.29 = bf16[2,64,768]{2,1,0:T(8,128)(2,1)S(1)} collective-permute-done((bf16[2,64,768]{2,1,0:T(8,128)(2,1)S(1)}, bf16[2,64,768]{2,1,0:T(8,128)(2,1)S(1)}, u32[]{:S(2)}, u32[]{:S(2)}) %collective-permute-start.29) | collective-permute-done | bytes 196640 | tf_op jit(solution)/shard_map/ppermute | solution.py:423
  695.5 4.2 collective-permute-done.30
  703.4 2.0 copy.99
  705.5 2.0 copy.98
  (258 shorter events, 80.9 us)
Async XLA Ops:
  0.6 7.3 %copy-start.27 = (f32[64,6144]{1,0:T(8,128)S(1)}, f32[64,6144]{1,0:T(8,128)}, u32[]{:S(2)}) copy-start(f32[64,6144]{1,0:T(8,128)} %param.14) | copy-start | bytes 4718596
  167.9 17.7 %copy-start.8 = (f32[4,128,256]{2,1,0:T(8,128)}, f32[4,128,256]{2,1,0:T(8,128)S(1)}, u32[]{:S(2)}) copy-start(f32[4,128,256]{2,1,0:T(8,128)S(1)} %get-tuple-element.129.second_ref) | copy-start | bytes 1572868
  167.9 17.7 %copy-start.9 = (f32[4,128,256]{2,1,0:T(8,128)}, f32[4,128,256]{2,1,0:T(8,128)S(1)}, u32[]{:S(2)}) copy-start(f32[4,128,256]{2,1,0:T(8,128)S(1)} %get-tuple-element.130.first_ref) | copy-start | bytes 1572868
  167.9 17.7 %copy-start.10 = (f32[4,128,256]{2,1,0:T(8,128)}, f32[4,128,256]{2,1,0:T(8,128)S(1)}, u32[]{:S(2)}) copy-start(f32[4,128,256]{2,1,0:T(8,128)S(1)} %get-tuple-element.131.cos_ref) | copy-start | bytes 1572868
  167.9 18.7 %copy-start.33 = (s32[1,2]{1,0:T(1,128)S(1)}, s32[1,2]{1,0:T(1,128)}, u32[]{:S(2)}) copy-start(s32[1,2]{1,0:T(1,128)} %param.11) | copy-start | bytes 28
  186.6 46.3 %copy-start = (bf16[8,256,512]{2,1,0:T(8,128)(2,1)}, bf16[8,256,512]{2,1,0:T(8,128)(2,1)S(1)}, u32[]{:S(2)}) copy-start(bf16[8,256,512]{2,1,0:T(8,128)(2,1)S(1)} %get-tuple-element.53) | copy-start | bytes 6291460
  186.6 46.3 %collective-permute-start = (bf16[8,256,512]{2,1,0:T(8,128)(2,1)S(1)}, bf16[8,256,512]{2,1,0:T(8,128)(2,1)}, u32[]{:S(2)}, u32[]{:S(2)}) collective-permute-start(bf16[8,256,512]{2,1,0:T(8,128)(2,1)S(1)} %get-tuple-element.53), channel_id=1, source_target_pairs={{0,1},{1,0},{2,3},{3,2},{4,5},{5,4},{6,7},{7,6},{8,9},{9,8},{10,11... | collective-permute-start | bytes 6291464 | tf_op jit(solution)/shard_map/ppermute | solution.py:1301
  190.0 100.4 %collective-permute-start.8 = (bf16[256,2048]{1,0:T(8,128)(2,1)}, bf16[256,2048]{1,0:T(8,128)(2,1)}, u32[]{:S(2)}, u32[]{:S(2)}) collective-permute-start(bf16[256,2048]{1,0:T(8,128)(2,1)} %bitcast.32), channel_id=1, source_target_pairs={{0,8},{8,0},{16,24},{24,16},{1,9},{9,1},{17,25},{25,17},{2,10},{10... | collective-permute-start | bytes 3145736 | tf_op jit(solution)/shard_map/ppermute | solution.py:386
  191.0 82.4 %collective-permute-start.7 = (bf16[256,2048]{1,0:T(8,128)(2,1)}, bf16[256,2048]{1,0:T(8,128)(2,1)}, u32[]{:S(2)}, u32[]{:S(2)}) collective-permute-start(bf16[256,2048]{1,0:T(8,128)(2,1)} %bitcast.32), channel_id=1, source_target_pairs={{0,6},{1,7},{2,0},{3,1},{4,2},{5,3},{6,4},{7,5},{8,14},{9,15},{10,... | collective-permute-start | bytes 3145736 | tf_op jit(solution)/shard_map/ppermute | solution.py:385
  191.0 82.4 %collective-permute-start.6 = (bf16[256,2048]{1,0:T(8,128)(2,1)}, bf16[256,2048]{1,0:T(8,128)(2,1)}, u32[]{:S(2)}, u32[]{:S(2)}) collective-permute-start(bf16[256,2048]{1,0:T(8,128)(2,1)} %bitcast.32), channel_id=1, source_target_pairs={{0,4},{1,5},{2,6},{3,7},{4,0},{5,1},{6,2},{7,3},{8,12},{9,13},{10,... | collective-permute-start | bytes 3145736 | tf_op jit(solution)/shard_map/ppermute | solution.py:385
  193.1 90.0 %collective-permute-start.5 = (bf16[256,2048]{1,0:T(8,128)(2,1)}, bf16[256,2048]{1,0:T(8,128)(2,1)}, u32[]{:S(2)}, u32[]{:S(2)}) collective-permute-start(bf16[256,2048]{1,0:T(8,128)(2,1)} %bitcast.32), channel_id=1, source_target_pairs={{0,2},{1,3},{2,4},{3,5},{4,6},{5,7},{6,0},{7,1},{8,10},{9,11},{10,... | collective-permute-start | bytes 3145736 | tf_op jit(solution)/shard_map/ppermute | solution.py:385
  234.1 20.5 %copy-start.7 = (bf16[8,256,704]{2,1,0:T(8,128)(2,1)S(1)}, bf16[8,256,704]{2,1,0:T(8,128)(2,1)}, u32[]{:S(2)}) copy-start(bf16[8,256,704]{2,1,0:T(8,128)(2,1)} %copy-done.6) | copy-start | bytes 8650756
  269.0 46.5 %collective-permute-start.1 = (bf16[4,256,2048]{2,1,0:T(8,128)(2,1)}, bf16[4,256,2048]{2,1,0:T(8,128)(2,1)}, u32[]{:S(2)}, u32[]{:S(2)}) collective-permute-start(bf16[4,256,2048]{2,1,0:T(8,128)(2,1)} %get-tuple-element.56), channel_id=1, source_target_pairs={{0,8},{8,0},{16,24},{24,16},{1,9},{9,1},{17,25},{25,17},{2,10},{10... | collective-permute-start | bytes 12582920 | tf_op jit(solution)/shard_map/ppermute | solution.py:390
  273.3 24.2 %collective-permute-start.11 = (bf16[256,2048]{1,0:T(8,128)(2,1)}, bf16[256,2048]{1,0:T(8,128)(2,1)S(1)}, u32[]{:S(2)}, u32[]{:S(2)}) collective-permute-start(bf16[256,2048]{1,0:T(8,128)(2,1)} %collective-permute-done.7), channel_id=1, source_target_pairs={{0,8},{8,0},{16,24},{24,16},{1,9},{9,1},{17,25},{25,17},{2,10},{10... | collective-permute-start | bytes 3145736 | tf_op jit(solution)/shard_map/ppermute | solution.py:386
  273.4 23.1 %collective-permute-start.10 = (bf16[256,2048]{1,0:T(8,128)(2,1)}, bf16[256,2048]{1,0:T(8,128)(2,1)S(1)}, u32[]{:S(2)}, u32[]{:S(2)}) collective-permute-start(bf16[256,2048]{1,0:T(8,128)(2,1)} %collective-permute-done.6), channel_id=1, source_target_pairs={{0,8},{8,0},{16,24},{24,16},{1,9},{9,1},{17,25},{25,17},{2,10},{10... | collective-permute-start | bytes 3145736 | tf_op jit(solution)/shard_map/ppermute | solution.py:386
  283.0 11.2 %collective-permute-start.9 = (bf16[256,2048]{1,0:T(8,128)(2,1)}, bf16[256,2048]{1,0:T(8,128)(2,1)}, u32[]{:S(2)}, u32[]{:S(2)}) collective-permute-start(bf16[256,2048]{1,0:T(8,128)(2,1)} %collective-permute-done.5), channel_id=1, source_target_pairs={{0,8},{8,0},{16,24},{24,16},{1,9},{9,1},{17,25},{25,17},{2,10},{10... | collective-permute-start | bytes 3145736 | tf_op jit(solution)/shard_map/ppermute | solution.py:386
  299.4 16.2 %copy-start.24 = (bf16[4,256,2048]{2,1,0:T(8,128)(2,1)S(1)}, bf16[4,256,2048]{2,1,0:T(8,128)(2,1)}, u32[]{:S(2)}) copy-start(bf16[4,256,2048]{2,1,0:T(8,128)(2,1)} %get-tuple-element.55) | copy-start | bytes 12582916
  315.5 8.6 %copy-start.13 = (bf16[8,256,256]{2,1,0:T(8,128)(2,1)S(1)}, bf16[8,256,256]{2,1,0:T(8,128)(2,1)}, u32[]{:S(2)}) copy-start(bf16[8,256,256]{2,1,0:T(8,128)(2,1)} %copy-done.11) | copy-start | bytes 3145732
  320.0 78.8 %collective-permute-start.2 = (bf16[256,2048]{1,0:T(8,128)(2,1)}, bf16[256,2048]{1,0:T(8,128)(2,1)S(1)}, u32[]{:S(2)}, u32[]{:S(2)}) collective-permute-start(bf16[256,2048]{1,0:T(8,128)(2,1)} %get-tuple-element.101), channel_id=1, source_target_pairs={{0,6},{1,7},{2,0},{3,1},{4,2},{5,3},{6,4},{7,5},{8,14},{9,15},{10,... | collective-permute-start | bytes 3145736 | tf_op jit(solution)/shard_map/ppermute | solution.py:398
  322.0 76.8 %collective-permute-start.4 = (bf16[256,2048]{1,0:T(8,128)(2,1)}, bf16[256,2048]{1,0:T(8,128)(2,1)}, u32[]{:S(2)}, u32[]{:S(2)}) collective-permute-start(bf16[256,2048]{1,0:T(8,128)(2,1)} %get-tuple-element.102), channel_id=1, source_target_pairs={{0,2},{1,3},{2,4},{3,5},{4,6},{5,7},{6,0},{7,1},{8,10},{9,11},{10,... | collective-permute-start | bytes 3145736 | tf_op jit(solution)/shard_map/ppermute | solution.py:398
  322.2 90.2 %collective-permute-start.3 = (bf16[256,2048]{1,0:T(8,128)(2,1)}, bf16[256,2048]{1,0:T(8,128)(2,1)}, u32[]{:S(2)}, u32[]{:S(2)}) collective-permute-start(bf16[256,2048]{1,0:T(8,128)(2,1)} %get-tuple-element.103), channel_id=1, source_target_pairs={{0,4},{1,5},{2,6},{3,7},{4,0},{5,1},{6,2},{7,3},{8,12},{9,13},{10,... | collective-permute-start | bytes 3145736 | tf_op jit(solution)/shard_map/ppermute | solution.py:398
  356.2 61.3 %collective-permute-start.12 = (bf16[8,256,256]{2,1,0:T(8,128)(2,1)S(1)}, bf16[8,256,256]{2,1,0:T(8,128)(2,1)S(1)}, u32[]{:S(2)}, u32[]{:S(2)}) collective-permute-start(bf16[8,256,256]{2,1,0:T(8,128)(2,1)S(1)} %bitcast.261), channel_id=1, source_target_pairs={{0,1},{1,0},{2,3},{3,2},{4,5},{5,4},{6,7},{7,6},{8,9},{9,8},{10,11... | collective-permute-start | bytes 3145736 | tf_op jit(solution)/shard_map/ppermute | solution.py:1316
  379.5 38.0 %collective-permute-start.13 = (bf16[8,256,256]{2,1,0:T(8,128)(2,1)S(1)}, bf16[8,256,256]{2,1,0:T(8,128)(2,1)S(1)}, u32[]{:S(2)}, u32[]{:S(2)}) collective-permute-start(bf16[8,256,256]{2,1,0:T(8,128)(2,1)S(1)} %bitcast.260), channel_id=1, source_target_pairs={{0,1},{1,0},{2,3},{3,2},{4,5},{5,4},{6,7},{7,6},{8,9},{9,8},{10,11... | collective-permute-start | bytes 3145736 | tf_op jit(solution)/shard_map/ppermute | solution.py:1317
  379.9 9.5 %copy-start.32 = (bf16[256,2048]{1,0:T(8,128)(2,1)S(1)}, bf16[256,2048]{1,0:T(8,128)(2,1)}, u32[]{:S(2)}) copy-start(bf16[256,2048]{1,0:T(8,128)(2,1)} %copy.89) | copy-start | bytes 3145732
  389.4 7.9 %copy-start.25 = (f32[2,2,176,2048]{3,2,1,0:T(8,128)}, f32[2,2,176,2048]{3,2,1,0:T(8,128)S(1)}, u32[]{:S(2)}) copy-start(f32[2,2,176,2048]{3,2,1,0:T(8,128)S(1)} %fusion.87) | copy-start | bytes 17301508
  397.2 20.3 %copy-start.29 = (f32[2,2,64,2048]{3,2,1,0:T(8,128)}, f32[2,2,64,2048]{3,2,1,0:T(8,128)S(1)}, u32[]{:S(2)}) copy-start(f32[2,2,64,2048]{3,2,1,0:T(8,128)S(1)} %fusion.86) | copy-start | bytes 6291460
  398.8 62.4 %collective-permute-start.32 = (bf16[2,64,2048]{2,1,0:T(8,128)(2,1)S(1)}, bf16[2,64,2048]{2,1,0:T(8,128)(2,1)}, u32[]{:S(2)}, u32[]{:S(2)}) collective-permute-start(bf16[2,64,2048]{2,1,0:T(8,128)(2,1)S(1)} %fusion.39), channel_id=1, source_target_pairs={{0,16},{8,24},{16,0},{24,8},{1,17},{9,25},{17,1},{25,9},{2,18},{10... | collective-permute-start | bytes 1572872 | tf_op jit(solution)/shard_map/ppermute | solution.py:414
  398.9 88.3 %collective-permute-start.34 = (bf16[4,256,768]{2,1,0:T(8,128)(2,1)}, bf16[4,256,768]{2,1,0:T(8,128)(2,1)}, u32[]{:S(2)}, u32[]{:S(2)}) collective-permute-start(bf16[4,256,768]{2,1,0:T(8,128)(2,1)} %weight_grad_send.3), channel_id=1, source_target_pairs={{0,16},{8,24},{16,0},{24,8},{1,17},{9,25},{17,1},{25,9},{2,18},{10... | collective-permute-start | bytes 4718600 | tf_op jit(solution)/shard_map/ppermute | solution.py:414
  412.4 71.6 %collective-permute-start.36 = (bf16[8,128,640]{2,1,0:T(8,128)(2,1)}, bf16[8,128,640]{2,1,0:T(8,128)(2,1)}, u32[]{:S(2)}, u32[]{:S(2)}) collective-permute-start(bf16[8,128,640]{2,1,0:T(8,128)(2,1)} %get-tuple-element.82), channel_id=1, source_target_pairs={{0,1},{1,0},{2,3},{3,2},{4,5},{5,4},{6,7},{7,6},{8,9},{9,8},{10,11... | collective-permute-start | bytes 3932168 | tf_op jit(solution)/shard_map/ppermute | solution.py:414
  461.1 2.7 collective-permute-start.18
  463.9 2.8 collective-permute-start.19
  465.9 11.9 %collective-permute-start.33 = (bf16[64,2048]{1,0:T(8,128)(2,1)S(1)}, bf16[64,2048]{1,0:T(8,128)(2,1)S(1)}, u32[]{:S(2)}, u32[]{:S(2)}) collective-permute-start(bf16[64,2048]{1,0:T(8,128)(2,1)S(1)} %fusion.54), channel_id=1, source_target_pairs={{0,1},{1,0},{2,3},{3,2},{4,5},{5,4},{6,7},{7,6},{8,9},{9,8},{10,11... | collective-permute-start | bytes 786440 | tf_op jit(solution)/shard_map/ppermute | solution.py:414
  466.8 14.3 %copy-start.28 = (bf16[2,176,2048]{2,1,0:T(8,128)(2,1)S(1)}, bf16[2,176,2048]{2,1,0:T(8,128)(2,1)}, u32[]{:S(2)}) copy-start(bf16[2,176,2048]{2,1,0:T(8,128)(2,1)} %fusion.15) | copy-start | bytes 4325380
  466.8 8.7 %collective-permute-start.20 = (f32[4,272]{1,0:T(4,128)S(1)}, f32[4,272]{1,0:T(4,128)S(1)}, u32[]{:S(2)}, u32[]{:S(2)}) collective-permute-start(f32[4,272]{1,0:T(4,128)S(1)} %bitcast.295), channel_id=1, source_target_pairs={{0,1},{1,0},{2,3},{3,2},{4,5},{5,4},{6,7},{7,6},{8,9},{9,8},{10,11... | collective-permute-start | bytes 13064 | tf_op jit(solution)/shard_map/ppermute | solution.py:439
  475.6 5.4 collective-permute-start.21
  475.8 5.3 collective-permute-start.23
  477.8 5.0 collective-permute-start.22
  481.0 31.7 %collective-permute-start.42 = (bf16[2,176,2048]{2,1,0:T(8,128)(2,1)S(1)}, bf16[2,176,2048]{2,1,0:T(8,128)(2,1)S(1)}, u32[]{:S(2)}, u32[]{:S(2)}) collective-permute-start(bf16[2,176,2048]{2,1,0:T(8,128)(2,1)S(1)} %copy-done.28), channel_id=1, source_target_pairs={{0,16},{8,24},{16,0},{24,8},{1,17},{9,25},{17,1},{25,9},{2,18},{10... | collective-permute-start | bytes 4325384 | tf_op jit(solution)/shard_map/ppermute | solution.py:414
  481.1 83.0 %collective-permute-start.14 = (bf16[4,256,2048]{2,1,0:T(8,128)(2,1)}, bf16[4,256,2048]{2,1,0:T(8,128)(2,1)S(1)}, u32[]{:S(2)}, u32[]{:S(2)}) collective-permute-start(bf16[4,256,2048]{2,1,0:T(8,128)(2,1)} %get-tuple-element.71), channel_id=1, source_target_pairs={{0,8},{8,0},{16,24},{24,16},{1,9},{9,1},{17,25},{25,17},{2,10},{10... | collective-permute-start | bytes 12582920 | tf_op jit(solution)/shard_map/ppermute | solution.py:390
  485.5 27.2 %slice-start = ((s8[5767168]{0:T(1024)(128)(4,1)}), s8[4194304]{0:T(1024)(128)(4,1)S(1)}, s32[]{:S(2)}) async-start(s8[5767168]{0:T(1024)(128)(4,1)} %bitcast.282), calls=%async_computation | async-start | bytes 8388608
  485.6 27.1 %slice-start.1 = ((s8[5767168]{0:T(1024)(128)(4,1)}), s8[1572864]{0:T(1024)(128)(4,1)S(1)}, s32[]{:S(2)}) async-start(s8[5767168]{0:T(1024)(128)(4,1)} %bitcast.282), calls=%async_computation.1 | async-start | bytes 3145728
  485.6 41.1 %collective-permute-start.37 = (bf16[2,4,64,640]{3,2,0,1:T(8,128)(2,1)S(1)}, bf16[2,4,64,640]{3,2,0,1:T(8,128)(2,1)S(1)}, u32[]{:S(2)}, u32[]{:S(2)}) collective-permute-start(bf16[2,4,64,640]{3,2,0,1:T(8,128)(2,1)S(1)} %fusion.37), channel_id=1, source_target_pairs={{0,16},{8,24},{16,0},{24,8},{1,17},{9,25},{17,1},{25,9},{2,18},{10... | collective-permute-start | bytes 1966088 | tf_op jit(solution)/shard_map/ppermute | solution.py:414
  489.1 37.8 %collective-permute-start.35 = (bf16[2,4,64,768]{3,2,0,1:T(8,128)(2,1)S(1)}, bf16[2,4,64,768]{3,2,0,1:T(8,128)(2,1)S(1)}, u32[]{:S(2)}, u32[]{:S(2)}) collective-permute-start(bf16[2,4,64,768]{3,2,0,1:T(8,128)(2,1)S(1)} %fusion.24), channel_id=1, source_target_pairs={{0,1},{1,0},{2,3},{3,2},{4,5},{5,4},{6,7},{7,6},{8,9},{9,8},{10,11... | collective-permute-start | bytes 2359304 | tf_op jit(solution)/shard_map/ppermute | solution.py:414
  513.2 15.9 %collective-permute-start.43 = (bf16[176,2048]{1,0:T(8,128)(2,1)S(1)}, bf16[176,2048]{1,0:T(8,128)(2,1)S(1)}, u32[]{:S(2)}, u32[]{:S(2)}) collective-permute-start(bf16[176,2048]{1,0:T(8,128)(2,1)S(1)} %fusion.28), channel_id=1, source_target_pairs={{0,1},{1,0},{2,3},{3,2},{4,5},{5,4},{6,7},{7,6},{8,9},{9,8},{10,11... | collective-permute-start | bytes 2162696 | tf_op jit(solution)/shard_map/ppermute | solution.py:414
  527.2 7.6 %collective-permute-start.38 = (bf16[2,64,1408]{2,1,0:T(8,128)(2,1)S(1)}, bf16[2,64,1408]{2,1,0:T(8,128)(2,1)S(1)}, u32[]{:S(2)}, u32[]{:S(2)}) collective-permute-start(bf16[2,64,1408]{2,1,0:T(8,128)(2,1)S(1)} %get-tuple-element.108), channel_id=1, source_target_pairs={{0,2},{1,3},{2,4},{3,5},{4,6},{5,7},{6,0},{7,1},{8,10},{9,11},{10,... | collective-permute-start | bytes 1081352 | tf_op jit(solution)/shard_map/ppermute | solution.py:423
  530.5 27.2 %collective-permute-start.39 = (bf16[2,64,1408]{2,1,0:T(8,128)(2,1)S(1)}, bf16[2,64,1408]{2,1,0:T(8,128)(2,1)S(1)}, u32[]{:S(2)}, u32[]{:S(2)}) collective-permute-start(bf16[2,64,1408]{2,1,0:T(8,128)(2,1)S(1)} %get-tuple-element.109), channel_id=1, source_target_pairs={{0,4},{1,5},{2,6},{3,7},{4,0},{5,1},{6,2},{7,3},{8,12},{9,13},{10,... | collective-permute-start | bytes 1081352 | tf_op jit(solution)/shard_map/ppermute | solution.py:423
  531.2 30.8 %collective-permute-start.40 = (bf16[2,64,1408]{2,1,0:T(8,128)(2,1)S(1)}, bf16[2,64,1408]{2,1,0:T(8,128)(2,1)S(1)}, u32[]{:S(2)}, u32[]{:S(2)}) collective-permute-start(bf16[2,64,1408]{2,1,0:T(8,128)(2,1)S(1)} %get-tuple-element.110), channel_id=1, source_target_pairs={{0,6},{1,7},{2,0},{3,1},{4,2},{5,3},{6,4},{7,5},{8,14},{9,15},{10,... | collective-permute-start | bytes 1081352 | tf_op jit(solution)/shard_map/ppermute | solution.py:423
  563.6 16.4 %collective-permute-start.41 = (bf16[4,64,1408]{2,1,0:T(8,128)(2,1)}, bf16[4,64,1408]{2,1,0:T(8,128)(2,1)}, u32[]{:S(2)}, u32[]{:S(2)}) collective-permute-start(bf16[4,64,1408]{2,1,0:T(8,128)(2,1)} %fusion.27), channel_id=1, source_target_pairs={{0,8},{8,0},{16,24},{24,16},{1,9},{9,1},{17,25},{25,17},{2,10},{10... | collective-permute-start | bytes 2162696 | tf_op jit(solution)/shard_map/ppermute | solution.py:430
  564.1 3.3 copy-start.23
  564.9 3.6 copy-start.1
  574.8 40.6 %collective-permute-start.24 = (bf16[4,256,384]{2,1,0:T(8,128)(2,1)}, bf16[4,256,384]{2,1,0:T(8,128)(2,1)}, u32[]{:S(2)}, u32[]{:S(2)}) collective-permute-start(bf16[4,256,384]{2,1,0:T(8,128)(2,1)} %weight_grad_send.2), channel_id=1, source_target_pairs={{0,16},{8,24},{16,0},{24,8},{1,17},{9,25},{17,1},{25,9},{2,18},{10... | collective-permute-start | bytes 2359304 | tf_op jit(solution)/shard_map/ppermute | solution.py:414
  583.6 15.7 %copy-start.19 = (f32[1,4,64,2,2,352]{5,4,3,2,1,0:T(2,128)S(1)}, f32[1,4,64,2,2,352]{5,4,3,2,1,0:T(2,128)}, u32[]{:S(2)}) copy-start(f32[1,4,64,2,2,352]{5,4,3,2,1,0:T(2,128)} %stack.147) | copy-start | bytes 4325380
  583.6 15.7 %copy-start.20 = (f32[1,4,64,2,2,352]{5,4,3,2,1,0:T(2,128)S(1)}, f32[1,4,64,2,2,352]{5,4,3,2,1,0:T(2,128)}, u32[]{:S(2)}) copy-start(f32[1,4,64,2,2,352]{5,4,3,2,1,0:T(2,128)} %reshape.499) | copy-start | bytes 4325380
  583.6 36.8 %collective-permute-start.15 = (bf16[256,2048]{1,0:T(8,128)(2,1)}, bf16[256,2048]{1,0:T(8,128)(2,1)}, u32[]{:S(2)}, u32[]{:S(2)}) collective-permute-start(bf16[256,2048]{1,0:T(8,128)(2,1)} %get-tuple-element.98), channel_id=1, source_target_pairs={{0,6},{1,7},{2,0},{3,1},{4,2},{5,3},{6,4},{7,5},{8,14},{9,15},{10,... | collective-permute-start | bytes 3145736 | tf_op jit(solution)/shard_map/ppermute | solution.py:398
  583.6 47.9 %collective-permute-start.17 = (bf16[256,2048]{1,0:T(8,128)(2,1)}, bf16[256,2048]{1,0:T(8,128)(2,1)}, u32[]{:S(2)}, u32[]{:S(2)}) collective-permute-start(bf16[256,2048]{1,0:T(8,128)(2,1)} %get-tuple-element.99), channel_id=1, source_target_pairs={{0,2},{1,3},{2,4},{3,5},{4,6},{5,7},{6,0},{7,1},{8,10},{9,11},{10,... | collective-permute-start | bytes 3145736 | tf_op jit(solution)/shard_map/ppermute | solution.py:398
  585.0 89.7 %collective-permute-start.16 = (bf16[256,2048]{1,0:T(8,128)(2,1)}, bf16[256,2048]{1,0:T(8,128)(2,1)}, u32[]{:S(2)}, u32[]{:S(2)}) collective-permute-start(bf16[256,2048]{1,0:T(8,128)(2,1)} %get-tuple-element.100), channel_id=1, source_target_pairs={{0,4},{1,5},{2,6},{3,7},{4,0},{5,1},{6,2},{7,3},{8,12},{9,13},{10,... | collective-permute-start | bytes 3145736 | tf_op jit(solution)/shard_map/ppermute | solution.py:398
  598.5 19.2 %collective-permute-start.26 = (bf16[8,128,384]{2,1,0:T(8,128)(2,1)}, bf16[8,128,384]{2,1,0:T(8,128)(2,1)}, u32[]{:S(2)}, u32[]{:S(2)}) collective-permute-start(bf16[8,128,384]{2,1,0:T(8,128)(2,1)} %get-tuple-element.79), channel_id=1, source_target_pairs={{0,1},{1,0},{2,3},{3,2},{4,5},{5,4},{6,7},{7,6},{8,9},{9,8},{10,11... | collective-permute-start | bytes 2359304 | tf_op jit(solution)/shard_map/ppermute | solution.py:414
  616.9 61.8 %collective-permute-start.25 = (bf16[2,4,64,384]{3,2,0,1:T(8,128)(2,1)S(1)}, bf16[2,4,64,384]{3,2,0,1:T(8,128)(2,1)S(1)}, u32[]{:S(2)}, u32[]{:S(2)}) collective-permute-start(bf16[2,4,64,384]{3,2,0,1:T(8,128)(2,1)S(1)} %fusion.41), channel_id=1, source_target_pairs={{0,1},{1,0},{2,3},{3,2},{4,5},{5,4},{6,7},{7,6},{8,9},{9,8},{10,11... | collective-permute-start | bytes 1179656 | tf_op jit(solution)/shard_map/ppermute | solution.py:414
  619.0 59.0 %copy-start.17 = (bf16[1,128,2,2048]{3,2,1,0:T(2,128)(2,1)S(1)}, bf16[1,128,2,2048]{3,2,1,0:T(2,128)(2,1)}, u32[]{:S(2)}) copy-start(bf16[1,128,2,2048]{3,2,1,0:T(2,128)(2,1)} %param.10) | copy-start | bytes 3145732
  619.1 59.8 %collective-permute-start.27 = (bf16[2,4,64,384]{3,2,0,1:T(8,128)(2,1)S(1)}, bf16[2,4,64,384]{3,2,0,1:T(8,128)(2,1)S(1)}, u32[]{:S(2)}, u32[]{:S(2)}) collective-permute-start(bf16[2,4,64,384]{3,2,0,1:T(8,128)(2,1)S(1)} %fusion.42), channel_id=1, source_target_pairs={{0,16},{8,24},{16,0},{24,8},{1,17},{9,25},{17,1},{25,9},{2,18},{10... | collective-permute-start | bytes 1179656 | tf_op jit(solution)/shard_map/ppermute | solution.py:414
  679.0 5.9 collective-permute-start.28
  679.1 16.3 %collective-permute-start.29 = (bf16[2,64,768]{2,1,0:T(8,128)(2,1)S(1)}, bf16[2,64,768]{2,1,0:T(8,128)(2,1)S(1)}, u32[]{:S(2)}, u32[]{:S(2)}) collective-permute-start(bf16[2,64,768]{2,1,0:T(8,128)(2,1)S(1)} %get-tuple-element.116), channel_id=1, source_target_pairs={{0,4},{1,5},{2,6},{3,7},{4,0},{5,1},{6,2},{7,3},{8,12},{9,13},{10,... | collective-permute-start | bytes 589832 | tf_op jit(solution)/shard_map/ppermute | solution.py:423
  683.1 16.6 %collective-permute-start.30 = (bf16[2,64,768]{2,1,0:T(8,128)(2,1)S(1)}, bf16[2,64,768]{2,1,0:T(8,128)(2,1)S(1)}, u32[]{:S(2)}, u32[]{:S(2)}) collective-permute-start(bf16[2,64,768]{2,1,0:T(8,128)(2,1)S(1)} %get-tuple-element.117), channel_id=1, source_target_pairs={{0,6},{1,7},{2,0},{3,1},{4,2},{5,3},{6,4},{7,5},{8,14},{9,15},{10,... | collective-permute-start | bytes 589832 | tf_op jit(solution)/shard_map/ppermute | solution.py:423
  700.2 7.8 %collective-permute-start.31 = (bf16[4,64,768]{2,1,0:T(8,128)(2,1)S(1)}, bf16[4,64,768]{2,1,0:T(8,128)(2,1)S(1)}, u32[]{:S(2)}, u32[]{:S(2)}) collective-permute-start(bf16[4,64,768]{2,1,0:T(8,128)(2,1)S(1)} %fusion.40), channel_id=1, source_target_pairs={{0,8},{8,0},{16,24},{24,16},{1,9},{9,1},{17,25},{25,17},{2,10},{10... | collective-permute-start | bytes 1179656 | tf_op jit(solution)/shard_map/ppermute | solution.py:430
  (16 other events, 30.5 us)

commit v3 on v2

--- a/solution.py
+++ b/solution.py
@@ -406,41 +406,6 @@
 
 def one_of(value, index, axis):
     return lax.dynamic_index_in_dim(value, index, axis, False)
-
-
-def summed(keep, send, over_x):
-    send = send.astype(jnp.bfloat16)
-    got = (
-        lax.ppermute(send, "bucket", ACROSS_X) if over_x else lax.ppermute(send, "blk", ACROSS_Y)
-    )
-    return keep + got.astype(jnp.float32)
-
-
-def rows_of_device(value, core, z):
-    parts = [one_of(value, z, 0)]
-    for step in range(1, DEPTH):
-        chunk = one_of(value, (z + step) % DEPTH, 0).astype(jnp.bfloat16)
-        parts.append(lax.ppermute(chunk, "blk", around(step)).astype(jnp.float32))
-    stacked = jnp.stack(parts)
-    ordered = jnp.concatenate(
-        [lax.dynamic_slice_in_dim(stacked, (z - j) % DEPTH, 1, 0) for j in range(DEPTH)]
-    )
-    mine = one_of(ordered, core, 1)
-    theirs = one_of(ordered, 1 - core, 1).astype(jnp.bfloat16)
-    got = lax.ppermute(theirs, "bucket", CORE).astype(jnp.float32)
-    return in_order(mine, got, core, 0)
-
-
-def vector_sums(terms, x, y, core, z):
-    for index, axis, name, pairs in ((x, 0, "bucket", ACROSS_X), (core, 0, "bucket", CORE)):
-        keep, send = one_of(terms, index, axis), one_of(terms, 1 - index, axis)
-        terms = keep + lax.ppermute(send, name, pairs)
-    keep, send = one_of(terms, y, 1), one_of(terms, 1 - y, 1)
-    terms = keep + lax.ppermute(send, "blk", ACROSS_Y)
-    total = one_of(terms, z, 0)
-    for step in range(1, DEPTH):
-        total = total + lax.ppermute(one_of(terms, (z + step) % DEPTH, 0), "blk", around(step))
-    return total
 
 
 def dot_rows(left, right):
@@ -1077,93 +1042,592 @@
     return [v.reshape(PIECES, ROWS, HEAD_COLS) for v in outs]
 
 
-def input_grad_kernel(
+def finish_kernel(
     dq_ref,
     dk_ref,
     dv_ref,
     odk_ref,
     odv_ref,
     gu_ref,
-    x_ref,
-    wi_ref,
-    wg_ref,
+    pieces_ref,
     cos_ref,
     first_ref,
     second_ref,
+    normed_ref,
+    gate_xs,
+    gate_xk,
+    gate_ys,
+    gate_yk,
+    heads_term,
+    hidden_term,
+    wi_ref,
+    wg_ref,
+    gain_ref,
+    cot_ref,
+    tokens_out,
+    heads_out,
+    hidden_out,
+    gate_rows,
+    inward_rows_out,
+    vec_out,
+    inward_xs,
+    inward_xk,
+    inward_ys,
+    inward_yk,
+    gate_xr,
+    gate_yr,
+    gate_y2s,
+    gate_y2r,
+    gate_x2s,
+    gate_x2r,
+    gate_fin,
+    inward_xr,
+    inward_yr,
+    inward_y2s,
+    inward_y2r,
+    inward_x2s,
+    inward_x2r,
+    inward_fin,
+    heads_r,
+    heads_2s,
+    heads_2r,
+    hidden_r,
+    hidden_2s,
+    hidden_2r,
+    core_send,
+    core_recv,
+    z_send,
+    z_recv,
+    own_sum,
     pg_ref,
-    own_ref,
-    other_ref,
-    gain_ref,
-    shift_ref,
-    bias_ref,
+    token_rows,
+    vec_sum,
+    vec_x,
+    vec_y,
+    core_s,
+    core_r,
+    z_s,
+    z_r,
+    stage_s,
+    stage_r,
+    rows_s,
+    rows_r,
+    vec_s,
+    vec_r,
+    local_sems,
 ):
-    tables = (cos_ref, first_ref, second_ref)
-    query = turned(dq_ref[0] * (HEAD_DIM**-0.5), *tables, -1.0)
-    key = turned(dk_ref[0] + odk_ref[0].astype(jnp.float32), *tables, -1.0)
-    value = dv_ref[0] + odv_ref[0].astype(jnp.float32)
-    low = jnp.concatenate([query, key, value], 1).astype(jnp.bfloat16)
-    pg_ref[0] = low
-    grad = transposed_times(low, inward_rows(wi_ref))
-    grad += transposed_times(gu_ref[0], wg_ref[...])
-    store_split(grad.astype(jnp.bfloat16), own_ref, other_ref)
-    hat, _ = normalised(x_ref[0])
-
-    @pl.when(pl.program_id(0) == 0)
-    def _():
-        gain_ref[...] = jnp.zeros_like(gain_ref)
-        shift_ref[...] = jnp.zeros_like(shift_ref)
-        bias_ref[...] = jnp.zeros_like(bias_ref)
-
-    gain_ref[...] += jnp.sum(grad * hat, axis=0, keepdims=True)
-    shift_ref[...] += jnp.sum(grad, axis=0, keepdims=True)
-    bias_ref[...] += jnp.sum(low.astype(jnp.float32), axis=0, keepdims=True)
-
-
-def input_grads(parts, other_key, other_value, gate_up_grad, pieces, weights, tables):
+    bucket, blk = lax.axis_index("bucket"), lax.axis_index("blk")
+    x, core = bucket // 2, bucket % 2
+    z, y = blk // 2, blk % 2
+    low = jnp.bfloat16
+    wide = jnp.float32
+
+    def device(xx, cc, zz, yy):
+        return (xx * 2 + cc, zz * 2 + yy)
+
+    x_mate, y_mate = device(1 - x, core, z, y), device(x, core, z, 1 - y)
+    core_mate = device(x, 1 - core, z, y)
+    members = [(flip, turn) for turn in (2, 1, 3, 0) for flip in (1, 0)][:-1]
+
+    def target(flip, turn):
+        return (core + flip) % 2, (z + turn) % DEPTH
+
+    barrier = pltpu.get_barrier_semaphore()
+    greeted = [device(x, *target(*m), y) for m in members] + [x_mate, y_mate]
+    for mate in greeted:
+        pl.semaphore_signal(
+            barrier, inc=1, device_id=mate, device_id_type=pl.DeviceIdType.MESH
+        )
+    pl.semaphore_wait(barrier, len(greeted))
+
+    started = []
+
+    def begin(copy):
+        copy.start()
+        started.append(copy)
+        return copy
+
+    gate_x = begin(remote(gate_xs, gate_xr, stage_s, stage_r, (0, 0), x_mate))
+    gate_y = begin(remote(gate_ys, gate_yr, stage_s, stage_r, (0, 1), y_mate))
+    heads_x = begin(remote(heads_term.at[1 - x], heads_r, stage_s, stage_r, (2, 0), x_mate))
+    hidden_y = [
+        begin(
+            remote(hidden_term.at[i, 1 - y], hidden_r.at[i], stage_s, stage_r, (3, i), y_mate)
+        )
+        for i in range(2)
+    ]
+    own_tokens = pltpu.make_async_copy(pieces_ref.at[0], token_rows, local_sems.at[0])
+    own_tokens.start()
+
+    vec_sum[...] = jnp.zeros_like(vec_sum)
+
+    def core_copy(k):
+        return remote(core_send.at[k], core_recv.at[k], core_s, core_r, k, core_mate)
+
+    def z_copy(k):
+        goal = device(x, core, (z + DEPTH - k) % DEPTH, y)
+        return remote(z_send.at[k - 1], z_recv.at[k - 1], z_s, z_r, k - 1, goal)
+
+    def piece_of(i):
+        k = DEPTH - 1 - i // 2
+        return k + DEPTH * (1 - i % 2)
+
+    def piece_body(
+        dq, dk, dv, odk, odv, gu, tokens, cos, first, second
+    ):
+        step = pl.program_id(0)
+        k = DEPTH - 1 - step // 2
+        piece = piece_of(step)
+        tables = (cos, first, second)
+        query = turned(dq[0] * (HEAD_DIM**-0.5), *tables, -1.0)
+        key = turned(dk[0] + odk[0].astype(wide), *tables, -1.0)
+        value = dv[0] + odv[0].astype(wide)
+        narrow = jnp.concatenate([query, key, value], 1).astype(low)
+        pg_ref[piece] = narrow
+        grad = transposed_times(narrow, inward_rows(wi_ref))
+        grad += transposed_times(gu[0], wg_ref[...])
+        hat, _ = normalised(tokens[0])
+        half = grad.shape[1] // 2
+        for row, total in (
+            (0, jnp.sum(grad * hat, axis=0, keepdims=True)),
+            (2, jnp.sum(grad, axis=0, keepdims=True)),
+        ):
+            vec_sum[row : row + 1] += total[:, :half]
+            vec_sum[row + 1 : row + 2] += total[:, half:]
+        vec_sum[4:5, : 3 * HEAD_COLS] += jnp.sum(narrow.astype(wide), axis=0, keepdims=True)
+
+        @pl.when(step % 2 == 0)
+        def _():
+            core_send[k] = grad.astype(low)
+            core_copy(k).start()
+
+        @pl.when(step % 2 == 1)
+        def _():
+            core_copy(k).wait_recv()
+            both = grad + core_recv[k].astype(wide)
+
+            @pl.when(k > 0)
+            def _():
+                z_send[k - 1] = both.astype(low)
+                z_copy(k).start()
+
+            @pl.when(k == 0)
+            def _():
+                own_sum[...] = both
+
+    def by_piece(width):
+        return pl.BlockSpec((1, ROWS, width), lambda i: (piece_of(i), 0, 0))
+
+    table_spec = pl.BlockSpec(
+        (1,) + cos_ref.shape[1:], lambda i: (piece_of(i) % DEPTH, 0, 0)
+    )
+    pltpu.emit_pipeline(
+        piece_body,
+        grid=(PIECES,),
+        in_specs=[by_piece(HEAD_COLS)] * 5
+        + [by_piece(gu_ref.shape[-1]), by_piece(pieces_ref.shape[-1])]
+        + [table_spec] * 3,
+    )(
+        dq_ref,
+        dk_ref,
+        dv_ref,
+        odk_ref,
+        odv_ref,
+        gu_ref,
+        pieces_ref,
+        cos_ref,
+        first_ref,
+        second_ref,
+    )
+    vector_x = remote(vec_sum, vec_x, vec_s, vec_r, 0, x_mate)
+    vector_x.start()
+
+    total, width = normed_ref.shape
+    size = width // PIECES
+    cut = 3 * HEAD_COLS // 2
+
+    def projected(first, last):
+        return pg_ref[...].reshape(total, 3 * HEAD_COLS)[:, first:last]
+
+    def send_body(left, out):
+        out[0] = times_transposed(left[...], projected(0, cut)).astype(low)
+
+    def keep_body(left, out):
+        out[0] = times_transposed(left[...], projected(0, cut))
+
+    def split_body(left, keep, send):
+        term = times_transposed(left[...], projected(cut, 2 * cut))
+        split_rows(term, y, keep, send)
+
+    def from_block(base):
+        return pl.BlockSpec((total, size), lambda i: (0, base + i))
+
+    def block_of(array):
+        return pl.BlockSpec((1,) + array.shape[1:], lambda i: (i, 0, 0))
+
+    pltpu.emit_pipeline(
+        send_body,
+        grid=(DEPTH,),
+        in_specs=[from_block((1 - x) * DEPTH)],
+        out_specs=[block_of(inward_xs)],
+    )(normed_ref, inward_xs)
+    inward_x = begin(remote(inward_xs, inward_xr, stage_s, stage_r, (1, 0), x_mate))
+    pltpu.emit_pipeline(
+        split_body,
+        grid=(PIECES,),
+        in_specs=[from_block(0)],
+        out_specs=[block_of(inward_yk), block_of(inward_ys)],
+    )(normed_ref, inward_yk, inward_ys)
+    inward_y = begin(remote(inward_ys, inward_yr, stage_s, stage_r, (1, 1), y_mate))
+
+    vector_x.wait_recv()
+    vec_sum_x = vec_sum[...] + vec_x[...]
+    vector_x.wait_send()
+    vec_sum[...] = vec_sum_x
+    vector_y = remote(vec_sum, vec_y, vec_s, vec_r, 1, y_mate)
+    vector_y.start()
+
+    def add_two(one, two, out):
+        out[...] = (one[...].astype(wide) + two[...].astype(wide)).astype(out.dtype)
+
+    def second_stage(which, xk, xr, yk, yr, y2s, y2r, x2s, x2r, first_x, first_y):
+        quarter = xk.shape[1] // 4
+        rows_at = pl.BlockSpec(
+            (1, quarter, xk.shape[2]), lambda i: (i // 2, (i % 2) * 2 + (1 - y), 0)
+        )
+        first_x.wait_recv()
+        pltpu.emit_pipeline(
+            add_two, grid=(PIECES,), in_specs=[rows_at, rows_at], out_specs=[block_of(y2s)]
+        )(xk, xr, y2s)
+        over_y = begin(remote(y2s, y2r, stage_s, stage_r, (which, 2), y_mate))
+        part = pl.BlockSpec((1,) + yk.shape[1:], lambda i: ((1 - x) * DEPTH + i, 0, 0))
+        first_y.wait_recv()
+        pltpu.emit_pipeline(
+            add_two, grid=(DEPTH,), in_specs=[part, part], out_specs=[block_of(x2s)]
+        )(yk, yr, x2s)
+        over_x = begin(remote(x2s, x2r, stage_s, stage_r, (which, 3), x_mate))
+        return over_y, over_x
+
+    def last_stage(which, xk, xr, yk, yr, y2r, x2r, fin, rows, over_y, over_x):
+        quarter = xk.shape[1] // 4
+        cut = xk.shape[2]
+        rows_at = pl.BlockSpec((1, quarter, cut), lambda i: (i // 2, (i % 2) * 2 + y, 0))
+        part = pl.BlockSpec(
+            (1, quarter, yk.shape[2]), lambda i: (x * DEPTH + i // 2, i % 2, 0)
+        )
+        last = pl.BlockSpec((1, quarter, yk.shape[2]), lambda i: (i // 2, i % 2, 0))
+
+        def body(one, two, three, four, five, six, out):
+            left = one[0] + two[0].astype(wide) + three[0].astype(wide)
+            right = four[0] + five[0].astype(wide) + six[0].astype(wide)
+            out[0] = jnp.concatenate([left, right], 1).astype(low)
+
+        over_y.wait_recv()
+        over_x.wait_recv()
+        pltpu.emit_pipeline(
+            body,
+            grid=(PIECES,),
+            in_specs=[rows_at, rows_at, block_of(y2r), part, part, last],
+            out_specs=[block_of(fin)],
+        )(xk, xr, y2r, yk, yr, x2r, fin)
+        slot = core * DEPTH + z
+        copies = []
+        for flip, turn in members:
+            cc, zz = target(flip, turn)
+            copies.append(
+                begin(
+                    remote(
+                        fin.at[cc * DEPTH + zz],
+                        rows.at[slot],
+                        rows_s,
+                        rows_r,
+                        (which, flip * DEPTH + turn),
+                        device(x, cc, zz, y),
+                    )
+                )
+            )
+        own = pltpu.make_async_copy(fin.at[slot], rows.at[slot], local_sems.at[1 + which])
+        own.start()
+        return copies, own
+
+    gate_second = second_stage(
+        0,
+        gate_xk,
+        gate_xr,
+        gate_yk,
+        gate_yr,
+        gate_y2s,
+        gate_y2r,
+        gate_x2s,
+        gate_x2r,
+        gate_x,
+        gate_y,
+    )
+
+    chunk = heads_term.shape[-1] // DEPTH
+
+    def flat_spec(rows):
+        return pl.BlockSpec((rows, chunk), lambda i: (0, i))
+
+    def row_sum(one, two, out):
+        spec = flat_spec(one.shape[0])
+        pltpu.emit_pipeline(
+            add_two, grid=(DEPTH,), in_specs=[spec, spec], out_specs=[spec]
+        )(one, two, out)
+
+    def row_total(one, two, three, out):
+        spec = flat_spec(one.shape[0])
+
+        def body(one, two, three, out):
+            out[...] = one[...].astype(wide) + two[...].astype(wide) + three[...].astype(wide)
+
+        pltpu.emit_pipeline(
+            body, grid=(DEPTH,), in_specs=[spec] * 3, out_specs=[spec]
+        )(one, two, three, out)
+
+    heads_x.wait_recv()
+    row_sum(heads_term.at[x, 1 - y], heads_r.at[1 - y], heads_2s)
+    heads_y = begin(remote(heads_2s, heads_2r, stage_s, stage_r, (2, 2), y_mate))
+    for copy in hidden_y:
+        copy.wait_recv()
+    row_sum(hidden_term.at[1 - x, y], hidden_r.at[1 - x], hidden_2s)
+    hidden_x = begin(remote(hidden_2s, hidden_2r, stage_s, stage_r, (3, 2), x_mate))
+
+    pltpu.emit_pipeline(
+        keep_body,
+        grid=(DEPTH,),
+        in_specs=[from_block(x * DEPTH)],
+        out_specs=[block_of(inward_xk)],
+    )(normed_ref, inward_xk)
+
+    vector_y.wait_recv()
+    vec_sum_y = vec_sum[...] + vec_y[...]
+    vector_y.wait_send()
+    slot = core * DEPTH + z
+    vec_out[slot] = vec_sum_y
+    vectors = []
+    for flip, turn in members:
+        cc, zz = target(flip, turn)
+        vectors.append(
+            begin(
+                remote(
+                    vec_out.at[slot],
+                    vec_out.at[slot],
+                    rows_s,
+                    rows_r,
+                    (2, flip * DEPTH + turn),
+                    device(x, cc, zz, y),
+                )
+            )
+        )
+
+    gate_rest = last_stage(
+        0,
+        gate_xk,
+        gate_xr,
+        gate_yk,
+        gate_yr,
+        gate_y2r,
+        gate_x2r,
+        gate_fin,
+        gate_rows,
+        *gate_second,
+    )
+    inward_second = second_stage(
+        1,
+        inward_xk,
+        inward_xr,
+        inward_yk,
+        inward_yr,
+        inward_y2s,
+        inward_y2r,
+        inward_x2s,
+        inward_x2r,
+        inward_x,
+        inward_y,
+    )
+    heads_y.wait_recv()
+    row_total(heads_term.at[x, y], heads_r.at[y], heads_2r, heads_out)
+    hidden_x.wait_recv()
+    row_total(hidden_term.at[x, y], hidden_r.at[x], hidden_2r, hidden_out)
+    inward_rest = last_stage(
+        1,
+        inward_xk,
+        inward_xr,
+        inward_yk,
+        inward_yr,
+        inward_y2r,
+        inward_x2r,
+        inward_fin,
+        inward_rows_out,
+        *inward_second,
+    )
+
+    own_tokens.wait()
+    for k in range(1, DEPTH):
+        z_copy(k).wait_recv()
+    for first in range(0, ROWS, 64):
+        rows = pl.ds(first, 64)
+        grad = own_sum[rows]
+        for k in range(DEPTH - 1):
+            grad = grad + z_recv[k, rows].astype(wide)
+        hat, inverse = normalised(token_rows[rows])
+        scaled = grad * gain_ref[...]
+        input_grad = inverse * (
+            scaled
+            - jnp.mean(scaled, axis=-1, keepdims=True)
+            - hat * jnp.mean(scaled * hat, axis=-1, keepdims=True)
+        )
+        tokens_out[rows] = (cot_ref[rows].astype(wide) + input_grad).astype(low)
+
+    for copies, own in (gate_rest, inward_rest):
+        own.wait()
+        for copy in copies:
+            copy.wait_recv()
+    for copy in vectors:
+        copy.wait_recv()
+    for copy in started:
+        copy.wait_send()
+    for k in range(DEPTH):
+        core_copy(k).wait_send()
+        if k > 0:
+            z_copy(k).wait_send()
+
+
+def finish(
+    parts, got_dk, got_dv, gate_up_grad, pieces, tables, normed, gate_up, heads, hidden, weights,
+    gain, cot
+):
+    low, wide = jnp.bfloat16, jnp.float32
     width = pieces.shape[-1]
-    hidden = gate_up_grad.shape[-1]
-    table_spec = pl.BlockSpec((1,) + tables[0].shape[1:], lambda i: (i % DEPTH, 0, 0))
-    return pl.pallas_call(
-        input_grad_kernel,
-        grid=(PIECES,),
-        in_specs=[other_first(HEAD_COLS)] * 5
-        + [other_first(hidden)]
-        + [other_first(width)]
-        + [whole_spec(w.shape) for w in weights]
-        + [table_spec] * 3,
-        out_specs=[other_first(3 * HEAD_COLS)]
-        + split_specs(width)
-        + [
-            whole_spec((1, width)),
-            whole_spec((1, width)),
-            whole_spec((1, 3 * HEAD_COLS)),
+    gate_xs, gate_xk, gate_ys, gate_yk = gate_up
+    rows = width // 32
+    anywhere = pl.BlockSpec(memory_space=pl.ANY)
+    inside = pl.BlockSpec(memory_space=pltpu.VMEM)
+    shape = jax.ShapeDtypeStruct
+    half = 3 * HEAD_COLS // 2
+
+    def staged(a, b):
+        return [
+            shape((DEPTH, 4 * rows, a), low),
+            shape((PIECES, 2 * rows, b), low),
+            shape((PIECES, rows, a), low),
+            shape((PIECES, rows, a), low),
+            shape((DEPTH, 2 * rows, b), low),
+            shape((DEPTH, 2 * rows, b), low),
+            shape((PIECES, rows, a + b), low),
+        ]
+
+    a, b = gate_xs.shape[-1], gate_ys.shape[-1]
+    heads_rows, hidden_rows = heads.shape[2], hidden.shape[2]
+    out_shapes = [
+        shape((ROWS, width), low),
+        shape((heads_rows, width), wide),
+        shape((hidden_rows, width), wide),
+        shape((PIECES, rows, a + b), low),
+        shape((PIECES, rows, 2 * half), low),
+        shape((PIECES, 8, width // 2), wide),
+        shape((DEPTH, 4 * rows, half), low),
+        shape((DEPTH, 4 * rows, half), wide),
+        shape((PIECES, 2 * rows, half), low),
+        shape((PIECES, 2 * rows, half), wide),
+    ]
+    out_shapes += staged(a, b) + staged(half, half)
+    out_shapes += [
+        shape((2, heads_rows, width), low),
+        shape((heads_rows, width), low),
+        shape((heads_rows, width), low),
+        shape((2, hidden_rows, width), low),
+        shape((hidden_rows, width), low),
+        shape((hidden_rows, width), low),
+    ]
+    out_specs = [inside] + [anywhere] * 4 + [inside] + [anywhere] * (len(out_shapes) - 6)
+    dma = pltpu.SemaphoreType.DMA
+    outs = pl.pallas_call(
+        finish_kernel,
+        in_specs=[anywhere] * 17 + [inside] * 4,
+        out_specs=out_specs,
+        out_shape=out_shapes,
+        scratch_shapes=[
+            pltpu.VMEM((DEPTH, ROWS, width), low),
+            pltpu.VMEM((DEPTH, ROWS, width), low),
+            pltpu.VMEM((DEPTH - 1, ROWS, width), low),
+            pltpu.VMEM((DEPTH - 1, ROWS, width), low),
+            pltpu.VMEM((ROWS, width), wide),
+            pltpu.VMEM((PIECES, ROWS, 3 * HEAD_COLS), low),
+            pltpu.VMEM((ROWS, width), low),
+            pltpu.VMEM((8, width // 2), wide),
+            pltpu.VMEM((8, width // 2), wide),
+            pltpu.VMEM((8, width // 2), wide),
+            dma((DEPTH,)),
+            dma((DEPTH,)),
+            dma((DEPTH - 1,)),
+            dma((DEPTH - 1,)),
+            dma((4, 4)),
+            dma((4, 4)),
+            dma((3, PIECES)),
+            dma((3, PIECES)),
+            dma((2,)),
+            dma((2,)),
+            dma((3,)),
         ],
-        out_shape=[jax.ShapeDtypeStruct((PIECES, ROWS, 3 * HEAD_COLS), jnp.bfloat16)]
-        + [jax.ShapeDtypeStruct((DEPTH, ROWS, width), jnp.bfloat16)] * 2
-        + [
-            jax.ShapeDtypeStruct((1, width), jnp.float32),
-            jax.ShapeDtypeStruct((1, width), jnp.float32),
-            jax.ShapeDtypeStruct((1, 3 * HEAD_COLS), jnp.float32),
-        ],
-        compiler_params=params(56),
-        cost_estimate=cost(2 * PIECES * ROWS * width * (3 * HEAD_COLS + hidden), 48 * MIB),
-        name="input_grads",
-    )(*parts, other_key, other_value, gate_up_grad, pieces, *weights, *tables)
-
-
-def rows_kernel(first, last, place_ref, left_ref, right_ref, out_ref):
-    term = times_transposed(left_ref[...], right_ref[:, first:last])
-    out_ref[0] = term.astype(out_ref.dtype)
-
-
-def split_rows_kernel(first, last, place_ref, left_ref, right_ref, keep_ref, send_ref):
-    y = place_ref[1]
-    term = times_transposed(left_ref[...], right_ref[:, first:last])
+        compiler_params=params(60, collective_id=1, has_side_effects=True),
+        cost_estimate=cost(0, 64 * MIB),
+        name="finish",
+    )(
+        *parts,
+        got_dk,
+        got_dv,
+        gate_up_grad,
+        pieces,
+        *tables,
+        normed,
+        *gate_up,
+        heads,
+        hidden,
+        *weights,
+        gain,
+        cot,
+    )
+    return outs[:6]
+
+
+def split_rows(term, y, keep_ref, send_ref):
     rows = term.shape[0] // 4
     even = jnp.concatenate([term[:rows], term[2 * rows : 3 * rows]], 0)
     odd = jnp.concatenate([term[rows : 2 * rows], term[3 * rows :]], 0)
     keep_ref[0] = jnp.where(y == 0, even, odd)
     send_ref[0] = jnp.where(y == 0, odd, even).astype(jnp.bfloat16)
+
+
+def place_kernel(parts, in_ref, out_ref):
+    each = in_ref.shape[2] // parts
+    for part in range(parts):
+        columns = slice(part * each, (part + 1) * each)
+        line = jnp.concatenate([in_ref[n, :, columns] for n in range(PIECES)], 1)
+        out_ref[:, part * PIECES * each : (part + 1) * PIECES * each] = line.astype(jnp.float32)
+
+
+def place_rows(value, parts):
+    rows, columns = value.shape[1], value.shape[2]
+    return pl.pallas_call(
+        functools.partial(place_kernel, parts),
+        out_shape=jax.ShapeDtypeStruct((rows, PIECES * columns), jnp.float32),
+        compiler_params=params(32),
+        cost_estimate=cost(0, 4 * MIB),
+        name="place_rows",
+    )(value)
+
+
+def rows_kernel(first, last, place_ref, left_ref, right_ref, out_ref):
+    term = times_transposed(left_ref[...], right_ref[:, first:last])
+    out_ref[0] = term.astype(out_ref.dtype)
+
+
+def split_rows_kernel(first, last, place_ref, left_ref, right_ref, keep_ref, send_ref):
+    y = place_ref[1]
+    term = times_transposed(left_ref[...], right_ref[:, first:last])
+    split_rows(term, y, keep_ref, send_ref)
 
 
 def weight_grad(place, left, right, first, last, part):
@@ -1303,6 +1767,7 @@
     attended = attend(place, after(queries, hidden), pairs, other_pairs, seqs)
     branch_own, branch_other = branch_terms(attended, hidden, rows_out)
     branch_sums = core_sums(branch_own, branch_other)
+    branch_sums = list(lax.optimization_barrier((*branch_sums, grads)))[:DEPTH]
     branch = scatter_pieces(branch_sums)
     branch = branch.reshape(seqs, group_len, width)
     inputs = own_tokens.astype(jnp.float32)
@@ -1319,88 +1784,53 @@
     flat_normed = after(normed, other_dk).reshape(total, width)
     flat_grads = after(grads, other_dk).reshape(total, width)
 
-    def row_sums(right):
-        rows, columns = own_rows, right.shape[-1]
-        right = right.reshape(total, columns)
-        cut = -(-columns // 256) * 128
-        send = weight_grad(place, flat_normed, right, 0, cut, "send")
-        y_keep, y_send = weight_grad(place, flat_normed, right, cut, columns, "split")
-        keep = weight_grad(place, flat_normed, right, 0, cut, "keep")
-        first = summed(keep, send, True).reshape(2, DEPTH, 2, rows, -1)
-        first = summed(one_of(first, y, 2), one_of(first, 1 - y, 2), False)
-        second = summed(y_keep, y_send, False).reshape(2, 2, DEPTH, rows, -1)
-        second = summed(one_of(second, x, 0), one_of(second, 1 - x, 0), True)
-        return jnp.transpose(jnp.concatenate([first, second], -1), (1, 0, 2, 3))
-
-    def device_rows(term, parts):
-        term = rows_of_device(term, core, z).reshape(2, DEPTH, own_rows, parts, 2, -1)
-        return jnp.transpose(term, (2, 3, 4, 0, 1, 5)).reshape(own_rows, -1)
-
-    gate_up_term = row_sums(gate_up_grad)
-    outward_term = times_transposed(attended.reshape(total, -1), flat_grads)
-    down_term = times_transposed(hidden.reshape(total, -1), flat_grads)
-
-    def owner_sums(term):
-        term = term.reshape(2, 2, -1, width)
-        term = summed(one_of(term, x, 0), one_of(term, 1 - x, 0), True)
-        return summed(one_of(term, y, 0), one_of(term, 1 - y, 0), False)
-
-    outward_sum = owner_sums(outward_term)
-    down_sum = owner_sums(down_term)
-    projected_grad, normed_own, normed_other, gain_term, shift_term, bias_term = input_grads(
-        (after(dq, branch), dk, dv),
+    right = gate_up_grad.reshape(total, -1)
+    columns = right.shape[1]
+    cut = -(-columns // 256) * 128
+    gate_up_send = weight_grad(place, flat_normed, right, 0, cut, "send")
+    gate_up_kept, gate_up_sent = weight_grad(place, flat_normed, right, cut, columns, "split")
+    gate_up_keep = weight_grad(place, flat_normed, right, 0, cut, "keep")
+    heads_term = times_transposed(attended.reshape(total, -1), flat_grads).astype(jnp.bfloat16)
+    hidden_term = times_transposed(hidden.reshape(total, -1), flat_grads).astype(jnp.bfloat16)
+    tokens_grad, outward_sum, down_sum, gate_up_rows, inward_rows_own, vectors = finish(
+        (after(dq, layer_out), dk, dv),
         got_dk,
         got_dv,
         gate_up_grad,
         pieces,
+        tables,
+        normed.reshape(total, width),
+        (gate_up_send, gate_up_keep, gate_up_sent, gate_up_kept),
+        heads_term.reshape(2, 2, -1, width),
+        hidden_term.reshape(2, 2, -1, width),
         (inward, gate_up),
-        tables,
-    )
-    normed_sums = core_sums(normed_own, normed_other)
-    normed_grad = scatter_pieces(normed_sums).reshape(seqs, group_len, width)
-    inward_term = row_sums(after(projected_grad, *normed_sums))
-    gate_up_sum = device_rows(gate_up_term, 2)
-    inward_sum = device_rows(inward_term, 3)
-
-    bias_parts = bias_term.reshape(3, 2, 1, 1, 2 * HEAD_DIM)
-    here = (
-        (jnp.arange(2)[:, None] == core) & (jnp.arange(DEPTH)[None, :] == z)
-    ).astype(jnp.float32)[None, None, :, :, None]
-    spread = bias_parts * here
-    key_rot = spread[1].reshape(2, 2, DEPTH, 2, HEAD_DIM)[..., :ROT]
-    bias_all = jnp.concatenate(
-        [spread[0].reshape(-1), spread[2].reshape(-1), key_rot.reshape(-1)]
-    )
-    grid = (2, 2, DEPTH, 2, -1)
-    vector_sum = vector_sums(
-        jnp.concatenate(
-            [gain_term.reshape(grid), shift_term.reshape(grid), bias_all.reshape(grid)], -1
-        ),
-        x,
-        y,
-        core,
-        z,
-    )
-
-    hat, inverse = normalised(own_tokens)
-    scaled = normed_grad * gain.reshape(width)
-    input_grad = inverse * (
-        scaled
-        - jnp.mean(scaled, axis=-1, keepdims=True)
-        - hat * jnp.mean(scaled * hat, axis=-1, keepdims=True)
-    )
-    tokens_grad = (own_cotangent + input_grad).astype(jnp.bfloat16)
+        gain,
+        jnp.transpose(cotangent[0], (1, 0, 2)).reshape(ROWS, width),
+    )
+    gate_up_sum = place_rows(gate_up_rows, 4)
+    inward_sum = place_rows(inward_rows_own, 6)
+
+    device = bucket * 2 * DEPTH + blk
+    sums = jnp.sum(vectors[:, :4], axis=0).reshape(2, -1, gain_share)
+    gain_sum = one_of(sums[0], device, 0)
+    shift_sum = one_of(sums[1], device, 0)
+    columns_sum = vectors[:, 4, : 3 * HEAD_COLS].reshape(PIECES, 3, 2, 2 * HEAD_DIM)
+    columns_sum = jnp.transpose(columns_sum, (1, 2, 0, 3)).reshape(3, -1)
+    key_rot = columns_sum[1].reshape(HEADS, HEAD_DIM)[:, :ROT]
+    bias_all = jnp.concatenate([columns_sum[0], columns_sum[2], key_rot.reshape(-1)])
+    bias_sum = one_of(bias_all.reshape(-1, bias_share), device, 0)
 
     def placed(value):
+        value = value.reshape(seqs, group_len, width)
         return jnp.transpose(value, (1, 0, 2)).reshape(tokens.shape)
 
     return (
         placed(layer_out),
         placed(tokens_grad),
-        vector_sum[:gain_share],
-        vector_sum[gain_share : 2 * gain_share],
+        gain_sum,
+        shift_sum,
         inward_sum,
-        vector_sum[2 * gain_share :],
+        bias_sum,
         outward_sum,
         gate_up_sum,
         down_sum,

time: 719 us -> 592 us (0.82)
  waiting for transfers between devices: 171 us -> 31.9 us
  Pallas kernels: 343 us -> 449 us
  starting transfers between devices: 45.1 us -> 11.5 us
  local copies, waits for them, and re-layouts: 82.2 us -> 48.8 us
  other arithmetic: 53 us -> 26.5 us
    pallas_call x1 -> x3, Pallas kernels: 37.7 us -> 167 us  [the longest x1 164 us: finish(): pl.pallas_call(finish_kernel, in_specs=[anywhere] * 17 + [inside] * 4, ou...]
    ppermute x26 -> x0, waiting for transfers between devices: 82.9 us -> none  [the longest x6 45.9 us: rows_of_device(): parts.append(lax.ppermute(chunk, 'blk', around(step)).astype(jnp.float32))]
    ppermute x6 -> x3, waiting for transfers between devices: 66.5 us -> 6.23 us  [scatter_pieces(): got = lax.ppermute(sums[step], 'blk', around(-step))]
    ppermute x26 -> x0, starting transfers between devices: 26.5 us -> none  [the longest x6 8.05 us: rows_of_device(): parts.append(lax.ppermute(chunk, 'blk', around(step)).astype(jnp.float32))]
    pallas_call x6 -> x3, Pallas kernels: 52 us -> 28.3 us  [weight_grad(): pl.pallas_call(functools.partial(split_rows_kernel if part == 'split' els...]
    add x16 -> x0, other arithmetic: 10.7 us -> none  [the longest x12 10.6 us: summed(): return keep + got.astype(jnp.float32)]
    another operation x5 -> x2, local copies, waits for them, and re-layouts: 8.23 us -> 0.07 us  [the longest x1 0.07 us: shards_grouped(): key_rot = columns_sum[1].reshape(HEADS, HEAD_DIM)[:, :ROT]]
    unnamed x83 -> x80, local copies, waits for them, and re-layouts: 33.9 us -> 29.8 us
  transfers between devices with their start and end apart: 44 -> 14, of which waited for: 15 -> 3; matrix products, arithmetic and copies ran while one was open for 14% -> 5% of each run, Pallas kernels for 27% -> 22%
where the time goes in v3:
time: 592 us; the launch traced here: 587 us
  Pallas kernels  449 us (76%)
  local copies, waits for them, and re-layouts  48.8 us (8%)
  waiting for transfers between devices  31.9 us (5%)
  other arithmetic  26.5 us (4%)
  matrix products  17.8 us (3%)
  starting transfers between devices  11.5 us (2%)
    pallas_call x1, Pallas kernels, finish(): pl.pallas_call(finish_kernel, in_specs=[anywhere] * 17 + [inside] * 4, ou...  164 us
    pallas_call x1, Pallas kernels, gather(): pl.pallas_call(gather_kernel, in_specs=[anywhere] * 4, out_specs=[anywher...  132 us
    pallas_call x1, Pallas kernels, attend_back(): pl.pallas_call(attend_back_kernel, grid_spec=pltpu.PrefetchScalarGridSpec...  32.1 us
    unnamed x80, local copies, waits for them, and re-layouts  29.8 us
    pallas_call x3, Pallas kernels, weight_grad(): pl.pallas_call(functools.partial(split_rows_kernel if part == 'split' els...  28.3 us
    pallas_call x1, Pallas kernels, attend(): pl.pallas_call(attend_kernel, grid_spec=pltpu.PrefetchScalarGridSpec(num_...  20.4 us
    pallas_call x1, Pallas kernels, feed(): pl.pallas_call(feed_kernel, grid=(PIECES,), in_specs=[piece_spec(width),...  19.6 us
    ppermute x1, waiting for transfers between devices, shards_grouped(): other_pairs = lax.ppermute(pairs, 'blk', ACROSS_Y)  18.1 us
  transfers between devices with their start and end apart: 14, of which 3 were waited for; matrix products, arithmetic and copies ran while one was open for 5% of the time, Pallas kernels for 22%

profile of v3, /device:TPU:11, one launch (start us, length us, event | category | flops | bytes accessed | tf_op | source)
XLA Modules:
  0.0 586.8 jit_solution(2629225093991080179)
XLA Ops:
  0.7 0.8 convert.16
  1.5 1.2 convert.17
  2.6 1.2 convert.18
  3.8 1.1 convert.19
  4.9 2.3 convert.20
  8.5 1.2 reshape.295
  10.1 3.1 convert_element_type.119
  13.2 4.4 reshape.296
  17.6 2.4 copy.52
  20.0 3.9 reshape.297.wg_ref
  23.9 1.2 pad_maximum_fusion.1.ro_ref
  25.1 0.8 fusion.10
  26.0 132.3 %gather.1 = (bf16[8,256,2048]{2,1,0:T(8,128)(2,1)}, bf16[2,2,4,2,80,768]{5,4,3,2,1,0:T(8,128)(2,1)S(1)}, bf16[2,2,4,2,64,1408]{5,4,3,2,1,0:T(8,128)(2,1)S(1)}, bf16[2,2,240,2048]{3,2,1,0:T(8,128)(2,1)S(1)}) custom-call(bf16[256,2048]{1,0:T(8,128)(2,1)S(1)} %bitcast.116, bf16[2,4,80,768]{3,2,1,0:T(8,128)(2,1)S(1)} %pad_maximum_fusion.wi_ref, ...), custom_call_target="tpu_custom_call" | custom-call | bytes 1048576 | tf_op jit(solution)/shard_map/gather/pallas_call | solution.py:673
  158.3 2.5 copy-done.1
  160.8 2.0 copy-done.3
  162.8 1.9 copy-done.2
  165.9 1.9 fusion.3
  167.9 17.7 %project.1 = (bf16[8,256,2048]{2,1,0:T(8,128)(2,1)}, bf16[8,256,256]{2,1,0:T(8,128)(2,1)S(1)}, bf16[8,256,512]{2,1,0:T(8,128)(2,1)S(1)}) custom-call(bf16[8,256,2048]{2,1,0:T(8,128)(2,1)} %get-tuple-element.47.x_ref.pieces_ref, f32[1,2048]{1,0:T(1,128)S(1)} %reshape.298.gain_ref, f32[1,2048]{1,0:T(1,128)S(1)} %reshape.299.shift_ref, ...), custom_call_target="tpu_custom_call" | custom-call | flops 100663296 | bytes 393216 | tf_op jit(solution)/shard_map/project/pallas_call | solution.py:754
  185.6 1.0 copy-done.10
  186.7 3.4 multiply_convert_fusion
  190.4 1.3 collective-permute-start.3
  191.6 1.7 collective-permute-start.2
  193.3 19.6 %feed.1 = (f32[8,256,704]{2,1,0:T(8,128)}, f32[8,256,704]{2,1,0:T(8,128)}, bf16[8,256,704]{2,1,0:T(8,128)(2,1)S(1)}) custom-call(bf16[8,256,2048]{2,1,0:T(8,128)(2,1)} %get-tuple-element.75.n_ref, bf16[2048,1408]{1,0:T(8,128)(2,1)} %bitcast.108), custom_call_target="tpu_custom_call" | custom-call | flops 184549376 | bytes 458752 | tf_op jit(solution)/shard_map/feed/pallas_call | solution.py:791
  213.0 1.7 copy-done.13
  214.7 18.1 %collective-permute-done = bf16[8,256,512]{2,1,0:T(8,128)(2,1)} collective-permute-done((bf16[8,256,512]{2,1,0:T(8,128)(2,1)S(1)}, bf16[8,256,512]{2,1,0:T(8,128)(2,1)}, u32[]{:S(2)}, u32[]{:S(2)}) %collective-permute-start) | collective-permute-done | bytes 2097184 | tf_op jit(solution)/shard_map/ppermute | solution.py:1765
  232.9 1.2 copy-done.11
  234.1 20.4 %attend.1 = bf16[2,4,2,128,256]{4,3,2,1,0:T(8,128)(2,1)S(1)} custom-call(s32[3]{0:T(128)S(1)} %pad_add_fusion.place_ref, bf16[2,4,2,128,256]{4,3,2,1,0:T(8,128)(2,1)S(1)} %bitcast.117, bf16[2,4,2,128,512]{4,3,2,1,0:T(8,128)(2,1)S(1)} %bitcast.104, bf16[2,4,2,128,512]{4,3,2,1,0:T(8,128)(2,1)S(1)} %bitcast.105, ...), custom_call_target="tpu_custom_call" | custom-call | flops 167772160 | bytes 131072 | tf_op jit(solution)/shard_map/attend/pallas_call | solution.py:1001
  254.5 14.6 %branch_terms.1 = (bf16[4,256,2048]{2,1,0:T(8,128)(2,1)}, bf16[4,256,2048]{2,1,0:T(8,128)(2,1)}) custom-call(bf16[8,256,256]{2,1,0:T(8,128)(2,1)S(1)} %bitcast.114, bf16[8,256,704]{2,1,0:T(8,128)(2,1)S(1)} %copy-done.14, bf16[4,240,2048]{2,1,0:T(8,128)(2,1)} %bitcast.112), custom_call_target="tpu_custom_call" | custom-call | flops 125829120 | bytes 262144 | tf_op jit(solution)/shard_map/branch_terms/pallas_call | solution.py:837
  269.2 1.9 collective-permute-start.1
  271.1 1.3 copy.39
  272.4 1.3 bitcast_dynamic-update-slice_fusion.7
  274.4 7.5 %collective-permute-done.2 = bf16[256,2048]{1,0:T(8,128)(2,1)} collective-permute-done((bf16[256,2048]{1,0:T(8,128)(2,1)}, bf16[256,2048]{1,0:T(8,128)(2,1)}, u32[]{:S(2)}, u32[]{:S(2)}) %collective-permute-start.2) | collective-permute-done | bytes 1048608 | tf_op jit(solution)/shard_map/ppermute | solution.py:385
  281.9 0.8 collective-permute-start.6
  282.8 1.3 bitcast_dynamic-update-slice_fusion.6
  284.1 1.3 bitcast_dynamic-update-slice_fusion.5
  285.3 1.3 bitcast_dynamic-update-slice_fusion.4
  287.1 4.0 copy-done.21
  291.4 16.2 %back.1 = (bf16[8,256,256]{2,1,0:T(8,128)(2,1)S(1)}, bf16[8,256,1408]{2,1,0:T(8,128)(2,1)}) custom-call(bf16[8,256,2048]{2,1,0:T(8,128)(2,1)} %copy-done.21, f32[8,256,704]{2,1,0:T(8,128)} %get-tuple-element.64.gate_ref, f32[8,256,704]{2,1,0:T(8,128)} %get-tuple-element.65.up_ref, bf16[4,240,2048]{2,1,0:T(8,128)(2,1)S(1)} %bitcast.113), custom_call_target="tpu_custom_call" | custom-call | flops 125829120 | bytes 458752 | tf_op jit(solution)/shard_map/back/pallas_call | solution.py:868
  307.6 5.4 fusion.2
  313.0 1.8 collective-permute-start.9
  314.8 1.6 collective-permute-start.10
  316.4 32.1 %attend_back.1 = (f32[2,4,2,128,256]{4,3,2,1,0:T(8,128)}, f32[2,4,2,128,256]{4,3,2,1,0:T(8,128)}, f32[2,4,2,128,256]{4,3,2,1,0:T(8,128)}, bf16[2,4,2,128,256]{4,...) custom-call(s32[3]{0:T(128)S(1)} %pad_add_fusion.place_ref, bf16[2,4,2,128,256]{4,3,2,1,0:T(8,128)(2,1)S(1)} %bitcast.118, ...), custom_call_target="tpu_custom_call" | custom-call | flops 419430400 | bytes 262144 | tf_op jit(solution)/shard_map/attend_back/pallas_call | solution.py:1025
  348.6 0.8 collective-permute-start.12
  349.4 9.7 %bitcast_convert_fusion = bf16[704,2048]{1,0:T(8,128)(2,1)} fusion(bf16[8,256,704]{2,1,0:T(8,128)(2,1)S(1)} %copy-done.15, bf16[8,256,2048]{2,1,0:T(8,128)(2,1)} %copy-done.21), kind=kOutput, calls=%fused_computation | convolution fusion | flops 5907021824 | bytes 14155776 | tf_op jit(solution)/shard_map/dot_general | solution.py:43
  359.0 0.7 collective-permute-start.13
  359.7 7.9 %weight_grad_send.1.gate_xs = bf16[4,256,768]{2,1,0:T(8,128)(2,1)S(1)} custom-call(s32[3]{0:T(128)S(1)} %pad_add_fusion.place_ref, bf16[2048,2048]{1,0:T(8,128)(2,1)} %bitcast.122, bf16[2048,1408]{1,0:T(8,128)(2,1)} %bitcast.126), custom_call_target="tpu_custom_call" | custom-call | flops 50331648 | bytes 163840 | tf_op jit(solution)/shard_map/weight_grad_send/pallas_call | solution.py:1656
  367.7 1.1 copy-done.6
  368.8 7.9 %weight_grad_keep.1.gate_xk = f32[4,256,768]{2,1,0:T(8,128)S(1)} custom-call(s32[3]{0:T(128)S(1)} %pad_add_fusion.place_ref, bf16[2048,2048]{1,0:T(8,128)(2,1)} %bitcast.123, bf16[2048,1408]{1,0:T(8,128)(2,1)} %bitcast.127), custom_call_target="tpu_custom_call" | custom-call | flops 50331648 | bytes 163840 | tf_op jit(solution)/shard_map/weight_grad_keep/pallas_call | solution.py:1656
  376.7 1.6 copy-done.5
  378.3 12.5 %weight_grad_split.1 = (f32[8,128,640]{2,1,0:T(8,128)S(1)}, bf16[8,128,640]{2,1,0:T(8,128)(2,1)S(1)}) custom-call(s32[3]{0:T(128)S(1)} %pad_add_fusion.place_ref, bf16[2048,2048]{1,0:T(8,128)(2,1)} %bitcast.124, bf16[2048,1408]{1,0:T(8,128)(2,1)} %bitcast.128), custom_call_target="tpu_custom_call" | custom-call | flops 83886080 | bytes 163840 | tf_op jit(solution)/shard_map/weight_grad_split/pallas_call | solution.py:1656
  390.8 8.1 %convolution_convert_fusion = bf16[256,2048]{1,0:T(8,128)(2,1)} fusion(bf16[2048,256]{1,0:T(8,128)(2,1)S(1)} %bitcast.115, bf16[2048,2048]{1,0:T(8,128)(2,1)} %bitcast.129), kind=kOutput, calls=%fused_computation.1 | convolution fusion | flops 2148007936 | bytes 10485760 | tf_op jit(solution)/shard_map/dot_general | solution.py:43
  399.0 6.2 %collective-permute-done.11 = bf16[256,2048]{1,0:T(8,128)(2,1)} collective-permute-done((bf16[256,2048]{1,0:T(8,128)(2,1)}, bf16[256,2048]{1,0:T(8,128)(2,1)}, u32[]{:S(2)}, u32[]{:S(2)}) %collective-permute-start.11) | collective-permute-done | bytes 1048608 | tf_op jit(solution)/shard_map/ppermute | solution.py:398
  405.2 1.9 convert_add_fusion
  407.1 0.6 add_convert_fusion
  407.8 1.0 copy-done.30
  409.0 164.2 %finish.1 = (bf16[256,2048]{1,0:T(8,128)(2,1)}, f32[64,2048]{1,0:T(8,128)}, f32[176,2048]{1,0:T(8,128)}, bf16[8,64,1408]{2,1,0:T(8,128)(2,1)}, bf16[8,64,768]{2,...) custom-call(f32[8,256,256]{2,1,0:T(8,128)} %bitcast.137, ...), custom_call_target="tpu_custom_call" | custom-call | bytes 1048576 | tf_op jit(solution)/shard_map/finish/pallas_call | solution.py:1546
  573.3 1.1 slice_reduce_fusion
  574.4 1.0 slice.96
  575.3 2.0 copy.43
  577.4 2.0 copy.53
  581.5 1.2 place_rows.2
  582.7 2.0 place_rows.3
  584.7 0.8 copy.65
  585.5 1.1 copy.66
  (121 shorter events, 7.1 us)
Async XLA Ops:
  0.6 6.6 %copy-start.27 = (f32[64,6144]{1,0:T(8,128)S(1)}, f32[64,6144]{1,0:T(8,128)}, u32[]{:S(2)}) copy-start(f32[64,6144]{1,0:T(8,128)} %param.14) | copy-start | bytes 4718596
  7.3 2.4 copy-start.22
  20.0 5.9 %copy-start.26 = (bf16[2,4,64,768]{3,2,1,0:T(8,128)(2,1)S(1)}, bf16[2,4,64,768]{3,2,1,0:T(8,128)(2,1)}, u32[]{:S(2)}) copy-start(bf16[2,4,64,768]{3,2,1,0:T(8,128)(2,1)} %reshape.295) | copy-start | bytes 2359300
  158.3 2.5 copy-start.1
  160.8 2.0 copy-start.3
  162.8 1.9 copy-start.2
  165.6 20.0 %copy-start.20 = (f32[1,2048]{1,0:T(1,128)}, f32[1,2048]{1,0:T(1,128)S(1)}, u32[]{:S(2)}) copy-start(f32[1,2048]{1,0:T(1,128)S(1)} %reshape.298.gain_ref) | copy-start | bytes 24580
  167.8 17.8 %copy-start.7 = (f32[4,128,256]{2,1,0:T(8,128)}, f32[4,128,256]{2,1,0:T(8,128)S(1)}, u32[]{:S(2)}) copy-start(f32[4,128,256]{2,1,0:T(8,128)S(1)} %get-tuple-element.107.second_ref) | copy-start | bytes 1572868
  167.8 17.8 %copy-start.8 = (f32[4,128,256]{2,1,0:T(8,128)}, f32[4,128,256]{2,1,0:T(8,128)S(1)}, u32[]{:S(2)}) copy-start(f32[4,128,256]{2,1,0:T(8,128)S(1)} %get-tuple-element.108.first_ref) | copy-start | bytes 1572868
  167.8 17.8 %copy-start.9 = (f32[4,128,256]{2,1,0:T(8,128)}, f32[4,128,256]{2,1,0:T(8,128)S(1)}, u32[]{:S(2)}) copy-start(f32[4,128,256]{2,1,0:T(8,128)S(1)} %get-tuple-element.109.cos_ref) | copy-start | bytes 1572868
  167.8 18.7 %copy-start.33 = (s32[1,2]{1,0:T(1,128)S(1)}, s32[1,2]{1,0:T(1,128)}, u32[]{:S(2)}) copy-start(s32[1,2]{1,0:T(1,128)} %param.11) | copy-start | bytes 28
  185.6 1.0 copy-start.10
  186.6 46.3 %copy-start = (bf16[8,256,512]{2,1,0:T(8,128)(2,1)}, bf16[8,256,512]{2,1,0:T(8,128)(2,1)S(1)}, u32[]{:S(2)}) copy-start(bf16[8,256,512]{2,1,0:T(8,128)(2,1)S(1)} %get-tuple-element.54) | copy-start | bytes 6291460
  186.6 46.3 %collective-permute-start = (bf16[8,256,512]{2,1,0:T(8,128)(2,1)S(1)}, bf16[8,256,512]{2,1,0:T(8,128)(2,1)}, u32[]{:S(2)}, u32[]{:S(2)}) collective-permute-start(bf16[8,256,512]{2,1,0:T(8,128)(2,1)S(1)} %get-tuple-element.54), channel_id=1, source_target_pairs={{0,1},{1,0},{2,3},{3,2},{4,5},{5,4},{6,7},{7,6},{8,9},{9,8},{10,11... | collective-permute-start | bytes 6291464 | tf_op jit(solution)/shard_map/ppermute | solution.py:1765
  190.0 83.7 %collective-permute-start.4 = (bf16[256,2048]{1,0:T(8,128)(2,1)}, bf16[256,2048]{1,0:T(8,128)(2,1)}, u32[]{:S(2)}, u32[]{:S(2)}) collective-permute-start(bf16[256,2048]{1,0:T(8,128)(2,1)} %bitcast.27), channel_id=1, source_target_pairs={{0,6},{1,7},{2,0},{3,1},{4,2},{5,3},{6,4},{7,5},{8,14},{9,15},{10,... | collective-permute-start | bytes 3145736 | tf_op jit(solution)/shard_map/ppermute | solution.py:385
  190.4 83.9 %collective-permute-start.3 = (bf16[256,2048]{1,0:T(8,128)(2,1)}, bf16[256,2048]{1,0:T(8,128)(2,1)}, u32[]{:S(2)}, u32[]{:S(2)}) collective-permute-start(bf16[256,2048]{1,0:T(8,128)(2,1)} %bitcast.27), channel_id=1, source_target_pairs={{0,4},{1,5},{2,6},{3,7},{4,0},{5,1},{6,2},{7,3},{8,12},{9,13},{10,... | collective-permute-start | bytes 3145736 | tf_op jit(solution)/shard_map/ppermute | solution.py:385
  191.6 90.3 %collective-permute-start.2 = (bf16[256,2048]{1,0:T(8,128)(2,1)}, bf16[256,2048]{1,0:T(8,128)(2,1)}, u32[]{:S(2)}, u32[]{:S(2)}) collective-permute-start(bf16[256,2048]{1,0:T(8,128)(2,1)} %bitcast.27), channel_id=1, source_target_pairs={{0,2},{1,3},{2,4},{3,5},{4,6},{5,7},{6,0},{7,1},{8,10},{9,11},{10,... | collective-permute-start | bytes 3145736 | tf_op jit(solution)/shard_map/ppermute | solution.py:385
  213.0 1.7 copy-start.13
  232.9 1.2 copy-start.11
  234.1 20.4 %copy-start.14 = (bf16[8,256,704]{2,1,0:T(8,128)(2,1)S(1)}, bf16[8,256,704]{2,1,0:T(8,128)(2,1)}, u32[]{:S(2)}) copy-start(bf16[8,256,704]{2,1,0:T(8,128)(2,1)} %copy-done.13) | copy-start | bytes 8650756
  254.5 16.6 %copy-start.25 = (bf16[1,128,2,2048]{3,2,1,0:T(2,128)(2,1)S(1)}, bf16[1,128,2,2048]{3,2,1,0:T(2,128)(2,1)}, u32[]{:S(2)}) copy-start(bf16[1,128,2,2048]{3,2,1,0:T(2,128)(2,1)} %param.19) | copy-start | bytes 3145732
  269.2 38.5 %collective-permute-start.1 = (bf16[4,256,2048]{2,1,0:T(8,128)(2,1)}, bf16[4,256,2048]{2,1,0:T(8,128)(2,1)}, u32[]{:S(2)}, u32[]{:S(2)}) collective-permute-start(bf16[4,256,2048]{2,1,0:T(8,128)(2,1)} %get-tuple-element.57), channel_id=1, source_target_pairs={{0,8},{8,0},{16,24},{24,16},{1,9},{9,1},{17,25},{25,17},{2,10},{10... | collective-permute-start | bytes 12582920 | tf_op jit(solution)/shard_map/ppermute | solution.py:390
  271.1 15.6 %collective-permute-start.5 = (bf16[256,2048]{1,0:T(8,128)(2,1)}, bf16[256,2048]{1,0:T(8,128)(2,1)S(1)}, u32[]{:S(2)}, u32[]{:S(2)}) collective-permute-start(bf16[256,2048]{1,0:T(8,128)(2,1)} %bitcast.27), channel_id=1, source_target_pairs={{0,8},{8,0},{16,24},{24,16},{1,9},{9,1},{17,25},{25,17},{2,10},{10... | collective-permute-start | bytes 3145736 | tf_op jit(solution)/shard_map/ppermute | solution.py:386
  273.7 13.2 %collective-permute-start.8 = (bf16[256,2048]{1,0:T(8,128)(2,1)}, bf16[256,2048]{1,0:T(8,128)(2,1)S(1)}, u32[]{:S(2)}, u32[]{:S(2)}) collective-permute-start(bf16[256,2048]{1,0:T(8,128)(2,1)} %collective-permute-done.4), channel_id=1, source_target_pairs={{0,8},{8,0},{16,24},{24,16},{1,9},{9,1},{17,25},{25,17},{2,10},{10... | collective-permute-start | bytes 3145736 | tf_op jit(solution)/shard_map/ppermute | solution.py:386
  274.3 12.6 %collective-permute-start.7 = (bf16[256,2048]{1,0:T(8,128)(2,1)}, bf16[256,2048]{1,0:T(8,128)(2,1)S(1)}, u32[]{:S(2)}, u32[]{:S(2)}) collective-permute-start(bf16[256,2048]{1,0:T(8,128)(2,1)} %collective-permute-done.3), channel_id=1, source_target_pairs={{0,8},{8,0},{16,24},{24,16},{1,9},{9,1},{17,25},{25,17},{2,10},{10... | collective-permute-start | bytes 3145736 | tf_op jit(solution)/shard_map/ppermute | solution.py:386
  281.9 4.8 collective-permute-start.6
  286.9 4.6 copy-start.4
  287.0 4.0 copy-start.21
  291.4 16.2 %copy-start.24 = (bf16[4,256,2048]{2,1,0:T(8,128)(2,1)S(1)}, bf16[4,256,2048]{2,1,0:T(8,128)(2,1)}, u32[]{:S(2)}) copy-start(bf16[4,256,2048]{2,1,0:T(8,128)(2,1)} %get-tuple-element.56) | copy-start | bytes 12582916
  307.6 8.8 %copy-start.12 = (bf16[8,256,256]{2,1,0:T(8,128)(2,1)S(1)}, bf16[8,256,256]{2,1,0:T(8,128)(2,1)}, u32[]{:S(2)}) copy-start(bf16[8,256,256]{2,1,0:T(8,128)(2,1)} %copy-done.10) | copy-start | bytes 3145732
  313.0 85.9 %collective-permute-start.9 = (bf16[256,2048]{1,0:T(8,128)(2,1)}, bf16[256,2048]{1,0:T(8,128)(2,1)S(1)}, u32[]{:S(2)}, u32[]{:S(2)}) collective-permute-start(bf16[256,2048]{1,0:T(8,128)(2,1)} %get-tuple-element.60), channel_id=1, source_target_pairs={{0,6},{1,7},{2,0},{3,1},{4,2},{5,3},{6,4},{7,5},{8,14},{9,15},{10,... | collective-permute-start | bytes 3145736 | tf_op jit(solution)/shard_map/ppermute | solution.py:398
  314.8 84.2 %collective-permute-start.10 = (bf16[256,2048]{1,0:T(8,128)(2,1)}, bf16[256,2048]{1,0:T(8,128)(2,1)S(1)}, u32[]{:S(2)}, u32[]{:S(2)}) collective-permute-start(bf16[256,2048]{1,0:T(8,128)(2,1)} %get-tuple-element.61), channel_id=1, source_target_pairs={{0,4},{1,5},{2,6},{3,7},{4,0},{5,1},{6,2},{7,3},{8,12},{9,13},{10,... | collective-permute-start | bytes 3145736 | tf_op jit(solution)/shard_map/ppermute | solution.py:398
  316.4 88.8 %collective-permute-start.11 = (bf16[256,2048]{1,0:T(8,128)(2,1)}, bf16[256,2048]{1,0:T(8,128)(2,1)}, u32[]{:S(2)}, u32[]{:S(2)}) collective-permute-start(bf16[256,2048]{1,0:T(8,128)(2,1)} %get-tuple-element.62), channel_id=1, source_target_pairs={{0,2},{1,3},{2,4},{3,5},{4,6},{5,7},{6,0},{7,1},{8,10},{9,11},{10,... | collective-permute-start | bytes 3145736 | tf_op jit(solution)/shard_map/ppermute | solution.py:398
  316.4 33.0 %copy-start.15 = (bf16[8,256,704]{2,1,0:T(8,128)(2,1)S(1)}, bf16[8,256,704]{2,1,0:T(8,128)(2,1)}, u32[]{:S(2)}) copy-start(bf16[8,256,704]{2,1,0:T(8,128)(2,1)} %copy-done.13) | copy-start | bytes 8650756
  348.6 59.2 %collective-permute-start.12 = (bf16[8,256,256]{2,1,0:T(8,128)(2,1)S(1)}, bf16[8,256,256]{2,1,0:T(8,128)(2,1)S(1)}, u32[]{:S(2)}, u32[]{:S(2)}) collective-permute-start(bf16[8,256,256]{2,1,0:T(8,128)(2,1)S(1)} %bitcast.121), channel_id=1, source_target_pairs={{0,1},{1,0},{2,3},{3,2},{4,5},{5,4},{6,7},{7,6},{8,9},{9,8},{10,11... | collective-permute-start | bytes 3145736 | tf_op jit(solution)/shard_map/ppermute | solution.py:1781
  359.0 48.7 %collective-permute-start.13 = (bf16[8,256,256]{2,1,0:T(8,128)(2,1)S(1)}, bf16[8,256,256]{2,1,0:T(8,128)(2,1)S(1)}, u32[]{:S(2)}, u32[]{:S(2)}) collective-permute-start(bf16[8,256,256]{2,1,0:T(8,128)(2,1)S(1)} %bitcast.120), channel_id=1, source_target_pairs={{0,1},{1,0},{2,3},{3,2},{4,5},{5,4},{6,7},{7,6},{8,9},{9,8},{10,11... | collective-permute-start | bytes 3145736 | tf_op jit(solution)/shard_map/ppermute | solution.py:1782
  367.6 1.1 copy-start.6
  376.7 1.6 copy-start.5
  390.8 8.2 %copy-start.16 = (f32[8,128,640]{2,1,0:T(8,128)}, f32[8,128,640]{2,1,0:T(8,128)S(1)}, u32[]{:S(2)}) copy-start(f32[8,128,640]{2,1,0:T(8,128)S(1)} %get-tuple-element.77.gate_yk) | copy-start | bytes 7864324
  390.8 8.2 %copy-start.18 = (bf16[8,128,640]{2,1,0:T(8,128)(2,1)}, bf16[8,128,640]{2,1,0:T(8,128)(2,1)S(1)}, u32[]{:S(2)}) copy-start(bf16[8,128,640]{2,1,0:T(8,128)(2,1)S(1)} %get-tuple-element.76.gate_ys) | copy-start | bytes 3932164
  399.0 8.1 %copy-start.23 = (bf16[1,128,2,2048]{3,2,1,0:T(2,128)(2,1)S(1)}, bf16[1,128,2,2048]{3,2,1,0:T(2,128)(2,1)}, u32[]{:S(2)}) copy-start(bf16[1,128,2,2048]{3,2,1,0:T(2,128)(2,1)} %param.10) | copy-start | bytes 3145732
  407.7 1.3 copy-start.29
  407.7 1.0 copy-start.30
  573.3 4.1 copy-start.31
  575.3 6.2 %copy-start.19 = (bf16[8,64,768]{2,1,0:T(8,128)(2,1)S(1)}, bf16[8,64,768]{2,1,0:T(8,128)(2,1)}, u32[]{:S(2)}) copy-start(bf16[8,64,768]{2,1,0:T(8,128)(2,1)} %get-tuple-element.81.in_ref) | copy-start | bytes 2359300
  577.4 5.3 copy-start.17
  582.7 2.0 copy-start.32
  582.7 2.8 copy-start.28

commit v4 on v3

--- a/solution.py
+++ b/solution.py
@@ -359,9 +359,8 @@
 EXTRA = 16
 LOCAL_HEADS = 4
 HEAD_COLS = LOCAL_HEADS * HEAD_DIM
-CORE = [(i, i ^ 1) for i in range(4)]
-ACROSS_X = [(i, i ^ 2) for i in range(4)]
-ACROSS_Y = [(i, i ^ 1) for i in range(8)]
+
+
 MIB = 1024 * 1024
 
 
@@ -377,31 +376,6 @@
     return jnp.where(
         index == 0, jnp.stack([own, other], axis), jnp.stack([other, own], axis)
     )
-
-
-def gather_pieces(value):
-    own = [value]
-    for step in range(1, DEPTH):
-        own.append(lax.ppermute(value, "blk", around(step)))
-    return own + [lax.ppermute(piece, "bucket", CORE) for piece in own]
-
-
-def core_sums(own, other):
-    other = lax.ppermute(other, "bucket", CORE)
-    sums = [own[k].astype(jnp.float32) + other[k].astype(jnp.float32) for k in range(DEPTH)]
-    return [sums[0]] + [value.astype(jnp.bfloat16) for value in sums[1:]]
-
-
-def scatter_pieces(sums):
-    total = sums[0]
-    for step in range(1, DEPTH):
-        got = lax.ppermute(sums[step], "blk", around(-step))
-        total = total + got.astype(jnp.float32)
-    return total
-
-
-def after(value, *earlier):
-    return lax.optimization_barrier((value,) + earlier)[0]
 
 
 def one_of(value, index, axis):
@@ -439,6 +413,111 @@
         device_id=device,
         device_id_type=pl.DeviceIdType.MESH,
     )
+
+
+class Chain:
+    def __init__(self, src, out, x, core, z, y, sems):
+        up_s, down_s, arrive, core_s, core_r, local = sems
+        self.z = z
+        self.out = out
+
+        def hop(k, src, slot, sends, dz):
+            return pltpu.make_async_remote_copy(
+                src_ref=src,
+                dst_ref=out.at[slot],
+                send_sem=sends.at[k],
+                recv_sem=arrive.at[slot],
+                device_id=(x * 2 + core, (z + dz) * 2 + y),
+                device_id_type=pl.DeviceIdType.MESH,
+            )
+
+        mate = (x * 2 + 1 - core, z * 2 + y)
+        self.ups = [hop(k, src if k == 0 else out.at[k], k + 1, up_s, 1) for k in range(3)]
+        self.downs = [
+            hop(k, src if k == 0 else out.at[DEPTH - k], 3 - k, down_s, -1) for k in range(3)
+        ]
+        self.cores = [
+            remote(src if k == 0 else out.at[k], out.at[DEPTH + k], core_s, core_r, k, mate)
+            for k in range(DEPTH)
+        ]
+        self.local = pltpu.make_async_copy(src, out.at[0], local)
+        inner = (z > 0) & (z < DEPTH - 1)
+        self.sent = [
+            (z < DEPTH - 1, self.ups[0]),
+            (z > 0, self.downs[0]),
+            (inner, self.ups[1]),
+            (inner, self.downs[1]),
+            (z == DEPTH - 2, self.ups[2]),
+            (z == 1, self.downs[2]),
+        ]
+
+    def start(self, *numbers):
+        for number in numbers:
+            condition, copy = self.sent[number]
+            pl.when(condition)(copy.start)
+
+    def first(self):
+        self.start(0, 1)
+        self.cores[0].start()
+        self.local.start()
+
+    def second(self):
+        @pl.when(self.z > 0)
+        def _():
+            self.ups[0].wait_recv()
+            self.cores[1].start()
+
+        self.start(2)
+
+        @pl.when(self.z < DEPTH - 1)
+        def _():
+            self.downs[0].wait_recv()
+            self.cores[3].start()
+
+        self.start(3)
+
+    def third(self):
+        self.ups[1].wait_recv()
+        self.cores[2].start()
+        self.start(4, 5)
+
+    def fourth(self):
+        @pl.when(self.z == DEPTH - 1)
+        def _():
+            self.ups[2].wait_recv()
+            self.cores[3].start()
+
+        @pl.when(self.z == 0)
+        def _():
+            self.downs[2].wait_recv()
+            self.cores[1].start()
+
+    def end(self):
+        for copy in self.cores:
+            copy.wait_recv()
+            copy.wait_send()
+        for condition, copy in self.sent:
+            pl.when(condition)(copy.wait_send)
+        self.local.wait()
+
+
+def chain_sems():
+    dma = pltpu.SemaphoreType.DMA
+    return [dma((3,)), dma((3,)), dma((DEPTH,)), dma((DEPTH,)), dma((DEPTH,)), dma(())]
+
+
+def greet(mates):
+    barrier = pltpu.get_barrier_semaphore()
+    for mate in mates:
+        pl.semaphore_signal(
+            barrier, inc=1, device_id=mate, device_id_type=pl.DeviceIdType.MESH
+        )
+    pl.semaphore_wait(barrier, len(mates))
+
+
+def coordinates():
+    bucket, blk = lax.axis_index("bucket"), lax.axis_index("blk")
+    return bucket // 2, bucket % 2, blk // 2, blk % 2
 
 
 def gather_kernel(
@@ -456,22 +535,15 @@
     across_r,
     rows_s,
     rows_r,
-    up_s,
-    down_s,
-    piece_r,
-    core_s,
-    core_r,
     local_sems,
+    *chain,
 ):
-    bucket, blk = lax.axis_index("bucket"), lax.axis_index("blk")
-    x, core = bucket // 2, bucket % 2
-    z, y = blk // 2, blk % 2
+    x, core, z, y = coordinates()
 
     def device(xx, cc, zz, yy):
         return (xx * 2 + cc, zz * 2 + yy)
 
     x_mate, y_mate = device(1 - x, core, z, y), device(x, core, z, 1 - y)
-    core_mate = device(x, 1 - core, z, y)
     members = [(flip, turn) for turn in (0, 1, 3, 2) for flip in (0, 1)]
 
     def target(flip, turn):
@@ -480,14 +552,7 @@
     def source(flip, turn):
         return (core + flip) % 2, (z + DEPTH - turn) % DEPTH
 
-    barrier = pltpu.get_barrier_semaphore()
-    greeted = [device(x, *target(*m), y) for m in members[1:]] + [x_mate, y_mate]
-    for mate in greeted:
-        pl.semaphore_signal(
-            barrier, inc=1, device_id=mate, device_id_type=pl.DeviceIdType.MESH
-        )
-    pl.semaphore_wait(barrier, len(greeted))
-
+    greet([device(x, *target(*m), y) for m in members[1:]] + [x_mate, y_mate])
     started = []
 
     def begin(copy):
@@ -499,7 +564,6 @@
         pltpu.make_async_copy(wi_ref.at[core, z], wi_out.at[x, core, z, y], local_sems.at[0]),
         pltpu.make_async_copy(wg_ref.at[core, z], wg_out.at[x, core, z, y], local_sems.at[1]),
         pltpu.make_async_copy(ro_ref, ro_out.at[x, y], local_sems.at[2]),
-        pltpu.make_async_copy(x_ref, pieces.at[0], local_sems.at[3]),
     ]
     for copy in local:
         copy.start()
@@ -520,41 +584,9 @@
             )
         return copies
 
-    def piece_copy(src, slot, sends, number, dz):
-        return pltpu.make_async_remote_copy(
-            src_ref=src,
-            dst_ref=pieces.at[slot],
-            send_sem=sends.at[number],
-            recv_sem=piece_r.at[slot],
-            device_id=device(x, core, z + dz, y),
-            device_id_type=pl.DeviceIdType.MESH,
-        )
-
-    def core_copy(slot):
-        src = x_ref if slot == 0 else pieces.at[slot]
-        return remote(src, pieces.at[DEPTH + slot], core_s, core_r, slot, core_mate)
-
-    ups = [piece_copy(x_ref if k == 0 else pieces.at[k], k + 1, up_s, k, 1) for k in range(3)]
-    downs = [
-        piece_copy(x_ref if k == 0 else pieces.at[DEPTH - k], 3 - k, down_s, k, -1)
-        for k in range(3)
-    ]
-
-    def start_if(condition, copy):
-        @pl.when(condition)
-        def _():
-            copy.start()
-
-    def sent_if(condition, copy):
-        @pl.when(condition)
-        def _():
-            copy.wait_send()
-
     inward = send_group(0, wi_ref, wi_out)
-    start_if(z < DEPTH - 1, ups[0])
-    start_if(z > 0, downs[0])
-    core_copies = [core_copy(slot) for slot in range(DEPTH)]
-    core_copies[0].start()
+    tokens = Chain(x_ref, pieces, x, core, z, y, chain)
+    tokens.first()
     rows_x = begin(remote(ro_ref, ro_out.at[x, y], rows_s, rows_r, 0, x_mate))
     rows_y = begin(remote(ro_ref, ro_out.at[x, y], rows_s, rows_r, 1, y_mate))
     gate_up = send_group(1, wg_ref, wg_out)
@@ -605,28 +637,11 @@
 
     inward_pairs = spread(0, wi_ref, wi_out, inward)
 
-    @pl.when(z > 0)
-    def _():
-        ups[0].wait_recv()
-        core_copies[1].start()
-
-    start_if((z > 0) & (z < DEPTH - 1), ups[1])
-
-    @pl.when(z < DEPTH - 1)
-    def _():
-        downs[0].wait_recv()
-        core_copies[3].start()
-
-    start_if((z > 0) & (z < DEPTH - 1), downs[1])
-
+    tokens.second()
     inward_corner = corner(0, wi_out, inward_pairs)
     gate_up_pairs = spread(1, wg_ref, wg_out, gate_up)
 
-    ups[1].wait_recv()
-    core_copies[2].start()
-    start_if(z == 2, ups[2])
-    start_if(z == 1, downs[2])
-
+    tokens.third()
     cut = (ro_ref.shape[0] // 32) * 16
     rows_y.wait_recv()
     low = ro_out.at[x, 1 - y, pl.ds(0, cut)]
@@ -636,32 +651,16 @@
     high_copy = begin(remote(high, high, rows_s, rows_r, 3, y_mate))
     gate_up_corner = corner(1, wg_out, gate_up_pairs)
 
-    @pl.when(z == DEPTH - 1)
-    def _():
-        ups[2].wait_recv()
-        core_copies[3].start()
-
-    @pl.when(z == 0)
-    def _():
-        downs[2].wait_recv()
-        core_copies[1].start()
+    tokens.fourth()
 
     for pairs in (inward_pairs, gate_up_pairs):
         for flip, turn in members:
             pairs[flip, turn][0 if flip == 0 else 1].wait_recv()
     for copy in inward_corner + gate_up_corner + [low_copy, high_copy]:
         copy.wait_recv()
-    for copy in core_copies:
-        copy.wait_recv()
-        copy.wait_send()
     for copy in started:
         copy.wait_send()
-    sent_if(z < DEPTH - 1, ups[0])
-    sent_if(z > 0, downs[0])
-    sent_if((z > 0) & (z < DEPTH - 1), ups[1])
-    sent_if((z > 0) & (z < DEPTH - 1), downs[1])
-    sent_if(z == 2, ups[2])
-    sent_if(z == 1, downs[2])
+    tokens.end()
     for copy in local:
         copy.wait()
 
@@ -688,12 +687,8 @@
             dma((4,)),
             dma((4,)),
             dma((3,)),
-            dma((3,)),
-            dma((DEPTH,)),
-            dma((DEPTH,)),
-            dma((DEPTH,)),
-            dma((4,)),
-        ],
+        ]
+        + chain_sems(),
         compiler_params=params(32, collective_id=0, has_side_effects=True),
         cost_estimate=cost(0, 64 * MIB),
         name="gather",
@@ -733,156 +728,166 @@
     return values * cos + sign * (ahead * first + behind * second)
 
 
-def project_kernel(
-    x_ref, gain_ref, shift_ref, w_ref, bias_ref, cos_ref, first_ref, second_ref, n_ref, q_ref, kv_ref
+def forward_kernel(
+    pieces_ref,
+    grad_ref,
+    cos_ref,
+    first_ref,
+    second_ref,
+    gain_ref,
+    shift_ref,
+    bias_ref,
+    wi_ref,
+    wg_ref,
+    rows_ref,
+    normed_out,
+    gate_out,
+    up_out,
+    grads_out,
+    q_ref,
+    kv_ref,
+    okv_ref,
+    hidden_ref,
+    att_ref,
+    own_sum,
+    terms,
+    core_send,
+    core_recv,
+    kv_s,
+    kv_r,
+    core_s,
+    core_r,
+    *chain,
 ):
-    hat, _ = normalised(x_ref[0])
-    normed = (hat * gain_ref[...] + shift_ref[...]).astype(jnp.bfloat16)
-    n_ref[0] = normed
-    projected = dot_rows(normed, inward_rows(w_ref)) + bias_ref[...]
-    tables = (cos_ref, first_ref, second_ref)
-    query = turned(projected[:, :HEAD_COLS], *tables, 1.0) * (HEAD_DIM**-0.5)
-    key = turned(projected[:, HEAD_COLS : 2 * HEAD_COLS], *tables, 1.0)
-    q_ref[0] = query.astype(jnp.bfloat16)
-    kv_ref[0, :, :HEAD_COLS] = key.astype(jnp.bfloat16)
-    kv_ref[0, :, HEAD_COLS:] = projected[:, 2 * HEAD_COLS :].astype(jnp.bfloat16)
-
-
-def project(pieces, gain, shift, weight, bias, tables):
+    x, core, z, y = coordinates()
+    low, wide = jnp.bfloat16, jnp.float32
+    core_mate = (x * 2 + 1 - core, z * 2 + y)
+    y_mate = (x * 2 + core, z * 2 + 1 - y)
+    below = (x * 2 + core, lax.rem(z + DEPTH - 1, DEPTH) * 2 + y)
+    above = (x * 2 + core, lax.rem(z + 1, DEPTH) * 2 + y)
+    greet([core_mate, y_mate, below, above])
+    grads = Chain(grad_ref, grads_out, x, core, z, y, chain)
+    grads.first()
+
+    def pair_copy(piece):
+        return remote(kv_ref.at[piece], okv_ref.at[piece], kv_s, kv_r, piece, y_mate)
+
+    def piece_body(tokens, cos, first, second, normed, gate_part, up_part):
+        piece = pl.program_id(0)
+        hat, _ = normalised(tokens[0])
+        narrow = (hat * gain_ref[...] + shift_ref[...]).astype(low)
+        normed[0] = narrow
+        projected = dot_rows(narrow, inward_rows(wi_ref)) + bias_ref[...]
+        tables = (cos, first, second)
+        query = turned(projected[:, :HEAD_COLS], *tables, 1.0) * (HEAD_DIM**-0.5)
+        key = turned(projected[:, HEAD_COLS : 2 * HEAD_COLS], *tables, 1.0)
+        kv_ref[piece] = jnp.concatenate([key, projected[:, 2 * HEAD_COLS :]], 1).astype(low)
+        pair_copy(piece).start()
+        q_ref[piece] = query.astype(low)
+        both = dot_rows(narrow, wg_ref[...])
+        hidden = both.shape[1] // 2
+        gate, up = both[:, :hidden], both[:, hidden:]
+        gate_part[0] = gate
+        up_part[0] = up
+        hidden_ref[piece] = (gate * jax.nn.sigmoid(gate) * up).astype(low)
+
+        @pl.when(piece == PIECES - 2)
+        def _():
+            grads.second()
+
+    table_spec = pl.BlockSpec((1,) + cos_ref.shape[1:], lambda i: (i % DEPTH, 0, 0))
+    pltpu.emit_pipeline(
+        piece_body,
+        grid=(PIECES,),
+        in_specs=[piece_spec(pieces_ref.shape[-1])] + [table_spec] * 3,
+        out_specs=[piece_spec(r.shape[-1]) for r in (normed_out, gate_out, up_out)],
+    )(pieces_ref, cos_ref, first_ref, second_ref, normed_out, gate_out, up_out)
+
+    for b in range(2):
+        for j in range(DEPTH):
+            pair_copy(b * DEPTH + j).wait_recv()
+
+        def attend(t, carry):
+            attend_one(Heads(b, t, z, y, q_ref, kv_ref, okv_ref), att_ref)
+            return carry
+
+        lax.fori_loop(0, 2 * LOCAL_HEADS // 2, attend, 0)
+        if b == 0:
+            grads.third()
+
+    def core_copy(k):
+        return remote(core_send.at[k], core_recv.at[k], core_s, core_r, k, core_mate)
+
+    def term(piece):
+        return dot_rows(att_ref[piece], outward_rows(rows_ref)) + dot_rows(
+            hidden_ref[piece], down_rows(rows_ref)
+        )
+
+    def branch(i, carry):
+        k = DEPTH - 1 - i
+        core_send[k] = term(DEPTH + k).astype(low)
+        core_copy(k).start()
+        own = term(k)
+        core_copy(k).wait_recv()
+        both = own + core_recv[k].astype(wide)
+
+        @pl.when(k > 0)
+        def _():
+            terms[k - 1] = both.astype(low)
+
+        @pl.when(k == 0)
+        def _():
+            own_sum[...] = both
+
+        return carry
+
+    lax.fori_loop(0, DEPTH, branch, 0)
+    grads.fourth()
+    grads.end()
+    for piece in range(PIECES):
+        pair_copy(piece).wait_send()
+    for k in range(DEPTH):
+        core_copy(k).wait_send()
+
+
+def forward(pieces, own_grad, tables, gain, shift, bias, inward, gate_up, rows_out):
+    low, wide = jnp.bfloat16, jnp.float32
     width = pieces.shape[-1]
-    table_spec = pl.BlockSpec((1,) + tables[0].shape[1:], lambda i: (i % DEPTH, 0, 0))
+    hidden = gate_up.shape[1] // 2
+    anywhere = pl.BlockSpec(memory_space=pl.ANY)
+    inside = pl.BlockSpec(memory_space=pltpu.VMEM)
+    shape = jax.ShapeDtypeStruct
+    dma = pltpu.SemaphoreType.DMA
     return pl.pallas_call(
-        project_kernel,
-        grid=(PIECES,),
-        in_specs=[
-            piece_spec(width),
-            whole_spec((1, width)),
-            whole_spec((1, width)),
-            whole_spec(weight.shape),
-            whole_spec(bias.shape),
-            table_spec,
-            table_spec,
-            table_spec,
+        forward_kernel,
+        in_specs=[anywhere] * 5 + [inside] * 6,
+        out_specs=[anywhere] * 4 + [inside] * 7,
+        out_shape=[
+            shape((PIECES, ROWS, width), low),
+            shape((PIECES, ROWS, hidden), wide),
+            shape((PIECES, ROWS, hidden), wide),
+            shape((PIECES, ROWS, width), low),
+            shape((PIECES, ROWS, HEAD_COLS), low),
+            shape((PIECES, ROWS, 2 * HEAD_COLS), low),
+            shape((PIECES, ROWS, 2 * HEAD_COLS), low),
+            shape((PIECES, ROWS, hidden), low),
+            shape((PIECES, ROWS, HEAD_COLS), low),
+            shape((ROWS, width), wide),
+            shape((DEPTH - 1, ROWS, width), low),
         ],
-        out_specs=[piece_spec(width), piece_spec(HEAD_COLS), piece_spec(2 * HEAD_COLS)],
-        out_shape=[
-            jax.ShapeDtypeStruct((PIECES, ROWS, width), jnp.bfloat16),
-            jax.ShapeDtypeStruct((PIECES, ROWS, HEAD_COLS), jnp.bfloat16),
-            jax.ShapeDtypeStruct((PIECES, ROWS, 2 * HEAD_COLS), jnp.bfloat16),
-        ],
-        compiler_params=params(48),
-        cost_estimate=cost(2 * PIECES * ROWS * width * 3 * HEAD_COLS, 24 * MIB),
-        name="project",
-    )(pieces, gain, shift, weight, bias, *tables)
-
-
-def feed_kernel(n_ref, w_ref, gate_ref, up_ref, hidden_ref):
-    both = dot_rows(n_ref[0], w_ref[...])
-    hidden = both.shape[1] // 2
-    gate, up = both[:, :hidden], both[:, hidden:]
-    gate_ref[0] = gate
-    up_ref[0] = up
-    hidden_ref[0] = (gate * jax.nn.sigmoid(gate) * up).astype(jnp.bfloat16)
-
-
-def feed(normed, weight):
-    width = normed.shape[-1]
-    hidden = weight.shape[1] // 2
-    return pl.pallas_call(
-        feed_kernel,
-        grid=(PIECES,),
-        in_specs=[piece_spec(width), whole_spec(weight.shape)],
-        out_specs=[piece_spec(hidden)] * 3,
-        out_shape=[
-            jax.ShapeDtypeStruct((PIECES, ROWS, hidden), jnp.float32),
-            jax.ShapeDtypeStruct((PIECES, ROWS, hidden), jnp.float32),
-            jax.ShapeDtypeStruct((PIECES, ROWS, hidden), jnp.bfloat16),
-        ],
-        compiler_params=params(48),
-        cost_estimate=cost(4 * PIECES * ROWS * width * hidden, 28 * MIB),
-        name="feed",
-    )(normed, weight)
-
-
-def store_split(value, own_ref, other_ref):
-    late = pl.program_id(0) >= DEPTH
-
-    @pl.when(jnp.logical_not(late))
-    def _():
-        other_ref[0] = value
-
-    @pl.when(late)
-    def _():
-        own_ref[0] = value
-
-
-def other_first(width):
-    return pl.BlockSpec((1, ROWS, width), lambda i: ((i + DEPTH) % PIECES, 0, 0))
-
-
-def split_specs(width):
-    return [
-        pl.BlockSpec((1, ROWS, width), lambda i: (jnp.maximum(i - DEPTH, 0), 0, 0)),
-        pl.BlockSpec((1, ROWS, width), lambda i: (jnp.minimum(i, DEPTH - 1), 0, 0)),
-    ]
-
-
-def branch_kernel(a_ref, h_ref, w_ref, own_ref, other_ref):
-    term = dot_rows(a_ref[0], outward_rows(w_ref)) + dot_rows(h_ref[0], down_rows(w_ref))
-    store_split(term.astype(jnp.bfloat16), own_ref, other_ref)
-
-
-def branch_terms(attended, hidden, rows_out):
-    width = rows_out.shape[-1]
-    return pl.pallas_call(
-        branch_kernel,
-        grid=(PIECES,),
-        in_specs=[
-            other_first(HEAD_COLS),
-            other_first(hidden.shape[-1]),
-            whole_spec(rows_out.shape),
-        ],
-        out_specs=split_specs(width),
-        out_shape=[jax.ShapeDtypeStruct((DEPTH, ROWS, width), jnp.bfloat16)] * 2,
-        compiler_params=params(48),
-        cost_estimate=cost(2 * PIECES * ROWS * width * (HEAD_COLS + hidden.shape[-1]), 16 * MIB),
-        name="branch_terms",
-    )(attended, hidden, rows_out)
-
-
-def back_kernel(g_ref, gate_ref, up_ref, w_ref, a_ref, gu_ref):
-    grad = g_ref[0]
-    a_ref[0] = transposed_times(grad, outward_rows(w_ref)).astype(jnp.bfloat16)
-    hidden_grad = transposed_times(grad, down_rows(w_ref))
-    gate = gate_ref[0]
-    sig = jax.nn.sigmoid(gate)
-    silu = gate * sig
-    gate_grad = hidden_grad * up_ref[0] * (sig + silu * (1.0 - sig))
-    up_grad = hidden_grad * silu
-    gu_ref[0] = jnp.concatenate([gate_grad, up_grad], 1).astype(jnp.bfloat16)
-
-
-def back(grads, gate, up, rows_out):
-    width = rows_out.shape[-1]
-    hidden = gate.shape[-1]
-    return pl.pallas_call(
-        back_kernel,
-        grid=(PIECES,),
-        in_specs=[
-            piece_spec(width),
-            piece_spec(hidden),
-            piece_spec(hidden),
-            whole_spec(rows_out.shape),
-        ],
-        out_specs=[piece_spec(HEAD_COLS), piece_spec(2 * hidden)],
-        out_shape=[
-            jax.ShapeDtypeStruct((PIECES, ROWS, HEAD_COLS), jnp.bfloat16),
-            jax.ShapeDtypeStruct((PIECES, ROWS, 2 * hidden), jnp.bfloat16),
-        ],
-        compiler_params=params(48),
-        cost_estimate=cost(2 * PIECES * ROWS * width * (HEAD_COLS + hidden), 28 * MIB),
-        name="back",
-    )(grads, gate, up, rows_out)
+        scratch_shapes=[
+            pltpu.VMEM((DEPTH, ROWS, width), low),
+            pltpu.VMEM((DEPTH, ROWS, width), low),
+            dma((PIECES,)),
+            dma((PIECES,)),
+            dma((DEPTH,)),
+            dma((DEPTH,)),
+        ]
+        + chain_sems(),
+        compiler_params=params(60, collective_id=2, has_side_effects=True),
+        cost_estimate=cost(0, 64 * MIB),
+        name="forward",
+    )(pieces, own_grad, *tables, gain, shift, bias, inward, gate_up, rows_out)
 
 
 def pair_rows(block):
@@ -912,59 +917,56 @@
     return weights * (1.0 / jnp.sum(weights, axis=-1, keepdims=True))
 
 
-def both_columns(own_ref, other_ref, z, count):
-    blocks = []
-    for j in range(count):
-        at = (z + DEPTH - j) % DEPTH
-        blocks += [own_ref[0, at, 0], other_ref[0, at, 0]]
-    return jnp.concatenate(blocks, 0)
-
-
-def attend_kernel(place_ref, q_ref, k_ref, v_ref, ok_ref, ov_ref, out_ref):
-    z, y = place_ref[0], place_ref[1]
-    keys = both_columns(k_ref, ok_ref, z, DEPTH)
-    values = both_columns(v_ref, ov_ref, z, DEPTH)
-    size = keys.shape[0] // DEPTH
+class Heads:
+    def __init__(self, b, t, z, y, q_ref, kv_ref, okv_ref):
+        size = ROWS // 2
+        pair = 2 * HEAD_DIM
+        self.b, self.z, self.y = b, z, y
+        self.rows = pl.ds(pl.multiple_of((t // 2) * size, size), size)
+        self.lanes = pl.ds(pl.multiple_of((t % 2) * pair, pair), pair)
+        value_lanes = pl.ds(pl.multiple_of(HEAD_COLS + (t % 2) * pair, pair), pair)
+        self.q_ref = q_ref
+
+        def both(lanes):
+            blocks = []
+            for j in range(DEPTH):
+                place = (self.piece(j), self.rows, lanes)
+                blocks += [kv_ref[place], okv_ref[place]]
+            return jnp.concatenate(blocks, 0)
+
+        self.keys, self.values = both(self.lanes), both(value_lanes)
+
+    def piece(self, j):
+        return self.b * DEPTH + lax.rem(self.z + DEPTH - j, DEPTH)
+
+    def place(self, j):
+        return self.piece(j), self.rows, self.lanes
+
+    def queries(self, j):
+        return pair_rows(self.q_ref[self.place(j)])
+
+
+def attend_one(heads, out_ref):
     for j in range(DEPTH):
-        at = (z + DEPTH - j) % DEPTH
-        count = (j + 1) * size
-        probs = block_probs(pair_rows(q_ref[0, at, 0]), keys[:count], j, y)
-        out = dot_rows(probs.astype(jnp.bfloat16), values[:count])
-        out_ref[0, at, 0] = pair_lanes(out).astype(jnp.bfloat16)
-
-
-def attend_back_kernel(
-    place_ref,
-    q_ref,
-    k_ref,
-    v_ref,
-    ok_ref,
-    ov_ref,
-    grad_ref,
-    dq_ref,
-    dk_ref,
-    dv_ref,
-    odk_ref,
-    odv_ref,
-    key_sum,
-    value_sum,
-):
-    z, y = place_ref[0], place_ref[1]
-    keys = both_columns(k_ref, ok_ref, z, DEPTH)
-    values = both_columns(v_ref, ov_ref, z, DEPTH)
-    size = keys.shape[0] // DEPTH
-    half = size // 2
+        count = (j + 1) * ROWS
+        probs = block_probs(heads.queries(j), heads.keys[:count], j, heads.y)
+        out = dot_rows(probs.astype(jnp.bfloat16), heads.values[:count])
+        out_ref[heads.place(j)] = pair_lanes(out).astype(jnp.bfloat16)
+
+
+def attend_back_one(heads, grad_ref, dq_ref, dk_ref, dv_ref, odk_ref, odv_ref, key_sum, value_sum):
+    half = ROWS // 2
     for j in reversed(range(DEPTH)):
-        at = (z + DEPTH - j) % DEPTH
-        count = (j + 1) * size
-        queries = pair_rows(q_ref[0, at, 0])
-        grads = pair_rows(grad_ref[0, at, 0])
-        probs = block_probs(queries, keys[:count], j, y)
+        count = (j + 1) * ROWS
+        queries = heads.queries(j)
+        grads = pair_rows(grad_ref[heads.place(j)])
+        keys, values = heads.keys[:count], heads.values[:count]
+        probs = block_probs(queries, keys, j, heads.y)
         low = probs.astype(jnp.bfloat16)
-        prob_grad = transposed_times(grads, values[:count])
+        prob_grad = transposed_times(grads, values)
         delta = jnp.sum(low.astype(jnp.float32) * prob_grad, axis=-1, keepdims=True)
         score_grad = (probs * (prob_grad - delta)).astype(jnp.bfloat16)
-        dq_ref[0, at, 0] = pair_lanes(dot_rows(score_grad, keys[:count]))
+        dq_ref[heads.place(j)] = pair_lanes(dot_rows(score_grad, keys))
         key_term = times_transposed(score_grad, queries)
         value_term = times_transposed(low, grads)
         if j == DEPTH - 1:
@@ -974,72 +976,250 @@
             key_sum[:count] += key_term
             value_sum[:count] += value_term
     for j in range(DEPTH):
-        at = (z + DEPTH - j) % DEPTH
-        low = j * size
-        dk_ref[0, at, 0] = key_sum[low : low + half]
-        dv_ref[0, at, 0] = value_sum[low : low + half]
-        odk_ref[0, at, 0] = key_sum[low + half : low + size].astype(jnp.bfloat16)
-        odv_ref[0, at, 0] = value_sum[low + half : low + size].astype(jnp.bfloat16)
-
-
-def sequence_specs(seqs, length):
-    def spec(first):
-        return pl.BlockSpec(
-            (1, DEPTH, 1, length, 2 * HEAD_DIM), lambda b, s, p, place: (b, 0, s, 0, first + p)
+        low = j * ROWS
+        place = heads.place(j)
+        dk_ref[place] = key_sum[low : low + half]
+        dv_ref[place] = value_sum[low : low + half]
+        odk_ref[place] = key_sum[low + half : low + ROWS].astype(jnp.bfloat16)
+        odv_ref[place] = value_sum[low + half : low + ROWS].astype(jnp.bfloat16)
+
+
+def backward_kernel(
+    grads_ref,
+    gate_ref,
+    up_ref,
+    normed_ref,
+    pieces_ref,
+    q_ref,
+    kv_ref,
+    okv_ref,
+    hidden_ref,
+    att_ref,
+    rows_ref,
+    own_sum,
+    terms,
+    valid_ref,
+    gate_xs,
+    gate_xk,
+    gate_ys,
+    gate_yk,
+    heads_out,
+    hidden_out,
+    gu_ref,
+    dq_ref,
+    dk_ref,
+    dv_ref,
+    got_dk,
+    got_dv,
+    layer_out,
+    attended_grad,
+    odk_ref,
+    odv_ref,
+    key_sum,
+    value_sum,
+    z_recv,
+    token_rows,
+    z_s,
+    z_r,
+    pair_s,
+    pair_r,
+    local_sem,
+):
+    x, core, z, y = coordinates()
+    low, wide = jnp.bfloat16, jnp.float32
+    y_mate = (x * 2 + core, z * 2 + 1 - y)
+
+    def z_mate(turn):
+        return (x * 2 + core, lax.rem(z + turn, DEPTH) * 2 + y)
+
+    greet([y_mate] + [z_mate(turn) for turn in range(1, DEPTH)])
+    scattered = [
+        remote(terms.at[k - 1], z_recv.at[k - 1], z_s, z_r, k - 1, z_mate(DEPTH - k))
+        for k in range(1, DEPTH)
+    ]
+    for copy in scattered:
+        copy.start()
+    own_tokens = pltpu.make_async_copy(pieces_ref.at[0], token_rows, local_sem)
+    own_tokens.start()
+
+    def piece_body(grad_part, gate_part, up_part):
+        piece = pl.program_id(0)
+        grad = grad_part[0]
+        attended_grad[piece] = transposed_times(grad, outward_rows(rows_ref)).astype(low)
+        hidden_grad = transposed_times(grad, down_rows(rows_ref))
+        gate = gate_part[0]
+        sig = jax.nn.sigmoid(gate)
+        silu = gate * sig
+        gate_grad = hidden_grad * up_part[0] * (sig + silu * (1.0 - sig))
+        up_grad = hidden_grad * silu
+        gu_ref[piece] = jnp.concatenate([gate_grad, up_grad], 1).astype(low)
+
+    pltpu.emit_pipeline(
+        piece_body,
+        grid=(PIECES,),
+        in_specs=[piece_spec(r.shape[-1]) for r in (grads_ref, gate_ref, up_ref)],
+    )(grads_ref, gate_ref, up_ref)
+
+    def pair_copies(b, t):
+        size, pair = ROWS // 2, 2 * HEAD_DIM
+        at = (
+            pl.ds(b * DEPTH, DEPTH),
+            pl.ds(pl.multiple_of((t // 2) * size, size), size),
+            pl.ds(pl.multiple_of((t % 2) * pair, pair), pair),
         )
-
-    return spec(0), spec(LOCAL_HEADS // 2)
-
-
-def as_sequences(value, seqs):
-    return value.reshape(2, DEPTH, seqs, ROWS // seqs, value.shape[-1])
-
-
-def attend(place, queries, pairs, other_pairs, seqs):
-    queries, pairs, other_pairs = (as_sequences(v, seqs) for v in (queries, pairs, other_pairs))
-    first, second = sequence_specs(seqs, ROWS // seqs)
-    out = pl.pallas_call(
-        attend_kernel,
-        grid_spec=pltpu.PrefetchScalarGridSpec(
-            num_scalar_prefetch=1,
-            grid=(2, seqs, LOCAL_HEADS // 2),
-            in_specs=[first, first, second, first, second],
-            out_specs=first,
-        ),
-        out_shape=jax.ShapeDtypeStruct(queries.shape, jnp.bfloat16),
-        compiler_params=params(48),
-        cost_estimate=cost(4 * 8 * 2 * 2 * 256 * 2560 * 128, 8 * MIB, 8 * 256 * 2560),
-        name="attend",
-    )(place, queries, pairs, pairs, other_pairs, other_pairs)
-    return out.reshape(PIECES, ROWS, HEAD_COLS)
-
-
-def attend_back(place, queries, pairs, other_pairs, grads, seqs):
-    queries, pairs, other_pairs, grads = (
-        as_sequences(v, seqs) for v in (queries, pairs, other_pairs, grads)
-    )
-    length = ROWS // seqs
-    first, second = sequence_specs(seqs, length)
-    wide = jax.ShapeDtypeStruct(queries.shape, jnp.float32)
-    narrow = jax.ShapeDtypeStruct(queries.shape, jnp.bfloat16)
-    outs = pl.pallas_call(
-        attend_back_kernel,
-        grid_spec=pltpu.PrefetchScalarGridSpec(
-            num_scalar_prefetch=1,
-            grid=(2, seqs, LOCAL_HEADS // 2),
-            in_specs=[first, first, second, first, second, first],
-            out_specs=[first] * 5,
-            scratch_shapes=[
-                pltpu.VMEM((2 * DEPTH * length, 2 * HEAD_DIM), jnp.float32),
-                pltpu.VMEM((2 * DEPTH * length, 2 * HEAD_DIM), jnp.float32),
-            ],
-        ),
-        out_shape=[wide, wide, wide, narrow, narrow],
-        compiler_params=params(48),
-        cost_estimate=cost(10 * 8 * 2 * 2 * 256 * 2560 * 128, 16 * MIB, 8 * 256 * 2560),
-        name="attend_back",
-    )(place, queries, pairs, pairs, other_pairs, other_pairs, grads)
-    return [v.reshape(PIECES, ROWS, HEAD_COLS) for v in outs]
+        number = b * DEPTH + t
+        return (
+            remote(odk_ref.at[at], got_dk.at[at], pair_s, pair_r, (0, number), y_mate),
+            remote(odv_ref.at[at], got_dv.at[at], pair_s, pair_r, (1, number), y_mate),
+        )
+
+    def attend_back(i, carry):
+        b, t = i // DEPTH, i % DEPTH
+        heads = Heads(b, t, z, y, q_ref, kv_ref, okv_ref)
+        attend_back_one(
+            heads, attended_grad, dq_ref, dk_ref, dv_ref, odk_ref, odv_ref, key_sum, value_sum
+        )
+        for copy in pair_copies(b, t):
+            copy.start()
+        return carry
+
+    lax.fori_loop(0, PIECES, attend_back, 0)
+
+    total, width = normed_ref.shape
+    size = width // PIECES
+    columns = gu_ref.shape[-1]
+    cut = gate_xs.shape[-1]
+
+    def right(first, last):
+        return gu_ref[...].reshape(total, columns)[:, first:last]
+
+    def whole_body(left, out):
+        out[0] = times_transposed(left[...], right(0, cut)).astype(out.dtype)
+
+    def split_body(left, keep, send):
+        split_rows(times_transposed(left[...], right(cut, columns)), y, keep, send)
+
+    def from_block(base):
+        return pl.BlockSpec((total, size), lambda i: (0, base + i))
+
+    def block_of(array):
+        return pl.BlockSpec((1,) + array.shape[1:], lambda i: (i, 0, 0))
+
+    pltpu.emit_pipeline(
+        whole_body,
+        grid=(DEPTH,),
+        in_specs=[from_block((1 - x) * DEPTH)],
+        out_specs=[block_of(gate_xs)],
+    )(normed_ref, gate_xs)
+    pltpu.emit_pipeline(
+        split_body,
+        grid=(PIECES,),
+        in_specs=[from_block(0)],
+        out_specs=[block_of(gate_yk), block_of(gate_ys)],
+    )(normed_ref, gate_yk, gate_ys)
+    pltpu.emit_pipeline(
+        whole_body,
+        grid=(DEPTH,),
+        in_specs=[from_block(x * DEPTH)],
+        out_specs=[block_of(gate_xk)],
+    )(normed_ref, gate_xk)
+
+    flat_grads = grads_ref.reshape(total, width)
+    wide_size = 2 * size
+
+    def rows_body(right, heads, hidden):
+        grad = right[...]
+        attended = att_ref[...].reshape(total, HEAD_COLS)
+        term = times_transposed(attended, grad).astype(low)
+        heads[...] = term.reshape(heads.shape)
+        hidden_rows = hidden_ref[...].reshape(total, hidden_ref.shape[-1])
+        term = times_transposed(hidden_rows, grad).astype(low)
+        hidden[...] = term.reshape(hidden.shape)
+
+    def column_block(array):
+        return pl.BlockSpec(array.shape[:2] + (wide_size,), lambda i: (0, 0, i))
+
+    pltpu.emit_pipeline(
+        rows_body,
+        grid=(width // wide_size,),
+        in_specs=[pl.BlockSpec((total, wide_size), lambda i: (0, i))],
+        out_specs=[column_block(heads_out), column_block(hidden_out)],
+    )(flat_grads, heads_out, hidden_out)
+
+    own_tokens.wait()
+    for copy in scattered:
+        copy.wait_recv()
+    for first in range(0, ROWS, 64):
+        rows = pl.ds(first, 64)
+        branch = own_sum[rows]
+        for k in range(DEPTH - 1):
+            branch = branch + z_recv[k, rows].astype(wide)
+        layer_out[rows] = (token_rows[rows].astype(wide) + valid_ref[rows] * branch).astype(low)
+
+    for b in range(2):
+        for t in range(DEPTH):
+            for copy in pair_copies(b, t):
+                copy.wait_recv()
+                copy.wait_send()
+    for copy in scattered:
+        copy.wait_send()
+
+
+def backward(
+    grads, gate, up, normed, pieces, queries, pairs, other_pairs, hidden, attended, rows_out,
+    own_sum, terms, valid
+):
+    low, wide = jnp.bfloat16, jnp.float32
+    width = pieces.shape[-1]
+    each = hidden.shape[-1]
+    columns = 2 * each
+    cut = -(-columns // 256) * 128
+    rows = width // 32
+    head_rows = HEAD_DIM
+    anywhere = pl.BlockSpec(memory_space=pl.ANY)
+    inside = pl.BlockSpec(memory_space=pltpu.VMEM)
+    shape = jax.ShapeDtypeStruct
+    dma = pltpu.SemaphoreType.DMA
+    return pl.pallas_call(
+        backward_kernel,
+        in_specs=[anywhere] * 5 + [inside] * 9,
+        out_specs=[anywhere] * 6 + [inside] * 7,
+        out_shape=[
+            shape((DEPTH, 4 * rows, cut), low),
+            shape((DEPTH, 4 * rows, cut), wide),
+            shape((PIECES, 2 * rows, columns - cut), low),
+            shape((PIECES, 2 * rows, columns - cut), wide),
+            shape((4, head_rows, width), low),
+            shape((4, each // 4, width), low),
+            shape((PIECES, ROWS, columns), low),
+            shape((PIECES, ROWS, HEAD_COLS), wide),
+            shape((PIECES, ROWS, HEAD_COLS), wide),
+            shape((PIECES, ROWS, HEAD_COLS), wide),
+            shape((PIECES, ROWS, HEAD_COLS), low),
+            shape((PIECES, ROWS, HEAD_COLS), low),
+            shape((ROWS, width), low),
+        ],
+        scratch_shapes=[
+            pltpu.VMEM((PIECES, ROWS, HEAD_COLS), low),
+            pltpu.VMEM((PIECES, ROWS, HEAD_COLS), low),
+            pltpu.VMEM((PIECES, ROWS, HEAD_COLS), low),
+            pltpu.VMEM((DEPTH * ROWS, 2 * HEAD_DIM), wide),
+            pltpu.VMEM((DEPTH * ROWS, 2 * HEAD_DIM), wide),
+            pltpu.VMEM((DEPTH - 1, ROWS, width), low),
+            pltpu.VMEM((ROWS, width), low),
+            dma((DEPTH - 1,)),
+            dma((DEPTH - 1,)),
+            dma((2, PIECES)),
+            dma((2, PIECES)),
+            dma(()),
+        ],
+        compiler_params=params(62, collective_id=3, has_side_effects=True),
+        cost_estimate=cost(0, 64 * MIB),
+        name="backward",
+    )(
+        grads, gate, up, normed, pieces, queries, pairs, other_pairs, hidden, attended, rows_out,
+        own_sum, terms, valid
+    )
 
 
 def finish_kernel(
@@ -1116,9 +1296,7 @@
     vec_r,
     local_sems,
 ):
-    bucket, blk = lax.axis_index("bucket"), lax.axis_index("blk")
-    x, core = bucket // 2, bucket % 2
-    z, y = blk // 2, blk % 2
+    x, core, z, y = coordinates()
     low = jnp.bfloat16
     wide = jnp.float32
 
@@ -1132,13 +1310,7 @@
     def target(flip, turn):
         return (core + flip) % 2, (z + turn) % DEPTH
 
-    barrier = pltpu.get_barrier_semaphore()
-    greeted = [device(x, *target(*m), y) for m in members] + [x_mate, y_mate]
-    for mate in greeted:
-        pl.semaphore_signal(
-            barrier, inc=1, device_id=mate, device_id_type=pl.DeviceIdType.MESH
-        )
-    pl.semaphore_wait(barrier, len(greeted))
+    greet([device(x, *target(*m), y) for m in members] + [x_mate, y_mate])
 
     started = []
 
@@ -1495,8 +1667,7 @@
 
 
 def finish(
-    parts, got_dk, got_dv, gate_up_grad, pieces, tables, normed, gate_up, heads, hidden, weights,
-    gain, cot
+    parts, gate_up_grad, pieces, tables, normed, gate_up, heads, hidden, weights, gain, cot
 ):
     low, wide = jnp.bfloat16, jnp.float32
     width = pieces.shape[-1]
@@ -1576,8 +1747,6 @@
         name="finish",
     )(
         *parts,
-        got_dk,
-        got_dv,
         gate_up_grad,
         pieces,
         *tables,
@@ -1617,60 +1786,6 @@
         cost_estimate=cost(0, 4 * MIB),
         name="place_rows",
     )(value)
-
-
-def rows_kernel(first, last, place_ref, left_ref, right_ref, out_ref):
-    term = times_transposed(left_ref[...], right_ref[:, first:last])
-    out_ref[0] = term.astype(out_ref.dtype)
-
-
-def split_rows_kernel(first, last, place_ref, left_ref, right_ref, keep_ref, send_ref):
-    y = place_ref[1]
-    term = times_transposed(left_ref[...], right_ref[:, first:last])
-    split_rows(term, y, keep_ref, send_ref)
-
-
-def weight_grad(place, left, right, first, last, part):
-    total, width = left.shape
-    columns = last - first
-    blocks = PIECES if part == "split" else PIECES // 2
-    if part == "split":
-        where = lambda i, place: (0, i)
-    elif part == "keep":
-        where = lambda i, place: (0, place[2] * DEPTH + i)
-    else:
-        where = lambda i, place: (0, (1 - place[2]) * DEPTH + i)
-    size = width // PIECES
-    high = size // 2 if part == "split" else size
-    spec = pl.BlockSpec((1, high, columns), lambda i, place: (i, 0, 0))
-    shape = (blocks, high, columns)
-    if part == "split":
-        specs = [spec, spec]
-        shapes = [
-            jax.ShapeDtypeStruct(shape, jnp.float32),
-            jax.ShapeDtypeStruct(shape, jnp.bfloat16),
-        ]
-    else:
-        specs = spec
-        shapes = jax.ShapeDtypeStruct(shape, jnp.float32 if part == "keep" else jnp.bfloat16)
-    return pl.pallas_call(
-        functools.partial(
-            split_rows_kernel if part == "split" else rows_kernel, first, last
-        ),
-        grid_spec=pltpu.PrefetchScalarGridSpec(
-            num_scalar_prefetch=1,
-            grid=(blocks,),
-            in_specs=[
-                pl.BlockSpec((total, size), where),
-                pl.BlockSpec(right.shape, lambda i, place: (0, 0)),
-            ],
-            out_specs=specs,
-        ),
-        out_shape=shapes,
-        compiler_params=params(48),
-        cost_estimate=cost(2 * total * size * blocks * columns, 10 * MIB),
-        name="weight_grad_" + part,
-    )(place, left, right)
 
 
 def lane_tables(positions):
@@ -1701,8 +1816,7 @@
 ):
     group_len, seqs, width = tokens.shape[1:]
     bucket, blk = lax.axis_index("bucket"), lax.axis_index("blk")
-    x, core = bucket // 2, bucket % 2
-    z, y = blk // 2, blk % 2
+    _, core, z, y = coordinates()
 
     own_rows = inward_weight.shape[0]
     hidden_each = gate_up_weight.shape[1] // (2 * 2 * 2 * DEPTH)
@@ -1750,62 +1864,55 @@
 
     position = blk * group_len + jnp.arange(group_len, dtype=jnp.int32)
     valid = (position[None, :] < lengths[0][:, None]).astype(jnp.float32)[..., None]
-    own_cotangent = jnp.transpose(cotangent[0], (1, 0, 2)).astype(jnp.float32)
-    own_grad = (own_cotangent * valid).astype(jnp.bfloat16)
-    grads = after(own_grad.reshape(ROWS, width), pieces)
-    grads = jnp.stack(gather_pieces(grads))
-
+    own_cotangent = jnp.transpose(cotangent[0], (1, 0, 2))
+    own_grad = (own_cotangent.astype(jnp.float32) * valid).astype(jnp.bfloat16)
     turns = (z - jnp.arange(DEPTH, dtype=jnp.int32)) % DEPTH
     tables = lane_tables(
         ((2 * turns + y) * group_len)[:, None] + jnp.arange(group_len, dtype=jnp.int32)
     )
-    place = jnp.stack([z, y, x]).astype(jnp.int32)
-
-    normed, queries, pairs = project(pieces, gain, shift, inward, own_bias, tables)
-    other_pairs = lax.ppermute(pairs, "blk", ACROSS_Y)
-    gate, up, hidden = feed(normed, gate_up)
-    attended = attend(place, after(queries, hidden), pairs, other_pairs, seqs)
-    branch_own, branch_other = branch_terms(attended, hidden, rows_out)
-    branch_sums = core_sums(branch_own, branch_other)
-    branch_sums = list(lax.optimization_barrier((*branch_sums, grads)))[:DEPTH]
-    branch = scatter_pieces(branch_sums)
-    branch = branch.reshape(seqs, group_len, width)
-    inputs = own_tokens.astype(jnp.float32)
-    layer_out = (inputs + valid * branch).astype(jnp.bfloat16)
-
-    attended_grad, gate_up_grad = back(after(grads, branch_own), gate, up, rows_out)
-    attended_grad = after(attended_grad, *branch_sums)
-    dq, dk, dv, other_dk, other_dv = attend_back(
-        place, queries, pairs, other_pairs, attended_grad, seqs
-    )
-    got_dk = lax.ppermute(other_dk, "blk", ACROSS_Y)
-    got_dv = lax.ppermute(other_dv, "blk", ACROSS_Y)
-    total = PIECES * ROWS
-    flat_normed = after(normed, other_dk).reshape(total, width)
-    flat_grads = after(grads, other_dk).reshape(total, width)
-
-    right = gate_up_grad.reshape(total, -1)
-    columns = right.shape[1]
-    cut = -(-columns // 256) * 128
-    gate_up_send = weight_grad(place, flat_normed, right, 0, cut, "send")
-    gate_up_kept, gate_up_sent = weight_grad(place, flat_normed, right, cut, columns, "split")
-    gate_up_keep = weight_grad(place, flat_normed, right, 0, cut, "keep")
-    heads_term = times_transposed(attended.reshape(total, -1), flat_grads).astype(jnp.bfloat16)
-    hidden_term = times_transposed(hidden.reshape(total, -1), flat_grads).astype(jnp.bfloat16)
+
+    normed, gate, up, grads, queries, pairs, other_pairs, hidden, attended, own_sum, terms = forward(
+        pieces,
+        own_grad.reshape(ROWS, width),
+        tables,
+        gain,
+        shift,
+        own_bias,
+        inward,
+        gate_up,
+        rows_out,
+    )
+    normed = normed.reshape(PIECES * ROWS, width)
+    gate_xs, gate_xk, gate_ys, gate_yk, heads_term, hidden_term, gate_up_grad, *parts, layer_out = (
+        backward(
+            grads,
+            gate,
+            up,
+            normed,
+            pieces,
+            queries,
+            pairs,
+            other_pairs,
+            hidden,
+            attended,
+            rows_out,
+            own_sum,
+            terms,
+            valid.reshape(ROWS, 1),
+        )
+    )
     tokens_grad, outward_sum, down_sum, gate_up_rows, inward_rows_own, vectors = finish(
-        (after(dq, layer_out), dk, dv),
-        got_dk,
-        got_dv,
+        parts,
         gate_up_grad,
         pieces,
         tables,
-        normed.reshape(total, width),
-        (gate_up_send, gate_up_keep, gate_up_sent, gate_up_kept),
+        normed,
+        (gate_xs, gate_xk, gate_ys, gate_yk),
         heads_term.reshape(2, 2, -1, width),
         hidden_term.reshape(2, 2, -1, width),
         (inward, gate_up),
         gain,
-        jnp.transpose(cotangent[0], (1, 0, 2)).reshape(ROWS, width),
+        own_cotangent.reshape(ROWS, width),
     )
     gate_up_sum = place_rows(gate_up_rows, 4)
     inward_sum = place_rows(inward_rows_own, 6)

time: 592 us -> 550 us (0.929)
  Pallas kernels: 449 us -> 499 us
  waiting for transfers between devices: 31.9 us -> 0 us
  local copies, waits for them, and re-layouts: 48.8 us -> 30.1 us
  matrix products: 17.8 us -> 0 us
  other arithmetic: 26.5 us -> 8.92 us
  starting transfers between devices: 11.5 us -> 0 us
    pallas_call x9 -> x2, Pallas kernels: 149 us -> 197 us  [the longest x1 107 us: backward(): pl.pallas_call(backward_kernel, in_specs=[anywhere] * 5 + [inside] * 9, o...]
    ppermute x14 -> x0, waiting for transfers between devices: 31.9 us -> none  [the longest x1 18.1 us: shards_grouped(): other_pairs = lax.ppermute(pairs, 'blk', ACROSS_Y)]
    dot_general x2 -> x0, matrix products: 17.8 us -> none  [times_transposed(): lax.dot_general(left, right, (((0,), (0,)), ((), ())), preferred_element_...]
    unnamed x80 -> x39, local copies, waits for them, and re-layouts: 29.8 us -> 13 us
    ppermute x14 -> x0, starting transfers between devices: 11.5 us -> none  [the longest x3 3.38 us: scatter_pieces(): got = lax.ppermute(sums[step], 'blk', around(-step))]
    convert_element_type x3 -> x1, other arithmetic: 9.4 us -> 1.47 us  [shards_grouped(): own_grad = (own_cotangent.astype(jnp.float32) * valid).astype(jnp.bfloat16)]
    another operation x6 -> x5, other arithmetic: 6.59 us -> 0.13 us
  transfers between devices with their start and end apart: 14 -> 0, of which waited for: 3 -> 0; matrix products, arithmetic and copies ran while one was open for 5% -> 0% of each run, Pallas kernels for 22% -> 0%
where the time goes in v4:
time: 550 us; the launch traced here: 539 us
  Pallas kernels  499 us (91%)
  local copies, waits for them, and re-layouts  30.1 us (5%)
  other arithmetic  8.92 us (2%)
    pallas_call x1, Pallas kernels, finish(): pl.pallas_call(finish_kernel, in_specs=[anywhere] * 17 + [inside] * 4, ou...  166 us
    pallas_call x1, Pallas kernels, gather(): pl.pallas_call(gather_kernel, in_specs=[anywhere] * 4, out_specs=[anywher...  132 us
    pallas_call x1, Pallas kernels, backward(): pl.pallas_call(backward_kernel, in_specs=[anywhere] * 5 + [inside] * 9, o...  107 us
    pallas_call x1, Pallas kernels, forward(): pl.pallas_call(forward_kernel, in_specs=[anywhere] * 5 + [inside] * 6, ou...  90.6 us
    unnamed x39, local copies, waits for them, and re-layouts  13 us

profile of v4, /device:TPU:11, one launch (start us, length us, event | category | flops | bytes accessed | tf_op | source)
XLA Modules:
  0.0 539.2 jit_solution(3810683186024530199)
XLA Ops:
  0.7 2.0 convert_element_type.58
  2.6 2.4 reshape.263
  5.1 1.2 copy.52
  6.3 1.1 reshape.264.wg_ref
  7.4 1.5 convert_element_type.57
  8.9 0.0 copy-start.16
  8.9 0.0 copy-start.17
  8.9 0.0 copy-start.15
  9.0 0.6 reshape.261
  9.5 0.6 copy.55
  10.1 0.4 reshape.262
  10.5 0.0 copy-done.16
  10.5 0.0 copy-start.6
  10.6 0.0 copy-done.15
  10.6 0.1 fusion.7
  10.7 0.0 copy-start.11
  10.7 0.1 pad_maximum_fusion.wi_ref
  10.8 1.1 copy-done.6
  11.9 0.1 convert.21
  12.0 0.0 copy-done.11
  12.1 0.1 pad_maximum_fusion.1.ro_ref
  12.2 1.0 copy-done.8
  13.1 0.3 copy.37
  13.5 132.3 %gather.1 = (bf16[8,256,2048]{2,1,0:T(8,128)(2,1)}, bf16[2,2,4,2,80,768]{5,4,3,2,1,0:T(8,128)(2,1)S(1)}, bf16[2,2,4,2,64,1408]{5,4,3,2,1,0:T(8,128)(2,1)S(1)}, bf16[2,2,240,2048]{3,2,1,0:T(8,128)(2,1)S(1)}) custom-call(bf16[256,2048]{1,0:T(8,128)(2,1)S(1)} %bitcast.63, bf16[2,4,80,768]{3,2,1,0:T(8,128)(2,1)S(1)} %pad_maximum_fusion.wi_ref, ...), custom_call_target="tpu_custom_call" | custom-call | bytes 1048576 | tf_op jit(solution)/shard_map/gather/pallas_call | solution.py:672
  145.8 2.4 copy-done
  148.3 1.9 copy-done.2
  150.2 1.8 copy-done.1
  152.0 0.3 convert_reduce_fusion
  152.3 0.1 reshape.289
  152.4 0.1 reshape.268
  152.5 0.1 slice.58
  152.7 0.1 reshape.271
  152.8 0.1 reshape.272
  152.9 0.6 reshape.275.bias_ref
  153.5 0.1 add_convert_fusion
  153.6 3.1 fusion
  156.7 0.1 fusion.22
  156.8 0.7 reshape.266.gain_ref
  157.5 0.1 compare_convert_fusion
  157.5 1.5 multiply_convert_fusion
  159.0 0.7 reshape.267.shift_ref
  159.7 90.6 %forward.1 = (bf16[8,256,2048]{2,1,0:T(8,128)(2,1)}, f32[8,256,704]{2,1,0:T(8,128)}, f32[8,256,704]{2,1,0:T(8,128)}, bf16[8,256,2048]{2,1,0:T(8,128)(2,1)}, bf16...) custom-call(bf16[8,256,2048]{2,1,0:T(8,128)(2,1)} %get-tuple-element, ...), custom_call_target="tpu_custom_call" | custom-call | bytes 1048576 | tf_op jit(solution)/shard_map/forward/pallas_call | solution.py:861
  250.2 0.8 copy.41.valid_ref
  251.0 106.5 %backward.1 = (bf16[4,256,768]{2,1,0:T(8,128)(2,1)}, f32[4,256,768]{2,1,0:T(8,128)}, bf16[8,128,640]{2,1,0:T(8,128)(2,1)}, f32[8,128,640]{2,1,0:T(8,128)}, bf16[...) custom-call(bf16[8,256,2048]{2,1,0:T(8,128)(2,1)} %get-tuple-element, ...), custom_call_target="tpu_custom_call" | custom-call | bytes 1048576 | tf_op jit(solution)/shard_map/backward/pallas_call | solution.py:1183
  357.6 1.3 copy.40
  358.9 166.1 %finish.1 = (bf16[256,2048]{1,0:T(8,128)(2,1)}, f32[64,2048]{1,0:T(8,128)}, f32[176,2048]{1,0:T(8,128)}, bf16[8,64,1408]{2,1,0:T(8,128)(2,1)}, bf16[8,64,768]{2,...) custom-call(f32[8,256,256]{2,1,0:T(8,128)} %get-tuple-element.59.dq_, ...), custom_call_target="tpu_custom_call" | custom-call | bytes 1048576 | tf_op jit(solution)/shard_map/finish/pallas_call | solution.py:1717
  525.0 0.0 copy-start.3
  525.0 1.4 copy-done.3
  526.4 2.0 place_rows.3
  528.4 1.0 slice.64
  529.4 0.1 reshape_squeeze.8
  529.5 0.1 reshape.287
  529.6 0.1 reshape.288
  529.7 0.6 constant_dynamic-slice_fusion
  530.3 1.2 place_rows.2
  531.5 0.0 copy-done.10
  531.5 2.0 copy.53
  533.6 0.1 squeeze.41
  533.7 0.5 fusion.16
  534.2 0.1 squeeze.43
  534.3 0.5 fusion.17
  534.8 2.0 copy.54
  536.9 0.8 copy.59
  537.7 1.1 copy.60
  (41 shorter events, 0.2 us)
Async XLA Ops:
  8.9 1.6 copy-start.16
  8.9 1.6 copy-start.17
  8.9 1.6 copy-start.15
  10.5 1.4 copy-start.6
  10.7 1.3 copy-start.11
  11.9 1.3 copy-start.8
  145.8 2.5 copy-start
  148.3 1.9 copy-start.2
  150.2 1.9 copy-start.1
  150.2 7.3 %copy-start.14 = (s32[1,2]{1,0:T(1,128)S(1)}, s32[1,2]{1,0:T(1,128)}, u32[]{:S(2)}) copy-start(s32[1,2]{1,0:T(1,128)} %param.11) | copy-start | bytes 28
  150.2 7.3 %copy-start.5 = (bf16[1,128,2,2048]{3,2,1,0:T(2,128)(2,1)S(1)}, bf16[1,128,2,2048]{3,2,1,0:T(2,128)(2,1)}, u32[]{:S(2)}) copy-start(bf16[1,128,2,2048]{3,2,1,0:T(2,128)(2,1)} %param.19) | copy-start | bytes 3145732
  525.0 1.4 copy-start.3
  526.4 3.9 copy-start.4
  528.4 3.2 copy-start.10
  530.3 3.3 copy-start.13
  530.3 4.5 copy-start.9
  533.6 3.3 copy-start.12
  533.6 4.1 copy-start.7

commit v5 on v4

--- a/solution.py
+++ b/solution.py
@@ -357,6 +357,7 @@
 PIECES = 2 * DEPTH
 ROWS = 256
 EXTRA = 16
+GATE_STEP = 4
 LOCAL_HEADS = 4
 HEAD_COLS = LOCAL_HEADS * HEAD_DIM
 
@@ -404,15 +405,23 @@
     return pl.BlockSpec(shape, lambda i: (0,) * len(shape))
 
 
-def remote(src, dst, sends, recvs, index, device):
+def remote_to(src, dst, send_sem, recv_sem, device):
     return pltpu.make_async_remote_copy(
         src_ref=src,
         dst_ref=dst,
-        send_sem=sends.at[index],
-        recv_sem=recvs.at[index],
+        send_sem=send_sem,
+        recv_sem=recv_sem,
         device_id=device,
         device_id_type=pl.DeviceIdType.MESH,
     )
+
+
+def remote(src, dst, sends, recvs, index, device):
+    return remote_to(src, dst, sends.at[index], recvs.at[index], device)
+
+
+def select(i, first, second, third):
+    return jnp.where(i == 0, first, jnp.where(i == 1, second, jnp.where(i == 2, third, 0)))
 
 
 class Chain:
@@ -1003,6 +1012,12 @@
     gate_xk,
     gate_ys,
     gate_yk,
+    gate_xr,
+    gate_yr,
+    gate_y2s,
+    gate_x2s,
+    gate_own_x,
+    gate_own_y,
     heads_out,
     hidden_out,
     gu_ref,
@@ -1023,6 +1038,8 @@
     z_r,
     pair_s,
     pair_r,
+    stage_s,
+    stage_r,
     local_sem,
 ):
     x, core, z, y = coordinates()
@@ -1032,7 +1049,8 @@
     def z_mate(turn):
         return (x * 2 + core, lax.rem(z + turn, DEPTH) * 2 + y)
 
-    greet([y_mate] + [z_mate(turn) for turn in range(1, DEPTH)])
+    x_mate = (2 - x * 2 + core, z * 2 + y)
+    greet([x_mate, y_mate] + [z_mate(turn) for turn in range(1, DEPTH)])
     scattered = [
         remote(terms.at[k - 1], z_recv.at[k - 1], z_s, z_r, k - 1, z_mate(DEPTH - k))
         for k in range(1, DEPTH)
@@ -1094,7 +1112,8 @@
         return gu_ref[...].reshape(total, columns)[:, first:last]
 
     def whole_body(left, out):
-        out[0] = times_transposed(left[...], right(0, cut)).astype(out.dtype)
+        term = times_transposed(left[...], right(0, cut)).astype(out.dtype)
+        out[...] = term.reshape(out.shape)
 
     def split_body(left, keep, send):
         split_rows(times_transposed(left[...], right(cut, columns)), y, keep, send)
@@ -1103,7 +1122,7 @@
         return pl.BlockSpec((total, size), lambda i: (0, base + i))
 
     def block_of(array):
-        return pl.BlockSpec((1,) + array.shape[1:], lambda i: (i, 0, 0))
+        return pl.BlockSpec((2,) + array.shape[1:], lambda i: (i,) + (0,) * (len(array.shape) - 1))
 
     pltpu.emit_pipeline(
         whole_body,
@@ -1111,18 +1130,16 @@
         in_specs=[from_block((1 - x) * DEPTH)],
         out_specs=[block_of(gate_xs)],
     )(normed_ref, gate_xs)
+    gate_x = remote(gate_xs, gate_xr, stage_s, stage_r, 0, x_mate)
+    gate_x.start()
     pltpu.emit_pipeline(
         split_body,
         grid=(PIECES,),
         in_specs=[from_block(0)],
         out_specs=[block_of(gate_yk), block_of(gate_ys)],
     )(normed_ref, gate_yk, gate_ys)
-    pltpu.emit_pipeline(
-        whole_body,
-        grid=(DEPTH,),
-        in_specs=[from_block(x * DEPTH)],
-        out_specs=[block_of(gate_xk)],
-    )(normed_ref, gate_xk)
+    gate_y = remote(gate_ys, gate_yr, stage_s, stage_r, 1, y_mate)
+    gate_y.start()
 
     flat_grads = grads_ref.reshape(total, width)
     wide_size = 2 * size
@@ -1146,6 +1163,51 @@
         out_specs=[column_block(heads_out), column_block(hidden_out)],
     )(flat_grads, heads_out, hidden_out)
 
+    pltpu.emit_pipeline(
+        whole_body,
+        grid=(DEPTH,),
+        in_specs=[from_block(x * DEPTH)],
+        out_specs=[block_of(gate_xk)],
+    )(normed_ref, gate_xk)
+
+    def sums_body(xk, xr, yk, yr, yk_own, yr_own, y2s, x2s, own_x, own_y):
+        y2s[0] = (xk[0, 1 - y] + xr[0, 1 - y].astype(wide)).astype(low)
+        own_x[0] = xk[0, y] + xr[0, y].astype(wide)
+        x2s[0] = (yk[0] + yr[0].astype(wide)).astype(low)
+        own_y[0] = yk_own[0] + yr_own[0].astype(wide)
+
+    def one_block(array, base=0):
+        return pl.BlockSpec(
+            (1,) + array.shape[1:], lambda i: (base + i,) + (0,) * (len(array.shape) - 1)
+        )
+
+    gate_x.wait_recv()
+    gate_y.wait_recv()
+    theirs, ours = (1 - x) * PIECES, x * PIECES
+    pltpu.emit_pipeline(
+        sums_body,
+        grid=(PIECES,),
+        in_specs=[
+            one_block(gate_xk),
+            one_block(gate_xr),
+            one_block(gate_yk, theirs),
+            one_block(gate_yr, theirs),
+            one_block(gate_yk, ours),
+            one_block(gate_yr, ours),
+        ],
+        out_specs=[one_block(r) for r in (gate_y2s, gate_x2s, gate_own_x, gate_own_y)],
+    )(
+        gate_xk,
+        gate_xr,
+        gate_yk,
+        gate_yr,
+        gate_yk,
+        gate_yr,
+        gate_y2s,
+        gate_x2s,
+        gate_own_x,
+        gate_own_y,
+    )
     own_tokens.wait()
     for copy in scattered:
         copy.wait_recv()
@@ -1162,6 +1224,8 @@
                 copy.wait_recv()
                 copy.wait_send()
     for copy in scattered:
+        copy.wait_send()
+    for copy in (gate_x, gate_y):
         copy.wait_send()
 
 
@@ -1183,12 +1247,18 @@
     return pl.pallas_call(
         backward_kernel,
         in_specs=[anywhere] * 5 + [inside] * 9,
-        out_specs=[anywhere] * 6 + [inside] * 7,
+        out_specs=[anywhere] * 12 + [inside] * 7,
         out_shape=[
-            shape((DEPTH, 4 * rows, cut), low),
-            shape((DEPTH, 4 * rows, cut), wide),
-            shape((PIECES, 2 * rows, columns - cut), low),
-            shape((PIECES, 2 * rows, columns - cut), wide),
+            shape((PIECES, 2, rows, cut), low),
+            shape((PIECES, 2, rows, cut), wide),
+            shape((2 * PIECES, rows, columns - cut), low),
+            shape((2 * PIECES, rows, columns - cut), wide),
+            shape((PIECES, 2, rows, cut), low),
+            shape((2 * PIECES, rows, columns - cut), low),
+            shape((PIECES, rows, cut), low),
+            shape((PIECES, rows, columns - cut), low),
+            shape((PIECES, rows, cut), wide),
+            shape((PIECES, rows, columns - cut), wide),
             shape((4, head_rows, width), low),
             shape((4, each // 4, width), low),
             shape((PIECES, ROWS, columns), low),
@@ -1211,6 +1281,8 @@
             dma((DEPTH - 1,)),
             dma((2, PIECES)),
             dma((2, PIECES)),
+            dma((2,)),
+            dma((2,)),
             dma(()),
         ],
         compiler_params=params(62, collective_id=3, has_side_effects=True),
@@ -1234,10 +1306,10 @@
     first_ref,
     second_ref,
     normed_ref,
-    gate_xs,
-    gate_xk,
-    gate_ys,
-    gate_yk,
+    gate_y2s,
+    gate_x2s,
+    gate_sum_x,
+    gate_sum_y,
     heads_term,
     hidden_term,
     wi_ref,
@@ -1250,24 +1322,6 @@
     gate_rows,
     inward_rows_out,
     vec_out,
-    inward_xs,
-    inward_xk,
-    inward_ys,
-    inward_yk,
-    gate_xr,
-    gate_yr,
-    gate_y2s,
-    gate_y2r,
-    gate_x2s,
-    gate_x2r,
-    gate_fin,
-    inward_xr,
-    inward_yr,
-    inward_y2s,
-    inward_y2r,
-    inward_x2s,
-    inward_x2r,
-    inward_fin,
     heads_r,
     heads_2s,
     heads_2r,
@@ -1277,17 +1331,36 @@
     core_send,
     core_recv,
     z_send,
-    z_recv,
+    below,
+    above,
     own_sum,
     pg_ref,
     token_rows,
     vec_sum,
     vec_x,
     vec_y,
+    gate_own_x,
+    gate_own_y,
+    gate_y2r,
+    gate_x2r,
+    gate_fin,
+    inward_xs,
+    inward_xr,
+    inward_xk,
+    inward_ys,
+    inward_yr,
+    inward_yk,
+    inward_y2s,
+    inward_y2r,
+    inward_x2s,
+    inward_x2r,
+    inward_fin,
     core_s,
     core_r,
-    z_s,
-    z_r,
+    up_s,
+    down_s,
+    below_r,
+    above_r,
     stage_s,
     stage_r,
     rows_s,
@@ -1319,36 +1392,167 @@
         started.append(copy)
         return copy
 
-    gate_x = begin(remote(gate_xs, gate_xr, stage_s, stage_r, (0, 0), x_mate))
-    gate_y = begin(remote(gate_ys, gate_yr, stage_s, stage_r, (0, 1), y_mate))
+    loads = [
+        pltpu.make_async_copy(gate_sum_x, gate_own_x, local_sems.at[2]),
+        pltpu.make_async_copy(gate_sum_y, gate_own_y, local_sems.at[3]),
+    ]
+    for load in loads:
+        load.start()
+    gate_y = begin(remote(gate_y2s, gate_y2r, stage_s, stage_r, (0, 2), y_mate))
+    gate_x = begin(remote(gate_x2s, gate_x2r, stage_s, stage_r, (0, 3), x_mate))
     heads_x = begin(remote(heads_term.at[1 - x], heads_r, stage_s, stage_r, (2, 0), x_mate))
     hidden_y = [
-        begin(
-            remote(hidden_term.at[i, 1 - y], hidden_r.at[i], stage_s, stage_r, (3, i), y_mate)
-        )
+        remote(hidden_term.at[i, 1 - y], hidden_r.at[i], stage_s, stage_r, (3, i), y_mate)
         for i in range(2)
     ]
-    own_tokens = pltpu.make_async_copy(pieces_ref.at[0], token_rows, local_sems.at[0])
+    own_tokens = pltpu.make_async_copy(pieces_ref.at[0], token_rows, local_sems.at[4])
     own_tokens.start()
 
     vec_sum[...] = jnp.zeros_like(vec_sum)
 
     def core_copy(k):
-        return remote(core_send.at[k], core_recv.at[k], core_s, core_r, k, core_mate)
-
-    def z_copy(k):
-        goal = device(x, core, (z + DEPTH - k) % DEPTH, y)
-        return remote(z_send.at[k - 1], z_recv.at[k - 1], z_s, z_r, k - 1, goal)
+        return remote(core_send.at[k % 2], core_recv.at[k], core_s, core_r, k, core_mate)
+
+    def up_copy(slot, number):
+        goal = device(x, core, z + 1, y)
+        return remote_to(
+            z_send.at[slot], below.at[number], up_s.at[slot], below_r.at[number], goal
+        )
+
+    def down_copy(slot, number):
+        goal = device(x, core, z - 1, y)
+        return remote_to(
+            z_send.at[slot], above.at[number], down_s.at[slot], above_r.at[number], goal
+        )
+
+    def order(i):
+        inner = jnp.where(z == 1, select(i, 2, 1, 3), select(i, 2, 3, 1))
+        outer = jnp.where(z == 0, select(i, 1, 2, 3), select(i, 3, 2, 1))
+        return jnp.where((z == 0) | (z == DEPTH - 1), outer, inner)
 
     def piece_of(i):
-        k = DEPTH - 1 - i // 2
-        return k + DEPTH * (1 - i % 2)
+        return order(i // 2) + DEPTH * (1 - i % 2)
+
+    def arrived(box, recvs, number):
+        copy = remote_to(box.at[number], box.at[number], up_s.at[0], recvs.at[number], core_mate)
+        copy.wait_recv()
+
+    def add_and(slot, box, recvs, number, copy):
+        arrived(box, recvs, number)
+        z_send[slot] = (z_send[slot].astype(wide) + box[number].astype(wide)).astype(low)
+        copy.start()
+
+    def first_hop():
+        @pl.when(z == 1)
+        def _():
+            add_and(0, below, below_r, 0, up_copy(0, 0))
+
+        @pl.when(z == DEPTH - 2)
+        def _():
+            add_and(0, above, above_r, 0, down_copy(0, 0))
+
+    def second_hop():
+        @pl.when(z == 1)
+        def _():
+            add_and(2, below, below_r, 1, up_copy(2, 1))
+
+        @pl.when(z == DEPTH - 2)
+        def _():
+            add_and(2, above, above_r, 1, down_copy(2, 1))
+
+    def third_hop():
+        @pl.when(z == 1)
+        def _():
+            add_and(1, above, above_r, 0, down_copy(1, 0))
+
+        @pl.when(z == DEPTH - 2)
+        def _():
+            add_and(1, below, below_r, 0, up_copy(1, 0))
+
+    def last_hop():
+        @pl.when(z == 0)
+        def _():
+            arrived(above, above_r, 0)
+            own_sum[...] += above[0].astype(wide)
+
+        @pl.when(z == 1)
+        def _():
+            arrived(below, below_r, 2)
+            arrived(above, above_r, 1)
+            own_sum[...] += below[2].astype(wide) + above[1].astype(wide)
+
+        @pl.when(z == DEPTH - 2)
+        def _():
+            arrived(below, below_r, 1)
+            arrived(above, above_r, 2)
+            own_sum[...] += below[1].astype(wide) + above[2].astype(wide)
+
+        @pl.when(z == DEPTH - 1)
+        def _():
+            arrived(below, below_r, 0)
+            own_sum[...] += below[0].astype(wide)
+
+    def sent_all():
+        @pl.when(z == 0)
+        def _():
+            for slot in range(DEPTH - 1):
+                up_copy(slot, slot).wait_send()
+
+        @pl.when(z == DEPTH - 1)
+        def _():
+            for slot in range(DEPTH - 1):
+                down_copy(slot, slot).wait_send()
+
+        @pl.when(z == 1)
+        def _():
+            up_copy(0, 0).wait_send()
+            up_copy(2, 1).wait_send()
+            down_copy(1, 0).wait_send()
+
+        @pl.when(z == DEPTH - 2)
+        def _():
+            down_copy(0, 0).wait_send()
+            down_copy(2, 1).wait_send()
+            up_copy(1, 0).wait_send()
+
+    def to_rows(which, fin, rows):
+        slot = core * DEPTH + z
+        copies = []
+        for flip, turn in members:
+            cc, zz = target(flip, turn)
+            copies.append(
+                remote(
+                    fin.at[cc * DEPTH + zz],
+                    rows.at[slot],
+                    rows_s,
+                    rows_r,
+                    (which, flip * DEPTH + turn),
+                    device(x, cc, zz, y),
+                )
+            )
+        copies.append(pltpu.make_async_copy(fin.at[slot], rows.at[slot], local_sems.at[which]))
+        return copies
+
+    def gate_done():
+        gate_y.wait_recv()
+        gate_x.wait_recv()
+        for load in loads:
+            load.wait()
+        gate_fin[...] = jnp.concatenate(
+            [
+                gate_own_x[...] + gate_y2r[...].astype(wide),
+                gate_own_y[...] + gate_x2r[...].astype(wide),
+            ],
+            2,
+        ).astype(low)
+        for copy in to_rows(0, gate_fin, gate_rows) + hidden_y:
+            copy.start()
 
     def piece_body(
         dq, dk, dv, odk, odv, gu, tokens, cos, first, second
     ):
         step = pl.program_id(0)
-        k = DEPTH - 1 - step // 2
+        turn = step // 2
         piece = piece_of(step)
         tables = (cos, first, second)
         query = turned(dq[0] * (HEAD_DIM**-0.5), *tables, -1.0)
@@ -1368,22 +1572,36 @@
             vec_sum[row + 1 : row + 2] += total[:, half:]
         vec_sum[4:5, : 3 * HEAD_COLS] += jnp.sum(narrow.astype(wide), axis=0, keepdims=True)
 
+        pl.when(step == GATE_STEP)(gate_done)
+        pl.when(step == PIECES - 1)(first_hop)
+
         @pl.when(step % 2 == 0)
         def _():
-            core_send[k] = grad.astype(low)
-            core_copy(k).start()
+            @pl.when(turn >= 2)
+            def _():
+                core_copy(turn - 2).wait_send()
+
+            core_send[turn % 2] = grad.astype(low)
+            core_copy(turn).start()
 
         @pl.when(step % 2 == 1)
         def _():
-            core_copy(k).wait_recv()
-            both = grad + core_recv[k].astype(wide)
-
-            @pl.when(k > 0)
+            core_copy(turn).wait_recv()
+            both = grad + core_recv[turn].astype(wide)
+
+            @pl.when(turn < DEPTH - 1)
             def _():
-                z_send[k - 1] = both.astype(low)
-                z_copy(k).start()
-
-            @pl.when(k == 0)
+                z_send[turn] = both.astype(low)
+
+                @pl.when(z == 0)
+                def _():
+                    up_copy(turn, turn).start()
+
+                @pl.when(z == DEPTH - 1)
+                def _():
+                    down_copy(turn, turn).start()
+
+            @pl.when(turn == DEPTH - 1)
             def _():
                 own_sum[...] = both
 
@@ -1418,38 +1636,39 @@
     size = width // PIECES
     cut = 3 * HEAD_COLS // 2
 
-    def projected(first, last):
-        return pg_ref[...].reshape(total, 3 * HEAD_COLS)[:, first:last]
-
-    def send_body(left, out):
-        out[0] = times_transposed(left[...], projected(0, cut)).astype(low)
-
-    def keep_body(left, out):
-        out[0] = times_transposed(left[...], projected(0, cut))
-
-    def split_body(left, keep, send):
-        term = times_transposed(left[...], projected(cut, 2 * cut))
-        split_rows(term, y, keep, send)
-
-    def from_block(base):
-        return pl.BlockSpec((total, size), lambda i: (0, base + i))
-
-    def block_of(array):
-        return pl.BlockSpec((1,) + array.shape[1:], lambda i: (i, 0, 0))
+    def block(i):
+        return jnp.where(i < DEPTH, (1 - x) * DEPTH + i, x * DEPTH + i - DEPTH)
+
+    inward_x = remote(inward_xs, inward_xr, stage_s, stage_r, (1, 0), x_mate)
+
+    def inward_body(left):
+        i = pl.program_id(0)
+        rhs = pg_ref[...].reshape(total, 3 * HEAD_COLS)
+        term = times_transposed(left[...], rhs)
+        first = term[:, :cut].reshape(2, 2, size // 4, cut)
+        at = pl.ds((i % DEPTH) * 2, 2)
+
+        @pl.when(i < DEPTH)
+        def _():
+            inward_xs[at] = first.astype(low)
+
+        @pl.when(i >= DEPTH)
+        def _():
+            inward_xk[at] = first
+
+        at = pl.ds(block(i) * 2, 2)
+        split_rows(term[:, cut:], y, inward_yk.at[at], inward_ys.at[at])
+
+        @pl.when(i == DEPTH - 1)
+        def _():
+            inward_x.start()
 
     pltpu.emit_pipeline(
-        send_body,
-        grid=(DEPTH,),
-        in_specs=[from_block((1 - x) * DEPTH)],
-        out_specs=[block_of(inward_xs)],
-    )(normed_ref, inward_xs)
-    inward_x = begin(remote(inward_xs, inward_xr, stage_s, stage_r, (1, 0), x_mate))
-    pltpu.emit_pipeline(
-        split_body,
+        inward_body,
         grid=(PIECES,),
-        in_specs=[from_block(0)],
-        out_specs=[block_of(inward_yk), block_of(inward_ys)],
-    )(normed_ref, inward_yk, inward_ys)
+        in_specs=[pl.BlockSpec((total, size), lambda i: (0, block(i)))],
+    )(normed_ref)
+    started.append(inward_x)
     inward_y = begin(remote(inward_ys, inward_yr, stage_s, stage_r, (1, 1), y_mate))
 
     vector_x.wait_recv()
@@ -1462,81 +1681,10 @@
     def add_two(one, two, out):
         out[...] = (one[...].astype(wide) + two[...].astype(wide)).astype(out.dtype)
 
-    def second_stage(which, xk, xr, yk, yr, y2s, y2r, x2s, x2r, first_x, first_y):
-        quarter = xk.shape[1] // 4
-        rows_at = pl.BlockSpec(
-            (1, quarter, xk.shape[2]), lambda i: (i // 2, (i % 2) * 2 + (1 - y), 0)
-        )
-        first_x.wait_recv()
-        pltpu.emit_pipeline(
-            add_two, grid=(PIECES,), in_specs=[rows_at, rows_at], out_specs=[block_of(y2s)]
-        )(xk, xr, y2s)
-        over_y = begin(remote(y2s, y2r, stage_s, stage_r, (which, 2), y_mate))
-        part = pl.BlockSpec((1,) + yk.shape[1:], lambda i: ((1 - x) * DEPTH + i, 0, 0))
-        first_y.wait_recv()
-        pltpu.emit_pipeline(
-            add_two, grid=(DEPTH,), in_specs=[part, part], out_specs=[block_of(x2s)]
-        )(yk, yr, x2s)
-        over_x = begin(remote(x2s, x2r, stage_s, stage_r, (which, 3), x_mate))
-        return over_y, over_x
-
-    def last_stage(which, xk, xr, yk, yr, y2r, x2r, fin, rows, over_y, over_x):
-        quarter = xk.shape[1] // 4
-        cut = xk.shape[2]
-        rows_at = pl.BlockSpec((1, quarter, cut), lambda i: (i // 2, (i % 2) * 2 + y, 0))
-        part = pl.BlockSpec(
-            (1, quarter, yk.shape[2]), lambda i: (x * DEPTH + i // 2, i % 2, 0)
-        )
-        last = pl.BlockSpec((1, quarter, yk.shape[2]), lambda i: (i // 2, i % 2, 0))
-
-        def body(one, two, three, four, five, six, out):
-            left = one[0] + two[0].astype(wide) + three[0].astype(wide)
-            right = four[0] + five[0].astype(wide) + six[0].astype(wide)
-            out[0] = jnp.concatenate([left, right], 1).astype(low)
-
-        over_y.wait_recv()
-        over_x.wait_recv()
-        pltpu.emit_pipeline(
-            body,
-            grid=(PIECES,),
-            in_specs=[rows_at, rows_at, block_of(y2r), part, part, last],
-            out_specs=[block_of(fin)],
-        )(xk, xr, y2r, yk, yr, x2r, fin)
-        slot = core * DEPTH + z
-        copies = []
-        for flip, turn in members:
-            cc, zz = target(flip, turn)
-            copies.append(
-                begin(
-                    remote(
-                        fin.at[cc * DEPTH + zz],
-                        rows.at[slot],
-                        rows_s,
-                        rows_r,
-                        (which, flip * DEPTH + turn),
-                        device(x, cc, zz, y),
-                    )
-                )
-            )
-        own = pltpu.make_async_copy(fin.at[slot], rows.at[slot], local_sems.at[1 + which])
-        own.start()
-        return copies, own
-
-    gate_second = second_stage(
-        0,
-        gate_xk,
-        gate_xr,
-        gate_yk,
-        gate_yr,
-        gate_y2s,
-        gate_y2r,
-        gate_x2s,
-        gate_x2r,
-        gate_x,
-        gate_y,
-    )
-
-    chunk = heads_term.shape[-1] // DEPTH
+    second_hop()
+    third_hop()
+
+    chunk = heads_term.shape[-1] // 2
 
     def flat_spec(rows):
         return pl.BlockSpec((rows, chunk), lambda i: (0, i))
@@ -1544,7 +1692,7 @@
     def row_sum(one, two, out):
         spec = flat_spec(one.shape[0])
         pltpu.emit_pipeline(
-            add_two, grid=(DEPTH,), in_specs=[spec, spec], out_specs=[spec]
+            add_two, grid=(2,), in_specs=[spec, spec], out_specs=[spec]
         )(one, two, out)
 
     def row_total(one, two, three, out):
@@ -1554,7 +1702,7 @@
             out[...] = one[...].astype(wide) + two[...].astype(wide) + three[...].astype(wide)
 
         pltpu.emit_pipeline(
-            body, grid=(DEPTH,), in_specs=[spec] * 3, out_specs=[spec]
+            body, grid=(2,), in_specs=[spec] * 3, out_specs=[spec]
         )(one, two, three, out)
 
     heads_x.wait_recv()
@@ -1564,13 +1712,6 @@
         copy.wait_recv()
     row_sum(hidden_term.at[1 - x, y], hidden_r.at[1 - x], hidden_2s)
     hidden_x = begin(remote(hidden_2s, hidden_2r, stage_s, stage_r, (3, 2), x_mate))
-
-    pltpu.emit_pipeline(
-        keep_body,
-        grid=(DEPTH,),
-        in_specs=[from_block(x * DEPTH)],
-        out_specs=[block_of(inward_xk)],
-    )(normed_ref, inward_xk)
 
     vector_y.wait_recv()
     vec_sum_y = vec_sum[...] + vec_y[...]
@@ -1593,56 +1734,36 @@
             )
         )
 
-    gate_rest = last_stage(
-        0,
-        gate_xk,
-        gate_xr,
-        gate_yk,
-        gate_yr,
-        gate_y2r,
-        gate_x2r,
-        gate_fin,
-        gate_rows,
-        *gate_second,
-    )
-    inward_second = second_stage(
-        1,
-        inward_xk,
-        inward_xr,
-        inward_yk,
-        inward_yr,
-        inward_y2s,
-        inward_y2r,
-        inward_x2s,
-        inward_x2r,
-        inward_x,
-        inward_y,
-    )
+    inward_x.wait_recv()
+    inward_y2s[...] = (inward_xk[:, 1 - y] + inward_xr[:, 1 - y].astype(wide)).astype(low)
+    inward_over_y = begin(remote(inward_y2s, inward_y2r, stage_s, stage_r, (1, 2), y_mate))
+    inward_y.wait_recv()
+    other = pl.ds((1 - x) * PIECES, PIECES)
+    inward_x2s[...] = (inward_yk[other] + inward_yr[other].astype(wide)).astype(low)
+    inward_over_x = begin(remote(inward_x2s, inward_x2r, stage_s, stage_r, (1, 3), x_mate))
     heads_y.wait_recv()
     row_total(heads_term.at[x, y], heads_r.at[y], heads_2r, heads_out)
     hidden_x.wait_recv()
     row_total(hidden_term.at[x, y], hidden_r.at[x], hidden_2r, hidden_out)
-    inward_rest = last_stage(
-        1,
-        inward_xk,
-        inward_xr,
-        inward_yk,
-        inward_yr,
-        inward_y2r,
-        inward_x2r,
-        inward_fin,
-        inward_rows_out,
-        *inward_second,
-    )
+    inward_over_y.wait_recv()
+    inward_over_x.wait_recv()
+    own = pl.ds(x * PIECES, PIECES)
+    inward_fin[...] = jnp.concatenate(
+        [
+            inward_xk[:, y] + inward_xr[:, y].astype(wide) + inward_y2r[...].astype(wide),
+            inward_yk[own] + inward_yr[own].astype(wide) + inward_x2r[...].astype(wide),
+        ],
+        2,
+    ).astype(low)
+    inward_rest = to_rows(1, inward_fin, inward_rows_out)
+    for copy in inward_rest:
+        copy.start()
 
     own_tokens.wait()
-    for k in range(1, DEPTH):
-        z_copy(k).wait_recv()
+    last_hop()
     for first in range(0, ROWS, 64):
         rows = pl.ds(first, 64)
         grad = own_sum[rows]
-        for k in range(DEPTH - 1):
-            grad = grad + z_recv[k, rows].astype(wide)
         hat, inverse = normalised(token_rows[rows])
         scaled = grad * gain_ref[...]
         input_grad = inverse * (
@@ -1652,18 +1773,17 @@
         )
         tokens_out[rows] = (cot_ref[rows].astype(wide) + input_grad).astype(low)
 
-    for copies, own in (gate_rest, inward_rest):
-        own.wait()
-        for copy in copies:
-            copy.wait_recv()
+    for copy in to_rows(0, gate_fin, gate_rows) + inward_rest:
+        copy.wait()
+    for copy in hidden_y:
+        copy.wait_send()
     for copy in vectors:
         copy.wait_recv()
     for copy in started:
         copy.wait_send()
-    for k in range(DEPTH):
-        core_copy(k).wait_send()
-        if k > 0:
-            z_copy(k).wait_send()
+    for turn in range(DEPTH - 2, DEPTH):
+        core_copy(turn).wait_send()
+    sent_all()
 
 
 def finish(
@@ -1671,25 +1791,13 @@
 ):
     low, wide = jnp.bfloat16, jnp.float32
     width = pieces.shape[-1]
-    gate_xs, gate_xk, gate_ys, gate_yk = gate_up
     rows = width // 32
     anywhere = pl.BlockSpec(memory_space=pl.ANY)
     inside = pl.BlockSpec(memory_space=pltpu.VMEM)
     shape = jax.ShapeDtypeStruct
     half = 3 * HEAD_COLS // 2
 
-    def staged(a, b):
-        return [
-            shape((DEPTH, 4 * rows, a), low),
-            shape((PIECES, 2 * rows, b), low),
-            shape((PIECES, rows, a), low),
-            shape((PIECES, rows, a), low),
-            shape((DEPTH, 2 * rows, b), low),
-            shape((DEPTH, 2 * rows, b), low),
-            shape((PIECES, rows, a + b), low),
-        ]
-
-    a, b = gate_xs.shape[-1], gate_ys.shape[-1]
+    a, b = (value.shape[-1] for value in gate_up[:2])
     heads_rows, hidden_rows = heads.shape[2], hidden.shape[2]
     out_shapes = [
         shape((ROWS, width), low),
@@ -1698,12 +1806,7 @@
         shape((PIECES, rows, a + b), low),
         shape((PIECES, rows, 2 * half), low),
         shape((PIECES, 8, width // 2), wide),
-        shape((DEPTH, 4 * rows, half), low),
-        shape((DEPTH, 4 * rows, half), wide),
-        shape((PIECES, 2 * rows, half), low),
-        shape((PIECES, 2 * rows, half), wide),
     ]
-    out_shapes += staged(a, b) + staged(half, half)
     out_shapes += [
         shape((2, heads_rows, width), low),
         shape((heads_rows, width), low),
@@ -1720,8 +1823,9 @@
         out_specs=out_specs,
         out_shape=out_shapes,
         scratch_shapes=[
+            pltpu.VMEM((2, ROWS, width), low),
             pltpu.VMEM((DEPTH, ROWS, width), low),
-            pltpu.VMEM((DEPTH, ROWS, width), low),
+            pltpu.VMEM((DEPTH - 1, ROWS, width), low),
             pltpu.VMEM((DEPTH - 1, ROWS, width), low),
             pltpu.VMEM((DEPTH - 1, ROWS, width), low),
             pltpu.VMEM((ROWS, width), wide),
@@ -1730,8 +1834,26 @@
             pltpu.VMEM((8, width // 2), wide),
             pltpu.VMEM((8, width // 2), wide),
             pltpu.VMEM((8, width // 2), wide),
+            pltpu.VMEM((PIECES, rows, a), wide),
+            pltpu.VMEM((PIECES, rows, b), wide),
+            pltpu.VMEM((PIECES, rows, a), low),
+            pltpu.VMEM((PIECES, rows, b), low),
+            pltpu.VMEM((PIECES, rows, a + b), low),
+            pltpu.VMEM((PIECES, 2, rows, half), low),
+            pltpu.VMEM((PIECES, 2, rows, half), low),
+            pltpu.VMEM((PIECES, 2, rows, half), wide),
+            pltpu.VMEM((2 * PIECES, rows, half), low),
+            pltpu.VMEM((2 * PIECES, rows, half), low),
+            pltpu.VMEM((2 * PIECES, rows, half), wide),
+            pltpu.VMEM((PIECES, rows, half), low),
+            pltpu.VMEM((PIECES, rows, half), low),
+            pltpu.VMEM((PIECES, rows, half), low),
+            pltpu.VMEM((PIECES, rows, half), low),
+            pltpu.VMEM((PIECES, rows, 2 * half), low),
             dma((DEPTH,)),
             dma((DEPTH,)),
+            dma((DEPTH - 1,)),
+            dma((DEPTH - 1,)),
             dma((DEPTH - 1,)),
             dma((DEPTH - 1,)),
             dma((4, 4)),
@@ -1740,9 +1862,9 @@
             dma((3, PIECES)),
             dma((2,)),
             dma((2,)),
-            dma((3,)),
+            dma((5,)),
         ],
-        compiler_params=params(60, collective_id=1, has_side_effects=True),
+        compiler_params=params(63, collective_id=1, has_side_effects=True),
         cost_estimate=cost(0, 64 * MIB),
         name="finish",
     )(
@@ -1765,8 +1887,8 @@
     rows = term.shape[0] // 4
     even = jnp.concatenate([term[:rows], term[2 * rows : 3 * rows]], 0)
     odd = jnp.concatenate([term[rows : 2 * rows], term[3 * rows :]], 0)
-    keep_ref[0] = jnp.where(y == 0, even, odd)
-    send_ref[0] = jnp.where(y == 0, odd, even).astype(jnp.bfloat16)
+    keep_ref[...] = jnp.where(y == 0, even, odd).reshape(keep_ref.shape)
+    send_ref[...] = jnp.where(y == 0, odd, even).astype(jnp.bfloat16).reshape(send_ref.shape)
 
 
 def place_kernel(parts, in_ref, out_ref):
@@ -1883,31 +2005,30 @@
         rows_out,
     )
     normed = normed.reshape(PIECES * ROWS, width)
-    gate_xs, gate_xk, gate_ys, gate_yk, heads_term, hidden_term, gate_up_grad, *parts, layer_out = (
-        backward(
-            grads,
-            gate,
-            up,
-            normed,
-            pieces,
-            queries,
-            pairs,
-            other_pairs,
-            hidden,
-            attended,
-            rows_out,
-            own_sum,
-            terms,
-            valid.reshape(ROWS, 1),
-        )
-    )
+    outs = backward(
+        grads,
+        gate,
+        up,
+        normed,
+        pieces,
+        queries,
+        pairs,
+        other_pairs,
+        hidden,
+        attended,
+        rows_out,
+        own_sum,
+        terms,
+        valid.reshape(ROWS, 1),
+    )
+    heads_term, hidden_term, gate_up_grad, *parts, layer_out = outs[10:]
     tokens_grad, outward_sum, down_sum, gate_up_rows, inward_rows_own, vectors = finish(
         parts,
         gate_up_grad,
         pieces,
         tables,
         normed,
-        (gate_xs, gate_xk, gate_ys, gate_yk),
+        outs[6:10],
         heads_term.reshape(2, 2, -1, width),
         hidden_term.reshape(2, 2, -1, width),
         (inward, gate_up),

time: 550 us -> 528 us (0.960)
  Pallas kernels: 499 us -> 478 us
    pallas_call x1, Pallas kernels: 166 us -> 128 us  [finish(): pl.pallas_call(finish_kernel, in_specs=[anywhere] * 17 + [inside] * 4, ou...]
    pallas_call x1, Pallas kernels: 107 us -> 124 us  [backward(): pl.pallas_call(backward_kernel, in_specs=[anywhere] * 5 + [inside] * 9, o...]
where the time goes in v5:
time: 528 us; the launch traced here: 519 us
  Pallas kernels  478 us (91%)
  local copies, waits for them, and re-layouts  30.1 us (6%)
  other arithmetic  8.92 us (2%)
    pallas_call x1, Pallas kernels, gather(): pl.pallas_call(gather_kernel, in_specs=[anywhere] * 4, out_specs=[anywher...  132 us
    pallas_call x1, Pallas kernels, finish(): pl.pallas_call(finish_kernel, in_specs=[anywhere] * 17 + [inside] * 4, ou...  128 us
    pallas_call x1, Pallas kernels, backward(): pl.pallas_call(backward_kernel, in_specs=[anywhere] * 5 + [inside] * 9, o...  124 us
    pallas_call x1, Pallas kernels, forward(): pl.pallas_call(forward_kernel, in_specs=[anywhere] * 5 + [inside] * 6, ou...  90.6 us
    unnamed x39, local copies, waits for them, and re-layouts  13 us

profile of v5, /device:TPU:11, one launch (start us, length us, event | category | flops | bytes accessed | tf_op | source)
XLA Modules:
  0.0 518.8 jit_solution(14927582032176177179)
XLA Ops:
  0.7 2.0 convert_element_type.58
  2.6 2.4 reshape.263
  5.1 1.2 copy.52
  6.3 1.1 reshape.264.wg_ref
  7.4 1.5 convert_element_type.57
  8.9 0.0 copy-start.16
  8.9 0.0 copy-start.17
  8.9 0.0 copy-start.15
  9.0 0.6 reshape.261
  9.5 0.6 copy.55
  10.1 0.4 reshape.262
  10.5 0.0 copy-start.6
  10.6 0.1 fusion.7
  10.7 0.0 copy-start.11
  10.7 0.1 pad_maximum_fusion.wi_ref
  10.8 1.1 copy-done.6
  11.9 0.1 convert.21
  12.0 0.0 copy-done.11
  12.1 0.1 pad_maximum_fusion.1.ro_ref
  12.2 1.0 copy-done.8
  13.1 0.3 copy.37
  13.5 132.3 %gather.1 = (bf16[8,256,2048]{2,1,0:T(8,128)(2,1)}, bf16[2,2,4,2,80,768]{5,4,3,2,1,0:T(8,128)(2,1)S(1)}, bf16[2,2,4,2,64,1408]{5,4,3,2,1,0:T(8,128)(2,1)S(1)}, bf16[2,2,240,2048]{3,2,1,0:T(8,128)(2,1)S(1)}) custom-call(bf16[256,2048]{1,0:T(8,128)(2,1)S(1)} %bitcast.63, bf16[2,4,80,768]{3,2,1,0:T(8,128)(2,1)S(1)} %pad_maximum_fusion.wi_ref, ...), custom_call_target="tpu_custom_call" | custom-call | bytes 1048576 | tf_op jit(solution)/shard_map/gather/pallas_call | solution.py:681
  145.8 2.4 copy-done
  148.3 1.9 copy-done.2
  150.2 1.8 copy-done.1
  152.0 0.3 convert_reduce_fusion
  152.3 0.1 reshape.289
  152.4 0.1 reshape.268
  152.5 0.1 slice.58
  152.7 0.1 reshape.271
  152.8 0.1 reshape.272
  152.9 0.6 reshape.275.bias_ref
  153.5 0.1 add_convert_fusion
  153.6 3.1 fusion
  156.7 0.1 fusion.22
  156.8 0.7 reshape.266.gain_ref
  157.5 0.1 compare_convert_fusion
  157.5 0.0 copy-done.5
  157.5 1.5 multiply_convert_fusion
  159.0 0.7 reshape.267.shift_ref
  159.7 90.6 %forward.1 = (bf16[8,256,2048]{2,1,0:T(8,128)(2,1)}, f32[8,256,704]{2,1,0:T(8,128)}, f32[8,256,704]{2,1,0:T(8,128)}, bf16[8,256,2048]{2,1,0:T(8,128)(2,1)}, bf16...) custom-call(bf16[8,256,2048]{2,1,0:T(8,128)(2,1)} %get-tuple-element, ...), custom_call_target="tpu_custom_call" | custom-call | bytes 1048576 | tf_op jit(solution)/shard_map/forward/pallas_call | solution.py:870
  250.3 0.8 copy.41.valid_ref
  251.1 123.9 %backward.1 = (bf16[8,2,64,768]{3,2,1,0:T(8,128)(2,1)}, f32[8,2,64,768]{3,2,1,0:T(8,128)}, bf16[16,64,640]{2,1,0:T(8,128)(2,1)}, f32[16,64,640]{2,1,0:T(8,128)},...) custom-call(bf16[8,256,2048]{2,1,0:T(8,128)(2,1)} %get-tuple-element, ...), custom_call_target="tpu_custom_call" | custom-call | bytes 1048576 | tf_op jit(solution)/shard_map/backward/pallas_call | solution.py:1247
  375.0 1.3 copy.40
  376.4 128.4 %finish.1 = (bf16[256,2048]{1,0:T(8,128)(2,1)}, f32[64,2048]{1,0:T(8,128)}, f32[176,2048]{1,0:T(8,128)}, bf16[8,64,1408]{2,1,0:T(8,128)(2,1)}, bf16[8,64,768]{2,...) custom-call(f32[8,256,256]{2,1,0:T(8,128)} %get-tuple-element.59.dq_, ...), custom_call_target="tpu_custom_call" | custom-call | bytes 1048576 | tf_op jit(solution)/shard_map/finish/pallas_call | solution.py:1820
  504.8 1.4 copy-done.3
  506.1 2.0 place_rows.3
  508.1 1.0 slice.64
  509.2 0.1 reshape_squeeze.8
  509.3 0.1 reshape.287
  509.4 0.1 reshape.288
  509.5 0.6 constant_dynamic-slice_fusion
  510.0 1.2 place_rows.2
  511.3 2.0 copy.53
  513.3 0.0 copy-done.13
  513.4 0.1 squeeze.41
  513.5 0.5 fusion.16
  514.0 0.1 squeeze.43
  514.1 0.5 fusion.17
  514.6 0.0 copy-done.9
  514.6 2.0 copy.54
  516.6 0.0 copy-done.12
  516.6 0.8 copy.59
  517.4 1.1 copy.60
  (41 shorter events, 0.2 us)
Async XLA Ops:
  8.9 1.6 copy-start.16
  8.9 1.6 copy-start.17
  8.9 1.6 copy-start.15
  10.5 1.4 copy-start.6
  10.7 1.3 copy-start.11
  11.9 1.3 copy-start.8
  145.8 2.5 copy-start
  148.3 1.9 copy-start.2
  150.2 1.9 copy-start.1
  150.2 7.3 %copy-start.14 = (s32[1,2]{1,0:T(1,128)S(1)}, s32[1,2]{1,0:T(1,128)}, u32[]{:S(2)}) copy-start(s32[1,2]{1,0:T(1,128)} %param.11) | copy-start | bytes 28
  150.2 7.4 %copy-start.5 = (bf16[1,128,2,2048]{3,2,1,0:T(2,128)(2,1)S(1)}, bf16[1,128,2,2048]{3,2,1,0:T(2,128)(2,1)}, u32[]{:S(2)}) copy-start(bf16[1,128,2,2048]{3,2,1,0:T(2,128)(2,1)} %param.19) | copy-start | bytes 3145732
  504.8 1.4 copy-start.3
  506.1 3.9 copy-start.4
  508.1 3.2 copy-start.10
  510.0 3.3 copy-start.13
  510.0 4.5 copy-start.9
  513.3 3.3 copy-start.12
  513.3 4.1 copy-start.7

commit v6 on v5

--- a/solution.py
+++ b/solution.py
@@ -356,8 +356,8 @@
 DEPTH = 4
 PIECES = 2 * DEPTH
 ROWS = 256
-EXTRA = 16
 GATE_STEP = 4
+HALFWAY = 5
 LOCAL_HEADS = 4
 HEAD_COLS = LOCAL_HEADS * HEAD_DIM
 
@@ -465,10 +465,12 @@
             condition, copy = self.sent[number]
             pl.when(condition)(copy.start)
 
+    def near(self):
+        self.cores[0].start()
+        self.local.start()
+
     def first(self):
         self.start(0, 1)
-        self.cores[0].start()
-        self.local.start()
 
     def second(self):
         @pl.when(self.z > 0)
@@ -501,13 +503,15 @@
             self.downs[2].wait_recv()
             self.cores[1].start()
 
-    def end(self):
+    def end(self, arrivals=True):
+        if arrivals:
+            for copy in self.cores:
+                copy.wait_recv()
+            self.local.wait()
         for copy in self.cores:
-            copy.wait_recv()
             copy.wait_send()
         for condition, copy in self.sent:
             pl.when(condition)(copy.wait_send)
-        self.local.wait()
 
 
 def chain_sems():
@@ -529,184 +533,9 @@
     return bucket // 2, bucket % 2, blk // 2, blk % 2
 
 
-def gather_kernel(
-    x_ref,
-    wi_ref,
-    wg_ref,
-    ro_ref,
-    pieces,
-    wi_out,
-    wg_out,
-    ro_out,
-    group_s,
-    group_r,
-    across_s,
-    across_r,
-    rows_s,
-    rows_r,
-    local_sems,
-    *chain,
-):
-    x, core, z, y = coordinates()
-
-    def device(xx, cc, zz, yy):
-        return (xx * 2 + cc, zz * 2 + yy)
-
-    x_mate, y_mate = device(1 - x, core, z, y), device(x, core, z, 1 - y)
-    members = [(flip, turn) for turn in (0, 1, 3, 2) for flip in (0, 1)]
-
-    def target(flip, turn):
-        return (core + flip) % 2, (z + turn) % DEPTH
-
-    def source(flip, turn):
-        return (core + flip) % 2, (z + DEPTH - turn) % DEPTH
-
-    greet([device(x, *target(*m), y) for m in members[1:]] + [x_mate, y_mate])
-    started = []
-
-    def begin(copy):
-        copy.start()
-        started.append(copy)
-        return copy
-
-    local = [
-        pltpu.make_async_copy(wi_ref.at[core, z], wi_out.at[x, core, z, y], local_sems.at[0]),
-        pltpu.make_async_copy(wg_ref.at[core, z], wg_out.at[x, core, z, y], local_sems.at[1]),
-        pltpu.make_async_copy(ro_ref, ro_out.at[x, y], local_sems.at[2]),
-    ]
-    for copy in local:
-        copy.start()
-
-    def send_group(which, ref, out):
-        copies = {}
-        for flip, turn in members[1:]:
-            cc, zz = target(flip, turn)
-            copies[flip, turn] = begin(
-                remote(
-                    ref.at[cc, zz],
-                    out.at[x, core, z, y],
-                    group_s,
-                    group_r,
-                    (which, flip * DEPTH + turn),
-                    device(x, cc, zz, y),
-                )
-            )
-        return copies
-
-    inward = send_group(0, wi_ref, wi_out)
-    tokens = Chain(x_ref, pieces, x, core, z, y, chain)
-    tokens.first()
-    rows_x = begin(remote(ro_ref, ro_out.at[x, y], rows_s, rows_r, 0, x_mate))
-    rows_y = begin(remote(ro_ref, ro_out.at[x, y], rows_s, rows_r, 1, y_mate))
-    gate_up = send_group(1, wg_ref, wg_out)
-
-    def spread(which, ref, out, copies):
-        pairs = {}
-        for member in members:
-            flip, turn = member
-            cc, zz = source(flip, turn)
-            if member == (0, 0):
-                src = ref.at[core, z]
-            else:
-                copies[member].wait_recv()
-                src = out.at[x, cc, zz, y]
-            number = flip * DEPTH + turn
-            pairs[member] = (
-                begin(
-                    remote(
-                        src, out.at[x, cc, zz, y], across_s, across_r, (which, 0, number), x_mate
-                    )
-                ),
-                begin(
-                    remote(
-                        src, out.at[x, cc, zz, y], across_s, across_r, (which, 1, number), y_mate
-                    )
-                ),
-            )
-        return pairs
-
-    def corner(which, out, pairs):
-        copies = []
-        for member in members:
-            flip, turn = member
-            cc, zz = source(flip, turn)
-            number = flip * DEPTH + turn
-            if flip == 0:
-                pairs[member][1].wait_recv()
-                part = out.at[x, cc, zz, 1 - y]
-                mate = x_mate
-            else:
-                pairs[member][0].wait_recv()
-                part = out.at[1 - x, cc, zz, y]
-                mate = y_mate
-            copies.append(
-                begin(remote(part, part, across_s, across_r, (which, 2, number), mate))
-            )
-        return copies
-
-    inward_pairs = spread(0, wi_ref, wi_out, inward)
-
-    tokens.second()
-    inward_corner = corner(0, wi_out, inward_pairs)
-    gate_up_pairs = spread(1, wg_ref, wg_out, gate_up)
-
-    tokens.third()
-    cut = (ro_ref.shape[0] // 32) * 16
-    rows_y.wait_recv()
-    low = ro_out.at[x, 1 - y, pl.ds(0, cut)]
-    low_copy = begin(remote(low, low, rows_s, rows_r, 2, x_mate))
-    rows_x.wait_recv()
-    high = ro_out.at[1 - x, y, pl.ds(cut, ro_ref.shape[0] - cut)]
-    high_copy = begin(remote(high, high, rows_s, rows_r, 3, y_mate))
-    gate_up_corner = corner(1, wg_out, gate_up_pairs)
-
-    tokens.fourth()
-
-    for pairs in (inward_pairs, gate_up_pairs):
-        for flip, turn in members:
-            pairs[flip, turn][0 if flip == 0 else 1].wait_recv()
-    for copy in inward_corner + gate_up_corner + [low_copy, high_copy]:
-        copy.wait_recv()
-    for copy in started:
-        copy.wait_send()
-    tokens.end()
-    for copy in local:
-        copy.wait()
-
-
-def gather(tokens, inward, gate_up, rows_out):
-    anywhere = pl.BlockSpec(memory_space=pl.ANY)
-    low = jnp.bfloat16
-    dma = pltpu.SemaphoreType.DMA
-    return pl.pallas_call(
-        gather_kernel,
-        in_specs=[anywhere] * 4,
-        out_specs=[anywhere] * 4,
-        out_shape=[
-            jax.ShapeDtypeStruct((PIECES,) + tokens.shape, low),
-            jax.ShapeDtypeStruct((2, 2, DEPTH, 2) + inward.shape[2:], low),
-            jax.ShapeDtypeStruct((2, 2, DEPTH, 2) + gate_up.shape[2:], low),
-            jax.ShapeDtypeStruct((2, 2) + rows_out.shape, low),
-        ],
-        scratch_shapes=[
-            dma((2, PIECES)),
-            dma((2, PIECES)),
-            dma((2, 3, PIECES)),
-            dma((2, 3, PIECES)),
-            dma((4,)),
-            dma((4,)),
-            dma((3,)),
-        ]
-        + chain_sems(),
-        compiler_params=params(32, collective_id=0, has_side_effects=True),
-        cost_estimate=cost(0, 64 * MIB),
-        name="gather",
-    )(tokens, inward, gate_up, rows_out)
-
-
 def inward_rows(ref):
     blocks, rows, columns = ref.shape
-    return ref[:, : rows - EXTRA].reshape(blocks * (rows - EXTRA), columns)
+    return ref[...].reshape(blocks * rows, columns)
 
 
 def outward_rows(ref):
@@ -738,21 +567,49 @@
 
 
 def forward_kernel(
-    pieces_ref,
-    grad_ref,
+    tokens_ref,
+    cot_ref,
+    inward_ref,
+    gate_up_ref,
+    outward_ref,
+    down_ref,
+    valid_ref,
+    shares_ref,
+    bias_ref,
+    frequency_ref,
+    pieces,
+    normed_out,
+    gate_out,
+    up_out,
+    grads_out,
+    wi_out,
+    wg_out,
+    ro_out,
+    q_out,
+    kv_out,
+    okv_out,
+    hidden_out,
+    att_out,
+    own_out,
+    terms_out,
+    cos_out,
+    first_out,
+    second_out,
+    gain_out,
+    vec_ref,
+    wi_own,
+    wg_own,
+    wi_ref,
+    wg_ref,
+    rows_ref,
     cos_ref,
     first_ref,
     second_ref,
     gain_ref,
     shift_ref,
-    bias_ref,
-    wi_ref,
-    wg_ref,
-    rows_ref,
-    normed_out,
-    gate_out,
-    up_out,
-    grads_out,
+    bias_rows,
+    own_bias,
+    own_grad,
     q_ref,
     kv_ref,
     okv_ref,
@@ -762,55 +619,328 @@
     terms,
     core_send,
     core_recv,
+    group_s,
+    group_r,
+    across_s,
+    across_r,
+    rows_s,
+    rows_r,
     kv_s,
     kv_r,
     core_s,
     core_r,
-    *chain,
+    local_sems,
+    out_sems,
+    *chains,
 ):
     x, core, z, y = coordinates()
     low, wide = jnp.bfloat16, jnp.float32
-    core_mate = (x * 2 + 1 - core, z * 2 + y)
-    y_mate = (x * 2 + core, z * 2 + 1 - y)
-    below = (x * 2 + core, lax.rem(z + DEPTH - 1, DEPTH) * 2 + y)
-    above = (x * 2 + core, lax.rem(z + 1, DEPTH) * 2 + y)
-    greet([core_mate, y_mate, below, above])
-    grads = Chain(grad_ref, grads_out, x, core, z, y, chain)
-    grads.first()
+
+    def device(xx, cc, zz, yy):
+        return (xx * 2 + cc, zz * 2 + yy)
+
+    def at(xx, cc, zz, yy):
+        return ((xx * 2 + cc) * DEPTH + zz) * 2 + yy
+
+    x_mate, y_mate = device(1 - x, core, z, y), device(x, core, z, 1 - y)
+    core_mate = device(x, 1 - core, z, y)
+    members = [(flip, turn) for turn in (0, 1, 3, 2) for flip in (0, 1)]
+
+    def target(flip, turn):
+        return (core + flip) % 2, (z + turn) % DEPTH
+
+    def source(flip, turn):
+        return (core + flip) % 2, (z + DEPTH - turn) % DEPTH
+
+    started = []
+    written = []
+
+    def begin(copy):
+        copy.start()
+        started.append(copy)
+        return copy
+
+    def write_out(*pairs):
+        for src, dst in pairs:
+            copy = pltpu.make_async_copy(src, dst, out_sems.at[len(written)])
+            copy.start()
+            written.append(copy)
+
+    def group_copies(which, own, full):
+        mine = at(x, core, z, y)
+        copies = {}
+        for flip, turn in members[1:]:
+            cc, zz = target(flip, turn)
+            copies[flip, turn] = remote(
+                own.at[cc * DEPTH + zz],
+                full.at[mine],
+                group_s,
+                group_r,
+                (which, flip * DEPTH + turn),
+                device(x, cc, zz, y),
+            )
+        return copies
+
+    def vector_copies():
+        mine = vec_ref.at[at(x, core, z, y)]
+        copies = {}
+        for flip, turn in members[1:]:
+            copies[flip, turn] = remote(
+                mine,
+                mine,
+                group_s,
+                group_r,
+                (2, flip * DEPTH + turn),
+                device(x, *target(flip, turn), y),
+            )
+        return copies
+
+    def rows_copies():
+        mine = rows_ref.at[x * 2 + y]
+        return [
+            remote(mine, mine, rows_s, rows_r, way, mate) for way, mate in enumerate((x_mate, y_mate))
+        ]
+
+    tokens = Chain(tokens_ref, pieces, x, core, z, y, chains[:6])
+    grads = Chain(own_grad, grads_out, x, core, z, y, chains[6:])
+    position = lax.broadcasted_iota(jnp.int32, (ROWS // 2, HEAD_COLS), 0)
+    lane = lax.broadcasted_iota(jnp.int32, (ROWS // 2, HEAD_COLS), 1) % HEAD_DIM
+    half = ROT // 2
+
+    share_lane = lax.broadcasted_iota(jnp.int32, shares_ref.shape, 1)
+    share_row = lax.broadcasted_iota(jnp.int32, shares_ref.shape, 0)
+    own_shares = jnp.where((share_lane // HEAD_DIM == y) | (share_row >= 2), shares_ref[...], 0.0)
+
+    def prepare(inward_f32, gate_up_f32, outward_f32, down_f32):
+        loads = [
+            pltpu.make_async_copy(src, dst, local_sems.at[n])
+            for n, (src, dst) in enumerate(
+                (
+                    (inward_ref, inward_f32),
+                    (gate_up_ref, gate_up_f32),
+                    (outward_ref, outward_f32),
+                    (down_ref, down_f32),
+                )
+            )
+        ]
+        for load in loads:
+            load.start()
+        greet([device(x, *target(*m), y) for m in members[1:]] + [x_mate, y_mate])
+        tokens.near()
+        loads[0].wait()
+        vec_ref[at(x, core, z, y)] = own_shares
+        for copy in vector_copies().values():
+            copy.start()
+        pair = 2 * HEAD_DIM
+        for n in range(PIECES):
+            starts = [part * PIECES * pair + n * pair for part in range(6)]
+            line = jnp.concatenate([inward_f32[:, c : c + pair] for c in starts], 1)
+            wi_own[n] = line.astype(low)
+        wi_ref[at(x, core, z, y)] = wi_own[core * DEPTH + z]
+        for copy in group_copies(0, wi_own, wi_ref).values():
+            copy.start()
+        loads[1].wait()
+        each = gate_up_f32.shape[1] // (4 * PIECES)
+        for n in range(PIECES):
+            starts = [part * PIECES * each + n * each for part in range(4)]
+            line = jnp.concatenate([gate_up_f32[:, c : c + each] for c in starts], 1)
+            wg_own[n] = line.astype(low)
+        wg_ref[at(x, core, z, y)] = wg_own[core * DEPTH + z]
+        loads[2].wait()
+        loads[3].wait()
+        rows_ref[x * 2 + y, :HEAD_DIM] = outward_f32[...].astype(low)
+        rows_ref[x * 2 + y, HEAD_DIM:] = down_f32[...].astype(low)
+
+    pl.run_scoped(
+        prepare,
+        *[
+            pltpu.VMEM(r.shape, r.dtype)
+            for r in (inward_ref, gate_up_ref, outward_ref, down_ref)
+        ],
+    )
+    inward = group_copies(0, wi_own, wi_ref)
+    gate_up = group_copies(1, wg_own, wg_ref)
+    vectors = vector_copies()
+    started += [*inward.values(), *gate_up.values(), *vectors.values()]
+
+    def spread(which, full, copies, halfway=None):
+        pairs = {}
+        for member in members:
+            if halfway is not None and member == members[HALFWAY]:
+                halfway()
+            flip, turn = member
+            cc, zz = source(flip, turn)
+            if member != (0, 0):
+                copies[member].wait_recv()
+            block = full.at[at(x, cc, zz, y)]
+            number = flip * DEPTH + turn
+            pairs[member] = tuple(
+                begin(remote(block, block, across_s, across_r, (which, way, number), mate))
+                for way, mate in enumerate((x_mate, y_mate))
+            )
+        return pairs
+
+    def by_x(which, flip):
+        return which != 1 or flip == 0
+
+    def corner(which, full, pairs):
+        copies = []
+        for member in members:
+            flip, turn = member
+            cc, zz = source(flip, turn)
+            number = flip * DEPTH + turn
+            if by_x(which, flip):
+                pairs[member][1].wait_recv()
+                block, mate = full.at[at(x, cc, zz, 1 - y)], x_mate
+            else:
+                pairs[member][0].wait_recv()
+                block, mate = full.at[at(1 - x, cc, zz, y)], y_mate
+            copies.append(
+                begin(remote(block, block, across_s, across_r, (which, 2, number), mate))
+            )
+        return copies
+
+    def complete(which, pairs, copies):
+        for flip, turn in members:
+            pairs[flip, turn][0 if by_x(which, flip) else 1].wait_recv()
+        for copy in copies:
+            copy.wait_recv()
+
+    frequency = frequency_ref[...]
+    for k in range(DEPTH):
+        first = (2 * lax.rem(z + DEPTH - k, DEPTH) + y) * (ROWS // 2)
+        angles = (first + position).astype(wide) * frequency
+        sine = jnp.sin(angles)
+        cos_ref[k] = jnp.cos(angles)
+        first_ref[k] = jnp.where(lane < half, -sine, 0.0)
+        second_ref[k] = jnp.where((lane >= half) & (lane < ROT), sine, 0.0)
+    own_grad[...] = (cot_ref[...].astype(wide) * valid_ref[...]).astype(low)
+    write_out((cos_ref, cos_out), (first_ref, first_out), (second_ref, second_out))
+
+    vector_pairs = spread(2, vec_ref, vectors)
+    inward_pairs = spread(0, wi_ref, inward)
+    for copy in gate_up.values():
+        copy.start()
+    vector_corner = corner(2, vec_ref, vector_pairs)
+    inward_corner = corner(0, wi_ref, inward_pairs)
+    gate_up_pairs = spread(1, wg_ref, gate_up, tokens.first)
+    complete(2, vector_pairs, vector_corner)
+    complete(0, inward_pairs, inward_corner)
+    write_out((wi_ref, wi_out))
+
+    shares = vec_ref[...].astype(low).astype(wide)
+    for row, vector in ((0, gain_ref), (1, shift_ref)):
+        line = shares[:, row]
+        vector[...] = jnp.concatenate(
+            [line[2 * i : 2 * i + 1] + line[2 * i + 1 : 2 * i + 2] for i in range(16)], 1
+        )
+    each = bias_ref.shape[1]
+    biases = jnp.concatenate([shares[:, 2], shares[:, 3]], 1)
+    flat = jnp.concatenate([biases[i : i + 1, :each] for i in range(32)], 1)
+    for i in range(flat.shape[1] // 128):
+        bias_rows[i : i + 1] = flat[:, i * 128 : (i + 1) * 128]
+    query_bias, key_bias, value_bias = [], [], []
+    gap = jnp.zeros((1, HEAD_DIM - ROT), wide)
+    for i in range(2):
+        row = i * PIECES + core * DEPTH + z
+        query_bias.append(bias_rows[pl.ds(row, 1)])
+        value_bias.append(bias_rows[pl.ds(2 * PIECES + row, 1)])
+        line = bias_rows[pl.ds(4 * PIECES + i * 2 + core, 1)]
+        heads = [line[:, 2 * ROT * j : 2 * ROT * (j + 1)] for j in range(DEPTH)]
+        chosen = jnp.where(
+            z == 0, heads[0], jnp.where(z == 1, heads[1], jnp.where(z == 2, heads[2], heads[3]))
+        )
+        key_bias += [chosen[:, :ROT], gap, chosen[:, ROT:], gap]
+    own_bias[...] = jnp.concatenate(query_bias + key_bias + value_bias, 1)
+    write_out((gain_ref, gain_out))
 
     def pair_copy(piece):
         return remote(kv_ref.at[piece], okv_ref.at[piece], kv_s, kv_r, piece, y_mate)
 
-    def piece_body(tokens, cos, first, second, normed, gate_part, up_part):
-        piece = pl.program_id(0)
-        hat, _ = normalised(tokens[0])
+    def project(piece, tokens_part, normed):
+        k = lax.rem(piece, DEPTH)
+        hat, _ = normalised(tokens_part[0])
         narrow = (hat * gain_ref[...] + shift_ref[...]).astype(low)
         normed[0] = narrow
-        projected = dot_rows(narrow, inward_rows(wi_ref)) + bias_ref[...]
-        tables = (cos, first, second)
+        projected = dot_rows(narrow, inward_rows(wi_ref)) + own_bias[...]
+        tables = (cos_ref.at[pl.ds(k, 1)], first_ref.at[pl.ds(k, 1)], second_ref.at[pl.ds(k, 1)])
         query = turned(projected[:, :HEAD_COLS], *tables, 1.0) * (HEAD_DIM**-0.5)
         key = turned(projected[:, HEAD_COLS : 2 * HEAD_COLS], *tables, 1.0)
         kv_ref[piece] = jnp.concatenate([key, projected[:, 2 * HEAD_COLS :]], 1).astype(low)
         pair_copy(piece).start()
         q_ref[piece] = query.astype(low)
-        both = dot_rows(narrow, wg_ref[...])
-        hidden = both.shape[1] // 2
-        gate, up = both[:, :hidden], both[:, hidden:]
-        gate_part[0] = gate
-        up_part[0] = up
-        hidden_ref[piece] = (gate * jax.nn.sigmoid(gate) * up).astype(low)
-
-        @pl.when(piece == PIECES - 2)
-        def _():
-            grads.second()
-
-    table_spec = pl.BlockSpec((1,) + cos_ref.shape[1:], lambda i: (i % DEPTH, 0, 0))
-    pltpu.emit_pipeline(
-        piece_body,
-        grid=(PIECES,),
-        in_specs=[piece_spec(pieces_ref.shape[-1])] + [table_spec] * 3,
-        out_specs=[piece_spec(r.shape[-1]) for r in (normed_out, gate_out, up_out)],
-    )(pieces_ref, cos_ref, first_ref, second_ref, normed_out, gate_out, up_out)
+
+    def piece_at(first, i):
+        turn = first + i // 2
+        near = jnp.where(z == 0, DEPTH - 1, 1)
+        k = jnp.where(
+            turn == 0, 0, jnp.where(turn == 1, near, jnp.where(turn == 2, 2, DEPTH - near))
+        )
+        return k + DEPTH * (i % 2)
+
+    def project_pieces(first, count):
+        spec = pl.BlockSpec((1,) + pieces.shape[1:], lambda i: (piece_at(first, i), 0, 0))
+        pltpu.emit_pipeline(
+            lambda *refs: project(piece_at(first, pl.program_id(0)), *refs),
+            grid=(2 * count,),
+            in_specs=[spec],
+            out_specs=[spec],
+        )(pieces, normed_out)
+
+    def feed(first, count):
+        def body(normed, gate_part, up_part):
+            piece = piece_at(first, pl.program_id(0))
+            both = dot_rows(normed[0], wg_ref[...].reshape(normed.shape[2], wg_ref.shape[2]))
+            hidden = both.shape[1] // 2
+            gate, up = both[:, :hidden], both[:, hidden:]
+            gate_part[0] = gate
+            up_part[0] = up
+            hidden_ref[piece] = (gate * jax.nn.sigmoid(gate) * up).astype(low)
+
+        def spec(array):
+            return pl.BlockSpec(
+                (1,) + array.shape[1:], lambda i: (piece_at(first, i), 0, 0)
+            )
+
+        pltpu.emit_pipeline(
+            body,
+            grid=(2 * count,),
+            in_specs=[spec(normed_out)],
+            out_specs=[spec(gate_out), spec(up_out)],
+        )(normed_out, gate_out, up_out)
+
+    near = jnp.where(z == 0, DEPTH - 1, 1)
+    far = DEPTH - near
+
+    def core_arrived(k):
+        remote(pieces.at[k], pieces.at[DEPTH + k], chains[3], chains[4], k, core_mate).wait_recv()
+
+    tokens.local.wait()
+    core_arrived(0)
+    project_pieces(0, 1)
+    tokens.second()
+    core_arrived(near)
+    project_pieces(1, 1)
+    gate_up_corner = corner(1, wg_ref, gate_up_pairs)
+    rows_x, rows_y = rows_copies()
+    begin(rows_x)
+    begin(rows_y)
+    tokens.third()
+    core_arrived(2)
+    project_pieces(2, 1)
+    complete(1, gate_up_pairs, gate_up_corner)
+    feed(0, 2)
+    tokens.fourth()
+    grads.near()
+    grads.first()
+    core_arrived(far)
+    project_pieces(3, 1)
+    rows_y.wait_recv()
+    block = rows_ref.at[x * 2 + 1 - y]
+    rows_corner = begin(remote(block, block, rows_s, rows_r, 2, x_mate))
+    feed(2, 2)
+    grads.second()
+    write_out((q_ref, q_out), (kv_ref, kv_out), (wg_ref, wg_out))
 
     for b in range(2):
         for j in range(DEPTH):
@@ -824,8 +954,12 @@
         if b == 0:
             grads.third()
 
+    rows_x.wait_recv()
+    rows_corner.wait_recv()
+    write_out((hidden_ref, hidden_out), (att_ref, att_out), (okv_ref, okv_out), (rows_ref, ro_out))
+
     def core_copy(k):
-        return remote(core_send.at[k], core_recv.at[k], core_s, core_r, k, core_mate)
+        return remote(core_send.at[k % 2], core_recv.at[k], core_s, core_r, k, core_mate)
 
     def term(piece):
         return dot_rows(att_ref[piece], outward_rows(rows_ref)) + dot_rows(
@@ -834,7 +968,12 @@
 
     def branch(i, carry):
         k = DEPTH - 1 - i
-        core_send[k] = term(DEPTH + k).astype(low)
+
+        @pl.when(i >= 2)
+        def _():
+            core_copy(k + 2).wait_send()
+
+        core_send[k % 2] = term(DEPTH + k).astype(low)
         core_copy(k).start()
         own = term(k)
         core_copy(k).wait_recv()
@@ -851,52 +990,116 @@
         return carry
 
     lax.fori_loop(0, DEPTH, branch, 0)
+    write_out((own_sum, own_out), (terms, terms_out))
     grads.fourth()
     grads.end()
+    tokens.end(False)
+    for k in range(2):
+        core_copy(k).wait_send()
     for piece in range(PIECES):
         pair_copy(piece).wait_send()
-    for k in range(DEPTH):
-        core_copy(k).wait_send()
-
-
-def forward(pieces, own_grad, tables, gain, shift, bias, inward, gate_up, rows_out):
+    for copy in started:
+        copy.wait_send()
+    for copy in written:
+        copy.wait()
+
+
+def forward(
+    tokens, cot, inward, gate_up, outward, down, valid, shares, bias, frequency
+):
     low, wide = jnp.bfloat16, jnp.float32
-    width = pieces.shape[-1]
-    hidden = gate_up.shape[1] // 2
+    rows, width = tokens.shape
+    own_rows = inward.shape[0]
+    group_columns = gate_up.shape[1] // PIECES
+    hidden = group_columns // 2
     anywhere = pl.BlockSpec(memory_space=pl.ANY)
     inside = pl.BlockSpec(memory_space=pltpu.VMEM)
     shape = jax.ShapeDtypeStruct
     dma = pltpu.SemaphoreType.DMA
+    wi_shape = shape((32, own_rows, 3 * HEAD_COLS), low)
+    wg_shape = shape((32, own_rows, group_columns), low)
+    ro_shape = shape((4, outward.shape[0] + down.shape[0], width), low)
+    table = shape((DEPTH, ROWS // 2, HEAD_COLS), wide)
+    heads = shape((PIECES, ROWS, HEAD_COLS), low)
+    pairs = shape((PIECES, ROWS, 2 * HEAD_COLS), low)
+    hidden_shape = shape((PIECES, ROWS, hidden), low)
+    own_shape = shape((ROWS, width), wide)
+    terms_shape = shape((DEPTH - 1, ROWS, width), low)
+    vector = shape((1, width), wide)
+
+    def scratch(*shapes):
+        return [pltpu.VMEM(s.shape, s.dtype) for s in shapes]
+
     return pl.pallas_call(
         forward_kernel,
-        in_specs=[anywhere] * 5 + [inside] * 6,
-        out_specs=[anywhere] * 4 + [inside] * 7,
+        in_specs=[anywhere] + [inside] + [anywhere] * 4 + [inside] * 4,
+        out_specs=[anywhere] * 19,
         out_shape=[
+            shape((PIECES, ROWS, width), low),
             shape((PIECES, ROWS, width), low),
             shape((PIECES, ROWS, hidden), wide),
             shape((PIECES, ROWS, hidden), wide),
             shape((PIECES, ROWS, width), low),
-            shape((PIECES, ROWS, HEAD_COLS), low),
-            shape((PIECES, ROWS, 2 * HEAD_COLS), low),
-            shape((PIECES, ROWS, 2 * HEAD_COLS), low),
-            shape((PIECES, ROWS, hidden), low),
-            shape((PIECES, ROWS, HEAD_COLS), low),
-            shape((ROWS, width), wide),
-            shape((DEPTH - 1, ROWS, width), low),
+            wi_shape,
+            wg_shape,
+            ro_shape,
+            heads,
+            pairs,
+            pairs,
+            hidden_shape,
+            heads,
+            own_shape,
+            terms_shape,
+            table,
+            table,
+            table,
+            vector,
         ],
-        scratch_shapes=[
-            pltpu.VMEM((DEPTH, ROWS, width), low),
-            pltpu.VMEM((DEPTH, ROWS, width), low),
+        scratch_shapes=scratch(
+            shape((32, 8, 128), wide),
+            shape((PIECES,) + wi_shape.shape[1:], low),
+            shape((PIECES,) + wg_shape.shape[1:], low),
+            wi_shape,
+            wg_shape,
+            ro_shape,
+            table,
+            table,
+            table,
+            vector,
+            vector,
+            shape((40, 128), wide),
+            shape((1, 3 * HEAD_COLS), wide),
+            shape((ROWS, width), low),
+            heads,
+            pairs,
+            pairs,
+            hidden_shape,
+            heads,
+            own_shape,
+            terms_shape,
+            shape((2, ROWS, width), low),
+            shape((DEPTH, ROWS, width), low),
+        )
+        + [
+            dma((3, PIECES)),
+            dma((3, PIECES)),
+            dma((3, 3, PIECES)),
+            dma((3, 3, PIECES)),
+            dma((4,)),
+            dma((4,)),
             dma((PIECES,)),
             dma((PIECES,)),
             dma((DEPTH,)),
             dma((DEPTH,)),
+            dma((4,)),
+            dma((14,)),
         ]
+        + chain_sems()
         + chain_sems(),
-        compiler_params=params(60, collective_id=2, has_side_effects=True),
+        compiler_params=params(62, collective_id=0, has_side_effects=True),
         cost_estimate=cost(0, 64 * MIB),
         name="forward",
-    )(pieces, own_grad, *tables, gain, shift, bias, inward, gate_up, rows_out)
+    )(tokens, cot, inward, gate_up, outward, down, valid, shares, bias, frequency)
 
 
 def pair_rows(block):
@@ -1910,20 +2113,6 @@
     )(value)
 
 
-def lane_tables(positions):
-    half = ROT // 2
-    place = jnp.arange(HEAD_COLS, dtype=jnp.int32) % HEAD_DIM
-    power = (place % half).astype(jnp.float32)
-    frequency = jnp.where(place < ROT, rotary_base ** (-(2.0 * power) / ROT), 0.0)
-    angles = positions.astype(jnp.float32)[..., None] * frequency
-    sine = jnp.sin(angles)
-    return (
-        jnp.cos(angles),
-        jnp.where(place < half, -sine, 0.0),
-        jnp.where((place >= half) & (place < ROT), sine, 0.0),
-    )
-
-
 def shards_grouped(
     tokens,
     lengths,
@@ -1938,72 +2127,49 @@
 ):
     group_len, seqs, width = tokens.shape[1:]
     bucket, blk = lax.axis_index("bucket"), lax.axis_index("blk")
-    _, core, z, y = coordinates()
-
-    own_rows = inward_weight.shape[0]
-    hidden_each = gate_up_weight.shape[1] // (2 * 2 * 2 * DEPTH)
+
     gain_share, bias_share = norm_gain.shape[0], inward_bias.shape[0]
-    shares = jnp.concatenate([norm_gain, norm_shift, inward_bias]).astype(jnp.bfloat16)
-    shares = jnp.pad(shares, (0, 3 * HEAD_COLS - shares.shape[0]))
-    inward = inward_weight.astype(jnp.bfloat16).reshape(own_rows, 3, 2, 2, DEPTH, 2 * HEAD_DIM)
-    inward = jnp.transpose(inward, (3, 4, 0, 1, 2, 5)).reshape(2, DEPTH, own_rows, 3 * HEAD_COLS)
-    inward = jnp.concatenate(
-        [inward, jnp.broadcast_to(shares, (2, DEPTH, EXTRA, 3 * HEAD_COLS))], 2
-    )
-    gate_up = gate_up_weight.astype(jnp.bfloat16).reshape(own_rows, 2, 2, 2, DEPTH, hidden_each)
-    gate_up = jnp.transpose(gate_up, (3, 4, 0, 1, 2, 5)).reshape(
-        2, DEPTH, own_rows, 4 * hidden_each
-    )
-    rows_out = jnp.concatenate([outward_weight, down_weight]).astype(jnp.bfloat16)
-    own_tokens = jnp.transpose(tokens[0], (1, 0, 2))
-    pieces, inward, gate_up, rows_out = gather(
-        own_tokens.reshape(ROWS, width), inward, gate_up, rows_out
-    )
-    vectors = inward[..., own_rows, :].reshape(-1, 3 * HEAD_COLS).astype(jnp.float32)
-    inward = inward.reshape((-1,) + inward.shape[4:])
-    gate_up = gate_up.reshape(width, -1)
-    rows_out = rows_out.reshape((-1,) + rows_out.shape[2:])
-
-    gain = vectors[:, :gain_share].reshape(1, width)
-    shift = vectors[:, gain_share : 2 * gain_share].reshape(1, width)
-    bias = vectors[:, 2 * gain_share : 2 * gain_share + bias_share].reshape(-1)
-
-    def own_columns(values, each):
-        split = values.reshape(2, 2, DEPTH, each)
-        return one_of(one_of(split, core, 1), z, 1)
-
-    key_bias = jnp.pad(
-        own_columns(bias[2 * width :], 2 * ROT).reshape(LOCAL_HEADS, ROT),
-        ((0, 0), (0, HEAD_DIM - ROT)),
-    )
-    own_bias = jnp.concatenate(
-        [
-            own_columns(bias[:width], 2 * HEAD_DIM).reshape(-1),
-            key_bias.reshape(-1),
-            own_columns(bias[width : 2 * width], 2 * HEAD_DIM).reshape(-1),
-        ]
-    ).reshape(1, -1)
-
+    shares = jnp.concatenate(
+        [norm_gain, norm_gain, norm_shift, norm_shift, inward_bias, jnp.zeros((624,), jnp.float32)]
+    ).reshape(8, 128)
+    own_tokens = jnp.transpose(tokens[0], (1, 0, 2)).reshape(ROWS, width)
+    own_cotangent = jnp.transpose(cotangent[0], (1, 0, 2)).reshape(ROWS, width)
     position = blk * group_len + jnp.arange(group_len, dtype=jnp.int32)
-    valid = (position[None, :] < lengths[0][:, None]).astype(jnp.float32)[..., None]
-    own_cotangent = jnp.transpose(cotangent[0], (1, 0, 2))
-    own_grad = (own_cotangent.astype(jnp.float32) * valid).astype(jnp.bfloat16)
-    turns = (z - jnp.arange(DEPTH, dtype=jnp.int32)) % DEPTH
-    tables = lane_tables(
-        ((2 * turns + y) * group_len)[:, None] + jnp.arange(group_len, dtype=jnp.int32)
-    )
-
-    normed, gate, up, grads, queries, pairs, other_pairs, hidden, attended, own_sum, terms = forward(
+    valid = (position[None, :] < lengths[0][:, None]).astype(jnp.float32).reshape(ROWS, 1)
+    lane = jnp.arange(HEAD_COLS, dtype=jnp.int32) % HEAD_DIM
+    power = (lane % (ROT // 2)).astype(jnp.float32)
+    frequency = jnp.where(lane < ROT, rotary_base ** (-(2.0 * power) / ROT), 0.0)
+    (
         pieces,
-        own_grad.reshape(ROWS, width),
-        tables,
-        gain,
-        shift,
-        own_bias,
+        normed,
+        gate,
+        up,
+        grads,
         inward,
         gate_up,
         rows_out,
-    )
+        queries,
+        pairs,
+        other_pairs,
+        hidden,
+        attended,
+        own_sum,
+        terms,
+        *tables,
+        gain,
+    ) = forward(
+        own_tokens,
+        own_cotangent,
+        inward_weight,
+        gate_up_weight,
+        outward_weight,
+        down_weight,
+        valid,
+        shares,
+        inward_bias.reshape(1, -1),
+        frequency.reshape(1, -1),
+    )
+    gate_up = gate_up.reshape(width, -1)
     normed = normed.reshape(PIECES * ROWS, width)
     outs = backward(
         grads,
@@ -2019,7 +2185,7 @@
         rows_out,
         own_sum,
         terms,
-        valid.reshape(ROWS, 1),
+        valid,
     )
     heads_term, hidden_term, gate_up_grad, *parts, layer_out = outs[10:]
     tokens_grad, outward_sum, down_sum, gate_up_rows, inward_rows_own, vectors = finish(
@@ -2033,7 +2199,7 @@
         hidden_term.reshape(2, 2, -1, width),
         (inward, gate_up),
         gain,
-        own_cotangent.reshape(ROWS, width),
+        own_cotangent,
     )
     gate_up_sum = place_rows(gate_up_rows, 4)
     inward_sum = place_rows(inward_rows_own, 6)

time: 528 us -> 475 us (0.90)
  Pallas kernels: 478 us -> 449 us
  local copies, waits for them, and re-layouts: 30.1 us -> 15.3 us
  other arithmetic: 8.92 us -> 1.43 us
    pallas_call x2 -> x1, Pallas kernels: 223 us -> 200 us  [forward(): pl.pallas_call(forward_kernel, in_specs=[anywhere] + [inside] + [anywhere...]
    unnamed x39 -> x14, local copies, waits for them, and re-layouts: 13 us -> 1.92 us
    pallas_call x1, Pallas kernels: 124 us -> 117 us  [backward(): pl.pallas_call(backward_kernel, in_specs=[anywhere] * 5 + [inside] * 9, o...]
    reshape x14 -> x1, local copies, waits for them, and re-layouts: 12.6 us -> 5.79 us  [placed(): return jnp.transpose(value, (1, 0, 2)).reshape(tokens.shape)]
where the time goes in v6:
time: 475 us; the launch traced here: 467 us
  Pallas kernels  449 us (95%)
  local copies, waits for them, and re-layouts  15.3 us (3%)
    pallas_call x1, Pallas kernels, forward(): pl.pallas_call(forward_kernel, in_specs=[anywhere] + [inside] + [anywhere...  200 us
    pallas_call x1, Pallas kernels, finish(): pl.pallas_call(finish_kernel, in_specs=[anywhere] * 17 + [inside] * 4, ou...  129 us
    pallas_call x1, Pallas kernels, backward(): pl.pallas_call(backward_kernel, in_specs=[anywhere] * 5 + [inside] * 9, o...  117 us

profile of v6, /device:TPU:11, one launch (start us, length us, event | category | flops | bytes accessed | tf_op | source)
XLA Modules:
  0.0 466.5 jit_solution(15140876426582300993)
XLA Ops:
  0.6 0.0 copy-start.3
  0.7 0.8 compare_convert_fusion
  1.5 0.6 compare_select_fusion.2.frequency_ref
  2.1 1.4 concatenate.6
  3.5 0.8 copy.25.valid_ref
  4.3 2.5 copy.23
  6.8 0.0 copy-done.3
  6.8 1.3 copy.24
  8.1 200.0 %forward.1 = (bf16[8,256,2048]{2,1,0:T(8,128)(2,1)}, bf16[8,256,2048]{2,1,0:T(8,128)(2,1)}, f32[8,256,704]{2,1,0:T(8,128)}, f32[8,256,704]{2,1,0:T(8,128)}, bf16...) custom-call(bf16[256,2048]{1,0:T(8,128)(2,1)} %bitcast.47, ...), custom_call_target="tpu_custom_call" | custom-call | bytes 1048576 | tf_op jit(solution)/shard_map/forward/pallas_call | solution.py:1033
  208.1 116.8 %backward.1 = (bf16[8,2,64,768]{3,2,1,0:T(8,128)(2,1)}, f32[8,2,64,768]{3,2,1,0:T(8,128)}, bf16[16,64,640]{2,1,0:T(8,128)(2,1)}, f32[16,64,640]{2,1,0:T(8,128)},...) custom-call(bf16[8,256,2048]{2,1,0:T(8,128)(2,1)} %get-tuple-element, ...), custom_call_target="tpu_custom_call" | custom-call | bytes 1048576 | tf_op jit(solution)/shard_map/backward/pallas_call | solution.py:1450
  324.9 128.8 %finish.1 = (bf16[256,2048]{1,0:T(8,128)(2,1)}, f32[64,2048]{1,0:T(8,128)}, f32[176,2048]{1,0:T(8,128)}, bf16[8,64,1408]{2,1,0:T(8,128)(2,1)}, bf16[8,64,768]{2,...) custom-call(f32[8,256,256]{2,1,0:T(8,128)} %get-tuple-element.61.dq_, ...), custom_call_target="tpu_custom_call" | custom-call | bytes 1048576 | tf_op jit(solution)/shard_map/finish/pallas_call | solution.py:2023
  453.7 0.0 copy-start.5
  453.8 0.0 copy-start.1
  453.8 5.8 %copy_bitcast_fusion = (bf16[1,128,2,2048]{3,2,1,0:T(2,128)(2,1)}, bf16[1,128,2,2048]{3,2,1,0:T(2,128)(2,1)}) fusion(bf16[2,128,2048]{2,1,0:T(8,128)(2,1)} %bitcast.52, bf16[2,128,2048]{2,1,0:T(8,128)(2,1)} %bitcast.51), kind=kLoop, calls=%fused_computation | loop fusion | bytes 4194304 | tf_op jit(solution)/shard_map/reshape | solution.py:2219
  459.6 0.0 copy-start
  459.6 0.0 copy-done.5
  459.7 0.1 squeeze.33
  459.7 0.1 squeeze.31
  459.8 0.5 fusion.6
  460.4 0.1 reshape_squeeze.7
  460.4 0.1 reshape.194
  460.5 0.1 reshape.195
  460.6 0.6 constant_dynamic-slice_fusion
  461.2 0.0 copy-done.1
  461.2 1.2 place_rows.2
  462.4 0.0 copy-done
  462.4 0.0 copy-start.4
  462.4 0.0 copy-start.2
  462.4 2.0 place_rows.3
  464.4 0.0 copy-done.4
  464.4 0.8 copy.36
  465.2 0.0 copy-done.2
  465.2 1.1 copy.37
  (8 shorter events, 0.1 us)
Async XLA Ops:
  0.6 6.2 %copy-start.3 = (bf16[1,128,2,2048]{3,2,1,0:T(2,128)(2,1)S(1)}, bf16[1,128,2,2048]{3,2,1,0:T(2,128)(2,1)}, u32[]{:S(2)}) copy-start(bf16[1,128,2,2048]{3,2,1,0:T(2,128)(2,1)} %param.19) | copy-start | bytes 3145732
  453.7 5.8 %copy-start.5 = (f32[8,8,1024]{2,1,0:T(8,128)S(1)}, f32[8,8,1024]{2,1,0:T(8,128)}, u32[]{:S(2)}) copy-start(f32[8,8,1024]{2,1,0:T(8,128)} %get-tuple-element.80) | copy-start | bytes 786436
  453.8 7.4 %copy-start.1 = (bf16[8,64,768]{2,1,0:T(8,128)(2,1)S(1)}, bf16[8,64,768]{2,1,0:T(8,128)(2,1)}, u32[]{:S(2)}) copy-start(bf16[8,64,768]{2,1,0:T(8,128)(2,1)} %get-tuple-element.81.in_ref) | copy-start | bytes 2359300
  459.6 2.9 copy-start
  462.4 2.0 copy-start.4
  462.4 2.8 copy-start.2

commit v7 on v6

--- a/solution.py
+++ b/solution.py
@@ -356,7 +356,7 @@
 DEPTH = 4
 PIECES = 2 * DEPTH
 ROWS = 256
-GATE_STEP = 4
+GATE_STEP = 6
 HALFWAY = 5
 LOCAL_HEADS = 4
 HEAD_COLS = LOCAL_HEADS * HEAD_DIM
@@ -512,6 +512,133 @@
             copy.wait_send()
         for condition, copy in self.sent:
             pl.when(condition)(copy.wait_send)
+
+
+def far_first(i, z):
+    inner = jnp.where(z == 1, select(i, 2, 1, 3), select(i, 2, 3, 1))
+    outer = jnp.where(z == 0, select(i, 1, 2, 3), select(i, 3, 2, 1))
+    return jnp.where((z == 0) | (z == DEPTH - 1), outer, inner)
+
+
+class ChainSum:
+    def __init__(self, send, below, above, own, x, core, z, y, sems):
+        self.send, self.below, self.above, self.own = send, below, above, own
+        self.z = z
+        self.up_s, self.down_s, self.below_r, self.above_r = sems
+        self.goal_up = (x * 2 + core, (z + 1) * 2 + y)
+        self.goal_down = (x * 2 + core, (z - 1) * 2 + y)
+
+    def up(self, slot, number):
+        return remote_to(
+            self.send.at[slot],
+            self.below.at[number],
+            self.up_s.at[slot],
+            self.below_r.at[number],
+            self.goal_up,
+        )
+
+    def down(self, slot, number):
+        return remote_to(
+            self.send.at[slot],
+            self.above.at[number],
+            self.down_s.at[slot],
+            self.above_r.at[number],
+            self.goal_down,
+        )
+
+    def when(self, z):
+        return pl.when(self.z == z)
+
+    def start(self, turn):
+        @self.when(0)
+        def _():
+            self.up(turn, turn).start()
+
+        @self.when(DEPTH - 1)
+        def _():
+            self.down(turn, turn).start()
+
+    def wait_below(self, number):
+        box = self.below.at[number]
+        remote_to(box, box, self.up_s.at[0], self.below_r.at[number], self.goal_up).wait_recv()
+
+    def wait_above(self, number):
+        box = self.above.at[number]
+        remote_to(box, box, self.down_s.at[0], self.above_r.at[number], self.goal_up).wait_recv()
+
+    def add(self, slot, value):
+        total = self.send[slot].astype(jnp.float32) + value.astype(jnp.float32)
+        self.send[slot] = total.astype(jnp.bfloat16)
+
+    def pass_up(self, slot, number, sent):
+        self.wait_below(number)
+        self.add(slot, self.below[number])
+        self.up(slot, sent).start()
+
+    def pass_down(self, slot, number, sent):
+        self.wait_above(number)
+        self.add(slot, self.above[number])
+        self.down(slot, sent).start()
+
+    def first_hop(self):
+        self.when(1)(lambda: self.pass_up(0, 0, 0))
+        self.when(DEPTH - 2)(lambda: self.pass_down(0, 0, 0))
+
+    def second_hop(self):
+        self.when(1)(lambda: self.pass_up(2, 1, 1))
+        self.when(DEPTH - 2)(lambda: self.pass_down(2, 1, 1))
+
+    def third_hop(self):
+        self.when(1)(lambda: self.pass_down(1, 0, 0))
+        self.when(DEPTH - 2)(lambda: self.pass_up(1, 0, 0))
+
+    def last_hop(self):
+        below, above, wide = self.below, self.above, jnp.float32
+
+        @self.when(0)
+        def _():
+            self.wait_above(0)
+            self.own[...] += above[0].astype(wide)
+
+        @self.when(1)
+        def _():
+            self.wait_below(2)
+            self.wait_above(1)
+            self.own[...] += below[2].astype(wide) + above[1].astype(wide)
+
+        @self.when(DEPTH - 2)
+        def _():
+            self.wait_below(1)
+            self.wait_above(2)
+            self.own[...] += below[1].astype(wide) + above[2].astype(wide)
+
+        @self.when(DEPTH - 1)
+        def _():
+            self.wait_below(0)
+            self.own[...] += below[0].astype(wide)
+
+    def sent_all(self):
+        @self.when(0)
+        def _():
+            for slot in range(DEPTH - 1):
+                self.up(slot, slot).wait_send()
+
+        @self.when(DEPTH - 1)
+        def _():
+            for slot in range(DEPTH - 1):
+                self.down(slot, slot).wait_send()
+
+        @self.when(1)
+        def _():
+            self.up(0, 0).wait_send()
+            self.up(2, 1).wait_send()
+            self.down(1, 0).wait_send()
+
+        @self.when(DEPTH - 2)
+        def _():
+            self.down(0, 0).wait_send()
+            self.down(2, 1).wait_send()
+            self.up(1, 0).wait_send()
 
 
 def chain_sems():
@@ -950,9 +1077,7 @@
             attend_one(Heads(b, t, z, y, q_ref, kv_ref, okv_ref), att_ref)
             return carry
 
-        lax.fori_loop(0, 2 * LOCAL_HEADS // 2, attend, 0)
-        if b == 0:
-            grads.third()
+        lax.fori_loop(0, LOCAL_HEADS, attend, 0)
 
     rows_x.wait_recv()
     rows_corner.wait_recv()
@@ -967,35 +1092,36 @@
         )
 
     def branch(i, carry):
-        k = DEPTH - 1 - i
+        k = far_first(i, z)
 
         @pl.when(i >= 2)
         def _():
-            core_copy(k + 2).wait_send()
-
-        core_send[k % 2] = term(DEPTH + k).astype(low)
-        core_copy(k).start()
+            core_copy(i - 2).wait_send()
+
+        core_send[i % 2] = term(DEPTH + k).astype(low)
+        core_copy(i).start()
         own = term(k)
-        core_copy(k).wait_recv()
-        both = own + core_recv[k].astype(wide)
-
-        @pl.when(k > 0)
+        core_copy(i).wait_recv()
+        both = own + core_recv[i].astype(wide)
+
+        @pl.when(i < DEPTH - 1)
         def _():
-            terms[k - 1] = both.astype(low)
-
-        @pl.when(k == 0)
+            terms[i] = both.astype(low)
+
+        @pl.when(i == DEPTH - 1)
         def _():
             own_sum[...] = both
 
         return carry
 
+    grads.third()
     lax.fori_loop(0, DEPTH, branch, 0)
     write_out((own_sum, own_out), (terms, terms_out))
     grads.fourth()
     grads.end()
     tokens.end(False)
-    for k in range(2):
-        core_copy(k).wait_send()
+    for i in range(DEPTH - 2, DEPTH):
+        core_copy(i).wait_send()
     for piece in range(PIECES):
         pair_copy(piece).wait_send()
     for copy in started:
@@ -1202,14 +1328,12 @@
     up_ref,
     normed_ref,
     pieces_ref,
-    q_ref,
-    kv_ref,
-    okv_ref,
-    hidden_ref,
-    att_ref,
-    rows_ref,
-    own_sum,
-    terms,
+    q_in,
+    kv_in,
+    okv_in,
+    rows_in,
+    own_in,
+    terms_in,
     valid_ref,
     gate_xs,
     gate_xk,
@@ -1221,47 +1345,76 @@
     gate_x2s,
     gate_own_x,
     gate_own_y,
-    heads_out,
-    hidden_out,
+    gu_out,
+    dq_out,
+    dk_out,
+    dv_out,
+    got_dk,
+    got_dv,
+    layer_out,
+    q_ref,
+    kv_ref,
+    okv_ref,
+    rows_ref,
+    own_sum,
+    terms,
     gu_ref,
     dq_ref,
     dk_ref,
     dv_ref,
-    got_dk,
-    got_dv,
-    layer_out,
     attended_grad,
     odk_ref,
     odv_ref,
     key_sum,
     value_sum,
-    z_recv,
+    below,
+    above,
     token_rows,
-    z_s,
-    z_r,
+    up_s,
+    down_s,
+    below_r,
+    above_r,
     pair_s,
     pair_r,
     stage_s,
     stage_r,
-    local_sem,
+    load_sems,
+    out_sems,
 ):
     x, core, z, y = coordinates()
     low, wide = jnp.bfloat16, jnp.float32
     y_mate = (x * 2 + core, z * 2 + 1 - y)
 
-    def z_mate(turn):
-        return (x * 2 + core, lax.rem(z + turn, DEPTH) * 2 + y)
-
     x_mate = (2 - x * 2 + core, z * 2 + y)
-    greet([x_mate, y_mate] + [z_mate(turn) for turn in range(1, DEPTH)])
-    scattered = [
-        remote(terms.at[k - 1], z_recv.at[k - 1], z_s, z_r, k - 1, z_mate(DEPTH - k))
-        for k in range(1, DEPTH)
-    ]
-    for copy in scattered:
-        copy.start()
-    own_tokens = pltpu.make_async_copy(pieces_ref.at[0], token_rows, local_sem)
-    own_tokens.start()
+    loads = {}
+    for src, dst in (
+        (terms_in, terms),
+        (rows_in, rows_ref),
+        (q_in, q_ref),
+        (kv_in, kv_ref),
+        (okv_in, okv_ref),
+        (own_in, own_sum),
+        (pieces_ref.at[0], token_rows),
+    ):
+        load = pltpu.make_async_copy(src, dst, load_sems.at[len(loads)])
+        load.start()
+        loads[len(loads)] = load
+    written = []
+
+    def write_out(*pairs):
+        for src, dst in pairs:
+            copy = pltpu.make_async_copy(src, dst, out_sems.at[len(written)])
+            copy.start()
+            written.append(copy)
+
+    below_mate = (x * 2 + core, lax.rem(z + DEPTH - 1, DEPTH) * 2 + y)
+    above_mate = (x * 2 + core, lax.rem(z + 1, DEPTH) * 2 + y)
+    greet([x_mate, y_mate, below_mate, above_mate])
+    sums = ChainSum(terms, below, above, own_sum, x, core, z, y, (up_s, down_s, below_r, above_r))
+    loads[0].wait()
+    for turn in range(DEPTH - 1):
+        sums.start(turn)
+    loads[1].wait()
 
     def piece_body(grad_part, gate_part, up_part):
         piece = pl.program_id(0)
@@ -1280,6 +1433,40 @@
         grid=(PIECES,),
         in_specs=[piece_spec(r.shape[-1]) for r in (grads_ref, gate_ref, up_ref)],
     )(grads_ref, gate_ref, up_ref)
+
+    write_out((gu_ref, gu_out))
+    total, width = normed_ref.shape
+    size = width // PIECES
+    columns = gu_ref.shape[-1]
+    cut = gate_xs.shape[-1]
+
+    def right(first, last):
+        return gu_ref[...].reshape(total, columns)[:, first:last]
+
+    def whole_body(left, out):
+        term = times_transposed(left[...], right(0, cut)).astype(out.dtype)
+        out[...] = term.reshape(out.shape)
+
+    def split_body(left, keep, send):
+        split_rows(times_transposed(left[...], right(cut, columns)), y, keep, send)
+
+    def from_block(base):
+        return pl.BlockSpec((total, size), lambda i: (0, base + i))
+
+    def block_of(array):
+        return pl.BlockSpec((2,) + array.shape[1:], lambda i: (i,) + (0,) * (len(array.shape) - 1))
+
+    pltpu.emit_pipeline(
+        whole_body,
+        grid=(DEPTH,),
+        in_specs=[from_block((1 - x) * DEPTH)],
+        out_specs=[block_of(gate_xs)],
+    )(normed_ref, gate_xs)
+    gate_x = remote(gate_xs, gate_xr, stage_s, stage_r, 0, x_mate)
+    gate_x.start()
+    sums.first_hop()
+    for n in (2, 3, 4):
+        loads[n].wait()
 
     def pair_copies(b, t):
         size, pair = ROWS // 2, 2 * HEAD_DIM
@@ -1306,35 +1493,10 @@
 
     lax.fori_loop(0, PIECES, attend_back, 0)
 
-    total, width = normed_ref.shape
-    size = width // PIECES
-    columns = gu_ref.shape[-1]
-    cut = gate_xs.shape[-1]
-
-    def right(first, last):
-        return gu_ref[...].reshape(total, columns)[:, first:last]
-
-    def whole_body(left, out):
-        term = times_transposed(left[...], right(0, cut)).astype(out.dtype)
-        out[...] = term.reshape(out.shape)
-
-    def split_body(left, keep, send):
-        split_rows(times_transposed(left[...], right(cut, columns)), y, keep, send)
-
-    def from_block(base):
-        return pl.BlockSpec((total, size), lambda i: (0, base + i))
-
-    def block_of(array):
-        return pl.BlockSpec((2,) + array.shape[1:], lambda i: (i,) + (0,) * (len(array.shape) - 1))
-
-    pltpu.emit_pipeline(
-        whole_body,
-        grid=(DEPTH,),
-        in_specs=[from_block((1 - x) * DEPTH)],
-        out_specs=[block_of(gate_xs)],
-    )(normed_ref, gate_xs)
-    gate_x = remote(gate_xs, gate_xr, stage_s, stage_r, 0, x_mate)
-    gate_x.start()
+    write_out((dq_ref, dq_out), (dk_ref, dk_out), (dv_ref, dv_out))
+    sums.second_hop()
+    sums.third_hop()
+
     pltpu.emit_pipeline(
         split_body,
         grid=(PIECES,),
@@ -1344,28 +1506,6 @@
     gate_y = remote(gate_ys, gate_yr, stage_s, stage_r, 1, y_mate)
     gate_y.start()
 
-    flat_grads = grads_ref.reshape(total, width)
-    wide_size = 2 * size
-
-    def rows_body(right, heads, hidden):
-        grad = right[...]
-        attended = att_ref[...].reshape(total, HEAD_COLS)
-        term = times_transposed(attended, grad).astype(low)
-        heads[...] = term.reshape(heads.shape)
-        hidden_rows = hidden_ref[...].reshape(total, hidden_ref.shape[-1])
-        term = times_transposed(hidden_rows, grad).astype(low)
-        hidden[...] = term.reshape(hidden.shape)
-
-    def column_block(array):
-        return pl.BlockSpec(array.shape[:2] + (wide_size,), lambda i: (0, 0, i))
-
-    pltpu.emit_pipeline(
-        rows_body,
-        grid=(width // wide_size,),
-        in_specs=[pl.BlockSpec((total, wide_size), lambda i: (0, i))],
-        out_specs=[column_block(heads_out), column_block(hidden_out)],
-    )(flat_grads, heads_out, hidden_out)
-
     pltpu.emit_pipeline(
         whole_body,
         grid=(DEPTH,),
@@ -1373,32 +1513,40 @@
         out_specs=[block_of(gate_xk)],
     )(normed_ref, gate_xk)
 
+    loads[5].wait()
+    loads[6].wait()
+    sums.last_hop()
+    for first in range(0, ROWS, 64):
+        rows = pl.ds(first, 64)
+        layer = token_rows[rows].astype(wide) + valid_ref[rows] * own_sum[rows]
+        layer_out[rows] = layer.astype(low)
+
     def sums_body(xk, xr, yk, yr, yk_own, yr_own, y2s, x2s, own_x, own_y):
-        y2s[0] = (xk[0, 1 - y] + xr[0, 1 - y].astype(wide)).astype(low)
-        own_x[0] = xk[0, y] + xr[0, y].astype(wide)
-        x2s[0] = (yk[0] + yr[0].astype(wide)).astype(low)
-        own_y[0] = yk_own[0] + yr_own[0].astype(wide)
-
-    def one_block(array, base=0):
+        y2s[...] = (xk[:, 1 - y] + xr[:, 1 - y].astype(wide)).astype(low)
+        own_x[...] = xk[:, y] + xr[:, y].astype(wide)
+        x2s[...] = (yk[...] + yr[...].astype(wide)).astype(low)
+        own_y[...] = yk_own[...] + yr_own[...].astype(wide)
+
+    def two_blocks(array, base=0):
         return pl.BlockSpec(
-            (1,) + array.shape[1:], lambda i: (base + i,) + (0,) * (len(array.shape) - 1)
+            (2,) + array.shape[1:], lambda i: (base + i,) + (0,) * (len(array.shape) - 1)
         )
 
     gate_x.wait_recv()
     gate_y.wait_recv()
-    theirs, ours = (1 - x) * PIECES, x * PIECES
+    theirs, ours = (1 - x) * DEPTH, x * DEPTH
     pltpu.emit_pipeline(
         sums_body,
-        grid=(PIECES,),
+        grid=(DEPTH,),
         in_specs=[
-            one_block(gate_xk),
-            one_block(gate_xr),
-            one_block(gate_yk, theirs),
-            one_block(gate_yr, theirs),
-            one_block(gate_yk, ours),
-            one_block(gate_yr, ours),
+            two_blocks(gate_xk),
+            two_blocks(gate_xr),
+            two_blocks(gate_yk, theirs),
+            two_blocks(gate_yr, theirs),
+            two_blocks(gate_yk, ours),
+            two_blocks(gate_yr, ours),
         ],
-        out_specs=[one_block(r) for r in (gate_y2s, gate_x2s, gate_own_x, gate_own_y)],
+        out_specs=[two_blocks(r) for r in (gate_y2s, gate_x2s, gate_own_x, gate_own_y)],
     )(
         gate_xk,
         gate_xr,
@@ -1411,46 +1559,39 @@
         gate_own_x,
         gate_own_y,
     )
-    own_tokens.wait()
-    for copy in scattered:
-        copy.wait_recv()
-    for first in range(0, ROWS, 64):
-        rows = pl.ds(first, 64)
-        branch = own_sum[rows]
-        for k in range(DEPTH - 1):
-            branch = branch + z_recv[k, rows].astype(wide)
-        layer_out[rows] = (token_rows[rows].astype(wide) + valid_ref[rows] * branch).astype(low)
-
     for b in range(2):
         for t in range(DEPTH):
             for copy in pair_copies(b, t):
                 copy.wait_recv()
                 copy.wait_send()
-    for copy in scattered:
-        copy.wait_send()
+    sums.sent_all()
+    for copy in written:
+        copy.wait()
     for copy in (gate_x, gate_y):
         copy.wait_send()
 
 
 def backward(
-    grads, gate, up, normed, pieces, queries, pairs, other_pairs, hidden, attended, rows_out,
-    own_sum, terms, valid
+    grads, gate, up, normed, pieces, queries, pairs, other_pairs, rows_out, own_sum, terms, valid
 ):
     low, wide = jnp.bfloat16, jnp.float32
     width = pieces.shape[-1]
-    each = hidden.shape[-1]
-    columns = 2 * each
-    cut = -(-columns // 256) * 128
+    columns = 2 * gate.shape[-1]
+    cut = columns - 128
     rows = width // 32
-    head_rows = HEAD_DIM
     anywhere = pl.BlockSpec(memory_space=pl.ANY)
     inside = pl.BlockSpec(memory_space=pltpu.VMEM)
     shape = jax.ShapeDtypeStruct
     dma = pltpu.SemaphoreType.DMA
+    heads = shape((PIECES, ROWS, HEAD_COLS), wide)
+    heads_low = shape((PIECES, ROWS, HEAD_COLS), low)
+    gate_up = shape((PIECES, ROWS, columns), low)
+    part = shape((DEPTH - 1, ROWS, width), low)
+    half = shape((DEPTH * ROWS, 2 * HEAD_DIM), wide)
     return pl.pallas_call(
         backward_kernel,
-        in_specs=[anywhere] * 5 + [inside] * 9,
-        out_specs=[anywhere] * 12 + [inside] * 7,
+        in_specs=[anywhere] * 11 + [inside],
+        out_specs=[anywhere] * 16 + [inside],
         out_shape=[
             shape((PIECES, 2, rows, cut), low),
             shape((PIECES, 2, rows, cut), wide),
@@ -1462,39 +1603,53 @@
             shape((PIECES, rows, columns - cut), low),
             shape((PIECES, rows, cut), wide),
             shape((PIECES, rows, columns - cut), wide),
-            shape((4, head_rows, width), low),
-            shape((4, each // 4, width), low),
-            shape((PIECES, ROWS, columns), low),
-            shape((PIECES, ROWS, HEAD_COLS), wide),
-            shape((PIECES, ROWS, HEAD_COLS), wide),
-            shape((PIECES, ROWS, HEAD_COLS), wide),
-            shape((PIECES, ROWS, HEAD_COLS), low),
-            shape((PIECES, ROWS, HEAD_COLS), low),
+            gate_up,
+            heads,
+            heads,
+            heads,
+            heads_low,
+            heads_low,
             shape((ROWS, width), low),
         ],
         scratch_shapes=[
-            pltpu.VMEM((PIECES, ROWS, HEAD_COLS), low),
-            pltpu.VMEM((PIECES, ROWS, HEAD_COLS), low),
-            pltpu.VMEM((PIECES, ROWS, HEAD_COLS), low),
-            pltpu.VMEM((DEPTH * ROWS, 2 * HEAD_DIM), wide),
-            pltpu.VMEM((DEPTH * ROWS, 2 * HEAD_DIM), wide),
-            pltpu.VMEM((DEPTH - 1, ROWS, width), low),
-            pltpu.VMEM((ROWS, width), low),
+            pltpu.VMEM(v.shape, v.dtype)
+            for v in (
+                queries,
+                pairs,
+                other_pairs,
+                rows_out,
+                own_sum,
+                terms,
+                gate_up,
+                heads,
+                heads,
+                heads,
+                heads_low,
+                heads_low,
+                heads_low,
+                half,
+                half,
+                part,
+                part,
+                shape((ROWS, width), low),
+            )
+        ]
+        + [
+            dma((DEPTH - 1,)),
+            dma((DEPTH - 1,)),
             dma((DEPTH - 1,)),
             dma((DEPTH - 1,)),
             dma((2, PIECES)),
             dma((2, PIECES)),
             dma((2,)),
             dma((2,)),
-            dma(()),
+            dma((7,)),
+            dma((4,)),
         ],
         compiler_params=params(62, collective_id=3, has_side_effects=True),
         cost_estimate=cost(0, 64 * MIB),
         name="backward",
-    )(
-        grads, gate, up, normed, pieces, queries, pairs, other_pairs, hidden, attended, rows_out,
-        own_sum, terms, valid
-    )
+    )(grads, gate, up, normed, pieces, queries, pairs, other_pairs, rows_out, own_sum, terms, valid)
 
 
 def finish_kernel(
@@ -1513,8 +1668,9 @@
     gate_x2s,
     gate_sum_x,
     gate_sum_y,
-    heads_term,
-    hidden_term,
+    grads_ref,
+    hidden_ref,
+    att_ref,
     wi_ref,
     wg_ref,
     gain_ref,
@@ -1525,6 +1681,8 @@
     gate_rows,
     inward_rows_out,
     vec_out,
+    heads_term,
+    hidden_term,
     heads_r,
     heads_2s,
     heads_2r,
@@ -1603,11 +1761,6 @@
         load.start()
     gate_y = begin(remote(gate_y2s, gate_y2r, stage_s, stage_r, (0, 2), y_mate))
     gate_x = begin(remote(gate_x2s, gate_x2r, stage_s, stage_r, (0, 3), x_mate))
-    heads_x = begin(remote(heads_term.at[1 - x], heads_r, stage_s, stage_r, (2, 0), x_mate))
-    hidden_y = [
-        remote(hidden_term.at[i, 1 - y], hidden_r.at[i], stage_s, stage_r, (3, i), y_mate)
-        for i in range(2)
-    ]
     own_tokens = pltpu.make_async_copy(pieces_ref.at[0], token_rows, local_sems.at[4])
     own_tokens.start()
 
@@ -1616,107 +1769,12 @@
     def core_copy(k):
         return remote(core_send.at[k % 2], core_recv.at[k], core_s, core_r, k, core_mate)
 
-    def up_copy(slot, number):
-        goal = device(x, core, z + 1, y)
-        return remote_to(
-            z_send.at[slot], below.at[number], up_s.at[slot], below_r.at[number], goal
-        )
-
-    def down_copy(slot, number):
-        goal = device(x, core, z - 1, y)
-        return remote_to(
-            z_send.at[slot], above.at[number], down_s.at[slot], above_r.at[number], goal
-        )
-
-    def order(i):
-        inner = jnp.where(z == 1, select(i, 2, 1, 3), select(i, 2, 3, 1))
-        outer = jnp.where(z == 0, select(i, 1, 2, 3), select(i, 3, 2, 1))
-        return jnp.where((z == 0) | (z == DEPTH - 1), outer, inner)
+    sums = ChainSum(
+        z_send, below, above, own_sum, x, core, z, y, (up_s, down_s, below_r, above_r)
+    )
 
     def piece_of(i):
-        return order(i // 2) + DEPTH * (1 - i % 2)
-
-    def arrived(box, recvs, number):
-        copy = remote_to(box.at[number], box.at[number], up_s.at[0], recvs.at[number], core_mate)
-        copy.wait_recv()
-
-    def add_and(slot, box, recvs, number, copy):
-        arrived(box, recvs, number)
-        z_send[slot] = (z_send[slot].astype(wide) + box[number].astype(wide)).astype(low)
-        copy.start()
-
-    def first_hop():
-        @pl.when(z == 1)
-        def _():
-            add_and(0, below, below_r, 0, up_copy(0, 0))
-
-        @pl.when(z == DEPTH - 2)
-        def _():
-            add_and(0, above, above_r, 0, down_copy(0, 0))
-
-    def second_hop():
-        @pl.when(z == 1)
-        def _():
-            add_and(2, below, below_r, 1, up_copy(2, 1))
-
-        @pl.when(z == DEPTH - 2)
-        def _():
-            add_and(2, above, above_r, 1, down_copy(2, 1))
-
-    def third_hop():
-        @pl.when(z == 1)
-        def _():
-            add_and(1, above, above_r, 0, down_copy(1, 0))
-
-        @pl.when(z == DEPTH - 2)
-        def _():
-            add_and(1, below, below_r, 0, up_copy(1, 0))
-
-    def last_hop():
-        @pl.when(z == 0)
-        def _():
-            arrived(above, above_r, 0)
-            own_sum[...] += above[0].astype(wide)
-
-        @pl.when(z == 1)
-        def _():
-            arrived(below, below_r, 2)
-            arrived(above, above_r, 1)
-            own_sum[...] += below[2].astype(wide) + above[1].astype(wide)
-
-        @pl.when(z == DEPTH - 2)
-        def _():
-            arrived(below, below_r, 1)
-            arrived(above, above_r, 2)
-            own_sum[...] += below[1].astype(wide) + above[2].astype(wide)
-
-        @pl.when(z == DEPTH - 1)
-        def _():
-            arrived(below, below_r, 0)
-            own_sum[...] += below[0].astype(wide)
-
-    def sent_all():
-        @pl.when(z == 0)
-        def _():
-            for slot in range(DEPTH - 1):
-                up_copy(slot, slot).wait_send()
-
-        @pl.when(z == DEPTH - 1)
-        def _():
-            for slot in range(DEPTH - 1):
-                down_copy(slot, slot).wait_send()
-
-        @pl.when(z == 1)
-        def _():
-            up_copy(0, 0).wait_send()
-            up_copy(2, 1).wait_send()
-            down_copy(1, 0).wait_send()
-
-        @pl.when(z == DEPTH - 2)
-        def _():
-            down_copy(0, 0).wait_send()
-            down_copy(2, 1).wait_send()
-            up_copy(1, 0).wait_send()
+        return far_first(i // 2, z) + DEPTH * (1 - i % 2)
 
     def to_rows(which, fin, rows):
         slot = core * DEPTH + z
@@ -1748,7 +1806,7 @@
             ],
             2,
         ).astype(low)
-        for copy in to_rows(0, gate_fin, gate_rows) + hidden_y:
+        for copy in to_rows(0, gate_fin, gate_rows):
             copy.start()
 
     def piece_body(
@@ -1776,7 +1834,7 @@
         vec_sum[4:5, : 3 * HEAD_COLS] += jnp.sum(narrow.astype(wide), axis=0, keepdims=True)
 
         pl.when(step == GATE_STEP)(gate_done)
-        pl.when(step == PIECES - 1)(first_hop)
+        pl.when(step == PIECES - 1)(sums.first_hop)
 
         @pl.when(step % 2 == 0)
         def _():
@@ -1795,14 +1853,7 @@
             @pl.when(turn < DEPTH - 1)
             def _():
                 z_send[turn] = both.astype(low)
-
-                @pl.when(z == 0)
-                def _():
-                    up_copy(turn, turn).start()
-
-                @pl.when(z == DEPTH - 1)
-                def _():
-                    down_copy(turn, turn).start()
+                sums.start(turn)
 
             @pl.when(turn == DEPTH - 1)
             def _():
@@ -1874,6 +1925,71 @@
     started.append(inward_x)
     inward_y = begin(remote(inward_ys, inward_yr, stage_s, stage_r, (1, 1), y_mate))
 
+    def rows_grads(att, hidden):
+        loads = [
+            pltpu.make_async_copy(att_ref, att, local_sems.at[5]),
+            pltpu.make_async_copy(hidden_ref, hidden, local_sems.at[6]),
+        ]
+        for load in loads:
+            load.start()
+        for load in loads:
+            load.wait()
+
+        def body(right, heads_part, hidden_part):
+            grad = right[...]
+            term = times_transposed(att[...].reshape(total, att.shape[2]), grad)
+            heads_part[...] = term.astype(low).reshape(heads_part.shape)
+            term = times_transposed(hidden[...].reshape(total, hidden.shape[2]), grad)
+            hidden_part[...] = term.astype(low).reshape(hidden_part.shape)
+
+        def columns_of(array):
+            return pl.BlockSpec(array.shape[:3] + (2 * size,), lambda i: (0, 0, 0, i))
+
+        pltpu.emit_pipeline(
+            body,
+            grid=(width // (2 * size),),
+            in_specs=[pl.BlockSpec((total, 2 * size), lambda i: (0, i))],
+            out_specs=[columns_of(heads_term), columns_of(hidden_term)],
+        )(grads_ref, heads_term, hidden_term)
+
+    sums.second_hop()
+    pl.run_scoped(
+        rows_grads, *[pltpu.VMEM(r.shape, r.dtype) for r in (att_ref, hidden_ref)]
+    )
+    inward_x.wait_recv()
+    inward_y2s[...] = (inward_xk[:, 1 - y] + inward_xr[:, 1 - y].astype(wide)).astype(low)
+    inward_over_y = begin(remote(inward_y2s, inward_y2r, stage_s, stage_r, (1, 2), y_mate))
+    inward_y.wait_recv()
+    other = pl.ds((1 - x) * PIECES, PIECES)
+    inward_x2s[...] = (inward_yk[other] + inward_yr[other].astype(wide)).astype(low)
+    inward_over_x = begin(remote(inward_x2s, inward_x2r, stage_s, stage_r, (1, 3), x_mate))
+    left, right = pl.ds(0, width // 2), pl.ds(width // 2, width // 2)
+    heads_x = begin(remote(heads_term.at[1 - x], heads_r, stage_s, stage_r, (2, 0), x_mate))
+    hidden_x = begin(
+        remote(
+            hidden_term.at[1 - x, :, :, left],
+            hidden_r.at[pl.ds(0, 2)],
+            stage_s,
+            stage_r,
+            (3, 0),
+            x_mate,
+        )
+    )
+    hidden_y = [
+        begin(
+            remote(
+                hidden_term.at[n, 1 - y, :, right],
+                hidden_r.at[2 + n],
+                stage_s,
+                stage_r,
+                (3, 1 + n),
+                y_mate,
+            )
+        )
+        for n in range(2)
+    ]
+    sums.third_hop()
+
     vector_x.wait_recv()
     vec_sum_x = vec_sum[...] + vec_x[...]
     vector_x.wait_send()
@@ -1881,40 +1997,19 @@
     vector_y = remote(vec_sum, vec_y, vec_s, vec_r, 1, y_mate)
     vector_y.start()
 
-    def add_two(one, two, out):
-        out[...] = (one[...].astype(wide) + two[...].astype(wide)).astype(out.dtype)
-
-    second_hop()
-    third_hop()
-
-    chunk = heads_term.shape[-1] // 2
-
-    def flat_spec(rows):
-        return pl.BlockSpec((rows, chunk), lambda i: (0, i))
-
-    def row_sum(one, two, out):
-        spec = flat_spec(one.shape[0])
-        pltpu.emit_pipeline(
-            add_two, grid=(2,), in_specs=[spec, spec], out_specs=[spec]
-        )(one, two, out)
-
-    def row_total(one, two, three, out):
-        spec = flat_spec(one.shape[0])
-
-        def body(one, two, three, out):
-            out[...] = one[...].astype(wide) + two[...].astype(wide) + three[...].astype(wide)
-
-        pltpu.emit_pipeline(
-            body, grid=(2,), in_specs=[spec] * 3, out_specs=[spec]
-        )(one, two, three, out)
-
-    heads_x.wait_recv()
-    row_sum(heads_term.at[x, 1 - y], heads_r.at[1 - y], heads_2s)
-    heads_y = begin(remote(heads_2s, heads_2r, stage_s, stage_r, (2, 2), y_mate))
-    for copy in hidden_y:
-        copy.wait_recv()
-    row_sum(hidden_term.at[1 - x, y], hidden_r.at[1 - x], hidden_2s)
-    hidden_x = begin(remote(hidden_2s, hidden_2r, stage_s, stage_r, (3, 2), x_mate))
+    inward_over_y.wait_recv()
+    inward_over_x.wait_recv()
+    own = pl.ds(x * PIECES, PIECES)
+    inward_fin[...] = jnp.concatenate(
+        [
+            inward_xk[:, y] + inward_xr[:, y].astype(wide) + inward_y2r[...].astype(wide),
+            inward_yk[own] + inward_yr[own].astype(wide) + inward_x2r[...].astype(wide),
+        ],
+        2,
+    ).astype(low)
+    inward_rest = to_rows(1, inward_fin, inward_rows_out)
+    for copy in inward_rest:
+        copy.start()
 
     vector_y.wait_recv()
     vec_sum_y = vec_sum[...] + vec_y[...]
@@ -1937,33 +2032,40 @@
             )
         )
 
-    inward_x.wait_recv()
-    inward_y2s[...] = (inward_xk[:, 1 - y] + inward_xr[:, 1 - y].astype(wide)).astype(low)
-    inward_over_y = begin(remote(inward_y2s, inward_y2r, stage_s, stage_r, (1, 2), y_mate))
-    inward_y.wait_recv()
-    other = pl.ds((1 - x) * PIECES, PIECES)
-    inward_x2s[...] = (inward_yk[other] + inward_yr[other].astype(wide)).astype(low)
-    inward_over_x = begin(remote(inward_x2s, inward_x2r, stage_s, stage_r, (1, 3), x_mate))
+    def row_sum(*refs):
+        spec = pl.BlockSpec((refs[0].shape[0], refs[0].shape[1] // 2), lambda i: (0, i))
+
+        def body(*parts):
+            total = parts[0][...].astype(wide)
+            for part in parts[1:-1]:
+                total = total + part[...].astype(wide)
+            parts[-1][...] = total.astype(parts[-1].dtype)
+
+        pltpu.emit_pipeline(
+            body, grid=(2,), in_specs=[spec] * (len(refs) - 1), out_specs=[spec]
+        )(*refs)
+
+    heads_x.wait_recv()
+    row_sum(heads_term.at[x, 1 - y], heads_r.at[1 - y], heads_2s)
+    heads_y = begin(remote(heads_2s, heads_2r, stage_s, stage_r, (2, 2), y_mate))
+    for copy in hidden_y:
+        copy.wait_recv()
+    row_sum(hidden_term.at[1 - x, y, :, right], hidden_r.at[2 + 1 - x], hidden_2s.at[1])
+    over_x = begin(remote(hidden_2s.at[1], hidden_2r.at[1], stage_s, stage_r, (2, 3), x_mate))
+    hidden_x.wait_recv()
+    row_sum(hidden_term.at[x, 1 - y, :, left], hidden_r.at[1 - y], hidden_2s.at[0])
+    over_y = begin(remote(hidden_2s.at[0], hidden_2r.at[0], stage_s, stage_r, (3, 3), y_mate))
     heads_y.wait_recv()
-    row_total(heads_term.at[x, y], heads_r.at[y], heads_2r, heads_out)
-    hidden_x.wait_recv()
-    row_total(hidden_term.at[x, y], hidden_r.at[x], hidden_2r, hidden_out)
-    inward_over_y.wait_recv()
-    inward_over_x.wait_recv()
-    own = pl.ds(x * PIECES, PIECES)
-    inward_fin[...] = jnp.concatenate(
-        [
-            inward_xk[:, y] + inward_xr[:, y].astype(wide) + inward_y2r[...].astype(wide),
-            inward_yk[own] + inward_yr[own].astype(wide) + inward_x2r[...].astype(wide),
-        ],
-        2,
-    ).astype(low)
-    inward_rest = to_rows(1, inward_fin, inward_rows_out)
-    for copy in inward_rest:
-        copy.start()
+    row_sum(heads_term.at[x, y], heads_r.at[y], heads_2r, heads_out)
+    over_x.wait_recv()
+    row_sum(
+        hidden_term.at[x, y, :, right], hidden_r.at[2 + x], hidden_2r.at[1], hidden_out.at[:, right]
+    )
+    over_y.wait_recv()
+    row_sum(hidden_term.at[x, y, :, left], hidden_r.at[y], hidden_2r.at[0], hidden_out.at[:, left])
 
     own_tokens.wait()
-    last_hop()
+    sums.last_hop()
     for first in range(0, ROWS, 64):
         rows = pl.ds(first, 64)
         grad = own_sum[rows]
@@ -1978,19 +2080,17 @@
 
     for copy in to_rows(0, gate_fin, gate_rows) + inward_rest:
         copy.wait()
-    for copy in hidden_y:
-        copy.wait_send()
     for copy in vectors:
         copy.wait_recv()
     for copy in started:
         copy.wait_send()
     for turn in range(DEPTH - 2, DEPTH):
         core_copy(turn).wait_send()
-    sent_all()
+    sums.sent_all()
 
 
 def finish(
-    parts, gate_up_grad, pieces, tables, normed, gate_up, heads, hidden, weights, gain, cot
+    parts, gate_up_grad, pieces, tables, normed, gate_up, grads, hidden, attended, weights, gain, cot
 ):
     low, wide = jnp.bfloat16, jnp.float32
     width = pieces.shape[-1]
@@ -2001,7 +2101,7 @@
     half = 3 * HEAD_COLS // 2
 
     a, b = (value.shape[-1] for value in gate_up[:2])
-    heads_rows, hidden_rows = heads.shape[2], hidden.shape[2]
+    heads_rows, hidden_rows = HEAD_DIM, hidden.shape[2] // 4
     out_shapes = [
         shape((ROWS, width), low),
         shape((heads_rows, width), wide),
@@ -2011,18 +2111,20 @@
         shape((PIECES, 8, width // 2), wide),
     ]
     out_shapes += [
+        shape((2, 2, heads_rows, width), low),
+        shape((2, 2, hidden_rows, width), low),
         shape((2, heads_rows, width), low),
         shape((heads_rows, width), low),
         shape((heads_rows, width), low),
-        shape((2, hidden_rows, width), low),
-        shape((hidden_rows, width), low),
-        shape((hidden_rows, width), low),
+        shape((4, hidden_rows, width // 2), low),
+        shape((2, hidden_rows, width // 2), low),
+        shape((2, hidden_rows, width // 2), low),
     ]
     out_specs = [inside] + [anywhere] * 4 + [inside] + [anywhere] * (len(out_shapes) - 6)
     dma = pltpu.SemaphoreType.DMA
     outs = pl.pallas_call(
         finish_kernel,
-        in_specs=[anywhere] * 17 + [inside] * 4,
+        in_specs=[anywhere] * 18 + [inside] * 4,
         out_specs=out_specs,
         out_shape=out_shapes,
         scratch_shapes=[
@@ -2065,7 +2167,7 @@
             dma((3, PIECES)),
             dma((2,)),
             dma((2,)),
-            dma((5,)),
+            dma((7,)),
         ],
         compiler_params=params(63, collective_id=1, has_side_effects=True),
         cost_estimate=cost(0, 64 * MIB),
@@ -2077,8 +2179,9 @@
         *tables,
         normed,
         *gate_up,
-        heads,
+        grads,
         hidden,
+        attended,
         *weights,
         gain,
         cot,
@@ -2171,6 +2274,10 @@
     )
     gate_up = gate_up.reshape(width, -1)
     normed = normed.reshape(PIECES * ROWS, width)
+    def placed(value):
+        value = value.reshape(seqs, group_len, width)
+        return jnp.transpose(value, (1, 0, 2)).reshape(tokens.shape)
+
     outs = backward(
         grads,
         gate,
@@ -2180,14 +2287,13 @@
         queries,
         pairs,
         other_pairs,
-        hidden,
-        attended,
         rows_out,
         own_sum,
         terms,
         valid,
     )
-    heads_term, hidden_term, gate_up_grad, *parts, layer_out = outs[10:]
+    gate_up_grad, *parts, layer_out = outs[10:]
+    layer_out, normed = lax.optimization_barrier((placed(layer_out), normed))
     tokens_grad, outward_sum, down_sum, gate_up_rows, inward_rows_own, vectors = finish(
         parts,
         gate_up_grad,
@@ -2195,8 +2301,9 @@
         tables,
         normed,
         outs[6:10],
-        heads_term.reshape(2, 2, -1, width),
-        hidden_term.reshape(2, 2, -1, width),
+        grads.reshape(PIECES * ROWS, width),
+        hidden,
+        attended,
         (inward, gate_up),
         gain,
         own_cotangent,
@@ -2214,12 +2321,8 @@
     bias_all = jnp.concatenate([columns_sum[0], columns_sum[2], key_rot.reshape(-1)])
     bias_sum = one_of(bias_all.reshape(-1, bias_share), device, 0)
 
-    def placed(value):
-        value = value.reshape(seqs, group_len, width)
-        return jnp.transpose(value, (1, 0, 2)).reshape(tokens.shape)
-
     return (
-        placed(layer_out),
+        layer_out,
         placed(tokens_grad),
         gain_sum,
         shift_sum,

time: 475 us -> 463 us (0.975)
  Pallas kernels: 449 us -> 434 us
    pallas_call x2, Pallas kernels: 246 us -> 237 us  [the longest x1 141 us: finish(): pl.pallas_call(finish_kernel, in_specs=[anywhere] * 18 + [inside] * 4, ou...]
    pallas_call x1, Pallas kernels: 200 us -> 193 us  [forward(): pl.pallas_call(forward_kernel, in_specs=[anywhere] + [inside] + [anywhere...]
where the time goes in v7:
time: 463 us; the launch traced here: 454 us
  Pallas kernels  434 us (94%)
  local copies, waits for them, and re-layouts  17.2 us (4%)
    pallas_call x1, Pallas kernels, forward(): pl.pallas_call(forward_kernel, in_specs=[anywhere] + [inside] + [anywhere...  193 us
    pallas_call x1, Pallas kernels, finish(): pl.pallas_call(finish_kernel, in_specs=[anywhere] * 18 + [inside] * 4, ou...  141 us
    pallas_call x1, Pallas kernels, backward(): pl.pallas_call(backward_kernel, in_specs=[anywhere] * 11 + [inside], out_...  96.3 us

profile of v7, /device:TPU:11, one launch (start us, length us, event | category | flops | bytes accessed | tf_op | source)
XLA Modules:
  0.0 454.2 jit_solution(7841363881752028850)
XLA Ops:
  0.6 0.0 copy-start.3
  0.7 0.8 compare_convert_fusion
  1.5 0.6 compare_select_fusion.2.frequency_ref
  2.1 1.4 concatenate.6
  3.5 0.8 copy.25.valid_ref
  4.3 2.5 copy.23
  6.8 0.0 copy-done.3
  6.8 1.3 copy.24
  8.1 193.0 %forward.1 = (bf16[8,256,2048]{2,1,0:T(8,128)(2,1)}, bf16[8,256,2048]{2,1,0:T(8,128)(2,1)}, f32[8,256,704]{2,1,0:T(8,128)}, f32[8,256,704]{2,1,0:T(8,128)}, bf16...) custom-call(bf16[256,2048]{1,0:T(8,128)(2,1)} %bitcast.49, ...), custom_call_target="tpu_custom_call" | custom-call | bytes 1048576 | tf_op jit(solution)/shard_map/forward/pallas_call | solution.py:1159
  201.1 96.3 %backward.1 = (bf16[8,2,64,1280]{3,2,1,0:T(8,128)(2,1)}, f32[8,2,64,1280]{3,2,1,0:T(8,128)}, bf16[16,64,128]{2,1,0:T(8,128)(2,1)}, f32[16,64,128]{2,1,0:T(8,128)...) custom-call(bf16[8,256,2048]{2,1,0:T(8,128)(2,1)} %get-tuple-element, ...), custom_call_target="tpu_custom_call" | custom-call | bytes 1048576 | tf_op jit(solution)/shard_map/backward/pallas_call | solution.py:1591
  297.4 3.3 copy.34
  300.7 141.2 %finish.1 = (bf16[256,2048]{1,0:T(8,128)(2,1)}, f32[64,2048]{1,0:T(8,128)}, f32[176,2048]{1,0:T(8,128)}, bf16[8,64,1408]{2,1,0:T(8,128)(2,1)}, bf16[8,64,768]{2,...) custom-call(f32[8,256,256]{2,1,0:T(8,128)} %get-tuple-element.60.dq_, ...), custom_call_target="tpu_custom_call" | custom-call | bytes 1048576 | tf_op jit(solution)/shard_map/finish/pallas_call | solution.py:2125
  441.9 0.0 copy-start.1
  441.9 0.0 copy-start
  441.9 3.4 copy.33
  445.4 1.0 slice_reduce_fusion
  446.3 1.0 slice.32
  447.3 0.1 squeeze.33
  447.4 0.1 squeeze.31
  447.5 0.5 fusion.6
  448.0 0.1 reshape_squeeze.7
  448.1 0.1 reshape.190
  448.2 0.1 reshape.191
  448.3 0.6 constant_dynamic-slice_fusion
  448.8 0.0 copy-done.1
  448.8 1.2 place_rows.2
  450.1 0.0 copy-done
  450.1 0.0 copy-start.4
  450.1 0.0 copy-start.2
  450.1 2.0 place_rows.3
  452.1 0.0 copy-done.4
  452.1 0.8 copy.38
  452.9 0.0 copy-done.2
  452.9 1.1 copy.39
  (6 shorter events, 0.0 us)
Async XLA Ops:
  0.6 6.2 %copy-start.3 = (bf16[1,128,2,2048]{3,2,1,0:T(2,128)(2,1)S(1)}, bf16[1,128,2,2048]{3,2,1,0:T(2,128)(2,1)}, u32[]{:S(2)}) copy-start(bf16[1,128,2,2048]{3,2,1,0:T(2,128)(2,1)} %param.19) | copy-start | bytes 3145732
  441.9 6.9 %copy-start.1 = (bf16[8,64,768]{2,1,0:T(8,128)(2,1)S(1)}, bf16[8,64,768]{2,1,0:T(8,128)(2,1)}, u32[]{:S(2)}) copy-start(bf16[8,64,768]{2,1,0:T(8,128)(2,1)} %get-tuple-element.81.in_ref) | copy-start | bytes 2359300
  441.9 8.2 %copy-start = (bf16[8,64,1408]{2,1,0:T(8,128)(2,1)S(1)}, bf16[8,64,1408]{2,1,0:T(8,128)(2,1)}, u32[]{:S(2)}) copy-start(bf16[8,64,1408]{2,1,0:T(8,128)(2,1)} %get-tuple-element.83.in_ref) | copy-start | bytes 4325380
  450.1 2.0 copy-start.4
  450.1 2.8 copy-start.2

commit v8 on v7

--- a/solution.py
+++ b/solution.py
@@ -471,6 +471,20 @@
 
     def first(self):
         self.start(0, 1)
+
+    def first_apart(self):
+        pl.when(self.z < DEPTH // 2)(self.ups[0].start)
+        pl.when(self.z >= DEPTH // 2)(self.downs[0].start)
+
+    def first_rest(self):
+        pl.when(self.z == DEPTH // 2)(self.ups[0].start)
+        pl.when(self.z == DEPTH // 2 - 1)(self.downs[0].start)
+
+    def inner(self, step):
+        pl.when((self.z > 0) & (self.z < DEPTH - 1))(step)
+
+    def outer(self, step):
+        pl.when((self.z == 0) | (self.z == DEPTH - 1))(step)
 
     def second(self):
         @pl.when(self.z > 0)
@@ -1053,20 +1067,21 @@
     begin(rows_x)
     begin(rows_y)
     tokens.third()
+    grads.near()
+    grads.first_apart()
     core_arrived(2)
     project_pieces(2, 1)
     complete(1, gate_up_pairs, gate_up_corner)
     feed(0, 2)
     tokens.fourth()
-    grads.near()
-    grads.first()
+    grads.first_rest()
     core_arrived(far)
     project_pieces(3, 1)
+    grads.inner(grads.second)
     rows_y.wait_recv()
     block = rows_ref.at[x * 2 + 1 - y]
     rows_corner = begin(remote(block, block, rows_s, rows_r, 2, x_mate))
     feed(2, 2)
-    grads.second()
     write_out((q_ref, q_out), (kv_ref, kv_out), (wg_ref, wg_out))
 
     for b in range(2):
@@ -1114,9 +1129,11 @@
 
         return carry
 
-    grads.third()
+    grads.inner(grads.third)
     lax.fori_loop(0, DEPTH, branch, 0)
     write_out((own_sum, own_out), (terms, terms_out))
+    grads.outer(grads.second)
+    grads.outer(grads.third)
     grads.fourth()
     grads.end()
     tokens.end(False)
@@ -1923,6 +1940,12 @@
         in_specs=[pl.BlockSpec((total, size), lambda i: (0, block(i)))],
     )(normed_ref)
     started.append(inward_x)
+    vector_x.wait_recv()
+    vec_sum_x = vec_sum[...] + vec_x[...]
+    vector_x.wait_send()
+    vec_sum[...] = vec_sum_x
+    vector_y = remote(vec_sum, vec_y, vec_s, vec_r, 1, y_mate)
+    vector_y.start()
     inward_y = begin(remote(inward_ys, inward_yr, stage_s, stage_r, (1, 1), y_mate))
 
     def rows_grads(att, hidden):
@@ -1952,65 +1975,9 @@
             out_specs=[columns_of(heads_term), columns_of(hidden_term)],
         )(grads_ref, heads_term, hidden_term)
 
-    sums.second_hop()
     pl.run_scoped(
         rows_grads, *[pltpu.VMEM(r.shape, r.dtype) for r in (att_ref, hidden_ref)]
     )
-    inward_x.wait_recv()
-    inward_y2s[...] = (inward_xk[:, 1 - y] + inward_xr[:, 1 - y].astype(wide)).astype(low)
-    inward_over_y = begin(remote(inward_y2s, inward_y2r, stage_s, stage_r, (1, 2), y_mate))
-    inward_y.wait_recv()
-    other = pl.ds((1 - x) * PIECES, PIECES)
-    inward_x2s[...] = (inward_yk[other] + inward_yr[other].astype(wide)).astype(low)
-    inward_over_x = begin(remote(inward_x2s, inward_x2r, stage_s, stage_r, (1, 3), x_mate))
-    left, right = pl.ds(0, width // 2), pl.ds(width // 2, width // 2)
-    heads_x = begin(remote(heads_term.at[1 - x], heads_r, stage_s, stage_r, (2, 0), x_mate))
-    hidden_x = begin(
-        remote(
-            hidden_term.at[1 - x, :, :, left],
-            hidden_r.at[pl.ds(0, 2)],
-            stage_s,
-            stage_r,
-            (3, 0),
-            x_mate,
-        )
-    )
-    hidden_y = [
-        begin(
-            remote(
-                hidden_term.at[n, 1 - y, :, right],
-                hidden_r.at[2 + n],
-                stage_s,
-                stage_r,
-                (3, 1 + n),
-                y_mate,
-            )
-        )
-        for n in range(2)
-    ]
-    sums.third_hop()
-
-    vector_x.wait_recv()
-    vec_sum_x = vec_sum[...] + vec_x[...]
-    vector_x.wait_send()
-    vec_sum[...] = vec_sum_x
-    vector_y = remote(vec_sum, vec_y, vec_s, vec_r, 1, y_mate)
-    vector_y.start()
-
-    inward_over_y.wait_recv()
-    inward_over_x.wait_recv()
-    own = pl.ds(x * PIECES, PIECES)
-    inward_fin[...] = jnp.concatenate(
-        [
-            inward_xk[:, y] + inward_xr[:, y].astype(wide) + inward_y2r[...].astype(wide),
-            inward_yk[own] + inward_yr[own].astype(wide) + inward_x2r[...].astype(wide),
-        ],
-        2,
-    ).astype(low)
-    inward_rest = to_rows(1, inward_fin, inward_rows_out)
-    for copy in inward_rest:
-        copy.start()
-
     vector_y.wait_recv()
     vec_sum_y = vec_sum[...] + vec_y[...]
     vector_y.wait_send()
@@ -2031,6 +1998,55 @@
                 )
             )
         )
+
+    sums.second_hop()
+    inward_x.wait_recv()
+    inward_y2s[...] = (inward_xk[:, 1 - y] + inward_xr[:, 1 - y].astype(wide)).astype(low)
+    inward_over_y = begin(remote(inward_y2s, inward_y2r, stage_s, stage_r, (1, 2), y_mate))
+    inward_y.wait_recv()
+    other = pl.ds((1 - x) * PIECES, PIECES)
+    inward_x2s[...] = (inward_yk[other] + inward_yr[other].astype(wide)).astype(low)
+    inward_over_x = begin(remote(inward_x2s, inward_x2r, stage_s, stage_r, (1, 3), x_mate))
+    left, right = pl.ds(0, width // 2), pl.ds(width // 2, width // 2)
+    heads_x = begin(remote(heads_term.at[1 - x], heads_r, stage_s, stage_r, (2, 0), x_mate))
+    hidden_x = begin(
+        remote(
+            hidden_term.at[1 - x, :, :, left],
+            hidden_r.at[pl.ds(0, 2)],
+            stage_s,
+            stage_r,
+            (3, 0),
+            x_mate,
+        )
+    )
+    hidden_y = [
+        begin(
+            remote(
+                hidden_term.at[n, 1 - y, :, right],
+                hidden_r.at[2 + n],
+                stage_s,
+                stage_r,
+                (3, 1 + n),
+                y_mate,
+            )
+        )
+        for n in range(2)
+    ]
+    sums.third_hop()
+
+    inward_over_y.wait_recv()
+    inward_over_x.wait_recv()
+    own = pl.ds(x * PIECES, PIECES)
+    inward_fin[...] = jnp.concatenate(
+        [
+            inward_xk[:, y] + inward_xr[:, y].astype(wide) + inward_y2r[...].astype(wide),
+            inward_yk[own] + inward_yr[own].astype(wide) + inward_x2r[...].astype(wide),
+        ],
+        2,
+    ).astype(low)
+    inward_rest = to_rows(1, inward_fin, inward_rows_out)
+    for copy in inward_rest:
+        copy.start()
 
     def row_sum(*refs):
         spec = pl.BlockSpec((refs[0].shape[0], refs[0].shape[1] // 2), lambda i: (0, i))

time: 463 us -> 460 us (level)
  no operation moved by 1% of the time
where the time goes in v8:
time: 460 us; the launch traced here: 453 us
  Pallas kernels  432 us (94%)
  local copies, waits for them, and re-layouts  17.2 us (4%)
    pallas_call x1, Pallas kernels, forward(): pl.pallas_call(forward_kernel, in_specs=[anywhere] + [inside] + [anywhere...  193 us
    pallas_call x1, Pallas kernels, finish(): pl.pallas_call(finish_kernel, in_specs=[anywhere] * 18 + [inside] * 4, ou...  141 us
    pallas_call x1, Pallas kernels, backward(): pl.pallas_call(backward_kernel, in_specs=[anywhere] * 11 + [inside], out_...  95.1 us

profile of v8, /device:TPU:11, one launch (start us, length us, event | category | flops | bytes accessed | tf_op | source)
XLA Modules:
  0.0 453.0 jit_solution(17696519200074099921)
XLA Ops:
  0.6 0.0 copy-start.3
  0.7 0.8 compare_convert_fusion
  1.5 0.6 compare_select_fusion.2.frequency_ref
  2.1 1.4 concatenate.6
  3.5 0.8 copy.25.valid_ref
  4.3 2.5 copy.23
  6.8 0.0 copy-done.3
  6.8 1.3 copy.24
  8.1 192.7 %forward.1 = (bf16[8,256,2048]{2,1,0:T(8,128)(2,1)}, bf16[8,256,2048]{2,1,0:T(8,128)(2,1)}, f32[8,256,704]{2,1,0:T(8,128)}, f32[8,256,704]{2,1,0:T(8,128)}, bf16...) custom-call(bf16[256,2048]{1,0:T(8,128)(2,1)} %bitcast.49, ...), custom_call_target="tpu_custom_call" | custom-call | bytes 1048576 | tf_op jit(solution)/shard_map/forward/pallas_call | solution.py:1176
  200.9 95.1 %backward.1 = (bf16[8,2,64,1280]{3,2,1,0:T(8,128)(2,1)}, f32[8,2,64,1280]{3,2,1,0:T(8,128)}, bf16[16,64,128]{2,1,0:T(8,128)(2,1)}, f32[16,64,128]{2,1,0:T(8,128)...) custom-call(bf16[8,256,2048]{2,1,0:T(8,128)(2,1)} %get-tuple-element, ...), custom_call_target="tpu_custom_call" | custom-call | bytes 1048576 | tf_op jit(solution)/shard_map/backward/pallas_call | solution.py:1608
  296.0 3.3 copy.34
  299.2 141.4 %finish.1 = (bf16[256,2048]{1,0:T(8,128)(2,1)}, f32[64,2048]{1,0:T(8,128)}, f32[176,2048]{1,0:T(8,128)}, bf16[8,64,1408]{2,1,0:T(8,128)(2,1)}, bf16[8,64,768]{2,...) custom-call(f32[8,256,256]{2,1,0:T(8,128)} %get-tuple-element.60.dq_, ...), custom_call_target="tpu_custom_call" | custom-call | bytes 1048576 | tf_op jit(solution)/shard_map/finish/pallas_call | solution.py:2141
  440.7 0.0 copy-start.1
  440.7 0.0 copy-start
  440.7 3.4 copy.33
  444.1 1.0 slice_reduce_fusion
  445.1 1.0 slice.32
  446.1 0.1 squeeze.33
  446.2 0.1 squeeze.31
  446.3 0.5 fusion.6
  446.8 0.1 reshape_squeeze.7
  446.9 0.1 reshape.190
  446.9 0.1 reshape.191
  447.0 0.6 constant_dynamic-slice_fusion
  447.6 0.0 copy-done.1
  447.6 1.2 place_rows.2
  448.9 0.0 copy-done
  448.9 0.0 copy-start.4
  448.9 0.0 copy-start.2
  448.9 2.0 place_rows.3
  450.9 0.0 copy-done.4
  450.9 0.8 copy.38
  451.7 0.0 copy-done.2
  451.7 1.1 copy.39
  (6 shorter events, 0.0 us)
Async XLA Ops:
  0.6 6.2 %copy-start.3 = (bf16[1,128,2,2048]{3,2,1,0:T(2,128)(2,1)S(1)}, bf16[1,128,2,2048]{3,2,1,0:T(2,128)(2,1)}, u32[]{:S(2)}) copy-start(bf16[1,128,2,2048]{3,2,1,0:T(2,128)(2,1)} %param.19) | copy-start | bytes 3145732
  440.7 6.9 %copy-start.1 = (bf16[8,64,768]{2,1,0:T(8,128)(2,1)S(1)}, bf16[8,64,768]{2,1,0:T(8,128)(2,1)}, u32[]{:S(2)}) copy-start(bf16[8,64,768]{2,1,0:T(8,128)(2,1)} %get-tuple-element.81.in_ref) | copy-start | bytes 2359300
  440.7 8.2 %copy-start = (bf16[8,64,1408]{2,1,0:T(8,128)(2,1)S(1)}, bf16[8,64,1408]{2,1,0:T(8,128)(2,1)}, u32[]{:S(2)}) copy-start(bf16[8,64,1408]{2,1,0:T(8,128)(2,1)} %get-tuple-element.83.in_ref) | copy-start | bytes 4325380
  448.9 2.0 copy-start.4
  448.9 2.8 copy-start.2

commit v9 on v8

--- a/solution.py
+++ b/solution.py
@@ -356,7 +356,7 @@
 DEPTH = 4
 PIECES = 2 * DEPTH
 ROWS = 256
-GATE_STEP = 6
+GATE_STEP = 5
 HALFWAY = 5
 LOCAL_HEADS = 4
 HEAD_COLS = LOCAL_HEADS * HEAD_DIM
@@ -1414,8 +1414,9 @@
         (pieces_ref.at[0], token_rows),
     ):
         load = pltpu.make_async_copy(src, dst, load_sems.at[len(loads)])
-        load.start()
         loads[len(loads)] = load
+    loads[0].start()
+    loads[1].start()
     written = []
 
     def write_out(*pairs):
@@ -1432,6 +1433,8 @@
     for turn in range(DEPTH - 1):
         sums.start(turn)
     loads[1].wait()
+    for n in range(2, len(loads)):
+        loads[n].start()
 
     def piece_body(grad_part, gate_part, up_part):
         piece = pl.program_id(0)
@@ -1594,7 +1597,7 @@
     low, wide = jnp.bfloat16, jnp.float32
     width = pieces.shape[-1]
     columns = 2 * gate.shape[-1]
-    cut = columns - 128
+    cut = columns - 256
     rows = width // 32
     anywhere = pl.BlockSpec(memory_space=pl.ANY)
     inside = pl.BlockSpec(memory_space=pltpu.VMEM)

time: 460 us -> 461 us (level)
    pallas_call x1, Pallas kernels: 95.1 us -> 102 us  [backward(): pl.pallas_call(backward_kernel, in_specs=[anywhere] * 11 + [inside], out_...]
    pallas_call x1, Pallas kernels: 141 us -> 136 us  [finish(): pl.pallas_call(finish_kernel, in_specs=[anywhere] * 18 + [inside] * 4, ou...]
where the time goes in v9:
time: 461 us; the launch traced here: 454 us
  Pallas kernels  434 us (94%)
  local copies, waits for them, and re-layouts  17.2 us (4%)
    pallas_call x1, Pallas kernels, forward(): pl.pallas_call(forward_kernel, in_specs=[anywhere] + [inside] + [anywhere...  193 us
    pallas_call x1, Pallas kernels, finish(): pl.pallas_call(finish_kernel, in_specs=[anywhere] * 18 + [inside] * 4, ou...  136 us
    pallas_call x1, Pallas kernels, backward(): pl.pallas_call(backward_kernel, in_specs=[anywhere] * 11 + [inside], out_...  102 us

profile of v9, /device:TPU:11, one launch (start us, length us, event | category | flops | bytes accessed | tf_op | source)
XLA Modules:
  0.0 454.1 jit_solution(10834681667578706053)
XLA Ops:
  0.6 0.0 copy-start.3
  0.7 0.8 compare_convert_fusion
  1.5 0.6 compare_select_fusion.2.frequency_ref
  2.1 1.4 concatenate.6
  3.5 0.8 copy.25.valid_ref
  4.3 2.5 copy.23
  6.8 0.0 copy-done.3
  6.8 1.3 copy.24
  8.1 192.7 %forward.1 = (bf16[8,256,2048]{2,1,0:T(8,128)(2,1)}, bf16[8,256,2048]{2,1,0:T(8,128)(2,1)}, f32[8,256,704]{2,1,0:T(8,128)}, f32[8,256,704]{2,1,0:T(8,128)}, bf16...) custom-call(bf16[256,2048]{1,0:T(8,128)(2,1)} %bitcast.49, ...), custom_call_target="tpu_custom_call" | custom-call | bytes 1048576 | tf_op jit(solution)/shard_map/forward/pallas_call | solution.py:1176
  200.9 101.6 %backward.1 = (bf16[8,2,64,1152]{3,2,1,0:T(8,128)(2,1)}, f32[8,2,64,1152]{3,2,1,0:T(8,128)}, bf16[16,64,256]{2,1,0:T(8,128)(2,1)}, f32[16,64,256]{2,1,0:T(8,128)...) custom-call(bf16[8,256,2048]{2,1,0:T(8,128)(2,1)} %get-tuple-element, ...), custom_call_target="tpu_custom_call" | custom-call | bytes 1048576 | tf_op jit(solution)/shard_map/backward/pallas_call | solution.py:1611
  302.5 3.3 copy.34
  305.8 136.0 %finish.1 = (bf16[256,2048]{1,0:T(8,128)(2,1)}, f32[64,2048]{1,0:T(8,128)}, f32[176,2048]{1,0:T(8,128)}, bf16[8,64,1408]{2,1,0:T(8,128)(2,1)}, bf16[8,64,768]{2,...) custom-call(f32[8,256,256]{2,1,0:T(8,128)} %get-tuple-element.60.dq_, ...), custom_call_target="tpu_custom_call" | custom-call | bytes 1048576 | tf_op jit(solution)/shard_map/finish/pallas_call | solution.py:2144
  441.8 0.0 copy-start.1
  441.8 0.0 copy-start
  441.8 3.4 copy.33
  445.3 1.0 slice_reduce_fusion
  446.2 1.0 slice.32
  447.2 0.1 squeeze.33
  447.3 0.1 squeeze.31
  447.4 0.5 fusion.6
  447.9 0.1 reshape_squeeze.7
  448.0 0.1 reshape.190
  448.1 0.1 reshape.191
  448.2 0.6 constant_dynamic-slice_fusion
  448.7 0.0 copy-done.1
  448.7 1.2 place_rows.2
  450.0 0.0 copy-done
  450.0 0.0 copy-start.4
  450.0 0.0 copy-start.2
  450.0 2.0 place_rows.3
  452.0 0.0 copy-done.4
  452.0 0.8 copy.38
  452.8 0.0 copy-done.2
  452.8 1.1 copy.39
  (6 shorter events, 0.0 us)
Async XLA Ops:
  0.6 6.2 %copy-start.3 = (bf16[1,128,2,2048]{3,2,1,0:T(2,128)(2,1)S(1)}, bf16[1,128,2,2048]{3,2,1,0:T(2,128)(2,1)}, u32[]{:S(2)}) copy-start(bf16[1,128,2,2048]{3,2,1,0:T(2,128)(2,1)} %param.19) | copy-start | bytes 3145732
  441.8 6.9 %copy-start.1 = (bf16[8,64,768]{2,1,0:T(8,128)(2,1)S(1)}, bf16[8,64,768]{2,1,0:T(8,128)(2,1)}, u32[]{:S(2)}) copy-start(bf16[8,64,768]{2,1,0:T(8,128)(2,1)} %get-tuple-element.81.in_ref) | copy-start | bytes 2359300
  441.8 8.2 %copy-start = (bf16[8,64,1408]{2,1,0:T(8,128)(2,1)S(1)}, bf16[8,64,1408]{2,1,0:T(8,128)(2,1)}, u32[]{:S(2)}) copy-start(bf16[8,64,1408]{2,1,0:T(8,128)(2,1)} %get-tuple-element.83.in_ref) | copy-start | bytes 4325380
  450.0 2.0 copy-start.4
  450.0 2.8 copy-start.2
